TPU v7x, 128 devices: a whole 4x4x4 slice. The times are simulated.
128 devices in a mesh: seq: 8 (over z, core), tensor: 16 (over x, y).
Axes of the slice: x: 4, y: 4, z: 4, core: 2. Of those that a mesh axis runs over, the one named last changes fastest.
Arguments:
- span_tokens: bfloat16 [1024, 16, 1024], P(('seq', 'tensor')), may hold values from -6 to 6
- enc_dest: int32 [1024], replicated, may hold values from 0 to 1023, as said below
- passages: int32 [8], replicated, may hold values from 1 to 8, as said below
- req_slot: int32 [8], replicated, may hold values from 0 to 7, as said below
- block_mask: int32 [8, 8, 8], replicated, may hold values 0 or 1
- enc_qkv: bfloat16 [1024, 3072], P('tensor'), may hold values from -0.1875 to 0.1875
- enc_out: bfloat16 [1024, 1024], P('tensor'), may hold values from -0.1875 to 0.1875
- enc_up: bfloat16 [1024, 2048], P('tensor'), may hold values from -0.1875 to 0.1875
- enc_down: bfloat16 [2048, 1024], P('tensor'), may hold values from -0.125 to 0.125
- proj_in: bfloat16 [1024, 1024], replicated, may hold values from -0.1875 to 0.1875
- proj_out: bfloat16 [1024, 8192], P('tensor'), may hold values from -0.1875 to 0.1875
- norm_gain: float32 [8192], replicated, may hold values from 0.1 to 1.9
- q_weight: bfloat16 [8192, 8192], P(None, 'tensor'), may hold values from -0.0625 to 0.0625
- key_value_weight: bfloat16 [2, 8192, 1024], P(None, None, 'tensor'), may hold values from -0.0625 to 0.0625
- out_weight: bfloat16 [8192, 8192], P('tensor'), may hold values from -0.0625 to 0.0625
Outputs:
- mixed: bfloat16 [1024, 8192], P(('seq', 'tensor'))
Inputs may be any that keep to these rules, and one draw needn't show every extreme that they name: `enc_dest`: every number once; the 8 slots of each device (in order of seq+tensor) hold exactly 1 spans of requests whose decoder slot lies with each index of seq. `req_slot`: every number once; decoder slot s is the request of seq index s. `passages`: some request has 8.
All inputs are finite; a program needn't handle non-finite values.
Results may differ from a plain program's by a relative error of at most 0.03.
Values may be sent and summed in bfloat16 or wider, within the bound.
No kernel may reach another device: no remote copies, remote signals or barrier semaphores. Data moves between devices by JAX's collectives and lax.ppermute only.
A program may use at most 128 MiB of HBM per device.

v0:
```python
import math

import jax
import jax.numpy as jnp
from jax import lax
from jax.experimental import pallas as pl
from jax.experimental.pallas import tpu as pltpu
from jax.sharding import PartitionSpec as P

QUERY_HEAD_COUNT = 64
KEY_VALUE_HEADS = 8
HEAD_WIDTH = 128
EH = 16
CPP = 16
SPAN_LIMIT = 128
SIDE = 4
AXES = ("seq", "tensor")


def device_id(plane, core, x, y):
    return ((plane * 2 + core) * SIDE + x) * SIDE + y


def every_device():
    return [
        (plane, core, x, y)
        for plane in range(SIDE)
        for core in range(2)
        for x in range(SIDE)
        for y in range(SIDE)
    ]


def first_axis_is_y(core, phase):
    return (core == 0) == (phase == 1)


def ring_pairs(phase, distance):
    pairs = []
    for plane, core, x, y in every_device():
        if first_axis_is_y(core, phase):
            target = device_id(plane, core, x, (y + distance) % SIDE)
        else:
            target = device_id(plane, core, (x + distance) % SIDE, y)
        pairs.append((device_id(plane, core, x, y), target))
    return pairs


def ring_groups(phase):
    groups = []
    for plane in range(SIDE):
        for core in range(2):
            for fixed in range(SIDE):
                groups.append(
                    [
                        device_id(plane, core, fixed, moving)
                        if first_axis_is_y(core, phase)
                        else device_id(plane, core, moving, fixed)
                        for moving in range(SIDE)
                    ]
                )
    return groups


def to_ring(value, phase, distance):
    return lax.ppermute(value, AXES, ring_pairs(phase, distance))


def to_core(value):
    return lax.ppermute(value, "seq", [(index, index ^ 1) for index in range(8)])


def short_gather(spread):
    return lax.all_to_all(spread, AXES, 0, 0, axis_index_groups=ring_groups(1))


VMEM = pl.BlockSpec(memory_space=pltpu.VMEM)
SMEM = pl.BlockSpec(memory_space=pltpu.SMEM)
MIB = 2**20


def shape_of(shape, dtype=jnp.bfloat16):
    return jax.ShapeDtypeStruct(shape, dtype)


def whole_call(body, name, info, arrays, outs, scratch=(), limit=24, flops=0):
    moved = sum(array.size * array.dtype.itemsize for array in arrays)
    return pl.pallas_call(
        body,
        name=name,
        out_shape=outs,
        in_specs=[SMEM] + [VMEM] * len(arrays),
        out_specs=jax.tree.map(lambda _: VMEM, outs),
        scratch_shapes=list(scratch),
        compiler_params=pltpu.CompilerParams(vmem_limit_bytes=limit * MIB),
        cost_estimate=pl.CostEstimate(flops=flops, bytes_accessed=moved, transcendentals=0),
    )(info, *arrays)


def dot32(left, right):
    return jnp.dot(left, right, preferred_element_type=jnp.float32)


def gelu_exact(values):
    return 0.5 * values * (1.0 + lax.erf(values * (0.5**0.5)))


def spread_qkv(info, weight, out):
    cols = weight.shape[1] // 6
    for part in range(3):
        start = pl.multiple_of((2 * part + info[16]) * cols, cols)
        piece = weight[:, pl.ds(start, cols)]
        for copy in range(SIDE):
            out[copy, :, part * cols : (part + 1) * cols] = piece


def spread_rest(info, out_weight, up_weight, down_weight, out):
    core = info[16]
    rows, width = out_weight.shape
    cols = width // 2
    units = down_weight.shape[0] // 2
    pieces = [out_weight[:, pl.ds(pl.multiple_of(core * cols, cols), cols)]]
    for pair in range(up_weight.shape[1] // (4 * units)):
        halves = []
        for step in range(2):
            low = (2 * pair + step) * 2 * units
            halves.append(
                jnp.where(
                    core == 0,
                    up_weight[:, low : low + units].astype(jnp.float32),
                    up_weight[:, low + units : low + 2 * units].astype(jnp.float32),
                )
            )
        pieces.append(jnp.concatenate(halves, axis=1).astype(jnp.bfloat16))
    pieces.append(down_weight[pl.ds(pl.multiple_of(core * units, units), units), :])
    for copy in range(SIDE):
        at = 0
        for piece in pieces:
            out[copy, :, at : at + piece.shape[1]] = piece
            at += piece.shape[1]


def spread_proj(info, weight, out):
    cols = out.shape[2]
    for index in range(out.shape[0]):
        start = pl.multiple_of((2 * index + info[16]) * cols, cols)
        out[index] = weight[:, pl.ds(start, cols)]


def both_rows(info, mine, other, rows_out, pieces_out):
    half, width = mine.shape
    core = info[16]
    rows_out[pl.ds(pl.multiple_of(core * half, half), half), :] = mine[...]
    rows_out[pl.ds(pl.multiple_of((1 - core) * half, half), half), :] = other[...]
    piece = pieces_out.shape[2]
    for index in range(width // piece):
        pieces_out[index] = rows_out[:, index * piece : (index + 1) * piece]


def ring_dot(info, pieces, blocks, low, high):
    total = None
    for at, block in enumerate(blocks):
        act = jnp.concatenate([pieces[info[4 * at + step]] for step in range(SIDE)], axis=1)
        weight = block[:, :, low:high].reshape(act.shape[1], high - low)
        part = dot32(act, weight)
        total = part if total is None else total + part
    return total


def span_attention(info, pieces, w0, w1, w2, w3, context, mixed):
    cols = w0.shape[2]
    third = cols // 3
    mixed[...] = ring_dot(info, pieces, (w0, w1, w2, w3), 0, cols).astype(jnp.bfloat16)
    size = context.shape[2]
    half = mixed.shape[0] // 2
    span = 16
    row = lax.broadcasted_iota(jnp.int32, (half, half), 0) // span
    col = lax.broadcasted_iota(jnp.int32, (half, half), 1) // span
    same = row == col
    for head in range(third // size):
        for part in range(2):
            rows = slice(part * half, (part + 1) * half)
            query = mixed[rows, head * size : (head + 1) * size]
            key = mixed[rows, third + head * size : third + (head + 1) * size]
            value = mixed[rows, 2 * third + head * size : 2 * third + (head + 1) * size]
            scores = lax.dot_general(
                query, key, (((1,), (1,)), ((), ())), preferred_element_type=jnp.float32
            ) / math.sqrt(size)
            scores = jnp.where(same, scores, -1e30)
            top = jnp.max(scores, axis=1, keepdims=True)
            powers = jnp.exp(scores - top)
            probs = powers / jnp.sum(powers, axis=1, keepdims=True)
            context[head, rows, :] = dot32(probs.astype(jnp.bfloat16), value).astype(jnp.bfloat16)


def context_out(info, mine, other, w0, w1, w2, w3, attended, pieces):
    heads = mine.shape[0]
    core = info[16]
    pieces[pl.ds(core * heads, heads)] = mine[...]
    pieces[pl.ds((1 - core) * heads, heads)] = other[...]
    cols = attended.shape[1]
    attended[...] = ring_dot(info, pieces, (w0, w1, w2, w3), 0, cols).astype(jnp.bfloat16)


def norm_up(info, rows, mine, other, w0, w1, w2, w3, first_out, inner, pieces):
    core = info[16]
    cols = mine.shape[1]
    width = rows.shape[1]
    near = mine[...].astype(jnp.float32)
    far = other[...].astype(jnp.float32)
    low = rows[:, :cols].astype(jnp.float32) + jnp.where(core == 0, near, far)
    high = rows[:, cols:].astype(jnp.float32) + jnp.where(core == 0, far, near)
    mean = (jnp.sum(low, 1, keepdims=True) + jnp.sum(high, 1, keepdims=True)) / width
    low, high = low - mean, high - mean
    var = (jnp.sum(low * low, 1, keepdims=True) + jnp.sum(high * high, 1, keepdims=True)) / width
    scale = lax.rsqrt(var + 1e-05)
    first_out[:, :cols] = (low * scale).astype(jnp.bfloat16)
    first_out[:, cols:] = (high * scale).astype(jnp.bfloat16)
    size = pieces.shape[2]
    for index in range(pieces.shape[0]):
        pieces[index] = first_out[:, index * size : (index + 1) * size]
    total = ring_dot(info, pieces, (w0, w1, w2, w3), cols, w0.shape[2])
    act = gelu_exact(total).astype(jnp.bfloat16)
    unit = inner.shape[2]
    for index in range(inner.shape[0]):
        inner[index] = act[:, index * unit : (index + 1) * unit]


def down(info, inner, w0, w1, w2, w3, kept, sent, total):
    core = info[16]
    total[...] = ring_dot(info, inner, (w0, w1, w2, w3), 0, w0.shape[2])
    half = kept.shape[0]
    kept[...] = total[pl.ds(pl.multiple_of(core * half, half), half), :]
    sent[...] = total[pl.ds(pl.multiple_of((1 - core) * half, half), half), :].astype(jnp.bfloat16)


def norm_pool(info, kept, arrived, first_out, pick, out, lanes):
    half, width = kept.shape
    rows = pl.ds(pl.multiple_of(info[16] * half, half), half)
    values = first_out[rows, :].astype(jnp.float32) + (
        kept[...] + arrived[...].astype(jnp.float32)
    )
    mean = jnp.mean(values, axis=1, keepdims=True)
    values = values - mean
    values = values * lax.rsqrt(jnp.mean(values * values, axis=1, keepdims=True) + 1e-05)
    spans = pick.shape[1]
    pooled = jnp.mean(values.reshape(spans, half // spans, width), axis=1).astype(jnp.bfloat16)
    by_slot = dot32(pick[...], pooled)
    for index in range(width // 128):
        lanes[:, index, :] = by_slot[:, index * 128 : (index + 1) * 128]
    out[...] = jnp.broadcast_to(lanes[...].astype(jnp.bfloat16)[:, None], out.shape)


def embed(info, arrived, order, proj_in, mine, other, out, lanes):
    core = info[16]
    lanes[...] = arrived[...].astype(jnp.float32)
    columns = [
        dot32(order[...], lanes[:, index, :].astype(jnp.bfloat16)).astype(jnp.bfloat16)
        for index in range(lanes.shape[1])
    ]
    arranged = jnp.concatenate(columns, axis=1)
    hidden = gelu_exact(dot32(arranged, proj_in[...])).astype(jnp.bfloat16)
    units = hidden.shape[1]
    cols = mine.shape[2]
    near = dot32(hidden, mine[...].reshape(units, cols))
    far = dot32(hidden, other[...].reshape(units, cols))
    low = jnp.where(core == 0, near, far).astype(jnp.bfloat16)
    high = jnp.where(core == 0, far, near).astype(jnp.bfloat16)
    for index in range(out.shape[0]):
        out[index, :, :cols] = low
        out[index, :, cols:] = high


def keys_values(emb, gain, weight, cosine, sine, swap, gained, scale, out, square, total_k, total_v):
    step = pl.program_id(0)

    @pl.when(step == 0)
    def _():
        square[...] = jnp.zeros_like(square)
        total_k[...] = jnp.zeros_like(total_k)
        total_v[...] = jnp.zeros_like(total_v)

    depth = emb.shape[2]
    for index in range(emb.shape[0]):
        wide = emb[index].astype(jnp.float32)
        square[...] += jnp.sum(wide * wide, axis=1, keepdims=True)
        act = (wide * gain[index]).astype(jnp.bfloat16)
        gained[index] = act
        total_k[...] += dot32(act, weight[0, index * depth : (index + 1) * depth, :])
        total_v[...] += dot32(act, weight[1, index * depth : (index + 1) * depth, :])

    @pl.when(step == pl.num_programs(0) - 1)
    def _():
        width = depth * emb.shape[0] * pl.num_programs(0)
        factor = lax.rsqrt(square[...] / width + 1e-05)
        scale[...] = factor
        key = total_k[...] * factor
        turned = jnp.dot(
            key, swap[...], preferred_element_type=jnp.float32, precision=lax.Precision.HIGHEST
        )
        out[0] = (key * cosine[...] + turned * sine[...]).astype(jnp.bfloat16)
        out[1] = (total_v[...] * factor).astype(jnp.bfloat16)


def queries(gained, weight, scale, cosine, sine, swap, out, total):
    step = pl.program_id(0)

    @pl.when(step == 0)
    def _():
        total[...] = jnp.zeros_like(total)

    act = jnp.concatenate([gained[index] for index in range(gained.shape[0])], axis=1)
    total[...] += dot32(act, weight[...])

    @pl.when(step == pl.num_programs(0) - 1)
    def _():
        for head in range(out.shape[1] // HEAD_WIDTH):
            lanes = slice(head * HEAD_WIDTH, (head + 1) * HEAD_WIDTH)
            query = total[:, lanes] * scale[...]
            turned = jnp.dot(
                query, swap[...], preferred_element_type=jnp.float32, precision=lax.Precision.HIGHEST
            )
            out[:, lanes] = (query * cosine[...] + turned * sine[...]).astype(jnp.bfloat16)


def attend_out(info, query, mine, partner, allowed, weight, out, context):
    @pl.when(pl.program_id(0) == 0)
    def _():
        odd = info[17] == 1
        own = mine[...].astype(jnp.float32)
        far = partner[...].astype(jnp.float32)
        low = jnp.where(odd, far, own)
        high = jnp.where(odd, own, far)
        pair = jnp.concatenate([low, high], axis=2).astype(jnp.bfloat16)
        key, value = pair[0], pair[1]
        for head in range(query.shape[1] // HEAD_WIDTH):
            lanes = slice(head * HEAD_WIDTH, (head + 1) * HEAD_WIDTH)
            scores = lax.dot_general(
                query[:, lanes], key, (((1,), (1,)), ((), ())), preferred_element_type=jnp.float32
            ) / math.sqrt(HEAD_WIDTH)
            scores = jnp.where(allowed[...] > 0, scores, -1e30)
            top = jnp.max(scores, axis=1, keepdims=True)
            powers = jnp.exp(scores - top)
            probs = powers / jnp.sum(powers, axis=1, keepdims=True)
            context[:, lanes] = dot32(probs.astype(jnp.bfloat16), value).astype(jnp.bfloat16)

    out[...] = dot32(context[...], weight[...]).astype(jnp.bfloat16)


def finish(info, terms, own, out):
    cols = own.shape[2]
    rows = own.shape[1]
    live = info[18] + lax.broadcasted_iota(jnp.int32, (rows, cols), 0) < info[19]
    for index in range(own.shape[0]):
        lanes = slice(index * cols, (index + 1) * cols)
        total = jnp.sum(terms[:, :, lanes].astype(jnp.float32), axis=0)
        total = total + own[index].astype(jnp.float32)
        out[:, lanes] = jnp.where(live, total, 0.0).astype(jnp.bfloat16)


def visibility(masks, live_count):
    positions = jnp.arange(SPAN_LIMIT)
    passage = positions // CPP
    expanded = jnp.repeat(jnp.repeat(masks, CPP, axis=0), CPP, axis=1) > 0
    same_passage = passage[:, None] == passage[None, :]
    earlier = positions[None, :] <= positions[:, None]
    key_live = positions[None, :] < live_count
    diagonal = positions[:, None] == positions[None, :]
    return diagonal | earlier & key_live & (same_passage | expanded)


def local(
    span_tokens,
    enc_dest,
    passages,
    req_slot,
    block_mask,
    enc_qkv,
    enc_out,
    enc_up,
    enc_down,
    proj_in,
    proj_out,
    norm_gain,
    q_weight,
    key_value_weight,
    out_weight,
):
    tensor_count = lax.axis_size("tensor")
    seq_count = lax.axis_size("seq")
    tensor_index = lax.axis_index("tensor")
    seq_index = lax.axis_index("seq")
    core = seq_index % 2
    device_count = tensor_count * seq_count
    rows = SPAN_LIMIT
    own_rows = rows // tensor_count
    spans, span_size, width = span_tokens.shape
    model_width = proj_out.shape[1]
    share = enc_qkv.shape[0]
    x_index, y_index = tensor_index // SIDE, tensor_index % SIDE

    requests = jnp.arange(req_slot.shape[0])
    dest_slot = jnp.sum(
        jnp.where(enc_dest[:, None] // SPAN_LIMIT == requests[None, :], req_slot[None, :], 0), axis=1
    ).reshape(device_count, own_rows)
    dest_place = (enc_dest % SPAN_LIMIT).reshape(device_count, own_rows)
    own_slots = lax.dynamic_slice_in_dim(
        dest_slot, seq_index * tensor_count + tensor_index, 1, 0
    )
    pick = (jnp.arange(seq_count)[:, None] == own_slots).astype(jnp.bfloat16)
    place_of = jnp.sum(jnp.where(dest_slot == seq_index, dest_place, 0), axis=1)
    order = (jnp.arange(rows)[:, None] == place_of[None, :]).astype(jnp.bfloat16)
    chosen = jnp.sum(jnp.where(req_slot == seq_index, requests, 0))
    live_count = jnp.sum(jnp.where(requests == chosen, passages, 0)) * CPP
    masks = jnp.sum(
        jnp.where(requests[:, None, None] == chosen, block_mask, 0), axis=0
    )
    allowed = visibility(masks, live_count).astype(jnp.float32)

    steps = jnp.array([0, SIDE - 1, 1, 2])[:, None]
    moving = jnp.arange(SIDE)[None, :]
    by_x = SIDE * ((x_index + steps) % SIDE) + moving
    by_y = SIDE * moving + (y_index + steps) % SIDE
    shards = jnp.where(core == 0, by_x, by_y).reshape(-1)
    scalars = jnp.stack([core, tensor_index % 2, tensor_index * own_rows, live_count])
    info = jnp.concatenate([shards, scalars]).astype(jnp.int32)

    positions = jnp.arange(rows).astype(jnp.float32)
    lane = jnp.arange(HEAD_WIDTH)
    frequency = jnp.exp(
        -(2.0 * (lane // 2).astype(jnp.float32) / HEAD_WIDTH) * math.log(500000.0)
    )
    angles = positions[:, None] * frequency[None, :]
    cosine, sine = jnp.cos(angles), jnp.sin(angles)
    swap = jnp.where(
        (lane[:, None] ^ 1) == lane[None, :], jnp.where(lane[None, :] % 2 == 0, -1.0, 1.0), 0.0
    ).astype(jnp.float32)

    own_tokens = span_tokens.reshape(spans * span_size, width)
    qkv_spread = whole_call(
        spread_qkv, "spread_qkv", info, [enc_qkv], shape_of((SIDE, share, 3 * width // 2))
    )
    qkv_block = short_gather(qkv_spread)
    units = enc_down.shape[0] // 2
    middle_cols = width // 2 + units * tensor_count
    rest_spread = whole_call(
        spread_rest,
        "spread_rest",
        info,
        [enc_out, enc_up, enc_down],
        shape_of((SIDE, share, middle_cols + width)),
    )
    rest_block = short_gather(rest_spread)
    other_tokens = to_core(own_tokens)
    token_rows, token_pieces = whole_call(
        both_rows,
        "both_rows",
        info,
        [own_tokens, other_tokens],
        (
            shape_of((2 * spans * span_size, width)),
            shape_of((tensor_count, 2 * spans * span_size, share)),
        ),
    )
    all_rows = token_rows.shape[0]

    def ring(block, relay):
        left = to_ring(block, 2, 1)
        right = to_ring(block, 2, -1)
        opposite = to_ring(left, 2, 1) if relay == 1 else to_ring(right, 2, -1)
        return [block, left, right, opposite]

    qkv = ring(qkv_block, 1)
    middle = ring(rest_block[:, :, :middle_cols], -1)
    lower = ring(rest_block[:, :, middle_cols:], 1)

    context = whole_call(
        span_attention,
        "span_attention",
        info,
        [token_pieces, *qkv],
        shape_of((tensor_count // 2, all_rows, share)),
        [pltpu.VMEM((all_rows, 3 * width // 2), jnp.bfloat16)],
        flops=2 * all_rows * width * 3 * width // 2,
    )
    attended = whole_call(
        context_out,
        "context_out",
        info,
        [context, to_core(context), *middle],
        shape_of((all_rows, width // 2)),
        [pltpu.VMEM((tensor_count, all_rows, share), jnp.bfloat16)],
        flops=2 * all_rows * width * width // 2,
    )
    first_out, inner = whole_call(
        norm_up,
        "norm_up",
        info,
        [token_rows, attended, to_core(attended), *middle],
        (shape_of((all_rows, width)), shape_of((tensor_count, all_rows, units))),
        [pltpu.VMEM((tensor_count, all_rows, share), jnp.bfloat16)],
        flops=2 * all_rows * width * width,
    )
    kept, sent = whole_call(
        down,
        "down",
        info,
        [inner, *lower],
        (
            shape_of((all_rows // 2, width), jnp.float32),
            shape_of((all_rows // 2, width)),
        ),
        [pltpu.VMEM((all_rows, width), jnp.float32)],
        flops=2 * all_rows * width * width,
    )
    outgoing = whole_call(
        norm_pool,
        "norm_pool",
        info,
        [kept, to_core(sent), first_out, pick],
        shape_of((seq_count, tensor_count, width // 128, 128)),
        [pltpu.VMEM((seq_count, width // 128, 128), jnp.float32)],
    )
    arrived = lax.all_to_all(
        outgoing.reshape(device_count, width // 128, 128), AXES, 0, 0
    )

    share_cols = model_width // tensor_count
    proj_mine = lax.all_to_all(
        whole_call(
            spread_proj,
            "spread_proj",
            info,
            [proj_out],
            shape_of((tensor_count, proj_out.shape[0], share_cols // 2)),
        ),
        "tensor",
        0,
        0,
    )
    proj_other = to_core(proj_mine)
    spread = whole_call(
        embed,
        "embed",
        info,
        [arrived, order, proj_in, proj_mine, proj_other],
        shape_of((tensor_count, rows, share_cols)),
        [pltpu.VMEM((device_count, width // 128, 128), jnp.float32)],
        flops=2 * rows * width * (width + share_cols),
    )
    embedded = lax.all_to_all(spread, "tensor", 0, 0)
    own_embedded = lax.dynamic_slice_in_dim(embedded, tensor_index * own_rows, own_rows, 1)

    query_cols = q_weight.shape[1]
    kv_cols = key_value_weight.shape[2]
    key_start = tensor_index * kv_cols % HEAD_WIDTH
    key_cosine = lax.dynamic_slice_in_dim(cosine, key_start, kv_cols, 1)
    key_sine = lax.dynamic_slice_in_dim(sine, key_start, kv_cols, 1)
    shards_step = 2
    grid = tensor_count // shards_step
    depth = shards_step * share_cols
    shard_spec = pl.BlockSpec((shards_step, rows, share_cols), lambda i: (i, 0, 0))

    def fixed(*shape):
        return pl.BlockSpec(shape, lambda i: (0,) * len(shape))

    gained, scale, own_kv = pl.pallas_call(
        keys_values,
        name="keys_values",
        grid=(grid,),
        out_shape=(
            shape_of((tensor_count, rows, share_cols)),
            shape_of((rows, 1), jnp.float32),
            shape_of((2, rows, kv_cols)),
        ),
        in_specs=[
            shard_spec,
            pl.BlockSpec((shards_step, 1, share_cols), lambda i: (i, 0, 0)),
            pl.BlockSpec((2, depth, kv_cols), lambda i: (0, i, 0)),
            fixed(rows, kv_cols),
            fixed(rows, kv_cols),
            fixed(kv_cols, kv_cols),
        ],
        out_specs=(shard_spec, fixed(rows, 1), fixed(2, rows, kv_cols)),
        scratch_shapes=[
            pltpu.VMEM((rows, 1), jnp.float32),
            pltpu.VMEM((rows, kv_cols), jnp.float32),
            pltpu.VMEM((rows, kv_cols), jnp.float32),
        ],
        compiler_params=pltpu.CompilerParams(vmem_limit_bytes=16 * MIB),
    )(
        embedded,
        norm_gain.reshape(tensor_count, 1, share_cols),
        key_value_weight,
        key_cosine,
        key_sine,
        swap[:kv_cols, :kv_cols],
    )
    partner_kv = lax.ppermute(
        own_kv, "tensor", [(index, index ^ 1) for index in range(tensor_count)]
    )
    query = pl.pallas_call(
        queries,
        name="queries",
        grid=(grid,),
        out_shape=shape_of((rows, query_cols)),
        in_specs=[
            shard_spec,
            pl.BlockSpec((depth, query_cols), lambda i: (i, 0)),
            fixed(rows, 1),
            fixed(rows, HEAD_WIDTH),
            fixed(rows, HEAD_WIDTH),
            fixed(HEAD_WIDTH, HEAD_WIDTH),
        ],
        out_specs=fixed(rows, query_cols),
        scratch_shapes=[pltpu.VMEM((rows, query_cols), jnp.float32)],
        compiler_params=pltpu.CompilerParams(vmem_limit_bytes=16 * MIB),
        cost_estimate=pl.CostEstimate(
            flops=2 * rows * model_width * query_cols,
            bytes_accessed=2 * model_width * query_cols,
            transcendentals=0,
        ),
    )(gained, q_weight, scale, cosine, sine, swap)
    out_step = 1024
    partial = pl.pallas_call(
        attend_out,
        name="attend_out",
        grid=(model_width // out_step,),
        out_shape=shape_of((rows, model_width)),
        in_specs=[
            SMEM,
            fixed(rows, query_cols),
            fixed(2, rows, kv_cols),
            fixed(2, rows, kv_cols),
            fixed(rows, rows),
            pl.BlockSpec((query_cols, out_step), lambda i: (0, i)),
        ],
        out_specs=pl.BlockSpec((rows, out_step), lambda i: (0, i)),
        scratch_shapes=[pltpu.VMEM((rows, query_cols), jnp.bfloat16)],
        compiler_params=pltpu.CompilerParams(vmem_limit_bytes=16 * MIB),
    )(info, query, own_kv, partner_kv, allowed, out_weight)
    terms = lax.all_to_all(
        partial.reshape(tensor_count, own_rows, model_width), "tensor", 0, 0
    )
    return whole_call(
        finish, "finish", info, [terms, own_embedded], shape_of((own_rows, model_width))
    )


def solution(mesh):
    return jax.shard_map(
        local,
        mesh=mesh,
        in_specs=(
            P(("seq", "tensor"), None, None),
            P(),
            P(),
            P(),
            P(),
            P("tensor", None),
            P("tensor", None),
            P("tensor", None),
            P("tensor", None),
            P(),
            P("tensor", None),
            P(),
            P(None, "tensor"),
            P(None, None, "tensor"),
            P("tensor", None),
        ),
        out_specs=P(("seq", "tensor"), None),
        check_vma=False,
    )
```

profile of v0, /device:TPU:0, one launch (start us, length us, event | category | flops | bytes accessed | tf_op | source)
XLA Modules:
  0.0 218.9 jit_solution(8769274601885839385)
XLA Ops:
  0.0 0.7 fusion.10
  0.8 1.4 fusion.18
  2.2 2.0 select_reduce_fusion.3
  5.0 1.0 copy-done.14
  6.0 1.5 spread_qkv.1
  7.4 4.5 %all-to-all-start = ((bf16[4,64,1536]{2,1,0:T(8,128)(2,1)}), bf16[4,64,1536]{2,1,0:T(8,128)(2,1)}, u32[]{:S(2)}, u32[]{:S(2)}) async-start(bf16[4,64,1536]{2,1,0:T(8,128)(2,1)} %spread_qkv.1), calls=%async_computation | async-start | bytes 1572864 | tf_op jit(solution)/shard_map/all_to_all | solution.py:74
  12.0 1.9 spread_rest.1
  13.9 7.7 %all-to-all-done.w0 = bf16[4,64,1536]{2,1,0:T(8,128)(2,1)} async-done(((bf16[4,64,1536]{2,1,0:T(8,128)(2,1)}), bf16[4,64,1536]{2,1,0:T(8,128)(2,1)}, u32[]{:S(2)}, u32[]{:S(2)}) %all-to-all-start) | async-done | bytes 786464 | tf_op jit(solution)/shard_map/all_to_all | solution.py:74
  21.6 3.5 %all-to-all-start.1 = ((bf16[4,64,2560]{2,1,0:T(8,128)(2,1)}), bf16[4,64,2560]{2,1,0:T(8,128)(2,1)S(1)}, u32[]{:S(2)}, u32[]{:S(2)}) async-start(bf16[4,64,2560]{2,1,0:T(8,128)(2,1)} %spread_rest.1), calls=%async_computation.1 | async-start | bytes 2621440 | tf_op jit(solution)/shard_map/all_to_all | solution.py:74
  25.1 1.6 collective-permute-start.1
  26.7 17.6 %all-to-all-done.1 = bf16[4,64,2560]{2,1,0:T(8,128)(2,1)S(1)} async-done(((bf16[4,64,2560]{2,1,0:T(8,128)(2,1)}), bf16[4,64,2560]{2,1,0:T(8,128)(2,1)S(1)}, u32[]{:S(2)}, u32[]{:S(2)}) %all-to-all-start.1) | async-done | bytes 1310752 | tf_op jit(solution)/shard_map/all_to_all | solution.py:74
  44.3 1.1 copy-done.20
  45.5 2.9 %collective-permute-start.6 = (bf16[4,64,1536]{2,1,0:T(8,128)(2,1)S(1)}, bf16[4,64,1536]{2,1,0:T(8,128)(2,1)S(1)}, u32[]{:S(2)}, u32[]{:S(2)}) collective-permute-start(bf16[4,64,1536]{2,1,0:T(8,128)(2,1)S(1)} %slice.12.w0), channel_id=1, source_target_pairs={{0,12},{1,13},{2,14},{3,15},{4,0},{5,1},{6,2},{7,3},{8,4},{9,5},{1... | collective-permute-start | bytes 2359304 | tf_op jit(solution)/shard_map/ppermute | solution.py:66
  48.4 0.9 collective-permute-start.2
  49.2 1.2 collective-permute-start.3
  50.4 0.2 collective-permute-start.5
  50.6 7.3 %collective-permute-done.6.w2 = bf16[4,64,1536]{2,1,0:T(8,128)(2,1)S(1)} collective-permute-done((bf16[4,64,1536]{2,1,0:T(8,128)(2,1)S(1)}, bf16[4,64,1536]{2,1,0:T(8,128)(2,1)S(1)}, u32[]{:S(2)}, u32[]{:S(2)}) %collective-permute-start.6) | collective-permute-done | bytes 786464 | tf_op jit(solution)/shard_map/ppermute | solution.py:66
  57.9 3.7 %collective-permute-start.7 = (bf16[4,64,1536]{2,1,0:T(8,128)(2,1)S(1)}, bf16[4,64,1536]{2,1,0:T(8,128)(2,1)S(1)}, u32[]{:S(2)}, u32[]{:S(2)}) collective-permute-start(bf16[4,64,1536]{2,1,0:T(8,128)(2,1)S(1)} %collective-permute-done.6.w2), channel_id=1, source_target_pairs={{0,12},{1,13},{2,14},{3,15},{4,0},{5,1},{6,2},{7,3},{8,4},{9,5},{1... | collective-permute-start | bytes 2359304 | tf_op jit(solution)/shard_map/ppermute | solution.py:66
  61.6 1.9 slice.13.w0
  63.5 0.9 both_rows.1
  64.4 0.8 copy-done.8
  65.2 1.2 collective-permute-done.2.w2
  66.4 8.4 %span_attention.1.mine = bf16[8,256,64]{2,1,0:T(8,128)(2,1)} custom-call(s32[20]{0:T(128)S(1)} %concatenate.3.info, bf16[16,256,64]{2,1,0:T(8,128)(2,1)S(1)} %get-tuple-element.15.pieces, bf16[4,64,1536]{2,1,0:T(8,128)(2,1)} %all-to-all-done.w0, bf16[4,64,1536]{2,1,0:T(8,128)(2,1)} %collective-permute-done.1.w1, ...), custom_call_target="tpu_custom_call" | custom-call | flops 805306368 | bytes 3670016 | tf_op jit(solution)/shard_map/span_attention/pallas_call | solution.py:88
  74.8 3.6 %collective-permute-start.10 = (bf16[4,64,1024]{2,1,0:T(8,128)(2,1)}, bf16[4,64,1024]{2,1,0:T(8,128)(2,1)}, u32[]{:S(2)}, u32[]{:S(2)}) collective-permute-start(bf16[4,64,1024]{2,1,0:T(8,128)(2,1)} %slice.13.w0), channel_id=1, source_target_pairs={{0,12},{1,13},{2,14},{3,15},{4,0},{5,1},{6,2},{7,3},{8,4},{9,5},{1... | collective-permute-start | bytes 1572872 | tf_op jit(solution)/shard_map/ppermute | solution.py:66
  78.4 0.6 spread_proj.1
  79.0 0.8 copy-done.6
  79.8 4.7 %all-to-all-start.3 = ((bf16[16,64,256]{2,1,0:T(8,128)(2,1)}), bf16[16,64,256]{2,1,0:T(8,128)(2,1)}, u32[]{:S(2)}, u32[]{:S(2)}) async-start(bf16[16,64,256]{2,1,0:T(8,128)(2,1)} %copy-done.6), calls=%async_computation.3 | async-start | bytes 1048576 | tf_op jit(solution)/shard_map/all_to_all | solution.py:529
  84.6 2.0 context_out.1.mine
  86.8 1.4 collective-permute-done.8.other
  88.3 1.0 copy-done.9
  89.3 2.8 %norm_up.1 = (bf16[256,1024]{1,0:T(8,128)(2,1)S(1)}, bf16[16,256,64]{2,1,0:T(8,128)(2,1)S(1)}) custom-call(s32[20]{0:T(128)S(1)} %concatenate.3.info, bf16[256,1024]{1,0:T(8,128)(2,1)S(1)} %copy-done.9, bf16[256,512]{1,0:T(8,128)(2,1)S(1)} %context_out.1.mine, bf16[256,512]{1,0:T(8,128)(2,1)} %collective-permute-done.8.other, ...), custom_call_target="tpu_custom_call" | custom-call | flops 536870912 | bytes 4194304 | tf_op jit(solution)/shard_map/norm_up/pallas_call | solution.py:88
  92.1 0.8 copy-done.10
  92.9 3.2 %down.1 = (f32[128,1024]{1,0:T(8,128)S(1)}, bf16[128,1024]{1,0:T(8,128)(2,1)}) custom-call(s32[20]{0:T(128)S(1)} %concatenate.3.info, bf16[16,256,64]{2,1,0:T(8,128)(2,1)S(1)} %get-tuple-element.16.inner, bf16[4,64,1024]{2,1,0:T(8,128)(2,1)} %slice.13.w0, bf16[4,64,1024]{2,1,0:T(8,128)(2,1)} %collective-permute-done.9.w1, ...), custom_call_target="tpu_custom_call" | custom-call | flops 536870912 | bytes 2621440 | tf_op jit(solution)/shard_map/down/pallas_call | solution.py:88
  96.1 0.8 copy-done.12
  96.9 0.1 collective-permute-start.12
  97.2 0.6 collective-permute-start.13
  97.8 0.9 collective-permute-done.12.arrived
  98.7 1.0 copy-done.13
  99.7 1.7 norm_pool.1
  101.4 11.2 %all-to-all-start.2 = ((bf16[128,8,128]{2,1,0:T(8,128)(2,1)}), bf16[128,8,128]{2,1,0:T(8,128)(2,1)S(1)}, u32[]{:S(2)}, u32[]{:S(2)}) async-start(bf16[128,8,128]{2,1,0:T(8,128)(2,1)} %bitcast.6), calls=%async_computation.2 | async-start | bytes 524288 | tf_op jit(solution)/shard_map/all_to_all | solution.py:524
  112.6 0.1 select_reduce_fusion
  112.8 10.7 %all-to-all-done.2.arrived = bf16[128,8,128]{2,1,0:T(8,128)(2,1)S(1)} async-done(((bf16[128,8,128]{2,1,0:T(8,128)(2,1)}), bf16[128,8,128]{2,1,0:T(8,128)(2,1)S(1)}, u32[]{:S(2)}, u32[]{:S(2)}) %all-to-all-start.2) | async-done | bytes 262176 | tf_op jit(solution)/shard_map/all_to_all | solution.py:524
  123.5 2.4 %embed.1 = bf16[16,128,512]{2,1,0:T(8,128)(2,1)S(1)} custom-call(s32[20]{0:T(128)S(1)} %concatenate.3.info, bf16[128,8,128]{2,1,0:T(8,128)(2,1)S(1)} %all-to-all-done.2.arrived, bf16[128,128]{1,0:T(8,128)(2,1)S(1)} %fusion.order, bf16[1024,1024]{1,0:T(8,128)(2,1)S(1)} %copy-done.5, bf16[16,64,256]{2,1,0:T(8,128)(2,1)} %all-to-all-done.3.mine, ...), custom_call_target="tpu_custom_call" | custom-call | flops 402653184 | bytes 3440640 | tf_op jit(solution)/shard_map/embed/pallas_call | solution.py:88
  125.9 1.4 copy-done.3
  127.3 3.7 %all-to-all-start.4 = ((bf16[16,128,512]{2,1,0:T(8,128)(2,1)}), bf16[16,128,512]{2,1,0:T(8,128)(2,1)S(1)}, u32[]{:S(2)}, u32[]{:S(2)}) async-start(bf16[16,128,512]{2,1,0:T(8,128)(2,1)} %copy-done.3), calls=%async_computation.4 | async-start | bytes 4194304 | tf_op jit(solution)/shard_map/all_to_all | solution.py:551
  131.2 4.8 %copy.23.weight = bf16[2,8192,64]{2,1,0:T(8,128)(2,1)} copy(bf16[2,8192,64]{1,2,0:T(8,128)(2,1)} %param.29) | data formatting | bytes 4194304 | tf_op args[13]
  136.0 0.6 iota_compare_fusion.7
  136.9 0.1 gt.16
  137.0 0.1 copy.25
  137.2 0.3 multiply_sine_fusion
  137.5 0.1 constant_dynamic-slice_fusion
  137.6 0.1 fusion.3.allowed
  137.7 24.0 %all-to-all-done.4.emb = bf16[16,128,512]{2,1,0:T(8,128)(2,1)S(1)} async-done(((bf16[16,128,512]{2,1,0:T(8,128)(2,1)}), bf16[16,128,512]{2,1,0:T(8,128)(2,1)S(1)}, u32[]{:S(2)}, u32[]{:S(2)}) %all-to-all-start.4) | async-done | bytes 2097184 | tf_op jit(solution)/shard_map/all_to_all | solution.py:551
  161.6 2.2 copy-done
  163.8 3.1 %keys_values.1 = (bf16[16,128,512]{2,1,0:T(8,128)(2,1)S(1)}, f32[128,1]{1,0:T(8,128)S(1)}, bf16[2,128,64]{2,1,0:T(8,128)(2,1)S(1)}) custom-call(bf16[16,128,512]{2,1,0:T(8,128)(2,1)S(1)} %all-to-all-done.4.emb, f32[16,1,512]{2,1,0:T(1,128)S(1)} %bitcast.16, bf16[2,8192,64]{2,1,0:T(8,128)(2,1)S(1)} %copy-done, f32[128,64]{1,0:T(8,128)S(1)} %get-tuple-element.31.cosine, ...), custom_call_target="tpu_custom_call" | custom-call | tf_op jit(solution)/shard_map/keys_values/pallas_call | solution.py:567
  166.9 0.7 collective-permute-start.14
  167.6 3.4 %copy-done.1 = bf16[8192,512]{1,0:T(8,128)(2,1)S(1)} copy-done((bf16[8192,512]{1,0:T(8,128)(2,1)S(1)}, bf16[8192,512]{1,0:T(8,128)(2,1)}, u32[]{:S(2)}) %copy-start.1) | copy-done | bytes 8388632
  170.9 3.0 %queries.1.query = bf16[128,512]{1,0:T(8,128)(2,1)S(1)} custom-call(bf16[16,128,512]{2,1,0:T(8,128)(2,1)S(1)} %get-tuple-element.20.gained, bf16[8192,512]{1,0:T(8,128)(2,1)S(1)} %copy-done.1, f32[128,1]{1,0:T(8,128)S(1)} %get-tuple-element.21.scale, f32[128,128]{1,0:T(8,128)S(1)} %get-tuple-element.26.cosine, f32[128,128]{1,0:T(8,128)S(1)} %get-tuple-element.25.sine, ...), custom_call_target="tpu_custom_call" | custom-call | flops 1073741824 | bytes 8388608 | tf_op jit(solution)/shard_map/queries/pallas_call | solution.py:602
  174.0 3.4 %copy-done.2 = bf16[512,8192]{1,0:T(8,128)(2,1)S(1)} copy-done((bf16[512,8192]{1,0:T(8,128)(2,1)S(1)}, bf16[512,8192]{1,0:T(8,128)(2,1)}, u32[]{:S(2)}) %copy-start.2) | copy-done | bytes 8388632
  177.3 5.3 %attend_out.1 = bf16[128,8192]{1,0:T(8,128)(2,1)S(1)} custom-call(s32[20]{0:T(128)S(1)} %concatenate.3.info, bf16[128,512]{1,0:T(8,128)(2,1)S(1)} %queries.1.query, bf16[2,128,64]{2,1,0:T(8,128)(2,1)S(1)} %get-tuple-element.22.mine, bf16[2,128,64]{2,1,0:T(8,128)(2,1)S(1)} %collective-permute-done.14.partner, f32[128,128]{1,0:T(8,128)S(1)} %fusion.3.allowed, ...), custom_call_target="tpu_custom_call" | custom-call | tf_op jit(solution)/shard_map/attend_out/pallas_call | solution.py:625
  182.6 1.3 copy-done.4
  184.0 4.4 %all-to-all-start.5 = ((bf16[16,8,8192]{2,1,0:T(8,128)(2,1)}), bf16[16,8,8192]{2,1,0:T(8,128)(2,1)}, u32[]{:S(2)}, u32[]{:S(2)}) async-start(bf16[16,8,8192]{2,1,0:T(8,128)(2,1)} %bitcast.13), calls=%async_computation.5 | async-start | bytes 4194304 | tf_op jit(solution)/shard_map/all_to_all | solution.py:642
  188.4 27.9 %all-to-all-done.5.terms = bf16[16,8,8192]{2,1,0:T(8,128)(2,1)} async-done(((bf16[16,8,8192]{2,1,0:T(8,128)(2,1)}), bf16[16,8,8192]{2,1,0:T(8,128)(2,1)}, u32[]{:S(2)}, u32[]{:S(2)}) %all-to-all-start.5) | async-done | bytes 2097184 | tf_op jit(solution)/shard_map/all_to_all | solution.py:642
  216.4 2.6 %finish.1 = bf16[8,8192]{1,0:T(8,128)(2,1)} custom-call(s32[20]{0:T(128)S(1)} %concatenate.3.info, bf16[16,8,8192]{2,1,0:T(8,128)(2,1)} %all-to-all-done.5.terms, bf16[16,8,512]{2,1,0:T(8,128)(2,1)S(1)} %constant_dynamic-slice_fusion.2.own), custom_call_target="tpu_custom_call" | custom-call | bytes 2228224 | tf_op jit(solution)/shard_map/finish/pallas_call | solution.py:88
  (77 shorter events, 1.2 us)
Async XLA Ops:
  5.0 1.0 copy-start.14
  5.9 6.0 %copy-start.15 = (bf16[64,2048]{1,0:T(8,128)(2,1)S(1)}, bf16[64,2048]{1,0:T(8,128)(2,1)}, u32[]{:S(2)}) copy-start(bf16[64,2048]{1,0:T(8,128)(2,1)} %up_weight.1) | copy-start | bytes 786436
  6.0 6.0 %copy-start.16 = (bf16[128,1024]{1,0:T(8,128)(2,1)S(1)}, bf16[128,1024]{1,0:T(8,128)(2,1)}, u32[]{:S(2)}) copy-start(bf16[128,1024]{1,0:T(8,128)(2,1)} %down_weight.1) | copy-start | bytes 786436
  6.0 6.0 %copy-start.18 = (bf16[64,1024]{1,0:T(8,128)(2,1)S(1)}, bf16[64,1024]{1,0:T(8,128)(2,1)}, u32[]{:S(2)}) copy-start(bf16[64,1024]{1,0:T(8,128)(2,1)} %out_weight.1) | copy-start | bytes 393220
  7.4 14.1 %all-to-all-start = ((bf16[4,64,1536]{2,1,0:T(8,128)(2,1)}), bf16[4,64,1536]{2,1,0:T(8,128)(2,1)}, u32[]{:S(2)}, u32[]{:S(2)}) async-start(bf16[4,64,1536]{2,1,0:T(8,128)(2,1)} %spread_qkv.1), calls=%async_computation | async-start | bytes 1572864 | tf_op jit(solution)/shard_map/all_to_all | solution.py:74
  13.9 36.5 %copy-start.17 = (bf16[8,16,1024]{2,1,0:T(8,128)(2,1)S(1)}, bf16[8,16,1024]{2,1,0:T(8,128)(2,1)}, u32[]{:S(2)}) copy-start(bf16[8,16,1024]{2,1,0:T(8,128)(2,1)} %param.16) | copy-start | bytes 786436
  21.6 22.7 %all-to-all-start.1 = ((bf16[4,64,2560]{2,1,0:T(8,128)(2,1)}), bf16[4,64,2560]{2,1,0:T(8,128)(2,1)S(1)}, u32[]{:S(2)}, u32[]{:S(2)}) async-start(bf16[4,64,2560]{2,1,0:T(8,128)(2,1)} %spread_rest.1), calls=%async_computation.1 | async-start | bytes 2621440 | tf_op jit(solution)/shard_map/all_to_all | solution.py:74
  25.1 24.1 %collective-permute-start.1 = (bf16[4,64,1536]{2,1,0:T(8,128)(2,1)}, bf16[4,64,1536]{2,1,0:T(8,128)(2,1)}, u32[]{:S(2)}, u32[]{:S(2)}) collective-permute-start(bf16[4,64,1536]{2,1,0:T(8,128)(2,1)} %all-to-all-done.w0), channel_id=1, source_target_pairs={{0,4},{1,5},{2,6},{3,7},{4,8},{5,9},{6,10},{7,11},{8,12},{9,13},{1... | collective-permute-start | bytes 2359304 | tf_op jit(solution)/shard_map/ppermute | solution.py:66
  44.3 1.1 copy-start.20
  45.5 12.4 %collective-permute-start.6 = (bf16[4,64,1536]{2,1,0:T(8,128)(2,1)S(1)}, bf16[4,64,1536]{2,1,0:T(8,128)(2,1)S(1)}, u32[]{:S(2)}, u32[]{:S(2)}) collective-permute-start(bf16[4,64,1536]{2,1,0:T(8,128)(2,1)S(1)} %slice.12.w0), channel_id=1, source_target_pairs={{0,12},{1,13},{2,14},{3,15},{4,0},{5,1},{6,2},{7,3},{8,4},{9,5},{1... | collective-permute-start | bytes 2359304 | tf_op jit(solution)/shard_map/ppermute | solution.py:66
  48.4 18.0 %collective-permute-start.2 = (bf16[4,64,1536]{2,1,0:T(8,128)(2,1)}, bf16[4,64,1536]{2,1,0:T(8,128)(2,1)S(1)}, u32[]{:S(2)}, u32[]{:S(2)}) collective-permute-start(bf16[4,64,1536]{2,1,0:T(8,128)(2,1)} %all-to-all-done.w0), channel_id=1, source_target_pairs={{0,12},{1,13},{2,14},{3,15},{4,0},{5,1},{6,2},{7,3},{8,4},{9,5},{1... | collective-permute-start | bytes 2359304 | tf_op jit(solution)/shard_map/ppermute | solution.py:66
  49.2 17.2 %collective-permute-start.3 = (bf16[4,64,1536]{2,1,0:T(8,128)(2,1)}, bf16[4,64,1536]{2,1,0:T(8,128)(2,1)S(1)}, u32[]{:S(2)}, u32[]{:S(2)}) collective-permute-start(bf16[4,64,1536]{2,1,0:T(8,128)(2,1)} %collective-permute-done.1.w1), channel_id=1, source_target_pairs={{0,4},{1,5},{2,6},{3,7},{4,8},{5,9},{6,10},{7,11},{8,12},{9,13},{1... | collective-permute-start | bytes 2359304 | tf_op jit(solution)/shard_map/ppermute | solution.py:66
  50.4 13.1 %collective-permute-start = (bf16[128,1024]{1,0:T(8,128)(2,1)S(1)}, bf16[128,1024]{1,0:T(8,128)(2,1)S(1)}, u32[]{:S(2)}, u32[]{:S(2)}) collective-permute-start(bf16[128,1024]{1,0:T(8,128)(2,1)S(1)} %bitcast.14), channel_id=1, source_target_pairs={{0,16},{16,0},{32,48},{48,32},{64,80},{80,64},{96,112},{112,96},{1... | collective-permute-start | bytes 786440 | tf_op jit(solution)/shard_map/ppermute | solution.py:70
  50.4 34.1 %collective-permute-start.5 = (bf16[4,64,1536]{2,1,0:T(8,128)(2,1)S(1)}, bf16[4,64,1536]{2,1,0:T(8,128)(2,1)S(1)}, u32[]{:S(2)}, u32[]{:S(2)}) collective-permute-start(bf16[4,64,1536]{2,1,0:T(8,128)(2,1)S(1)} %slice.12.w0), channel_id=1, source_target_pairs={{0,4},{1,5},{2,6},{3,7},{4,8},{5,9},{6,10},{7,11},{8,12},{9,13},{1... | collective-permute-start | bytes 2359304 | tf_op jit(solution)/shard_map/ppermute | solution.py:66
  57.9 26.7 %collective-permute-start.7 = (bf16[4,64,1536]{2,1,0:T(8,128)(2,1)S(1)}, bf16[4,64,1536]{2,1,0:T(8,128)(2,1)S(1)}, u32[]{:S(2)}, u32[]{:S(2)}) collective-permute-start(bf16[4,64,1536]{2,1,0:T(8,128)(2,1)S(1)} %collective-permute-done.6.w2), channel_id=1, source_target_pairs={{0,12},{1,13},{2,14},{3,15},{4,0},{5,1},{6,2},{7,3},{8,4},{9,5},{1... | collective-permute-start | bytes 2359304 | tf_op jit(solution)/shard_map/ppermute | solution.py:66
  63.5 14.9 %collective-permute-start.9 = (bf16[4,64,1024]{2,1,0:T(8,128)(2,1)}, bf16[4,64,1024]{2,1,0:T(8,128)(2,1)}, u32[]{:S(2)}, u32[]{:S(2)}) collective-permute-start(bf16[4,64,1024]{2,1,0:T(8,128)(2,1)} %slice.13.w0), channel_id=1, source_target_pairs={{0,4},{1,5},{2,6},{3,7},{4,8},{5,9},{6,10},{7,11},{8,12},{9,13},{1... | collective-permute-start | bytes 1572872 | tf_op jit(solution)/shard_map/ppermute | solution.py:66
  64.4 0.8 copy-start.8
  66.4 12.0 %copy-start.7 = (bf16[64,8192]{1,0:T(8,128)(2,1)S(1)}, bf16[64,8192]{1,0:T(8,128)(2,1)}, u32[]{:S(2)}) copy-start(bf16[64,8192]{1,0:T(8,128)(2,1)} %weight.6) | copy-start | bytes 3145732
  74.8 9.8 %collective-permute-start.4 = (bf16[8,256,64]{2,1,0:T(8,128)(2,1)}, bf16[8,256,64]{2,1,0:T(8,128)(2,1)}, u32[]{:S(2)}, u32[]{:S(2)}) collective-permute-start(bf16[8,256,64]{2,1,0:T(8,128)(2,1)} %span_attention.1.mine), channel_id=1, source_target_pairs={{0,16},{16,0},{32,48},{48,32},{64,80},{80,64},{96,112},{112,96},{1... | collective-permute-start | bytes 786440 | tf_op jit(solution)/shard_map/ppermute | solution.py:70
  74.8 18.1 %collective-permute-start.10 = (bf16[4,64,1024]{2,1,0:T(8,128)(2,1)}, bf16[4,64,1024]{2,1,0:T(8,128)(2,1)}, u32[]{:S(2)}, u32[]{:S(2)}) collective-permute-start(bf16[4,64,1024]{2,1,0:T(8,128)(2,1)} %slice.13.w0), channel_id=1, source_target_pairs={{0,12},{1,13},{2,14},{3,15},{4,0},{5,1},{6,2},{7,3},{8,4},{9,5},{1... | collective-permute-start | bytes 1572872 | tf_op jit(solution)/shard_map/ppermute | solution.py:66
  78.4 14.5 %collective-permute-start.11 = (bf16[4,64,1024]{2,1,0:T(8,128)(2,1)}, bf16[4,64,1024]{2,1,0:T(8,128)(2,1)}, u32[]{:S(2)}, u32[]{:S(2)}) collective-permute-start(bf16[4,64,1024]{2,1,0:T(8,128)(2,1)} %collective-permute-done.9.w1), channel_id=1, source_target_pairs={{0,4},{1,5},{2,6},{3,7},{4,8},{5,9},{6,10},{7,11},{8,12},{9,13},{1... | collective-permute-start | bytes 1572872 | tf_op jit(solution)/shard_map/ppermute | solution.py:66
  79.0 0.8 copy-start.6
  79.8 17.3 %all-to-all-start.3 = ((bf16[16,64,256]{2,1,0:T(8,128)(2,1)}), bf16[16,64,256]{2,1,0:T(8,128)(2,1)}, u32[]{:S(2)}, u32[]{:S(2)}) async-start(bf16[16,64,256]{2,1,0:T(8,128)(2,1)} %copy-done.6), calls=%async_computation.3 | async-start | bytes 1048576 | tf_op jit(solution)/shard_map/all_to_all | solution.py:529
  84.5 2.1 copy-start.22
  84.5 2.1 copy-start.23
  86.5 1.7 collective-permute-start.8
  88.3 1.0 copy-start.9
  92.1 0.8 copy-start.10
  92.9 5.8 %copy-start.11 = (bf16[256,1024]{1,0:T(8,128)(2,1)S(1)}, bf16[256,1024]{1,0:T(8,128)(2,1)}, u32[]{:S(2)}) copy-start(bf16[256,1024]{1,0:T(8,128)(2,1)} %copy-done.10) | copy-start | bytes 1572868
  92.9 30.6 %copy-start.5 = (bf16[1024,1024]{1,0:T(8,128)(2,1)S(1)}, bf16[1024,1024]{1,0:T(8,128)(2,1)}, u32[]{:S(2)}) copy-start(bf16[1024,1024]{1,0:T(8,128)(2,1)} %proj_in.1) | copy-start | bytes 6291460
  96.1 0.8 copy-start.12
  96.9 1.7 collective-permute-start.12
  97.2 15.6 %collective-permute-start.13 = (bf16[16,64,256]{2,1,0:T(8,128)(2,1)}, bf16[16,64,256]{2,1,0:T(8,128)(2,1)S(1)}, u32[]{:S(2)}, u32[]{:S(2)}) collective-permute-start(bf16[16,64,256]{2,1,0:T(8,128)(2,1)} %all-to-all-done.3.mine), channel_id=1, source_target_pairs={{0,16},{16,0},{32,48},{48,32},{64,80},{80,64},{96,112},{112,96},{1... | collective-permute-start | bytes 1572872 | tf_op jit(solution)/shard_map/ppermute | solution.py:70
  98.7 1.0 copy-start.13
  101.4 22.1 %all-to-all-start.2 = ((bf16[128,8,128]{2,1,0:T(8,128)(2,1)}), bf16[128,8,128]{2,1,0:T(8,128)(2,1)S(1)}, u32[]{:S(2)}, u32[]{:S(2)}) async-start(bf16[128,8,128]{2,1,0:T(8,128)(2,1)} %bitcast.6), calls=%async_computation.2 | async-start | bytes 524288 | tf_op jit(solution)/shard_map/all_to_all | solution.py:524
  125.9 1.4 copy-start.3
  127.3 34.3 %all-to-all-start.4 = ((bf16[16,128,512]{2,1,0:T(8,128)(2,1)}), bf16[16,128,512]{2,1,0:T(8,128)(2,1)S(1)}, u32[]{:S(2)}, u32[]{:S(2)}) async-start(bf16[16,128,512]{2,1,0:T(8,128)(2,1)} %copy-done.3), calls=%async_computation.4 | async-start | bytes 4194304 | tf_op jit(solution)/shard_map/all_to_all | solution.py:551
  131.2 5.4 %copy-start.21 = (s32[8,8,8]{2,1,0:T(8,128)S(1)}, s32[8,8,8]{2,1,0:T(8,128)}, u32[]{:S(2)}) copy-start(s32[8,8,8]{2,1,0:T(8,128)} %param.20) | copy-start | bytes 6148
  131.2 30.5 %copy-start.19 = (f32[8192]{0:T(1024)S(1)}, f32[8192]{0:T(1024)}, u32[]{:S(2)}) copy-start(f32[8192]{0:T(1024)} %param.27) | copy-start | bytes 98308
  161.6 2.2 copy-start
  166.9 7.0 %collective-permute-start.14 = (bf16[2,128,64]{2,1,0:T(8,128)(2,1)S(1)}, bf16[2,128,64]{2,1,0:T(8,128)(2,1)S(1)}, u32[]{:S(2)}, u32[]{:S(2)}) collective-permute-start(bf16[2,128,64]{2,1,0:T(8,128)(2,1)S(1)} %get-tuple-element.22.mine), channel_id=1, source_target_pairs={{0,1},{1,0},{2,3},{3,2},{4,5},{5,4},{6,7},{7,6},{8,9},{9,8},{10,11... | collective-permute-start | bytes 98312 | tf_op jit(solution)/shard_map/ppermute | solution.py:599
  167.6 3.4 %copy-start.1 = (bf16[8192,512]{1,0:T(8,128)(2,1)S(1)}, bf16[8192,512]{1,0:T(8,128)(2,1)}, u32[]{:S(2)}) copy-start(bf16[8192,512]{1,0:T(8,128)(2,1)} %weight.7) | copy-start | bytes 25165828
  173.9 3.4 %copy-start.2 = (bf16[512,8192]{1,0:T(8,128)(2,1)S(1)}, bf16[512,8192]{1,0:T(8,128)(2,1)}, u32[]{:S(2)}) copy-start(bf16[512,8192]{1,0:T(8,128)(2,1)} %weight.8) | copy-start | bytes 25165828
  182.6 1.3 copy-start.4
  184.0 32.4 %all-to-all-start.5 = ((bf16[16,8,8192]{2,1,0:T(8,128)(2,1)}), bf16[16,8,8192]{2,1,0:T(8,128)(2,1)}, u32[]{:S(2)}, u32[]{:S(2)}) async-start(bf16[16,8,8192]{2,1,0:T(8,128)(2,1)} %bitcast.13), calls=%async_computation.5 | async-start | bytes 4194304 | tf_op jit(solution)/shard_map/all_to_all | solution.py:642
where the time goes:
time: 220 us; the launch traced here: 219 us
  waiting for transfers between devices  98.8 us (45%)
  starting transfers between devices  47.6 us (22%)
  Pallas kernels  39.3 us (18%)
  local copies, waits for them, and re-layouts  26.6 us (12%)
  other arithmetic  5.53 us (3%)
    all_to_all x1, waiting for transfers between devices, local(): lax.all_to_all(partial.reshape(tensor_count, own_rows, model_width), 'ten...  27.9 us
    pallas_call x11, Pallas kernels, whole_call(): pl.pallas_call(body, name=name, out_shape=outs, in_specs=[SMEM] + [VMEM]...  27.9 us
    all_to_all x2, waiting for transfers between devices, short_gather(): return lax.all_to_all(spread, AXES, 0, 0, axis_index_groups=ring_groups(1))  25.3 us
    all_to_all x1, waiting for transfers between devices, local(): embedded = lax.all_to_all(spread, 'tensor', 0, 0)  24 us
    unnamed x49, local copies, waits for them, and re-layouts  23.8 us
    ppermute x9, starting transfers between devices, to_ring(): return lax.ppermute(value, AXES, ring_pairs(phase, distance))  14 us
    all_to_all x1, starting transfers between devices, local(): lax.all_to_all(outgoing.reshape(device_count, width // 128, 128), AXES, 0...  11.2 us
    all_to_all x1, waiting for transfers between devices, local(): lax.all_to_all(outgoing.reshape(device_count, width // 128, 128), AXES, 0...  10.7 us
  transfers between devices with their start and end apart: 21, of which 9 were waited for; matrix products, arithmetic and copies ran while one was open for 4% of the time, Pallas kernels for 11%

commit v1 on v0

v1 whole, which is shorter than its diff:
```python
import math

import jax
import jax.numpy as jnp
from jax import lax
from jax.experimental import pallas as pl
from jax.experimental.pallas import tpu as pltpu
from jax.sharding import PartitionSpec as P

QUERY_HEAD_COUNT = 64
KEY_VALUE_HEADS = 8
HEAD_WIDTH = 128
EH = 16
CPP = 16
SPAN_LIMIT = 128
SIDE = 4
AXES = ("seq", "tensor")


def device_id(plane, core, x, y):
    return ((plane * 2 + core) * SIDE + x) * SIDE + y


def every_device():
    return [
        (plane, core, x, y)
        for plane in range(SIDE)
        for core in range(2)
        for x in range(SIDE)
        for y in range(SIDE)
    ]


def first_axis_is_y(core, phase):
    return (core == 0) == (phase == 1)


def ring_pairs(phase, distance):
    pairs = []
    for plane, core, x, y in every_device():
        if first_axis_is_y(core, phase):
            target = device_id(plane, core, x, (y + distance) % SIDE)
        else:
            target = device_id(plane, core, (x + distance) % SIDE, y)
        pairs.append((device_id(plane, core, x, y), target))
    return pairs


def ring_groups(phase):
    groups = []
    for plane in range(SIDE):
        for core in range(2):
            for fixed in range(SIDE):
                groups.append(
                    [
                        device_id(plane, core, fixed, moving)
                        if first_axis_is_y(core, phase)
                        else device_id(plane, core, moving, fixed)
                        for moving in range(SIDE)
                    ]
                )
    return groups


def to_ring(value, phase, distance):
    return lax.ppermute(value, AXES, ring_pairs(phase, distance))


def to_core(value):
    return lax.ppermute(value, "seq", [(index, index ^ 1) for index in range(8)])


def short_ring(block):
    return [block] + [to_ring(block, 1, distance) for distance in (1, -1, 2)]


VMEM = pl.BlockSpec(memory_space=pltpu.VMEM)
SMEM = pl.BlockSpec(memory_space=pltpu.SMEM)
MIB = 2**20


def shape_of(shape, dtype=jnp.bfloat16):
    return jax.ShapeDtypeStruct(shape, dtype)


def whole_call(body, name, info, arrays, outs, scratch=(), limit=12, flops=0, out_space=pltpu.VMEM, after=()):
    count = len(arrays)

    def run(*refs):
        body(*refs[: 1 + count], *refs[1 + count + len(after) :])

    moved = sum(array.size * array.dtype.itemsize for array in arrays)
    return pl.pallas_call(
        run,
        name=name,
        out_shape=outs,
        in_specs=[SMEM] + [VMEM] * count + [pl.BlockSpec(memory_space=pl.ANY)] * len(after),
        out_specs=jax.tree.map(lambda _: pl.BlockSpec(memory_space=out_space), outs),
        scratch_shapes=list(scratch),
        compiler_params=pltpu.CompilerParams(vmem_limit_bytes=limit * MIB),
        cost_estimate=pl.CostEstimate(flops=flops, bytes_accessed=moved, transcendentals=0),
    )(info, *arrays, *after)


def dot32(left, right):
    return jnp.dot(left, right, preferred_element_type=jnp.float32)


def gelu_exact(values):
    return 0.5 * values * (1.0 + lax.erf(values * (0.5**0.5)))


def take_qkv(info, weight, out):
    cols = weight.shape[1] // 6
    for part in range(3):
        start = pl.multiple_of((2 * part + info[16]) * cols, cols)
        out[:, part * cols : (part + 1) * cols] = weight[:, pl.ds(start, cols)]


def take_rest(info, out_weight, up_weight, down_weight, out):
    core = info[16]
    rows, width = out_weight.shape
    cols = width // 2
    units = down_weight.shape[0] // 2
    out[:, :cols] = out_weight[:, pl.ds(pl.multiple_of(core * cols, cols), cols)]
    at = cols
    for pair in range(up_weight.shape[1] // (4 * units)):
        halves = []
        for step in range(2):
            low = (2 * pair + step) * 2 * units
            halves.append(
                jnp.where(
                    core == 0,
                    up_weight[:, low : low + units].astype(jnp.float32),
                    up_weight[:, low + units : low + 2 * units].astype(jnp.float32),
                )
            )
        piece = jnp.concatenate(halves, axis=1).astype(jnp.bfloat16)
        out[:, at : at + 2 * units] = piece
        at += 2 * units
    out[:, at:] = down_weight[pl.ds(pl.multiple_of(core * units, units), units), :]


def join_qkv(info, own, left, right, opposite, out):
    for index, block in enumerate((own, left, right, opposite)):
        out[index] = block[...]


def join_rest(info, own, left, right, opposite, middle, lower):
    cols = middle.shape[2]
    for index, block in enumerate((own, left, right, opposite)):
        middle[index] = block[:, :cols]
        lower[index] = block[:, cols:]


def spread_proj(info, weight, out):
    cols = out.shape[2]
    for index in range(out.shape[0]):
        start = pl.multiple_of((2 * index + info[16]) * cols, cols)
        out[index] = weight[:, pl.ds(start, cols)]


def both_rows(info, mine, other, pieces_out):
    half, width = mine.shape
    core = info[16]
    piece = pieces_out.shape[2]
    near = pl.ds(pl.multiple_of(core * half, half), half)
    far = pl.ds(pl.multiple_of((1 - core) * half, half), half)
    for index in range(width // piece):
        pieces_out[index, near, :] = mine[:, index * piece : (index + 1) * piece]
        pieces_out[index, far, :] = other[:, index * piece : (index + 1) * piece]


def ring_dot(info, pieces, blocks, low, high):
    total = None
    for at, block in enumerate(blocks):
        act = jnp.concatenate([pieces[info[4 * at + step]] for step in range(SIDE)], axis=1)
        weight = block[:, :, low:high].reshape(act.shape[1], high - low)
        part = dot32(act, weight)
        total = part if total is None else total + part
    return total


def masked_softmax(scores, seen, size):
    scores = [jnp.where(seen, score / math.sqrt(size), -1e30) for score in scores]
    tops = [jnp.max(score, axis=1, keepdims=True) for score in scores]
    powers = [jnp.exp(score - top) for score, top in zip(scores, tops)]
    sums = [jnp.sum(power, axis=1, keepdims=True) for power in powers]
    return [(power / total).astype(jnp.bfloat16) for power, total in zip(powers, sums)]


def span_attention(info, pieces, w0, w1, w2, w3, context, mixed):
    cols = w0.shape[2]
    third = cols // 3
    mixed[...] = ring_dot(info, pieces, (w0, w1, w2, w3), 0, cols).astype(jnp.bfloat16)
    size = context.shape[2]
    half = mixed.shape[0] // 2
    span = 16
    row = lax.broadcasted_iota(jnp.int32, (half, half), 0) // span
    col = lax.broadcasted_iota(jnp.int32, (half, half), 1) // span
    same = row == col
    heads = third // size
    units = [
        (head, slice(part * half, (part + 1) * half)) for head in range(heads) for part in range(2)
    ]
    scores = [
        lax.dot_general(
            mixed[rows, head * size : (head + 1) * size],
            mixed[rows, third + head * size : third + (head + 1) * size],
            (((1,), (1,)), ((), ())),
            preferred_element_type=jnp.float32,
        )
        for head, rows in units
    ]
    probs = masked_softmax(scores, same, size)
    for (head, rows), prob in zip(units, probs):
        value = mixed[rows, 2 * third + head * size : 2 * third + (head + 1) * size]
        context[head, rows, :] = dot32(prob, value).astype(jnp.bfloat16)


def context_out(info, mine, other, w0, w1, w2, w3, attended, pieces):
    heads = mine.shape[0]
    core = info[16]
    pieces[pl.ds(core * heads, heads)] = mine[...]
    pieces[pl.ds((1 - core) * heads, heads)] = other[...]
    cols = attended.shape[1]
    attended[...] = ring_dot(info, pieces, (w0, w1, w2, w3), 0, cols).astype(jnp.bfloat16)


def norm_up(info, near_rows, far_rows, mine, other, w0, w1, w2, w3, first_out, inner, pieces, rows):
    core = info[16]
    cols = mine.shape[1]
    half, width = near_rows.shape
    rows[pl.ds(pl.multiple_of(core * half, half), half), :] = near_rows[...]
    rows[pl.ds(pl.multiple_of((1 - core) * half, half), half), :] = far_rows[...]
    near = mine[...].astype(jnp.float32)
    far = other[...].astype(jnp.float32)
    low = rows[:, :cols].astype(jnp.float32) + jnp.where(core == 0, near, far)
    high = rows[:, cols:].astype(jnp.float32) + jnp.where(core == 0, far, near)
    mean = (jnp.sum(low, 1, keepdims=True) + jnp.sum(high, 1, keepdims=True)) / width
    low, high = low - mean, high - mean
    var = (jnp.sum(low * low, 1, keepdims=True) + jnp.sum(high * high, 1, keepdims=True)) / width
    scale = lax.rsqrt(var + 1e-05)
    first_out[:, :cols] = (low * scale).astype(jnp.bfloat16)
    first_out[:, cols:] = (high * scale).astype(jnp.bfloat16)
    size = pieces.shape[2]
    for index in range(pieces.shape[0]):
        pieces[index] = first_out[:, index * size : (index + 1) * size]
    total = ring_dot(info, pieces, (w0, w1, w2, w3), cols, w0.shape[2])
    act = gelu_exact(total).astype(jnp.bfloat16)
    unit = inner.shape[2]
    for index in range(inner.shape[0]):
        inner[index] = act[:, index * unit : (index + 1) * unit]


def down(info, inner, first_out, w0, w1, w2, w3, kept, sent, total):
    core = info[16]
    total[...] = ring_dot(info, inner, (w0, w1, w2, w3), 0, w0.shape[2])
    half = kept.shape[0]
    rows = pl.ds(pl.multiple_of(core * half, half), half)
    kept[...] = total[rows, :] + first_out[rows, :].astype(jnp.float32)
    sent[...] = total[pl.ds(pl.multiple_of((1 - core) * half, half), half), :].astype(jnp.bfloat16)


def norm_pool(info, kept, arrived, pick, out, lanes):
    half, width = kept.shape
    values = kept[...] + arrived[...].astype(jnp.float32)
    mean = jnp.mean(values, axis=1, keepdims=True)
    values = values - mean
    values = values * lax.rsqrt(jnp.mean(values * values, axis=1, keepdims=True) + 1e-05)
    spans = pick.shape[1]
    pooled = jnp.mean(values.reshape(spans, half // spans, width), axis=1).astype(jnp.bfloat16)
    by_slot = dot32(pick[...], pooled)
    for index in range(width // 128):
        lanes[:, index, :] = by_slot[:, index * 128 : (index + 1) * 128]
    out[...] = jnp.broadcast_to(lanes[...].astype(jnp.bfloat16)[:, None], out.shape)


def embed(info, arrived, order, proj_in, mine, other, out, lanes, result, sems):
    core = info[16]
    lanes[...] = arrived[...].astype(jnp.float32)
    columns = [
        dot32(order[...], lanes[:, index, :].astype(jnp.bfloat16)).astype(jnp.bfloat16)
        for index in range(lanes.shape[1])
    ]
    arranged = jnp.concatenate(columns, axis=1)
    hidden = gelu_exact(dot32(arranged, proj_in[...])).astype(jnp.bfloat16)
    units = hidden.shape[1]
    cols = mine.shape[2]
    near = dot32(hidden, mine[...].reshape(units, cols))
    far = dot32(hidden, other[...].reshape(units, cols))
    low = jnp.where(core == 0, near, far).astype(jnp.bfloat16)
    high = jnp.where(core == 0, far, near).astype(jnp.bfloat16)
    result[:, :cols] = low
    result[:, cols:] = high
    copies = [
        pltpu.make_async_copy(result, out.at[index], sems.at[index]) for index in range(out.shape[0])
    ]
    for copy in copies:
        copy.start()
    for copy in copies:
        copy.wait()


def keys_values(emb, gain, weight_hbm, cosine, sine, swap, gained, scale, out, weight, sems):
    count, rows, depth = emb.shape
    parts = sems.shape[0]
    step = weight.shape[1] // parts

    def fetch(part):
        span = pl.ds(part * step, step)
        return pltpu.make_async_copy(
            weight_hbm.at[:, span, :], weight.at[:, span, :], sems.at[part]
        )

    for part in range(parts):
        fetch(part).start()
    square = jnp.zeros((rows, 1), jnp.float32)
    for index in range(count):
        wide = emb[index].astype(jnp.float32)
        square += jnp.sum(wide * wide, axis=1, keepdims=True)
        gained[index] = (wide * gain[index]).astype(jnp.bfloat16)
    factor = lax.rsqrt(square / (count * depth) + 1e-05)
    scale[...] = factor
    key = jnp.zeros((rows, weight.shape[2]), jnp.float32)
    value = jnp.zeros((rows, weight.shape[2]), jnp.float32)
    for part in range(parts):
        fetch(part).wait()
        for index in range(part * step // depth, (part + 1) * step // depth):
            span = slice(index * depth, (index + 1) * depth)
            key += dot32(gained[index], weight[0, span, :])
            value += dot32(gained[index], weight[1, span, :])
    key = key * factor
    turned = jnp.dot(
        key, swap[...], preferred_element_type=jnp.float32, precision=lax.Precision.HIGHEST
    )
    out[0] = (key * cosine[...] + turned * sine[...]).astype(jnp.bfloat16)
    out[1] = (value * factor).astype(jnp.bfloat16)


def queries(gained, weight_hbm, scale, cosine, sine, swap, out, weight, total, sems):
    count, rows, depth = gained.shape
    parts = sems.shape[0]
    step = weight.shape[0] // parts

    def fetch(part):
        span = pl.ds(part * step, step)
        return pltpu.make_async_copy(weight_hbm.at[span, :], weight.at[span, :], sems.at[part])

    for part in range(parts):
        fetch(part).start()
    for part in range(parts):
        fetch(part).wait()
        span = range(part * step // depth, (part + 1) * step // depth)
        act = jnp.concatenate([gained[index] for index in span], axis=1)
        term = dot32(act, weight[part * step : (part + 1) * step, :])
        total[...] = term if part == 0 else total[...] + term
    for head in range(out.shape[1] // HEAD_WIDTH):
        lanes = slice(head * HEAD_WIDTH, (head + 1) * HEAD_WIDTH)
        query = total[:, lanes] * scale[...]
        turned = jnp.dot(
            query, swap[...], preferred_element_type=jnp.float32, precision=lax.Precision.HIGHEST
        )
        out[:, lanes] = (query * cosine[...] + turned * sine[...]).astype(jnp.bfloat16)


def attend_out(
    info, query, mine, partner, allowed, weight_hbm, out, weight, context, result, sems, out_sems
):
    parts = sems.shape[0]
    step = weight.shape[1] // parts

    def fetch(part):
        span = pl.ds(part * step, step)
        return pltpu.make_async_copy(weight_hbm.at[:, span], weight.at[:, span], sems.at[part])

    def store(part):
        span = pl.ds(part * step, step)
        return pltpu.make_async_copy(result.at[:, span], out.at[:, span], out_sems.at[part])

    for part in range(parts):
        fetch(part).start()
    odd = info[17] == 1
    own = mine[...].astype(jnp.float32)
    far = partner[...].astype(jnp.float32)
    low = jnp.where(odd, far, own)
    high = jnp.where(odd, own, far)
    pair = jnp.concatenate([low, high], axis=2).astype(jnp.bfloat16)
    key, value = pair[0], pair[1]
    heads = [
        slice(head * HEAD_WIDTH, (head + 1) * HEAD_WIDTH)
        for head in range(query.shape[1] // HEAD_WIDTH)
    ]
    scores = [
        lax.dot_general(
            query[:, lanes], key, (((1,), (1,)), ((), ())), preferred_element_type=jnp.float32
        )
        for lanes in heads
    ]
    for lanes, prob in zip(heads, masked_softmax(scores, allowed[...] > 0, HEAD_WIDTH)):
        context[:, lanes] = dot32(prob, value).astype(jnp.bfloat16)
    for part in range(parts):
        fetch(part).wait()
        span = slice(part * step, (part + 1) * step)
        result[:, span] = dot32(context[...], weight[:, span]).astype(jnp.bfloat16)
        store(part).start()
    for part in range(parts):
        store(part).wait()


def finish(info, terms, own, out):
    cols = own.shape[2]
    rows = own.shape[1]
    live = info[18] + lax.broadcasted_iota(jnp.int32, (rows, cols), 0) < info[19]
    for index in range(own.shape[0]):
        lanes = slice(index * cols, (index + 1) * cols)
        total = jnp.sum(terms[:, :, lanes].astype(jnp.float32), axis=0)
        total = total + own[index].astype(jnp.float32)
        out[:, lanes] = jnp.where(live, total, 0.0).astype(jnp.bfloat16)


def visibility(masks, live_count):
    positions = jnp.arange(SPAN_LIMIT)
    passage = positions // CPP
    expanded = jnp.repeat(jnp.repeat(masks, CPP, axis=0), CPP, axis=1) > 0
    same_passage = passage[:, None] == passage[None, :]
    earlier = positions[None, :] <= positions[:, None]
    key_live = positions[None, :] < live_count
    diagonal = positions[:, None] == positions[None, :]
    return diagonal | earlier & key_live & (same_passage | expanded)


def local(
    span_tokens,
    enc_dest,
    passages,
    req_slot,
    block_mask,
    enc_qkv,
    enc_out,
    enc_up,
    enc_down,
    proj_in,
    proj_out,
    norm_gain,
    q_weight,
    key_value_weight,
    out_weight,
):
    tensor_count = lax.axis_size("tensor")
    seq_count = lax.axis_size("seq")
    tensor_index = lax.axis_index("tensor")
    seq_index = lax.axis_index("seq")
    core = seq_index % 2
    device_count = tensor_count * seq_count
    rows = SPAN_LIMIT
    own_rows = rows // tensor_count
    spans, span_size, width = span_tokens.shape
    model_width = proj_out.shape[1]
    share = enc_qkv.shape[0]
    x_index, y_index = tensor_index // SIDE, tensor_index % SIDE

    steps = jnp.array([0, SIDE - 1, 1, 2])
    outer, inside = jnp.repeat(steps, SIDE), jnp.tile(steps, SIDE)
    by_x = SIDE * ((x_index + outer) % SIDE) + (y_index + inside) % SIDE
    by_y = SIDE * ((x_index + inside) % SIDE) + (y_index + outer) % SIDE
    shards = jnp.where(core == 0, by_x, by_y)
    scalars = jnp.stack([core, tensor_index % 2, tensor_index * own_rows])
    info = jnp.concatenate([shards, scalars]).astype(jnp.int32)

    requests = jnp.arange(req_slot.shape[0])
    dest_slot = jnp.sum(
        jnp.where(enc_dest[:, None] // SPAN_LIMIT == requests[None, :], req_slot[None, :], 0), axis=1
    ).reshape(device_count, own_rows)
    dest_place = (enc_dest % SPAN_LIMIT).reshape(device_count, own_rows)
    own_slots = lax.dynamic_slice_in_dim(
        dest_slot, seq_index * tensor_count + tensor_index, 1, 0
    )
    pick = (jnp.arange(seq_count)[:, None] == own_slots).astype(jnp.bfloat16)
    place_of = jnp.sum(jnp.where(dest_slot == seq_index, dest_place, 0), axis=1)
    order = (jnp.arange(rows)[:, None] == place_of[None, :]).astype(jnp.bfloat16)
    chosen = jnp.sum(jnp.where(req_slot == seq_index, requests, 0))
    live_count = jnp.sum(jnp.where(requests == chosen, passages, 0)) * CPP
    masks = jnp.sum(
        jnp.where(requests[:, None, None] == chosen, block_mask, 0), axis=0
    )
    allowed = visibility(masks, live_count).astype(jnp.float32)
    live_info = jnp.concatenate([info, live_count[None]]).astype(jnp.int32)

    positions = jnp.arange(rows).astype(jnp.float32)
    lane = jnp.arange(HEAD_WIDTH)
    frequency = jnp.exp(
        -(2.0 * (lane // 2).astype(jnp.float32) / HEAD_WIDTH) * math.log(500000.0)
    )
    angles = positions[:, None] * frequency[None, :]
    cosine, sine = jnp.cos(angles), jnp.sin(angles)
    swap = jnp.where(
        (lane[:, None] ^ 1) == lane[None, :], jnp.where(lane[None, :] % 2 == 0, -1.0, 1.0), 0.0
    ).astype(jnp.float32)

    own_tokens = span_tokens.reshape(spans * span_size, width)
    own_qkv = whole_call(
        take_qkv, "take_qkv", info, [enc_qkv], shape_of((share, 3 * width // 2)), limit=4
    )
    units = enc_down.shape[0] // 2
    middle_cols = width // 2 + units * tensor_count
    own_rest = whole_call(
        take_rest,
        "take_rest",
        info,
        [enc_out, enc_up, enc_down],
        shape_of((share, middle_cols + width)),
        limit=4,
    )
    qkv_block = whole_call(
        join_qkv,
        "join_qkv",
        info,
        short_ring(own_qkv),
        shape_of((SIDE, share, 3 * width // 2)),
        limit=6,
    )
    def ring(block, relay):
        left = to_ring(block, 2, 1)
        right = to_ring(block, 2, -1)
        opposite = to_ring(left, 2, 1) if relay == 1 else to_ring(right, 2, -1)
        return [block, left, right, opposite]

    qkv = ring(qkv_block, 1)
    middle_block, lower_block = whole_call(
        join_rest,
        "join_rest",
        info,
        short_ring(own_rest),
        (shape_of((SIDE, share, middle_cols)), shape_of((SIDE, share, width))),
        limit=8,
        after=qkv[1:3],
    )
    other_tokens = to_core(own_tokens)
    token_pieces = whole_call(
        both_rows,
        "both_rows",
        info,
        [own_tokens, other_tokens],
        shape_of((tensor_count, 2 * spans * span_size, share)),
    )
    all_rows = 2 * spans * span_size

    middle = ring(middle_block, -1)
    lower = ring(lower_block, 1)

    share_cols = model_width // tensor_count
    proj_mine = lax.all_to_all(
        whole_call(
            spread_proj,
            "spread_proj",
            info,
            [proj_out],
            shape_of((tensor_count, proj_out.shape[0], share_cols // 2)),
            after=[qkv_block],
        ),
        "tensor",
        0,
        0,
    )
    proj_other = to_core(proj_mine)
    context = whole_call(
        span_attention,
        "span_attention",
        info,
        [token_pieces, *qkv],
        shape_of((tensor_count // 2, all_rows, share)),
        [pltpu.VMEM((all_rows, 3 * width // 2), jnp.bfloat16)],
        flops=2 * all_rows * width * 3 * width // 2,
        after=[proj_mine],
    )
    attended = whole_call(
        context_out,
        "context_out",
        info,
        [context, to_core(context), *middle],
        shape_of((all_rows, width // 2)),
        [pltpu.VMEM((tensor_count, all_rows, share), jnp.bfloat16)],
        flops=2 * all_rows * width * width // 2,
    )
    first_out, inner = whole_call(
        norm_up,
        "norm_up",
        info,
        [own_tokens, other_tokens, attended, to_core(attended), *middle],
        (shape_of((all_rows, width)), shape_of((tensor_count, all_rows, units))),
        [
            pltpu.VMEM((tensor_count, all_rows, share), jnp.bfloat16),
            pltpu.VMEM((all_rows, width), jnp.bfloat16),
        ],
        flops=2 * all_rows * width * width,
    )
    kept, sent = whole_call(
        down,
        "down",
        info,
        [inner, first_out, *lower],
        (
            shape_of((all_rows // 2, width), jnp.float32),
            shape_of((all_rows // 2, width)),
        ),
        [pltpu.VMEM((all_rows, width), jnp.float32)],
        flops=2 * all_rows * width * width,
    )
    outgoing = whole_call(
        norm_pool,
        "norm_pool",
        info,
        [kept, to_core(sent), pick],
        shape_of((seq_count, tensor_count, width // 128, 128)),
        [pltpu.VMEM((seq_count, width // 128, 128), jnp.float32)],
    )
    arrived = lax.all_to_all(
        outgoing.reshape(device_count, width // 128, 128), AXES, 0, 0
    )

    spread = whole_call(
        embed,
        "embed",
        info,
        [arrived, order, proj_in, proj_mine, proj_other],
        shape_of((tensor_count, rows, share_cols)),
        [
            pltpu.VMEM((device_count, width // 128, 128), jnp.float32),
            pltpu.VMEM((rows, share_cols), jnp.bfloat16),
            pltpu.SemaphoreType.DMA((tensor_count,)),
        ],
        limit=50,
        flops=2 * rows * width * (width + share_cols),
        out_space=pltpu.HBM,
    )
    embedded = lax.all_to_all(spread, "tensor", 0, 0)
    own_embedded = lax.dynamic_slice_in_dim(embedded, tensor_index * own_rows, own_rows, 1)

    query_cols = q_weight.shape[1]
    kv_cols = key_value_weight.shape[2]
    key_start = tensor_index * kv_cols % HEAD_WIDTH
    key_cosine = lax.dynamic_slice_in_dim(cosine, key_start, kv_cols, 1)
    key_sine = lax.dynamic_slice_in_dim(sine, key_start, kv_cols, 1)
    parts = 8
    hbm = pl.BlockSpec(memory_space=pltpu.HBM)
    gained, scale, own_kv = pl.pallas_call(
        keys_values,
        name="keys_values",
        out_shape=(
            shape_of((tensor_count, rows, share_cols)),
            shape_of((rows, 1), jnp.float32),
            shape_of((2, rows, kv_cols)),
        ),
        in_specs=[VMEM, VMEM, hbm, VMEM, VMEM, VMEM],
        out_specs=(VMEM, VMEM, VMEM),
        scratch_shapes=[
            pltpu.VMEM((2, model_width, kv_cols), jnp.bfloat16),
            pltpu.SemaphoreType.DMA((parts,)),
        ],
        compiler_params=pltpu.CompilerParams(vmem_limit_bytes=56 * MIB),
    )(
        embedded,
        norm_gain.reshape(tensor_count, 1, share_cols),
        key_value_weight,
        key_cosine,
        key_sine,
        swap[:kv_cols, :kv_cols],
    )
    partner_kv = lax.ppermute(
        own_kv, "tensor", [(index, index ^ 1) for index in range(tensor_count)]
    )
    query = pl.pallas_call(
        queries,
        name="queries",
        out_shape=shape_of((rows, query_cols)),
        in_specs=[VMEM, hbm, VMEM, VMEM, VMEM, VMEM],
        out_specs=VMEM,
        scratch_shapes=[
            pltpu.VMEM((model_width, query_cols), jnp.bfloat16),
            pltpu.VMEM((rows, query_cols), jnp.float32),
            pltpu.SemaphoreType.DMA((parts,)),
        ],
        compiler_params=pltpu.CompilerParams(vmem_limit_bytes=52 * MIB),
        cost_estimate=pl.CostEstimate(
            flops=2 * rows * model_width * query_cols,
            bytes_accessed=2 * model_width * query_cols,
            transcendentals=0,
        ),
    )(gained, q_weight, scale, cosine, sine, swap)
    partial = pl.pallas_call(
        attend_out,
        name="attend_out",
        out_shape=shape_of((rows, model_width)),
        in_specs=[SMEM, VMEM, VMEM, VMEM, VMEM, hbm],
        out_specs=hbm,
        scratch_shapes=[
            pltpu.VMEM((query_cols, model_width), jnp.bfloat16),
            pltpu.VMEM((rows, query_cols), jnp.bfloat16),
            pltpu.VMEM((rows, model_width), jnp.bfloat16),
            pltpu.SemaphoreType.DMA((parts,)),
            pltpu.SemaphoreType.DMA((parts,)),
        ],
        compiler_params=pltpu.CompilerParams(vmem_limit_bytes=54 * MIB),
    )(info, query, own_kv, partner_kv, allowed, out_weight)
    terms = lax.all_to_all(
        partial.reshape(tensor_count, own_rows, model_width), "tensor", 0, 0
    )
    return whole_call(
        finish, "finish", live_info, [terms, own_embedded], shape_of((own_rows, model_width))
    )


def solution(mesh):
    return jax.shard_map(
        local,
        mesh=mesh,
        in_specs=(
            P(("seq", "tensor"), None, None),
            P(),
            P(),
            P(),
            P(),
            P("tensor", None),
            P("tensor", None),
            P("tensor", None),
            P("tensor", None),
            P(),
            P("tensor", None),
            P(),
            P(None, "tensor"),
            P(None, None, "tensor"),
            P("tensor", None),
        ),
        out_specs=P(("seq", "tensor"), None),
        check_vma=False,
    )
```

time: 220 us -> 202 us (0.918)
  local copies, waits for them, and re-layouts: 26.6 us -> 14.6 us
  waiting for transfers between devices: 98.8 us -> 91.8 us
  Pallas kernels: 39.3 us -> 42.8 us
    all_to_all x2 -> x0, waiting for transfers between devices: 25.3 us -> none  [short_gather(): return lax.all_to_all(spread, AXES, 0, 0, axis_index_groups=ring_groups(1))]
    ppermute x9 -> x15, waiting for transfers between devices: 8.56 us -> 30.8 us  [to_ring(): return lax.ppermute(value, AXES, ring_pairs(phase, distance))]
    unnamed x49 -> x39, local copies, waits for them, and re-layouts: 23.8 us -> 11.2 us
    ppermute x9 -> x15, starting transfers between devices: 14 us -> 23.1 us  [to_ring(): return lax.ppermute(value, AXES, ring_pairs(phase, distance))]
    all_to_all x2 -> x0, starting transfers between devices: 8.09 us -> none  [short_gather(): return lax.all_to_all(spread, AXES, 0, 0, axis_index_groups=ring_groups(1))]
    all_to_all x1, waiting for transfers between devices: 24 us -> 20.1 us  [local(): embedded = lax.all_to_all(spread, 'tensor', 0, 0)]
    all_to_all x1, starting transfers between devices: 11.2 us -> 7.47 us  [local(): lax.all_to_all(outgoing.reshape(device_count, width // 128, 128), AXES, 0...]
    pallas_call x14 -> x16, Pallas kernels: 39.3 us -> 42.8 us  [the longest x13 24.8 us: whole_call(): pl.pallas_call(run, name=name, out_shape=outs, in_specs=[SMEM] + [VMEM] *...]
  transfers between devices with their start and end apart: 21 -> 25, of which waited for: 9 -> 17; matrix products, arithmetic and copies ran while one was open for 4% -> 6% of each run, Pallas kernels for 11% -> 10%
where the time goes in v1:
time: 202 us; the launch traced here: 201 us
  waiting for transfers between devices  91.8 us (45%)
  starting transfers between devices  46.4 us (23%)
  Pallas kernels  42.8 us (21%)
  local copies, waits for them, and re-layouts  14.6 us (7%)
  other arithmetic  4.79 us (2%)
    ppermute x15, waiting for transfers between devices, to_ring(): return lax.ppermute(value, AXES, ring_pairs(phase, distance))  30.8 us
    all_to_all x1, waiting for transfers between devices, local(): lax.all_to_all(partial.reshape(tensor_count, own_rows, model_width), 'ten...  26.9 us
    pallas_call x13, Pallas kernels, whole_call(): pl.pallas_call(run, name=name, out_shape=outs, in_specs=[SMEM] + [VMEM] *...  24.8 us
    ppermute x15, starting transfers between devices, to_ring(): return lax.ppermute(value, AXES, ring_pairs(phase, distance))  23.1 us
    all_to_all x1, waiting for transfers between devices, local(): embedded = lax.all_to_all(spread, 'tensor', 0, 0)  20.1 us
    unnamed x39, local copies, waits for them, and re-layouts  11.2 us
    all_to_all x1, waiting for transfers between devices, local(): lax.all_to_all(outgoing.reshape(device_count, width // 128, 128), AXES, 0...  10.2 us
    all_to_all x1, starting transfers between devices, local(): lax.all_to_all(outgoing.reshape(device_count, width // 128, 128), AXES, 0...  7.47 us
  transfers between devices with their start and end apart: 25, of which 17 were waited for; matrix products, arithmetic and copies ran while one was open for 6% of the time, Pallas kernels for 10%

profile of v1, /device:TPU:0, one launch (start us, length us, event | category | flops | bytes accessed | tf_op | source)
XLA Modules:
  0.0 201.5 jit_solution(12273450588413532044)
XLA Ops:
  0.0 0.7 broadcast_add_fusion
  1.3 1.0 copy-done.7
  2.3 0.6 take_qkv.1.refs_1_
  2.8 1.7 collective-permute-start.1
  4.6 1.6 collective-permute-start.2
  6.1 2.1 %collective-permute-start.3 = (bf16[64,1536]{1,0:T(8,128)(2,1)S(1)}, bf16[64,1536]{1,0:T(8,128)(2,1)S(1)}, u32[]{:S(2)}, u32[]{:S(2)}) collective-permute-start(bf16[64,1536]{1,0:T(8,128)(2,1)S(1)} %take_qkv.1.refs_1_), channel_id=1, source_target_pairs={{0,2},{1,3},{2,0},{3,1},{4,6},{5,7},{6,4},{7,5},{8,10},{9,11},{10,... | collective-permute-start | bytes 589832 | tf_op jit(solution)/shard_map/ppermute | solution.py:66
  8.2 1.6 collective-permute-done.1.refs_2_
  10.2 3.1 %collective-permute-done.3.refs_4_ = bf16[64,1536]{1,0:T(8,128)(2,1)S(1)} collective-permute-done((bf16[64,1536]{1,0:T(8,128)(2,1)S(1)}, bf16[64,1536]{1,0:T(8,128)(2,1)S(1)}, u32[]{:S(2)}, u32[]{:S(2)}) %collective-permute-start.3) | collective-permute-done | bytes 196640 | tf_op jit(solution)/shard_map/ppermute | solution.py:66
  13.3 0.6 join_qkv.1.refs_2_
  13.9 1.6 collective-permute-start.4
  15.6 1.7 collective-permute-start.5
  17.2 0.8 take_rest.1.refs_1_
  18.0 1.4 collective-permute-start.8
  19.4 1.9 collective-permute-start.9
  21.3 0.9 collective-permute-start.10
  22.2 6.2 %collective-permute-done.8.refs_2_ = bf16[64,2560]{1,0:T(8,128)(2,1)S(1)} collective-permute-done((bf16[64,2560]{1,0:T(8,128)(2,1)S(1)}, bf16[64,2560]{1,0:T(8,128)(2,1)S(1)}, u32[]{:S(2)}, u32[]{:S(2)}) %collective-permute-start.8) | collective-permute-done | bytes 327712 | tf_op jit(solution)/shard_map/ppermute | solution.py:66
  28.4 2.9 %collective-permute-done.9.refs_3_ = bf16[64,2560]{1,0:T(8,128)(2,1)S(1)} collective-permute-done((bf16[64,2560]{1,0:T(8,128)(2,1)S(1)}, bf16[64,2560]{1,0:T(8,128)(2,1)S(1)}, u32[]{:S(2)}, u32[]{:S(2)}) %collective-permute-start.9) | collective-permute-done | bytes 327712 | tf_op jit(solution)/shard_map/ppermute | solution.py:66
  31.3 1.8 collective-permute-done.10.refs_4_
  33.1 1.1 collective-permute-done.4.refs_3_.refs_5_
  34.6 1.4 join_rest.1
  36.0 2.9 %collective-permute-start.12 = (bf16[4,64,1536]{2,1,0:T(8,128)(2,1)S(1)}, bf16[4,64,1536]{2,1,0:T(8,128)(2,1)}, u32[]{:S(2)}, u32[]{:S(2)}) collective-permute-start(bf16[4,64,1536]{2,1,0:T(8,128)(2,1)S(1)} %get-tuple-element.14.refs_3_.refs_5_), channel_id=1, source_target_pairs={{0,12},{1,13},{2,14},{3,15},{4,0},{5,1},{6,2},{7,3},{8,4},{9,5},{1... | collective-permute-start | bytes 2359304 | tf_op jit(solution)/shard_map/ppermute | solution.py:66
  38.9 1.4 spread_proj.1
  40.3 6.1 %all-to-all-start = ((bf16[16,64,256]{2,1,0:T(8,128)(2,1)}), bf16[16,64,256]{2,1,0:T(8,128)(2,1)S(1)}, u32[]{:S(2)}, u32[]{:S(2)}) async-start(bf16[16,64,256]{2,1,0:T(8,128)(2,1)} %spread_proj.1), calls=%async_computation | async-start | bytes 1048576 | tf_op jit(solution)/shard_map/all_to_all | solution.py:553
  46.5 1.9 collective-permute-start.11
  48.4 4.3 %collective-permute-done.12.refs_5_.refs_7_ = bf16[4,64,1536]{2,1,0:T(8,128)(2,1)} collective-permute-done((bf16[4,64,1536]{2,1,0:T(8,128)(2,1)S(1)}, bf16[4,64,1536]{2,1,0:T(8,128)(2,1)}, u32[]{:S(2)}, u32[]{:S(2)}) %collective-permute-start.12) | collective-permute-done | bytes 786464 | tf_op jit(solution)/shard_map/ppermute | solution.py:66
  52.7 3.8 %collective-permute-start.13 = (bf16[4,64,1536]{2,1,0:T(8,128)(2,1)}, bf16[4,64,1536]{2,1,0:T(8,128)(2,1)}, u32[]{:S(2)}, u32[]{:S(2)}) collective-permute-start(bf16[4,64,1536]{2,1,0:T(8,128)(2,1)} %collective-permute-done.12.refs_5_.refs_7_), channel_id=1, source_target_pairs={{0,12},{1,13},{2,14},{3,15},{4,0},{5,1},{6,2},{7,3},{8,4},{9,5},{1... | collective-permute-start | bytes 2359304 | tf_op jit(solution)/shard_map/ppermute | solution.py:66
  56.4 1.5 collective-permute-done.refs_2_
  58.0 0.9 both_rows.1.refs_1_
  58.8 0.7 copy-done.4
  59.6 1.1 copy-done.1
  60.7 3.5 %span_attention.1.refs_1_ = bf16[8,256,64]{2,1,0:T(8,128)(2,1)S(1)} custom-call(s32[19]{0:T(128)S(1)} %pad_add_fusion.refs_0_.info, bf16[16,256,64]{2,1,0:T(8,128)(2,1)S(1)} %both_rows.1.refs_1_, bf16[4,64,1536]{2,1,0:T(8,128)(2,1)S(1)} %join_qkv.1.refs_2_, bf16[4,64,1536]{2,1,0:T(8,128)(2,1)} %collective-permute-done.4.refs_3_.refs_5_, ...), custom_call_target="tpu_custom_call" | custom-call | flops 805306368 | bytes 3670016 | tf_op jit(solution)/shard_map/span_attention/pallas_call | solution.py:93
  64.4 1.7 collective-permute-start.16
  66.1 6.0 %collective-permute-done.15.refs_4_ = bf16[4,64,1024]{2,1,0:T(8,128)(2,1)} collective-permute-done((bf16[4,64,1024]{2,1,0:T(8,128)(2,1)}, bf16[4,64,1024]{2,1,0:T(8,128)(2,1)}, u32[]{:S(2)}, u32[]{:S(2)}) %collective-permute-start.15) | collective-permute-done | bytes 524320 | tf_op jit(solution)/shard_map/ppermute | solution.py:66
  72.1 2.3 %context_out.1.refs_3_ = bf16[256,512]{1,0:T(8,128)(2,1)S(1)} custom-call(s32[19]{0:T(128)S(1)} %pad_add_fusion.refs_0_.info, bf16[8,256,64]{2,1,0:T(8,128)(2,1)S(1)} %span_attention.1.refs_1_, bf16[8,256,64]{2,1,0:T(8,128)(2,1)S(1)} %collective-permute-done.7.refs_2_, bf16[4,64,1536]{2,1,0:T(8,128)(2,1)S(1)} %get-tuple-element.14.refs_3_.refs_5_, ...), custom_call_target="tpu_custom_call" | custom-call | flops 268435456 | bytes 3670016 | tf_op jit(solution)/shard_map/context_out/pallas_call | solution.py:93
  75.2 1.1 collective-permute-done.14.refs_4_
  76.3 3.5 %norm_up.1 = (bf16[256,1024]{1,0:T(8,128)(2,1)S(1)}, bf16[16,256,64]{2,1,0:T(8,128)(2,1)S(1)}) custom-call(s32[19]{0:T(128)S(1)} %pad_add_fusion.refs_0_.info, bf16[128,1024]{1,0:T(8,128)(2,1)S(1)} %bitcast.15, bf16[128,1024]{1,0:T(8,128)(2,1)S(1)} %copy-done.5, bf16[256,512]{1,0:T(8,128)(2,1)S(1)} %context_out.1.refs_3_, ...), custom_call_target="tpu_custom_call" | custom-call | flops 536870912 | bytes 4194304 | tf_op jit(solution)/shard_map/norm_up/pallas_call | solution.py:93
  79.7 3.1 %collective-permute-done.17.refs_6_ = bf16[4,64,1024]{2,1,0:T(8,128)(2,1)} collective-permute-done((bf16[4,64,1024]{2,1,0:T(8,128)(2,1)}, bf16[4,64,1024]{2,1,0:T(8,128)(2,1)}, u32[]{:S(2)}, u32[]{:S(2)}) %collective-permute-start.17) | collective-permute-done | bytes 524320 | tf_op jit(solution)/shard_map/ppermute | solution.py:66
  82.8 2.3 %down.1 = (f32[128,1024]{1,0:T(8,128)S(1)}, bf16[128,1024]{1,0:T(8,128)(2,1)S(1)}) custom-call(s32[19]{0:T(128)S(1)} %pad_add_fusion.refs_0_.info, bf16[16,256,64]{2,1,0:T(8,128)(2,1)S(1)} %get-tuple-element.15.refs_1_, bf16[256,1024]{1,0:T(8,128)(2,1)S(1)} %get-tuple-element.16.refs_2_, bf16[4,64,1024]{2,1,0:T(8,128)(2,1)} %get-tuple-element.17.refs_3_, ...), custom_call_target="tpu_custom_call" | custom-call | flops 536870912 | bytes 3145728 | tf_op jit(solution)/shard_map/down/pallas_call | solution.py:93
  85.7 1.0 collective-permute-done.18.refs_2_
  86.7 1.7 norm_pool.1
  88.4 7.5 %all-to-all-start.1 = ((bf16[128,8,128]{2,1,0:T(8,128)(2,1)}), bf16[128,8,128]{2,1,0:T(8,128)(2,1)S(1)}, u32[]{:S(2)}, u32[]{:S(2)}) async-start(bf16[128,8,128]{2,1,0:T(8,128)(2,1)} %bitcast.6), calls=%async_computation.1 | async-start | bytes 524288 | tf_op jit(solution)/shard_map/all_to_all | solution.py:618
  95.9 0.6 fusion.19
  96.6 10.2 %all-to-all-done.1.refs_1_ = bf16[128,8,128]{2,1,0:T(8,128)(2,1)S(1)} async-done(((bf16[128,8,128]{2,1,0:T(8,128)(2,1)}), bf16[128,8,128]{2,1,0:T(8,128)(2,1)S(1)}, u32[]{:S(2)}, u32[]{:S(2)}) %all-to-all-start.1) | async-done | bytes 262176 | tf_op jit(solution)/shard_map/all_to_all | solution.py:618
  106.8 4.4 %embed.1 = bf16[16,128,512]{2,1,0:T(8,128)(2,1)} custom-call(s32[19]{0:T(128)S(1)} %pad_add_fusion.refs_0_.info, bf16[128,8,128]{2,1,0:T(8,128)(2,1)S(1)} %all-to-all-done.1.refs_1_, bf16[128,128]{1,0:T(8,128)(2,1)S(1)} %fusion.refs_2_, bf16[1024,1024]{1,0:T(8,128)(2,1)} %refs_3_.3, bf16[16,64,256]{2,1,0:T(8,128)(2,1)S(1)} %all-to-all-done.refs_6_.refs_4_, ...), custom_call_target="tpu_custom_call" | custom-call | flops 402653184 | bytes 3440640 | tf_op jit(solution)/shard_map/embed/pallas_call | solution.py:93
  111.2 3.7 %all-to-all-start.2 = ((bf16[16,128,512]{2,1,0:T(8,128)(2,1)}), bf16[16,128,512]{2,1,0:T(8,128)(2,1)S(1)}, u32[]{:S(2)}, u32[]{:S(2)}) async-start(bf16[16,128,512]{2,1,0:T(8,128)(2,1)} %embed.1), calls=%async_computation.2 | async-start | bytes 4194304 | tf_op jit(solution)/shard_map/all_to_all | solution.py:637
  114.9 1.3 select_reduce_fusion.3
  116.9 4.8 %copy.23.weight_hbm = bf16[2,8192,64]{2,1,0:T(8,128)(2,1)} copy(bf16[2,8192,64]{1,2,0:T(8,128)(2,1)} %param.29) | data formatting | bytes 4194304 | tf_op args[13]
  121.8 0.6 slice.4.swap
  122.4 0.6 iota_compare_fusion.7
  124.0 0.7 constant_dynamic-slice_fusion.1
  124.7 0.7 fusion.3.allowed
  125.4 20.1 %all-to-all-done.2.emb = bf16[16,128,512]{2,1,0:T(8,128)(2,1)S(1)} async-done(((bf16[16,128,512]{2,1,0:T(8,128)(2,1)}), bf16[16,128,512]{2,1,0:T(8,128)(2,1)S(1)}, u32[]{:S(2)}, u32[]{:S(2)}) %all-to-all-start.2) | async-done | bytes 2097184 | tf_op jit(solution)/shard_map/all_to_all | solution.py:637
  145.5 1.4 copy-done.13
  146.9 6.3 %keys_values.1 = (bf16[16,128,512]{2,1,0:T(8,128)(2,1)}, f32[128,1]{1,0:T(8,128)}, bf16[2,128,64]{2,1,0:T(8,128)(2,1)}) custom-call(bf16[16,128,512]{2,1,0:T(8,128)(2,1)} %copy-done.13, f32[16,1,512]{2,1,0:T(1,128)} %bitcast.18, bf16[2,8192,64]{2,1,0:T(8,128)(2,1)} %copy.23.weight_hbm, f32[128,64]{1,0:T(8,128)} %get-tuple-element.30.cosine, ...), custom_call_target="tpu_custom_call" | custom-call | tf_op jit(solution)/shard_map/keys_values/pallas_call | solution.py:647
  153.2 0.9 collective-permute-start.20
  154.1 0.8 copy-done.12
  154.9 5.7 %queries.1.query = bf16[128,512]{1,0:T(8,128)(2,1)S(1)} custom-call(bf16[16,128,512]{2,1,0:T(8,128)(2,1)} %get-tuple-element.20.gained, bf16[8192,512]{1,0:T(8,128)(2,1)} %weight_hbm.3, f32[128,1]{1,0:T(8,128)S(1)} %copy-done.12, f32[128,128]{1,0:T(8,128)S(1)} %get-tuple-element.26.cosine, f32[128,128]{1,0:T(8,128)S(1)} %get-tuple-element.25.sine, ...), custom_call_target="tpu_custom_call" | custom-call | flops 1073741824 | bytes 8388608 | tf_op jit(solution)/shard_map/queries/pallas_call | solution.py:673
  160.6 0.6 copy-done.6
  161.3 0.6 copy-done.14
  161.9 5.9 %attend_out.1 = bf16[128,8192]{1,0:T(8,128)(2,1)} custom-call(s32[19]{0:T(128)} %copy-done.11, bf16[128,512]{1,0:T(8,128)(2,1)} %copy-done.6, bf16[2,128,64]{2,1,0:T(8,128)(2,1)} %get-tuple-element.22.mine, bf16[2,128,64]{2,1,0:T(8,128)(2,1)} %copy-done.14, f32[128,128]{1,0:T(8,128)} %fusion.3.allowed, bf16[512,8192]{1,0:T(8,128)(2,1)} %weight_hbm.4), custom_call_target="tpu_custom_call" | custom-call | tf_op jit(solution)/shard_map/attend_out/pallas_call | solution.py:691
  167.9 4.1 %all-to-all-start.3 = ((bf16[16,8,8192]{2,1,0:T(8,128)(2,1)}), bf16[16,8,8192]{2,1,0:T(8,128)(2,1)S(1)}, u32[]{:S(2)}, u32[]{:S(2)}) async-start(bf16[16,8,8192]{2,1,0:T(8,128)(2,1)} %bitcast.16), calls=%async_computation.3 | async-start | bytes 4194304 | tf_op jit(solution)/shard_map/all_to_all | solution.py:706
  172.1 0.9 constant_dynamic-slice_fusion.refs_2_
  173.0 26.9 %all-to-all-done.3.refs_1_ = bf16[16,8,8192]{2,1,0:T(8,128)(2,1)S(1)} async-done(((bf16[16,8,8192]{2,1,0:T(8,128)(2,1)}), bf16[16,8,8192]{2,1,0:T(8,128)(2,1)S(1)}, u32[]{:S(2)}, u32[]{:S(2)}) %all-to-all-start.3) | async-done | bytes 2097184 | tf_op jit(solution)/shard_map/all_to_all | solution.py:706
  200.0 1.5 finish.1
  (83 shorter events, 3.9 us)
Async XLA Ops:
  1.3 1.0 copy-start.7
  2.3 104.6 %copy-start.11 = (s32[19]{0:T(128)}, s32[19]{0:T(128)S(1)}, u32[]{:S(2)}) copy-start(s32[19]{0:T(128)S(1)} %pad_add_fusion.refs_0_.info) | copy-start | bytes 232
  2.3 15.0 %copy-start.8 = (bf16[64,2048]{1,0:T(8,128)(2,1)S(1)}, bf16[64,2048]{1,0:T(8,128)(2,1)}, u32[]{:S(2)}) copy-start(bf16[64,2048]{1,0:T(8,128)(2,1)} %refs_2_.1) | copy-start | bytes 786436
  2.3 15.0 %copy-start.9 = (bf16[128,1024]{1,0:T(8,128)(2,1)S(1)}, bf16[128,1024]{1,0:T(8,128)(2,1)}, u32[]{:S(2)}) copy-start(bf16[128,1024]{1,0:T(8,128)(2,1)} %refs_3_.2) | copy-start | bytes 786436
  2.3 15.0 %copy-start.10 = (bf16[64,1024]{1,0:T(8,128)(2,1)S(1)}, bf16[64,1024]{1,0:T(8,128)(2,1)}, u32[]{:S(2)}) copy-start(bf16[64,1024]{1,0:T(8,128)(2,1)} %refs_1_.5) | copy-start | bytes 393220
  2.8 6.9 %collective-permute-start.1 = (bf16[64,1536]{1,0:T(8,128)(2,1)S(1)}, bf16[64,1536]{1,0:T(8,128)(2,1)S(1)}, u32[]{:S(2)}, u32[]{:S(2)}) collective-permute-start(bf16[64,1536]{1,0:T(8,128)(2,1)S(1)} %take_qkv.1.refs_1_), channel_id=1, source_target_pairs={{0,1},{1,2},{2,3},{3,0},{4,5},{5,6},{6,7},{7,4},{8,9},{9,10},{10,1... | collective-permute-start | bytes 589832 | tf_op jit(solution)/shard_map/ppermute | solution.py:66
  4.6 5.7 %collective-permute-start.2 = (bf16[64,1536]{1,0:T(8,128)(2,1)S(1)}, bf16[64,1536]{1,0:T(8,128)(2,1)S(1)}, u32[]{:S(2)}, u32[]{:S(2)}) collective-permute-start(bf16[64,1536]{1,0:T(8,128)(2,1)S(1)} %take_qkv.1.refs_1_), channel_id=1, source_target_pairs={{0,3},{1,0},{2,1},{3,2},{4,7},{5,4},{6,5},{7,6},{8,11},{9,8},{10,9... | collective-permute-start | bytes 589832 | tf_op jit(solution)/shard_map/ppermute | solution.py:66
  6.1 7.2 %collective-permute-start.3 = (bf16[64,1536]{1,0:T(8,128)(2,1)S(1)}, bf16[64,1536]{1,0:T(8,128)(2,1)S(1)}, u32[]{:S(2)}, u32[]{:S(2)}) collective-permute-start(bf16[64,1536]{1,0:T(8,128)(2,1)S(1)} %take_qkv.1.refs_1_), channel_id=1, source_target_pairs={{0,2},{1,3},{2,0},{3,1},{4,6},{5,7},{6,4},{7,5},{8,10},{9,11},{10,... | collective-permute-start | bytes 589832 | tf_op jit(solution)/shard_map/ppermute | solution.py:66
  13.9 25.0 %copy-start.2 = (bf16[64,8192]{1,0:T(8,128)(2,1)S(1)}, bf16[64,8192]{1,0:T(8,128)(2,1)}, u32[]{:S(2)}) copy-start(bf16[64,8192]{1,0:T(8,128)(2,1)} %refs_1_.4) | copy-start | bytes 3145732
  13.9 20.3 %collective-permute-start.4 = (bf16[4,64,1536]{2,1,0:T(8,128)(2,1)S(1)}, bf16[4,64,1536]{2,1,0:T(8,128)(2,1)}, u32[]{:S(2)}, u32[]{:S(2)}) collective-permute-start(bf16[4,64,1536]{2,1,0:T(8,128)(2,1)S(1)} %join_qkv.1.refs_2_), channel_id=1, source_target_pairs={{0,4},{1,5},{2,6},{3,7},{4,8},{5,9},{6,10},{7,11},{8,12},{9,13},{1... | collective-permute-start | bytes 2359304 | tf_op jit(solution)/shard_map/ppermute | solution.py:66
  15.6 19.0 %collective-permute-start.5 = (bf16[4,64,1536]{2,1,0:T(8,128)(2,1)S(1)}, bf16[4,64,1536]{2,1,0:T(8,128)(2,1)S(1)}, u32[]{:S(2)}, u32[]{:S(2)}) collective-permute-start(bf16[4,64,1536]{2,1,0:T(8,128)(2,1)S(1)} %join_qkv.1.refs_2_), channel_id=1, source_target_pairs={{0,12},{1,13},{2,14},{3,15},{4,0},{5,1},{6,2},{7,3},{8,4},{9,5},{1... | collective-permute-start | bytes 2359304 | tf_op jit(solution)/shard_map/ppermute | solution.py:66
  18.0 10.4 %collective-permute-start.8 = (bf16[64,2560]{1,0:T(8,128)(2,1)S(1)}, bf16[64,2560]{1,0:T(8,128)(2,1)S(1)}, u32[]{:S(2)}, u32[]{:S(2)}) collective-permute-start(bf16[64,2560]{1,0:T(8,128)(2,1)S(1)} %take_rest.1.refs_1_), channel_id=1, source_target_pairs={{0,1},{1,2},{2,3},{3,0},{4,5},{5,6},{6,7},{7,4},{8,9},{9,10},{10,1... | collective-permute-start | bytes 983048 | tf_op jit(solution)/shard_map/ppermute | solution.py:66
  19.4 11.9 %collective-permute-start.9 = (bf16[64,2560]{1,0:T(8,128)(2,1)S(1)}, bf16[64,2560]{1,0:T(8,128)(2,1)S(1)}, u32[]{:S(2)}, u32[]{:S(2)}) collective-permute-start(bf16[64,2560]{1,0:T(8,128)(2,1)S(1)} %take_rest.1.refs_1_), channel_id=1, source_target_pairs={{0,3},{1,0},{2,1},{3,2},{4,7},{5,4},{6,5},{7,6},{8,11},{9,8},{10,9... | collective-permute-start | bytes 983048 | tf_op jit(solution)/shard_map/ppermute | solution.py:66
  21.3 11.8 %collective-permute-start.10 = (bf16[64,2560]{1,0:T(8,128)(2,1)S(1)}, bf16[64,2560]{1,0:T(8,128)(2,1)S(1)}, u32[]{:S(2)}, u32[]{:S(2)}) collective-permute-start(bf16[64,2560]{1,0:T(8,128)(2,1)S(1)} %take_rest.1.refs_1_), channel_id=1, source_target_pairs={{0,2},{1,3},{2,0},{3,1},{4,6},{5,7},{6,4},{7,5},{8,10},{9,11},{10,... | collective-permute-start | bytes 983048 | tf_op jit(solution)/shard_map/ppermute | solution.py:66
  34.6 1.5 copy-start
  36.0 20.4 %copy-start.3 = (bf16[8,16,1024]{2,1,0:T(8,128)(2,1)S(1)}, bf16[8,16,1024]{2,1,0:T(8,128)(2,1)}, u32[]{:S(2)}) copy-start(bf16[8,16,1024]{2,1,0:T(8,128)(2,1)} %param.16) | copy-start | bytes 786436
  36.0 16.6 %collective-permute-start.12 = (bf16[4,64,1536]{2,1,0:T(8,128)(2,1)S(1)}, bf16[4,64,1536]{2,1,0:T(8,128)(2,1)}, u32[]{:S(2)}, u32[]{:S(2)}) collective-permute-start(bf16[4,64,1536]{2,1,0:T(8,128)(2,1)S(1)} %get-tuple-element.14.refs_3_.refs_5_), channel_id=1, source_target_pairs={{0,12},{1,13},{2,14},{3,15},{4,0},{5,1},{6,2},{7,3},{8,4},{9,5},{1... | collective-permute-start | bytes 2359304 | tf_op jit(solution)/shard_map/ppermute | solution.py:66
  38.9 20.7 %collective-permute-start.6 = (bf16[4,64,1536]{2,1,0:T(8,128)(2,1)}, bf16[4,64,1536]{2,1,0:T(8,128)(2,1)}, u32[]{:S(2)}, u32[]{:S(2)}) collective-permute-start(bf16[4,64,1536]{2,1,0:T(8,128)(2,1)} %collective-permute-done.4.refs_3_.refs_5_), channel_id=1, source_target_pairs={{0,4},{1,5},{2,6},{3,7},{4,8},{5,9},{6,10},{7,11},{8,12},{9,13},{1... | collective-permute-start | bytes 2359304 | tf_op jit(solution)/shard_map/ppermute | solution.py:66
  40.3 19.2 %all-to-all-start = ((bf16[16,64,256]{2,1,0:T(8,128)(2,1)}), bf16[16,64,256]{2,1,0:T(8,128)(2,1)S(1)}, u32[]{:S(2)}, u32[]{:S(2)}) async-start(bf16[16,64,256]{2,1,0:T(8,128)(2,1)} %spread_proj.1), calls=%async_computation | async-start | bytes 1048576 | tf_op jit(solution)/shard_map/all_to_all | solution.py:553
  46.5 25.6 %collective-permute-start.11 = (bf16[4,64,1536]{2,1,0:T(8,128)(2,1)S(1)}, bf16[4,64,1536]{2,1,0:T(8,128)(2,1)}, u32[]{:S(2)}, u32[]{:S(2)}) collective-permute-start(bf16[4,64,1536]{2,1,0:T(8,128)(2,1)S(1)} %get-tuple-element.14.refs_3_.refs_5_), channel_id=1, source_target_pairs={{0,4},{1,5},{2,6},{3,7},{4,8},{5,9},{6,10},{7,11},{8,12},{9,13},{1... | collective-permute-start | bytes 2359304 | tf_op jit(solution)/shard_map/ppermute | solution.py:66
  52.7 19.4 %collective-permute-start.13 = (bf16[4,64,1536]{2,1,0:T(8,128)(2,1)}, bf16[4,64,1536]{2,1,0:T(8,128)(2,1)}, u32[]{:S(2)}, u32[]{:S(2)}) collective-permute-start(bf16[4,64,1536]{2,1,0:T(8,128)(2,1)} %collective-permute-done.12.refs_5_.refs_7_), channel_id=1, source_target_pairs={{0,12},{1,13},{2,14},{3,15},{4,0},{5,1},{6,2},{7,3},{8,4},{9,5},{1... | collective-permute-start | bytes 2359304 | tf_op jit(solution)/shard_map/ppermute | solution.py:66
  56.4 1.5 collective-permute-start
  56.4 15.7 %collective-permute-start.15 = (bf16[4,64,1024]{2,1,0:T(8,128)(2,1)}, bf16[4,64,1024]{2,1,0:T(8,128)(2,1)}, u32[]{:S(2)}, u32[]{:S(2)}) collective-permute-start(bf16[4,64,1024]{2,1,0:T(8,128)(2,1)} %get-tuple-element.17.refs_3_), channel_id=1, source_target_pairs={{0,4},{1,5},{2,6},{3,7},{4,8},{5,9},{6,10},{7,11},{8,12},{9,13},{1... | collective-permute-start | bytes 1572872 | tf_op jit(solution)/shard_map/ppermute | solution.py:66
  58.8 0.7 copy-start.4
  59.6 1.1 copy-start.1
  64.2 10.5 %copy-start.16 = (s32[1024]{0:T(1024)S(1)}, s32[1024]{0:T(1024)}, u32[]{:S(2)}) copy-start(s32[1024]{0:T(1024)} %param.17) | copy-start | bytes 12292
  64.2 10.6 %copy-start.17 = (s32[8]{0:T(128)S(1)}, s32[8]{0:T(128)}, u32[]{:S(2)}) copy-start(s32[8]{0:T(128)} %param.19) | copy-start | bytes 100
  64.2 12.0 %copy-start.5 = (bf16[128,1024]{1,0:T(8,128)(2,1)S(1)}, bf16[128,1024]{1,0:T(8,128)(2,1)}, u32[]{:S(2)}) copy-start(bf16[128,1024]{1,0:T(8,128)(2,1)} %copy-done.4) | copy-start | bytes 786436
  64.2 7.9 %collective-permute-start.7 = (bf16[8,256,64]{2,1,0:T(8,128)(2,1)S(1)}, bf16[8,256,64]{2,1,0:T(8,128)(2,1)S(1)}, u32[]{:S(2)}, u32[]{:S(2)}) collective-permute-start(bf16[8,256,64]{2,1,0:T(8,128)(2,1)S(1)} %span_attention.1.refs_1_), channel_id=1, source_target_pairs={{0,16},{16,0},{32,48},{48,32},{64,80},{80,64},{96,112},{112,96},{1... | collective-permute-start | bytes 786440 | tf_op jit(solution)/shard_map/ppermute | solution.py:70
  64.4 15.3 %collective-permute-start.16 = (bf16[4,64,1024]{2,1,0:T(8,128)(2,1)}, bf16[4,64,1024]{2,1,0:T(8,128)(2,1)}, u32[]{:S(2)}, u32[]{:S(2)}) collective-permute-start(bf16[4,64,1024]{2,1,0:T(8,128)(2,1)} %get-tuple-element.17.refs_3_), channel_id=1, source_target_pairs={{0,12},{1,13},{2,14},{3,15},{4,0},{5,1},{6,2},{7,3},{8,4},{9,5},{1... | collective-permute-start | bytes 1572872 | tf_op jit(solution)/shard_map/ppermute | solution.py:66
  72.1 10.7 %collective-permute-start.17 = (bf16[4,64,1024]{2,1,0:T(8,128)(2,1)}, bf16[4,64,1024]{2,1,0:T(8,128)(2,1)}, u32[]{:S(2)}, u32[]{:S(2)}) collective-permute-start(bf16[4,64,1024]{2,1,0:T(8,128)(2,1)} %collective-permute-done.15.refs_4_), channel_id=1, source_target_pairs={{0,4},{1,5},{2,6},{3,7},{4,8},{5,9},{6,10},{7,11},{8,12},{9,13},{1... | collective-permute-start | bytes 1572872 | tf_op jit(solution)/shard_map/ppermute | solution.py:66
  74.5 1.8 collective-permute-start.14
  85.1 1.6 collective-permute-start.18
  85.2 11.3 %collective-permute-start.19 = (bf16[16,64,256]{2,1,0:T(8,128)(2,1)S(1)}, bf16[16,64,256]{2,1,0:T(8,128)(2,1)S(1)}, u32[]{:S(2)}, u32[]{:S(2)}) collective-permute-start(bf16[16,64,256]{2,1,0:T(8,128)(2,1)S(1)} %all-to-all-done.refs_6_.refs_4_), channel_id=1, source_target_pairs={{0,16},{16,0},{32,48},{48,32},{64,80},{80,64},{96,112},{112,96},{1... | collective-permute-start | bytes 1572872 | tf_op jit(solution)/shard_map/ppermute | solution.py:70
  88.4 18.4 %all-to-all-start.1 = ((bf16[128,8,128]{2,1,0:T(8,128)(2,1)}), bf16[128,8,128]{2,1,0:T(8,128)(2,1)S(1)}, u32[]{:S(2)}, u32[]{:S(2)}) async-start(bf16[128,8,128]{2,1,0:T(8,128)(2,1)} %bitcast.6), calls=%async_computation.1 | async-start | bytes 524288 | tf_op jit(solution)/shard_map/all_to_all | solution.py:618
  111.2 3.8 %copy-start.18 = (s32[8]{0:T(128)S(1)}, s32[8]{0:T(128)}, u32[]{:S(2)}) copy-start(s32[8]{0:T(128)} %param.18) | copy-start | bytes 100
  111.2 34.4 %all-to-all-start.2 = ((bf16[16,128,512]{2,1,0:T(8,128)(2,1)}), bf16[16,128,512]{2,1,0:T(8,128)(2,1)S(1)}, u32[]{:S(2)}, u32[]{:S(2)}) async-start(bf16[16,128,512]{2,1,0:T(8,128)(2,1)} %embed.1), calls=%async_computation.2 | async-start | bytes 4194304 | tf_op jit(solution)/shard_map/all_to_all | solution.py:637
  116.9 6.2 %copy-start.15 = (s32[8,8,8]{2,1,0:T(8,128)S(1)}, s32[8,8,8]{2,1,0:T(8,128)}, u32[]{:S(2)}) copy-start(s32[8,8,8]{2,1,0:T(8,128)} %param.20) | copy-start | bytes 6148
  145.5 1.4 copy-start.13
  153.2 8.1 %collective-permute-start.20 = (bf16[2,128,64]{2,1,0:T(8,128)(2,1)}, bf16[2,128,64]{2,1,0:T(8,128)(2,1)S(1)}, u32[]{:S(2)}, u32[]{:S(2)}) collective-permute-start(bf16[2,128,64]{2,1,0:T(8,128)(2,1)} %get-tuple-element.22.mine), channel_id=1, source_target_pairs={{0,1},{1,0},{2,3},{3,2},{4,5},{5,4},{6,7},{7,6},{8,9},{9,8},{10,11... | collective-permute-start | bytes 98312 | tf_op jit(solution)/shard_map/ppermute | solution.py:670
  154.1 0.8 copy-start.12
  160.6 0.7 copy-start.6
  161.3 0.6 copy-start.14
  167.9 32.1 %all-to-all-start.3 = ((bf16[16,8,8192]{2,1,0:T(8,128)(2,1)}), bf16[16,8,8192]{2,1,0:T(8,128)(2,1)S(1)}, u32[]{:S(2)}, u32[]{:S(2)}) async-start(bf16[16,8,8192]{2,1,0:T(8,128)(2,1)} %bitcast.16), calls=%async_computation.3 | async-start | bytes 4194304 | tf_op jit(solution)/shard_map/all_to_all | solution.py:706

commit v2 on v1

--- a/solution.py
+++ b/solution.py
@@ -1,3 +1,4 @@
+import functools
 import math
 
 import jax
@@ -72,6 +73,12 @@
 
 def short_ring(block):
     return [block] + [to_ring(block, 1, distance) for distance in (1, -1, 2)]
+
+
+def short_relay(block):
+    left = to_ring(block, 1, 1)
+    right = to_ring(block, 1, -1)
+    return [block, left, right, to_ring(right, 1, -1)]
 
 
 VMEM = pl.BlockSpec(memory_space=pltpu.VMEM)
@@ -141,7 +148,7 @@
     out[:, at:] = down_weight[pl.ds(pl.multiple_of(core * units, units), units), :]
 
 
-def join_qkv(info, own, left, right, opposite, out):
+def join_blocks(info, own, left, right, opposite, out):
     for index, block in enumerate((own, left, right, opposite)):
         out[index] = block[...]
 
@@ -276,7 +283,7 @@
     out[...] = jnp.broadcast_to(lanes[...].astype(jnp.bfloat16)[:, None], out.shape)
 
 
-def embed(info, arrived, order, proj_in, mine, other, out, lanes, result, sems):
+def embed(info, arrived, order, proj_in, mine, other, out, lanes):
     core = info[16]
     lanes[...] = arrived[...].astype(jnp.float32)
     columns = [
@@ -289,104 +296,92 @@
     cols = mine.shape[2]
     near = dot32(hidden, mine[...].reshape(units, cols))
     far = dot32(hidden, other[...].reshape(units, cols))
-    low = jnp.where(core == 0, near, far).astype(jnp.bfloat16)
-    high = jnp.where(core == 0, far, near).astype(jnp.bfloat16)
-    result[:, :cols] = low
-    result[:, cols:] = high
-    copies = [
-        pltpu.make_async_copy(result, out.at[index], sems.at[index]) for index in range(out.shape[0])
-    ]
-    for copy in copies:
-        copy.start()
-    for copy in copies:
-        copy.wait()
-
-
-def keys_values(emb, gain, weight_hbm, cosine, sine, swap, gained, scale, out, weight, sems):
-    count, rows, depth = emb.shape
-    parts = sems.shape[0]
-    step = weight.shape[1] // parts
-
-    def fetch(part):
-        span = pl.ds(part * step, step)
-        return pltpu.make_async_copy(
-            weight_hbm.at[:, span, :], weight.at[:, span, :], sems.at[part]
-        )
-
-    for part in range(parts):
-        fetch(part).start()
-    square = jnp.zeros((rows, 1), jnp.float32)
-    for index in range(count):
-        wide = emb[index].astype(jnp.float32)
-        square += jnp.sum(wide * wide, axis=1, keepdims=True)
-        gained[index] = (wide * gain[index]).astype(jnp.bfloat16)
-    factor = lax.rsqrt(square / (count * depth) + 1e-05)
+    out[:, :cols] = jnp.where(core == 0, near, far).astype(jnp.bfloat16)
+    out[:, cols:] = jnp.where(core == 0, far, near).astype(jnp.bfloat16)
+
+
+def project(info, *refs, starts, count):
+    blocks, refs = refs[:count], refs[count:]
+    gain, q_weight, kv_weight = refs[:3]
+    before = refs[3:6] if len(refs) > 6 else None
+    q_total, kv_total, square = refs[-3:]
+    depth = blocks[0].shape[2]
+    queries, both = None, None
+    squares = None
+    for at, block in zip(starts, blocks):
+        for step in range(SIDE):
+            shard = info[SIDE * at + step]
+            wide = block[step].astype(jnp.float32)
+            act = (wide * gain[shard]).astype(jnp.bfloat16)
+            span = pl.ds(pl.multiple_of(shard * depth, depth), depth)
+            q_term = dot32(act, q_weight[span, :])
+            kv_term = dot32(act, kv_weight[span, :])
+            term = jnp.sum(wide * wide, axis=1, keepdims=True)
+            queries = q_term if queries is None else queries + q_term
+            both = kv_term if both is None else both + kv_term
+            squares = term if squares is None else squares + term
+    if before is not None:
+        queries, both, squares = queries + before[0][...], both + before[1][...], squares + before[2][...]
+    q_total[...] = queries
+    kv_total[...] = both
+    square[...] = squares
+
+
+def turn(values, cosine, sine, swap):
+    turned = jnp.dot(
+        values, swap, preferred_element_type=jnp.float32, precision=lax.Precision.HIGHEST
+    )
+    return values * cosine + turned * sine
+
+
+def last_keys(info, block, gain, kv_weight, kv_before, sq_before, cosine, sine, swap, out, scale):
+    depth = block.shape[2]
+    both = kv_before[...]
+    squares = sq_before[...]
+    for step in range(SIDE):
+        shard = info[SIDE * 3 + step]
+        wide = block[step].astype(jnp.float32)
+        act = (wide * gain[shard]).astype(jnp.bfloat16)
+        span = pl.ds(pl.multiple_of(shard * depth, depth), depth)
+        both += dot32(act, kv_weight[span, :])
+        squares += jnp.sum(wide * wide, axis=1, keepdims=True)
+    factor = lax.rsqrt(squares / (depth * SIDE * SIDE) + 1e-05)
     scale[...] = factor
-    key = jnp.zeros((rows, weight.shape[2]), jnp.float32)
-    value = jnp.zeros((rows, weight.shape[2]), jnp.float32)
-    for part in range(parts):
-        fetch(part).wait()
-        for index in range(part * step // depth, (part + 1) * step // depth):
-            span = slice(index * depth, (index + 1) * depth)
-            key += dot32(gained[index], weight[0, span, :])
-            value += dot32(gained[index], weight[1, span, :])
-    key = key * factor
-    turned = jnp.dot(
-        key, swap[...], preferred_element_type=jnp.float32, precision=lax.Precision.HIGHEST
-    )
-    out[0] = (key * cosine[...] + turned * sine[...]).astype(jnp.bfloat16)
-    out[1] = (value * factor).astype(jnp.bfloat16)
-
-
-def queries(gained, weight_hbm, scale, cosine, sine, swap, out, weight, total, sems):
-    count, rows, depth = gained.shape
-    parts = sems.shape[0]
-    step = weight.shape[0] // parts
-
-    def fetch(part):
-        span = pl.ds(part * step, step)
-        return pltpu.make_async_copy(weight_hbm.at[span, :], weight.at[span, :], sems.at[part])
-
-    for part in range(parts):
-        fetch(part).start()
-    for part in range(parts):
-        fetch(part).wait()
-        span = range(part * step // depth, (part + 1) * step // depth)
-        act = jnp.concatenate([gained[index] for index in span], axis=1)
-        term = dot32(act, weight[part * step : (part + 1) * step, :])
-        total[...] = term if part == 0 else total[...] + term
+    both = both * factor
+    cols = out.shape[2]
+    out[0] = turn(both[:, :cols], cosine[...], sine[...], swap[...]).astype(jnp.bfloat16)
+    out[1] = both[:, cols:].astype(jnp.bfloat16)
+
+
+def last_queries(info, block, gain, q_weight, q_before, scale, cosine, sine, swap, out):
+    depth = block.shape[2]
+    total = q_before[...]
+    for step in range(SIDE):
+        shard = info[SIDE * 3 + step]
+        act = (block[step].astype(jnp.float32) * gain[shard]).astype(jnp.bfloat16)
+        span = pl.ds(pl.multiple_of(shard * depth, depth), depth)
+        total += dot32(act, q_weight[span, :])
     for head in range(out.shape[1] // HEAD_WIDTH):
         lanes = slice(head * HEAD_WIDTH, (head + 1) * HEAD_WIDTH)
         query = total[:, lanes] * scale[...]
-        turned = jnp.dot(
-            query, swap[...], preferred_element_type=jnp.float32, precision=lax.Precision.HIGHEST
-        )
-        out[:, lanes] = (query * cosine[...] + turned * sine[...]).astype(jnp.bfloat16)
-
-
-def attend_out(
-    info, query, mine, partner, allowed, weight_hbm, out, weight, context, result, sems, out_sems
-):
-    parts = sems.shape[0]
+        out[:, lanes] = turn(query, cosine[...], sine[...], swap[...]).astype(jnp.bfloat16)
+
+
+def attend_out(info, query, mine, partner, allowed, weight, out, context, result, out_sems):
+    parts = out_sems.shape[0]
     step = weight.shape[1] // parts
-
-    def fetch(part):
-        span = pl.ds(part * step, step)
-        return pltpu.make_async_copy(weight_hbm.at[:, span], weight.at[:, span], sems.at[part])
 
     def store(part):
         span = pl.ds(part * step, step)
         return pltpu.make_async_copy(result.at[:, span], out.at[:, span], out_sems.at[part])
 
-    for part in range(parts):
-        fetch(part).start()
     odd = info[17] == 1
     own = mine[...].astype(jnp.float32)
     far = partner[...].astype(jnp.float32)
     low = jnp.where(odd, far, own)
     high = jnp.where(odd, own, far)
-    pair = jnp.concatenate([low, high], axis=2).astype(jnp.bfloat16)
-    key, value = pair[0], pair[1]
+    both = jnp.concatenate([low, high], axis=2).astype(jnp.bfloat16)
+    key, value = both[0], both[1]
     heads = [
         slice(head * HEAD_WIDTH, (head + 1) * HEAD_WIDTH)
         for head in range(query.shape[1] // HEAD_WIDTH)
@@ -400,7 +395,6 @@
     for lanes, prob in zip(heads, masked_softmax(scores, allowed[...] > 0, HEAD_WIDTH)):
         context[:, lanes] = dot32(prob, value).astype(jnp.bfloat16)
     for part in range(parts):
-        fetch(part).wait()
         span = slice(part * step, (part + 1) * step)
         result[:, span] = dot32(context[...], weight[:, span]).astype(jnp.bfloat16)
         store(part).start()
@@ -408,15 +402,16 @@
         store(part).wait()
 
 
-def finish(info, terms, own, out):
-    cols = own.shape[2]
-    rows = own.shape[1]
+def finish(info, terms, *refs):
+    own, out = refs[:-1], refs[-1]
+    rows, cols = own[0].shape[1:]
     live = info[18] + lax.broadcasted_iota(jnp.int32, (rows, cols), 0) < info[19]
-    for index in range(own.shape[0]):
-        lanes = slice(index * cols, (index + 1) * cols)
-        total = jnp.sum(terms[:, :, lanes].astype(jnp.float32), axis=0)
-        total = total + own[index].astype(jnp.float32)
-        out[:, lanes] = jnp.where(live, total, 0.0).astype(jnp.bfloat16)
+    for at, block in enumerate(own):
+        for step in range(SIDE):
+            lanes = pl.ds(pl.multiple_of(info[SIDE * at + step] * cols, cols), cols)
+            total = jnp.sum(terms[:, :, lanes].astype(jnp.float32), axis=0)
+            total = total + block[step].astype(jnp.float32)
+            out[:, lanes] = jnp.where(live, total, 0.0).astype(jnp.bfloat16)
 
 
 def visibility(masks, live_count):
@@ -502,53 +497,6 @@
     own_qkv = whole_call(
         take_qkv, "take_qkv", info, [enc_qkv], shape_of((share, 3 * width // 2)), limit=4
     )
-    units = enc_down.shape[0] // 2
-    middle_cols = width // 2 + units * tensor_count
-    own_rest = whole_call(
-        take_rest,
-        "take_rest",
-        info,
-        [enc_out, enc_up, enc_down],
-        shape_of((share, middle_cols + width)),
-        limit=4,
-    )
-    qkv_block = whole_call(
-        join_qkv,
-        "join_qkv",
-        info,
-        short_ring(own_qkv),
-        shape_of((SIDE, share, 3 * width // 2)),
-        limit=6,
-    )
-    def ring(block, relay):
-        left = to_ring(block, 2, 1)
-        right = to_ring(block, 2, -1)
-        opposite = to_ring(left, 2, 1) if relay == 1 else to_ring(right, 2, -1)
-        return [block, left, right, opposite]
-
-    qkv = ring(qkv_block, 1)
-    middle_block, lower_block = whole_call(
-        join_rest,
-        "join_rest",
-        info,
-        short_ring(own_rest),
-        (shape_of((SIDE, share, middle_cols)), shape_of((SIDE, share, width))),
-        limit=8,
-        after=qkv[1:3],
-    )
-    other_tokens = to_core(own_tokens)
-    token_pieces = whole_call(
-        both_rows,
-        "both_rows",
-        info,
-        [own_tokens, other_tokens],
-        shape_of((tensor_count, 2 * spans * span_size, share)),
-    )
-    all_rows = 2 * spans * span_size
-
-    middle = ring(middle_block, -1)
-    lower = ring(lower_block, 1)
-
     share_cols = model_width // tensor_count
     proj_mine = lax.all_to_all(
         whole_call(
@@ -557,13 +505,60 @@
             info,
             [proj_out],
             shape_of((tensor_count, proj_out.shape[0], share_cols // 2)),
-            after=[qkv_block],
+            after=[own_qkv],
         ),
         "tensor",
         0,
         0,
     )
     proj_other = to_core(proj_mine)
+    units = enc_down.shape[0] // 2
+    middle_cols = width // 2 + units * tensor_count
+    own_rest = whole_call(
+        take_rest,
+        "take_rest",
+        info,
+        [enc_out, enc_up, enc_down],
+        shape_of((share, middle_cols + width)),
+        limit=4,
+    )
+    qkv_block = whole_call(
+        join_blocks,
+        "join_qkv",
+        info,
+        short_ring(own_qkv),
+        shape_of((SIDE, share, 3 * width // 2)),
+        limit=6,
+    )
+    def ring(block, relay):
+        left = to_ring(block, 2, 1)
+        right = to_ring(block, 2, -1)
+        opposite = to_ring(left, 2, 1) if relay == 1 else to_ring(right, 2, -1)
+        return [block, left, right, opposite]
+
+    qkv = ring(qkv_block, 1)
+    middle_block, lower_block = whole_call(
+        join_rest,
+        "join_rest",
+        info,
+        short_relay(own_rest),
+        (shape_of((SIDE, share, middle_cols)), shape_of((SIDE, share, width))),
+        limit=8,
+        after=[*qkv[1:3], proj_mine],
+    )
+    other_tokens = to_core(own_tokens)
+    token_pieces = whole_call(
+        both_rows,
+        "both_rows",
+        info,
+        [own_tokens, other_tokens],
+        shape_of((tensor_count, 2 * spans * span_size, share)),
+    )
+    all_rows = 2 * spans * span_size
+
+    middle = ring(middle_block, -1)
+    lower = ring(lower_block, 1)
+
     context = whole_call(
         span_attention,
         "span_attention",
@@ -572,7 +567,6 @@
         shape_of((tensor_count // 2, all_rows, share)),
         [pltpu.VMEM((all_rows, 3 * width // 2), jnp.bfloat16)],
         flops=2 * all_rows * width * 3 * width // 2,
-        after=[proj_mine],
     )
     attended = whole_call(
         context_out,
@@ -619,23 +613,24 @@
         outgoing.reshape(device_count, width // 128, 128), AXES, 0, 0
     )
 
-    spread = whole_call(
+    own_cols = whole_call(
         embed,
         "embed",
         info,
         [arrived, order, proj_in, proj_mine, proj_other],
-        shape_of((tensor_count, rows, share_cols)),
-        [
-            pltpu.VMEM((device_count, width // 128, 128), jnp.float32),
-            pltpu.VMEM((rows, share_cols), jnp.bfloat16),
-            pltpu.SemaphoreType.DMA((tensor_count,)),
-        ],
-        limit=50,
+        shape_of((rows, share_cols)),
+        [pltpu.VMEM((device_count, width // 128, 128), jnp.float32)],
         flops=2 * rows * width * (width + share_cols),
-        out_space=pltpu.HBM,
-    )
-    embedded = lax.all_to_all(spread, "tensor", 0, 0)
-    own_embedded = lax.dynamic_slice_in_dim(embedded, tensor_index * own_rows, own_rows, 1)
+    )
+    first_block = whole_call(
+        join_blocks,
+        "join_columns",
+        info,
+        short_ring(own_cols),
+        shape_of((SIDE, rows, share_cols)),
+        limit=4,
+    )
+    embedded = ring(first_block, 1)
 
     query_cols = q_weight.shape[1]
     kv_cols = key_value_weight.shape[2]
@@ -643,71 +638,78 @@
     key_cosine = lax.dynamic_slice_in_dim(cosine, key_start, kv_cols, 1)
     key_sine = lax.dynamic_slice_in_dim(sine, key_start, kv_cols, 1)
     parts = 8
-    hbm = pl.BlockSpec(memory_space=pltpu.HBM)
-    gained, scale, own_kv = pl.pallas_call(
-        keys_values,
-        name="keys_values",
-        out_shape=(
-            shape_of((tensor_count, rows, share_cols)),
-            shape_of((rows, 1), jnp.float32),
-            shape_of((2, rows, kv_cols)),
-        ),
-        in_specs=[VMEM, VMEM, hbm, VMEM, VMEM, VMEM],
-        out_specs=(VMEM, VMEM, VMEM),
-        scratch_shapes=[
-            pltpu.VMEM((2, model_width, kv_cols), jnp.bfloat16),
-            pltpu.SemaphoreType.DMA((parts,)),
+    gain = norm_gain.reshape(tensor_count, 1, share_cols)
+    kv_pair = jnp.concatenate([key_value_weight[0], key_value_weight[1]], axis=1)
+    sums = (
+        shape_of((rows, query_cols), jnp.float32),
+        shape_of((rows, 2 * kv_cols), jnp.float32),
+        shape_of((rows, 1), jnp.float32),
+    )
+    block_flops = 2 * rows * model_width // SIDE * (query_cols + 2 * kv_cols)
+    totals = whole_call(
+        functools.partial(project, starts=(0,), count=1),
+        "project_own",
+        info,
+        [embedded[0], gain, q_weight, kv_pair],
+        sums,
+        flops=block_flops,
+    )
+    totals = whole_call(
+        functools.partial(project, starts=(1, 2), count=2),
+        "project_near",
+        info,
+        [embedded[1], embedded[2], gain, q_weight, kv_pair, *totals],
+        sums,
+        flops=2 * block_flops,
+    )
+    own_kv, scale = whole_call(
+        last_keys,
+        "last_keys",
+        info,
+        [
+            embedded[3],
+            gain,
+            kv_pair,
+            totals[1],
+            totals[2],
+            key_cosine,
+            key_sine,
+            swap[:kv_cols, :kv_cols],
         ],
-        compiler_params=pltpu.CompilerParams(vmem_limit_bytes=56 * MIB),
-    )(
-        embedded,
-        norm_gain.reshape(tensor_count, 1, share_cols),
-        key_value_weight,
-        key_cosine,
-        key_sine,
-        swap[:kv_cols, :kv_cols],
+        (shape_of((2, rows, kv_cols)), shape_of((rows, 1), jnp.float32)),
     )
     partner_kv = lax.ppermute(
         own_kv, "tensor", [(index, index ^ 1) for index in range(tensor_count)]
     )
-    query = pl.pallas_call(
-        queries,
-        name="queries",
-        out_shape=shape_of((rows, query_cols)),
-        in_specs=[VMEM, hbm, VMEM, VMEM, VMEM, VMEM],
-        out_specs=VMEM,
-        scratch_shapes=[
-            pltpu.VMEM((model_width, query_cols), jnp.bfloat16),
-            pltpu.VMEM((rows, query_cols), jnp.float32),
-            pltpu.SemaphoreType.DMA((parts,)),
-        ],
-        compiler_params=pltpu.CompilerParams(vmem_limit_bytes=52 * MIB),
-        cost_estimate=pl.CostEstimate(
-            flops=2 * rows * model_width * query_cols,
-            bytes_accessed=2 * model_width * query_cols,
-            transcendentals=0,
-        ),
-    )(gained, q_weight, scale, cosine, sine, swap)
+    query = whole_call(
+        last_queries,
+        "last_queries",
+        info,
+        [embedded[3], gain, q_weight, totals[0], scale, cosine, sine, swap],
+        shape_of((rows, query_cols)),
+        flops=block_flops,
+    )
     partial = pl.pallas_call(
         attend_out,
         name="attend_out",
         out_shape=shape_of((rows, model_width)),
-        in_specs=[SMEM, VMEM, VMEM, VMEM, VMEM, hbm],
-        out_specs=hbm,
+        in_specs=[SMEM, VMEM, VMEM, VMEM, VMEM, VMEM],
+        out_specs=pl.BlockSpec(memory_space=pltpu.HBM),
         scratch_shapes=[
-            pltpu.VMEM((query_cols, model_width), jnp.bfloat16),
             pltpu.VMEM((rows, query_cols), jnp.bfloat16),
             pltpu.VMEM((rows, model_width), jnp.bfloat16),
             pltpu.SemaphoreType.DMA((parts,)),
-            pltpu.SemaphoreType.DMA((parts,)),
         ],
-        compiler_params=pltpu.CompilerParams(vmem_limit_bytes=54 * MIB),
+        compiler_params=pltpu.CompilerParams(vmem_limit_bytes=16 * MIB),
     )(info, query, own_kv, partner_kv, allowed, out_weight)
     terms = lax.all_to_all(
         partial.reshape(tensor_count, own_rows, model_width), "tensor", 0, 0
     )
+    own_embedded = [
+        lax.dynamic_slice_in_dim(block, tensor_index * own_rows, own_rows, 1) for block in embedded
+    ]
     return whole_call(
-        finish, "finish", live_info, [terms, own_embedded], shape_of((own_rows, model_width))
+        finish, "finish", live_info, [terms, *own_embedded], shape_of((own_rows, model_width))
     )
 
 

time: 202 us -> 201 us (level)
  waiting for transfers between devices: 91.8 us -> 77.9 us
  local copies, waits for them, and re-layouts: 14.6 us -> 25.4 us
  Pallas kernels: 42.8 us -> 34.8 us
  starting transfers between devices: 46.4 us -> 51.5 us
  other arithmetic: 4.79 us -> 9.19 us
    all_to_all x1 -> x0, waiting for transfers between devices: 20.1 us -> none  [local(): embedded = lax.all_to_all(spread, 'tensor', 0, 0)]
    pallas_call x2 -> x0, Pallas kernels: 12 us -> none  [the longest x1 6.29 us: local(): pl.pallas_call(keys_values, name='keys_values', out_shape=(shape_of((tens...]
    unnamed x39 -> x68, local copies, waits for them, and re-layouts: 11.2 us -> 21.2 us
    ppermute x15 -> x21, starting transfers between devices: 23.1 us -> 31.1 us  [to_ring(): return lax.ppermute(value, AXES, ring_pairs(phase, distance))]
    pallas_call x13 -> x18, Pallas kernels: 24.8 us -> 30.9 us  [whole_call(): pl.pallas_call(run, name=name, out_shape=outs, in_specs=[SMEM] + [VMEM] *...]
    ppermute x15 -> x21, waiting for transfers between devices: 30.8 us -> 36.1 us  [to_ring(): return lax.ppermute(value, AXES, ring_pairs(phase, distance))]
    all_to_all x1 -> x0, starting transfers between devices: 3.73 us -> none  [local(): embedded = lax.all_to_all(spread, 'tensor', 0, 0)]
    concatenate x0 -> x1, other arithmetic: none -> 3.4 us  [local(): jnp.concatenate([key_value_weight[0], key_value_weight[1]], axis=1)]
  transfers between devices with their start and end apart: 25 -> 30, of which waited for: 17 -> 17; matrix products, arithmetic and copies ran while one was open for 6% -> 8% of each run, Pallas kernels for 10% -> 11%
where the time goes in v2:
time: 201 us; the launch traced here: 200 us
  waiting for transfers between devices  77.9 us (39%)
  starting transfers between devices  51.5 us (26%)
  Pallas kernels  34.8 us (17%)
  local copies, waits for them, and re-layouts  25.4 us (13%)
  other arithmetic  9.19 us (5%)
    ppermute x21, waiting for transfers between devices, to_ring(): return lax.ppermute(value, AXES, ring_pairs(phase, distance))  36.1 us
    ppermute x21, starting transfers between devices, to_ring(): return lax.ppermute(value, AXES, ring_pairs(phase, distance))  31.1 us
    pallas_call x18, Pallas kernels, whole_call(): pl.pallas_call(run, name=name, out_shape=outs, in_specs=[SMEM] + [VMEM] *...  30.9 us
    all_to_all x1, waiting for transfers between devices, local(): lax.all_to_all(partial.reshape(tensor_count, own_rows, model_width), 'ten...  24.8 us
    unnamed x68, local copies, waits for them, and re-layouts  21.2 us
    all_to_all x1, waiting for transfers between devices, local(): lax.all_to_all(outgoing.reshape(device_count, width // 128, 128), AXES, 0...  10.8 us
    all_to_all x1, starting transfers between devices, local(): lax.all_to_all(outgoing.reshape(device_count, width // 128, 128), AXES, 0...  10 us
    all_to_all x1, starting transfers between devices, local(): lax.all_to_all(partial.reshape(tensor_count, own_rows, model_width), 'ten...  5.15 us
  transfers between devices with their start and end apart: 30, of which 17 were waited for; matrix products, arithmetic and copies ran while one was open for 8% of the time, Pallas kernels for 11%

profile of v2, /device:TPU:0, one launch (start us, length us, event | category | flops | bytes accessed | tf_op | source)
XLA Modules:
  0.0 200.0 jit_solution(11229716089339195312)
XLA Ops:
  0.0 0.7 broadcast_add_fusion
  1.3 1.0 copy-done.14
  2.9 1.7 collective-permute-start.1
  4.6 1.6 collective-permute-start.2
  6.2 2.1 %collective-permute-start.3 = (bf16[64,1536]{1,0:T(8,128)(2,1)S(1)}, bf16[64,1536]{1,0:T(8,128)(2,1)S(1)}, u32[]{:S(2)}, u32[]{:S(2)}) collective-permute-start(bf16[64,1536]{1,0:T(8,128)(2,1)S(1)} %take_qkv.1.refs_1_.refs_2_), channel_id=1, source_target_pairs={{0,2},{1,3},{2,0},{3,1},{4,6},{5,7},{6,4},{7,5},{8,10},{9,11},{10,... | collective-permute-start | bytes 589832 | tf_op jit(solution)/shard_map/ppermute | solution.py:67
  8.3 1.6 collective-permute-done.1.refs_2_
  10.3 3.1 %collective-permute-done.3.refs_4_ = bf16[64,1536]{1,0:T(8,128)(2,1)S(1)} collective-permute-done((bf16[64,1536]{1,0:T(8,128)(2,1)S(1)}, bf16[64,1536]{1,0:T(8,128)(2,1)S(1)}, u32[]{:S(2)}, u32[]{:S(2)}) %collective-permute-start.3) | collective-permute-done | bytes 196640 | tf_op jit(solution)/shard_map/ppermute | solution.py:67
  14.0 1.6 collective-permute-start.4
  15.6 1.7 collective-permute-start.5
  17.3 0.8 take_rest.1.refs_1_
  18.1 2.0 collective-permute-start.9
  20.1 1.4 spread_proj.1
  21.5 4.1 %all-to-all-start = ((bf16[16,64,256]{2,1,0:T(8,128)(2,1)}), bf16[16,64,256]{2,1,0:T(8,128)(2,1)S(1)}, u32[]{:S(2)}, u32[]{:S(2)}) async-start(bf16[16,64,256]{2,1,0:T(8,128)(2,1)} %spread_proj.1), calls=%async_computation | async-start | bytes 1048576 | tf_op jit(solution)/shard_map/all_to_all | solution.py:501
  25.6 1.9 collective-permute-start.8
  27.6 2.3 %collective-permute-done.9.refs_3_ = bf16[64,2560]{1,0:T(8,128)(2,1)S(1)} collective-permute-done((bf16[64,2560]{1,0:T(8,128)(2,1)S(1)}, bf16[64,2560]{1,0:T(8,128)(2,1)S(1)}, u32[]{:S(2)}, u32[]{:S(2)}) %collective-permute-start.9) | collective-permute-done | bytes 327712 | tf_op jit(solution)/shard_map/ppermute | solution.py:67
  29.9 4.8 %collective-permute-start.10 = (bf16[64,2560]{1,0:T(8,128)(2,1)S(1)}, bf16[64,2560]{1,0:T(8,128)(2,1)}, u32[]{:S(2)}, u32[]{:S(2)}) collective-permute-start(bf16[64,2560]{1,0:T(8,128)(2,1)S(1)} %collective-permute-done.9.refs_3_), channel_id=1, source_target_pairs={{0,3},{1,0},{2,1},{3,2},{4,7},{5,4},{6,5},{7,6},{8,11},{9,8},{10,9... | collective-permute-start | bytes 983048 | tf_op jit(solution)/shard_map/ppermute | solution.py:67
  35.4 2.2 %collective-permute-done.8.refs_2_ = bf16[64,2560]{1,0:T(8,128)(2,1)S(1)} collective-permute-done((bf16[64,2560]{1,0:T(8,128)(2,1)S(1)}, bf16[64,2560]{1,0:T(8,128)(2,1)S(1)}, u32[]{:S(2)}, u32[]{:S(2)}) %collective-permute-start.8) | collective-permute-done | bytes 327712 | tf_op jit(solution)/shard_map/ppermute | solution.py:67
  38.4 2.4 %all-to-all-done.refs_7_.refs_4_ = bf16[16,64,256]{2,1,0:T(8,128)(2,1)S(1)} async-done(((bf16[16,64,256]{2,1,0:T(8,128)(2,1)}), bf16[16,64,256]{2,1,0:T(8,128)(2,1)S(1)}, u32[]{:S(2)}, u32[]{:S(2)}) %all-to-all-start) | async-done | bytes 524320 | tf_op jit(solution)/shard_map/all_to_all | solution.py:501
  40.8 1.0 copy-done.16
  41.8 1.0 copy-done.18
  42.8 2.2 %join_rest.1 = (bf16[4,64,1536]{2,1,0:T(8,128)(2,1)S(1)}, bf16[4,64,1024]{2,1,0:T(8,128)(2,1)}) custom-call(s32[19]{0:T(128)S(1)} %pad_add_fusion.refs_0_.info, bf16[64,2560]{1,0:T(8,128)(2,1)S(1)} %take_rest.1.refs_1_, bf16[64,2560]{1,0:T(8,128)(2,1)S(1)} %copy-done.18, bf16[64,2560]{1,0:T(8,128)(2,1)S(1)} %copy-done.16, ...), custom_call_target="tpu_custom_call" | custom-call | bytes 1310720 | tf_op jit(solution)/shard_map/join_rest/pallas_call | solution.py:100
  45.0 3.2 %collective-permute-start.12 = (bf16[4,64,1536]{2,1,0:T(8,128)(2,1)S(1)}, bf16[4,64,1536]{2,1,0:T(8,128)(2,1)}, u32[]{:S(2)}, u32[]{:S(2)}) collective-permute-start(bf16[4,64,1536]{2,1,0:T(8,128)(2,1)S(1)} %get-tuple-element.19.refs_3_.refs_5_), channel_id=1, source_target_pairs={{0,12},{1,13},{2,14},{3,15},{4,0},{5,1},{6,2},{7,3},{8,4},{9,5},{1... | collective-permute-start | bytes 2359304 | tf_op jit(solution)/shard_map/ppermute | solution.py:67
  48.2 1.5 fusion.24
  49.7 2.8 %copy.31 = bf16[1,8192,64]{2,1,0:T(8,128)(2,1)} copy(bf16[1,8192,64]{1,2,0:T(8,128)(2,1)} %get-tuple-element.34) | data formatting | bytes 2097152
  52.5 1.8 copy.30
  54.3 3.4 %collective-permute-done.12.refs_5_.refs_7_ = bf16[4,64,1536]{2,1,0:T(8,128)(2,1)} collective-permute-done((bf16[4,64,1536]{2,1,0:T(8,128)(2,1)S(1)}, bf16[4,64,1536]{2,1,0:T(8,128)(2,1)}, u32[]{:S(2)}, u32[]{:S(2)}) %collective-permute-start.12) | collective-permute-done | bytes 786464 | tf_op jit(solution)/shard_map/ppermute | solution.py:67
  57.7 3.8 %collective-permute-start.13 = (bf16[4,64,1536]{2,1,0:T(8,128)(2,1)}, bf16[4,64,1536]{2,1,0:T(8,128)(2,1)S(1)}, u32[]{:S(2)}, u32[]{:S(2)}) collective-permute-start(bf16[4,64,1536]{2,1,0:T(8,128)(2,1)} %collective-permute-done.12.refs_5_.refs_7_), channel_id=1, source_target_pairs={{0,12},{1,13},{2,14},{3,15},{4,0},{5,1},{6,2},{7,3},{8,4},{9,5},{1... | collective-permute-start | bytes 2359304 | tf_op jit(solution)/shard_map/ppermute | solution.py:67
  61.5 3.4 %pad_maximum_fusion.refs_4_.refs_5_.refs_3_ = bf16[8192,128]{1,0:T(8,128)(2,1)S(1)} fusion(bf16[8192,64]{1,0:T(8,128)(2,1)} %bitcast.24, bf16[8192,64]{1,0:T(8,128)(2,1)} %bitcast.25), kind=kLoop, calls=%fused_computation | loop fusion | flops 4194304 | bytes 4194304 | tf_op jit(solution)/shard_map/concatenate | solution.py:642
  65.6 1.4 both_rows.1.refs_1_
  67.0 9.0 %collective-permute-done.6.refs_5_ = bf16[4,64,1536]{2,1,0:T(8,128)(2,1)S(1)} collective-permute-done((bf16[4,64,1536]{2,1,0:T(8,128)(2,1)}, bf16[4,64,1536]{2,1,0:T(8,128)(2,1)S(1)}, u32[]{:S(2)}, u32[]{:S(2)}) %collective-permute-start.6) | collective-permute-done | bytes 786464 | tf_op jit(solution)/shard_map/ppermute | solution.py:67
  76.0 3.2 %span_attention.1.refs_1_ = bf16[8,256,64]{2,1,0:T(8,128)(2,1)S(1)} custom-call(s32[19]{0:T(128)S(1)} %pad_add_fusion.refs_0_.info, bf16[16,256,64]{2,1,0:T(8,128)(2,1)S(1)} %both_rows.1.refs_1_, bf16[4,64,1536]{2,1,0:T(8,128)(2,1)S(1)} %copy-done.8, bf16[4,64,1536]{2,1,0:T(8,128)(2,1)} %collective-permute-done.4.refs_3_.refs_5_, ...), custom_call_target="tpu_custom_call" | custom-call | flops 805306368 | bytes 3670016 | tf_op jit(solution)/shard_map/span_attention/pallas_call | solution.py:100
  79.5 2.2 %collective-permute-done.15.refs_4_ = bf16[4,64,1024]{2,1,0:T(8,128)(2,1)} collective-permute-done((bf16[4,64,1024]{2,1,0:T(8,128)(2,1)}, bf16[4,64,1024]{2,1,0:T(8,128)(2,1)}, u32[]{:S(2)}, u32[]{:S(2)}) %collective-permute-start.15) | collective-permute-done | bytes 524320 | tf_op jit(solution)/shard_map/ppermute | solution.py:67
  82.3 3.1 %context_out.1.refs_3_ = bf16[256,512]{1,0:T(8,128)(2,1)} custom-call(s32[19]{0:T(128)S(1)} %pad_add_fusion.refs_0_.info, bf16[8,256,64]{2,1,0:T(8,128)(2,1)S(1)} %span_attention.1.refs_1_, bf16[8,256,64]{2,1,0:T(8,128)(2,1)S(1)} %collective-permute-done.7.refs_2_, bf16[4,64,1536]{2,1,0:T(8,128)(2,1)S(1)} %get-tuple-element.19.refs_3_.refs_5_, ...), custom_call_target="tpu_custom_call" | custom-call | flops 268435456 | bytes 3670016 | tf_op jit(solution)/shard_map/context_out/pallas_call | solution.py:100
  86.1 1.9 select_reduce_fusion.3
  88.1 1.1 copy-done.4
  89.3 1.1 copy-done.6
  90.4 3.3 %norm_up.1 = (bf16[256,1024]{1,0:T(8,128)(2,1)S(1)}, bf16[16,256,64]{2,1,0:T(8,128)(2,1)S(1)}) custom-call(s32[19]{0:T(128)S(1)} %pad_add_fusion.refs_0_.info, bf16[128,1024]{1,0:T(8,128)(2,1)} %bitcast.4.refs_1_, bf16[128,1024]{1,0:T(8,128)(2,1)} %collective-permute-done.refs_2_, bf16[256,512]{1,0:T(8,128)(2,1)} %context_out.1.refs_3_, ...), custom_call_target="tpu_custom_call" | custom-call | flops 536870912 | bytes 4194304 | tf_op jit(solution)/shard_map/norm_up/pallas_call | solution.py:100
  93.7 2.3 %down.1 = (f32[128,1024]{1,0:T(8,128)S(1)}, bf16[128,1024]{1,0:T(8,128)(2,1)S(1)}) custom-call(s32[19]{0:T(128)S(1)} %pad_add_fusion.refs_0_.info, bf16[16,256,64]{2,1,0:T(8,128)(2,1)S(1)} %get-tuple-element.20.refs_1_, bf16[256,1024]{1,0:T(8,128)(2,1)S(1)} %get-tuple-element.21.refs_2_, bf16[4,64,1024]{2,1,0:T(8,128)(2,1)} %get-tuple-element.22.refs_3_, ...), custom_call_target="tpu_custom_call" | custom-call | flops 536870912 | bytes 3145728 | tf_op jit(solution)/shard_map/down/pallas_call | solution.py:100
  96.8 1.0 collective-permute-done.18.refs_2_
  97.8 1.7 norm_pool.1
  99.5 10.0 %all-to-all-start.1 = ((bf16[128,8,128]{2,1,0:T(8,128)(2,1)}), bf16[128,8,128]{2,1,0:T(8,128)(2,1)S(1)}, u32[]{:S(2)}, u32[]{:S(2)}) async-start(bf16[128,8,128]{2,1,0:T(8,128)(2,1)} %bitcast.6), calls=%async_computation.1 | async-start | bytes 524288 | tf_op jit(solution)/shard_map/all_to_all | solution.py:612
  109.6 10.8 %all-to-all-done.1.refs_1_ = bf16[128,8,128]{2,1,0:T(8,128)(2,1)S(1)} async-done(((bf16[128,8,128]{2,1,0:T(8,128)(2,1)}), bf16[128,8,128]{2,1,0:T(8,128)(2,1)S(1)}, u32[]{:S(2)}, u32[]{:S(2)}) %all-to-all-start.1) | async-done | bytes 262176 | tf_op jit(solution)/shard_map/all_to_all | solution.py:612
  120.4 1.6 copy-done.11
  122.0 2.3 %embed.1.refs_1_ = bf16[128,512]{1,0:T(8,128)(2,1)S(1)} custom-call(s32[19]{0:T(128)S(1)} %pad_add_fusion.refs_0_.info, bf16[128,8,128]{2,1,0:T(8,128)(2,1)S(1)} %all-to-all-done.1.refs_1_, bf16[128,128]{1,0:T(8,128)(2,1)S(1)} %fusion.refs_2_, bf16[1024,1024]{1,0:T(8,128)(2,1)S(1)} %copy-done.11, bf16[16,64,256]{2,1,0:T(8,128)(2,1)S(1)} %all-to-all-done.refs_7_.refs_4_, ...), custom_call_target="tpu_custom_call" | custom-call | flops 402653184 | bytes 3440640 | tf_op jit(solution)/shard_map/embed/pallas_call | solution.py:100
  125.0 2.6 %collective-permute-start.21 = (bf16[128,512]{1,0:T(8,128)(2,1)S(1)}, bf16[128,512]{1,0:T(8,128)(2,1)S(1)}, u32[]{:S(2)}, u32[]{:S(2)}) collective-permute-start(bf16[128,512]{1,0:T(8,128)(2,1)S(1)} %embed.1.refs_1_), channel_id=1, source_target_pairs={{0,3},{1,0},{2,1},{3,2},{4,7},{5,4},{6,5},{7,6},{8,11},{9,8},{10,9... | collective-permute-start | bytes 393224 | tf_op jit(solution)/shard_map/ppermute | solution.py:67
  128.3 2.3 %collective-permute-done.20.refs_2_ = bf16[128,512]{1,0:T(8,128)(2,1)S(1)} collective-permute-done((bf16[128,512]{1,0:T(8,128)(2,1)S(1)}, bf16[128,512]{1,0:T(8,128)(2,1)S(1)}, u32[]{:S(2)}, u32[]{:S(2)}) %collective-permute-start.20) | collective-permute-done | bytes 131104 | tf_op jit(solution)/shard_map/ppermute | solution.py:67
  130.5 1.0 collective-permute-done.21.refs_3_
  131.5 2.5 %collective-permute-done.22.refs_4_ = bf16[128,512]{1,0:T(8,128)(2,1)S(1)} collective-permute-done((bf16[128,512]{1,0:T(8,128)(2,1)S(1)}, bf16[128,512]{1,0:T(8,128)(2,1)S(1)}, u32[]{:S(2)}, u32[]{:S(2)}) %collective-permute-start.22) | collective-permute-done | bytes 131104 | tf_op jit(solution)/shard_map/ppermute | solution.py:67
  135.4 2.7 %collective-permute-start.25 = (bf16[4,128,512]{2,1,0:T(8,128)(2,1)S(1)}, bf16[4,128,512]{2,1,0:T(8,128)(2,1)}, u32[]{:S(2)}, u32[]{:S(2)}) collective-permute-start(bf16[4,128,512]{2,1,0:T(8,128)(2,1)S(1)} %join_columns.1.refs_1_), channel_id=1, source_target_pairs={{0,12},{1,13},{2,14},{3,15},{4,0},{5,1},{6,2},{7,3},{8,4},{9,5},{1... | collective-permute-start | bytes 1572872 | tf_op jit(solution)/shard_map/ppermute | solution.py:67
  139.2 6.0 %collective-permute-done.23.refs_1_ = bf16[4,128,512]{2,1,0:T(8,128)(2,1)} collective-permute-done((bf16[4,128,512]{2,1,0:T(8,128)(2,1)S(1)}, bf16[4,128,512]{2,1,0:T(8,128)(2,1)}, u32[]{:S(2)}, u32[]{:S(2)}) %collective-permute-start.23) | collective-permute-done | bytes 524320 | tf_op jit(solution)/shard_map/ppermute | solution.py:67
  145.7 3.4 %copy-done = bf16[8192,512]{1,0:T(8,128)(2,1)S(1)} copy-done((bf16[8192,512]{1,0:T(8,128)(2,1)S(1)}, bf16[8192,512]{1,0:T(8,128)(2,1)}, u32[]{:S(2)}) %copy-start) | copy-done | bytes 8388632
  149.0 1.1 project_own.1
  150.2 3.5 %copy-done.1 = bf16[8192,512]{1,0:T(8,128)(2,1)S(1)} copy-done((bf16[8192,512]{1,0:T(8,128)(2,1)S(1)}, bf16[8192,512]{1,0:T(8,128)(2,1)}, u32[]{:S(2)}) %copy-start.1) | copy-done | bytes 8388632
  153.7 2.4 %project_near.1 = (f32[128,512]{1,0:T(8,128)S(1)}, f32[128,128]{1,0:T(8,128)S(1)}, f32[128,1]{1,0:T(8,128)S(1)}) custom-call(s32[19]{0:T(128)S(1)} %pad_add_fusion.refs_0_.info, bf16[4,128,512]{2,1,0:T(8,128)(2,1)} %collective-permute-done.23.refs_1_, bf16[4,128,512]{2,1,0:T(8,128)(2,1)} %collective-permute-done.25.refs_2_, f32[16,1,512]{2,1,0:T(1,128)S(1)} %bitcast.21, ...), custom_call_target="tpu_custom_call" | custom-call | flops 671088640 | bytes 11895296 | tf_op jit(solution)/shard_map/project_near/pallas_call | solution.py:100
  156.1 1.1 last_keys.1
  157.6 1.3 last_queries.1.query
  158.9 2.8 %collective-permute-done.26.partner = bf16[2,128,64]{2,1,0:T(8,128)(2,1)S(1)} collective-permute-done((bf16[2,128,64]{2,1,0:T(8,128)(2,1)S(1)}, bf16[2,128,64]{2,1,0:T(8,128)(2,1)S(1)}, u32[]{:S(2)}, u32[]{:S(2)}) %collective-permute-start.26) | collective-permute-done | bytes 32800 | tf_op jit(solution)/shard_map/ppermute | solution.py:681
  161.7 3.9 %attend_out.1 = bf16[128,8192]{1,0:T(8,128)(2,1)S(1)} custom-call(s32[19]{0:T(128)S(1)} %pad_add_fusion.refs_0_.info, bf16[128,512]{1,0:T(8,128)(2,1)S(1)} %last_queries.1.query, bf16[2,128,64]{2,1,0:T(8,128)(2,1)S(1)} %get-tuple-element.32.mine, bf16[2,128,64]{2,1,0:T(8,128)(2,1)S(1)} %collective-permute-done.26.partner, f32[128,128]{1,0:T(8,128)S(1)} %fusion.3.allowed, ...), custom_call_target="tpu_custom_call" | custom-call | tf_op jit(solution)/shard_map/attend_out/pallas_call | solution.py:692
  165.6 1.3 copy-done.2
  167.0 5.2 %all-to-all-start.2 = ((bf16[16,8,8192]{2,1,0:T(8,128)(2,1)}), bf16[16,8,8192]{2,1,0:T(8,128)(2,1)S(1)}, u32[]{:S(2)}, u32[]{:S(2)}) async-start(bf16[16,8,8192]{2,1,0:T(8,128)(2,1)} %bitcast.19), calls=%async_computation.2 | async-start | bytes 4194304 | tf_op jit(solution)/shard_map/all_to_all | solution.py:705
  172.2 0.8 constant_dynamic-slice_fusion.2.refs_3_
  173.0 0.8 constant_dynamic-slice_fusion.1.refs_4_
  173.7 24.8 %all-to-all-done.2.refs_1_ = bf16[16,8,8192]{2,1,0:T(8,128)(2,1)S(1)} async-done(((bf16[16,8,8192]{2,1,0:T(8,128)(2,1)}), bf16[16,8,8192]{2,1,0:T(8,128)(2,1)S(1)}, u32[]{:S(2)}, u32[]{:S(2)}) %all-to-all-start.2) | async-done | bytes 2097184 | tf_op jit(solution)/shard_map/all_to_all | solution.py:705
  198.5 1.5 finish.1
  (132 shorter events, 10.7 us)
Async XLA Ops:
  0.0 20.1 %copy-start.12 = (bf16[64,8192]{1,0:T(8,128)(2,1)S(1)}, bf16[64,8192]{1,0:T(8,128)(2,1)}, u32[]{:S(2)}) copy-start(bf16[64,8192]{1,0:T(8,128)(2,1)} %refs_1_.5) | copy-start | bytes 3145732
  1.3 1.0 copy-start.14
  2.3 15.0 %copy-start.19 = (bf16[64,2048]{1,0:T(8,128)(2,1)S(1)}, bf16[64,2048]{1,0:T(8,128)(2,1)}, u32[]{:S(2)}) copy-start(bf16[64,2048]{1,0:T(8,128)(2,1)} %refs_2_.1) | copy-start | bytes 786436
  2.3 15.0 %copy-start.20 = (bf16[128,1024]{1,0:T(8,128)(2,1)S(1)}, bf16[128,1024]{1,0:T(8,128)(2,1)}, u32[]{:S(2)}) copy-start(bf16[128,1024]{1,0:T(8,128)(2,1)} %refs_3_.4) | copy-start | bytes 786436
  2.3 15.0 %copy-start.21 = (bf16[64,1024]{1,0:T(8,128)(2,1)S(1)}, bf16[64,1024]{1,0:T(8,128)(2,1)}, u32[]{:S(2)}) copy-start(bf16[64,1024]{1,0:T(8,128)(2,1)} %refs_1_.4) | copy-start | bytes 393220
  2.9 6.9 %collective-permute-start.1 = (bf16[64,1536]{1,0:T(8,128)(2,1)S(1)}, bf16[64,1536]{1,0:T(8,128)(2,1)S(1)}, u32[]{:S(2)}, u32[]{:S(2)}) collective-permute-start(bf16[64,1536]{1,0:T(8,128)(2,1)S(1)} %take_qkv.1.refs_1_.refs_2_), channel_id=1, source_target_pairs={{0,1},{1,2},{2,3},{3,0},{4,5},{5,6},{6,7},{7,4},{8,9},{9,10},{10,1... | collective-permute-start | bytes 589832 | tf_op jit(solution)/shard_map/ppermute | solution.py:67
  4.6 5.7 %collective-permute-start.2 = (bf16[64,1536]{1,0:T(8,128)(2,1)S(1)}, bf16[64,1536]{1,0:T(8,128)(2,1)S(1)}, u32[]{:S(2)}, u32[]{:S(2)}) collective-permute-start(bf16[64,1536]{1,0:T(8,128)(2,1)S(1)} %take_qkv.1.refs_1_.refs_2_), channel_id=1, source_target_pairs={{0,3},{1,0},{2,1},{3,2},{4,7},{5,4},{6,5},{7,6},{8,11},{9,8},{10,9... | collective-permute-start | bytes 589832 | tf_op jit(solution)/shard_map/ppermute | solution.py:67
  6.2 7.2 %collective-permute-start.3 = (bf16[64,1536]{1,0:T(8,128)(2,1)S(1)}, bf16[64,1536]{1,0:T(8,128)(2,1)S(1)}, u32[]{:S(2)}, u32[]{:S(2)}) collective-permute-start(bf16[64,1536]{1,0:T(8,128)(2,1)S(1)} %take_qkv.1.refs_1_.refs_2_), channel_id=1, source_target_pairs={{0,2},{1,3},{2,0},{3,1},{4,6},{5,7},{6,4},{7,5},{8,10},{9,11},{10,... | collective-permute-start | bytes 589832 | tf_op jit(solution)/shard_map/ppermute | solution.py:67
  14.0 31.0 %copy-start.7 = (bf16[4,64,1536]{2,1,0:T(8,128)(2,1)}, bf16[4,64,1536]{2,1,0:T(8,128)(2,1)S(1)}, u32[]{:S(2)}) copy-start(bf16[4,64,1536]{2,1,0:T(8,128)(2,1)S(1)} %join_qkv.1.refs_2_) | copy-start | bytes 2359300
  14.0 26.8 %collective-permute-start.4 = (bf16[4,64,1536]{2,1,0:T(8,128)(2,1)S(1)}, bf16[4,64,1536]{2,1,0:T(8,128)(2,1)}, u32[]{:S(2)}, u32[]{:S(2)}) collective-permute-start(bf16[4,64,1536]{2,1,0:T(8,128)(2,1)S(1)} %join_qkv.1.refs_2_), channel_id=1, source_target_pairs={{0,4},{1,5},{2,6},{3,7},{4,8},{5,9},{6,10},{7,11},{8,12},{9,13},{1... | collective-permute-start | bytes 2359304 | tf_op jit(solution)/shard_map/ppermute | solution.py:67
  15.6 25.2 %collective-permute-start.5 = (bf16[4,64,1536]{2,1,0:T(8,128)(2,1)S(1)}, bf16[4,64,1536]{2,1,0:T(8,128)(2,1)S(1)}, u32[]{:S(2)}, u32[]{:S(2)}) collective-permute-start(bf16[4,64,1536]{2,1,0:T(8,128)(2,1)S(1)} %join_qkv.1.refs_2_), channel_id=1, source_target_pairs={{0,12},{1,13},{2,14},{3,15},{4,0},{5,1},{6,2},{7,3},{8,4},{9,5},{1... | collective-permute-start | bytes 2359304 | tf_op jit(solution)/shard_map/ppermute | solution.py:67
  18.1 11.8 %collective-permute-start.9 = (bf16[64,2560]{1,0:T(8,128)(2,1)S(1)}, bf16[64,2560]{1,0:T(8,128)(2,1)S(1)}, u32[]{:S(2)}, u32[]{:S(2)}) collective-permute-start(bf16[64,2560]{1,0:T(8,128)(2,1)S(1)} %take_rest.1.refs_1_), channel_id=1, source_target_pairs={{0,3},{1,0},{2,1},{3,2},{4,7},{5,4},{6,5},{7,6},{8,11},{9,8},{10,9... | collective-permute-start | bytes 983048 | tf_op jit(solution)/shard_map/ppermute | solution.py:67
  21.5 19.3 %all-to-all-start = ((bf16[16,64,256]{2,1,0:T(8,128)(2,1)}), bf16[16,64,256]{2,1,0:T(8,128)(2,1)S(1)}, u32[]{:S(2)}, u32[]{:S(2)}) async-start(bf16[16,64,256]{2,1,0:T(8,128)(2,1)} %spread_proj.1), calls=%async_computation | async-start | bytes 1048576 | tf_op jit(solution)/shard_map/all_to_all | solution.py:501
  25.6 12.0 %collective-permute-start.8 = (bf16[64,2560]{1,0:T(8,128)(2,1)S(1)}, bf16[64,2560]{1,0:T(8,128)(2,1)S(1)}, u32[]{:S(2)}, u32[]{:S(2)}) collective-permute-start(bf16[64,2560]{1,0:T(8,128)(2,1)S(1)} %take_rest.1.refs_1_), channel_id=1, source_target_pairs={{0,1},{1,2},{2,3},{3,0},{4,5},{5,6},{6,7},{7,4},{8,9},{9,10},{10,1... | collective-permute-start | bytes 983048 | tf_op jit(solution)/shard_map/ppermute | solution.py:67
  29.9 10.9 %collective-permute-start.10 = (bf16[64,2560]{1,0:T(8,128)(2,1)S(1)}, bf16[64,2560]{1,0:T(8,128)(2,1)}, u32[]{:S(2)}, u32[]{:S(2)}) collective-permute-start(bf16[64,2560]{1,0:T(8,128)(2,1)S(1)} %collective-permute-done.9.refs_3_), channel_id=1, source_target_pairs={{0,3},{1,0},{2,1},{3,2},{4,7},{5,4},{6,5},{7,6},{8,11},{9,8},{10,9... | collective-permute-start | bytes 983048 | tf_op jit(solution)/shard_map/ppermute | solution.py:67
  34.7 0.7 copy-start.15
  35.4 30.1 %collective-permute-start = (bf16[128,1024]{1,0:T(8,128)(2,1)}, bf16[128,1024]{1,0:T(8,128)(2,1)}, u32[]{:S(2)}, u32[]{:S(2)}) collective-permute-start(bf16[128,1024]{1,0:T(8,128)(2,1)} %bitcast.4.refs_1_), channel_id=1, source_target_pairs={{0,16},{16,0},{32,48},{48,32},{64,80},{80,64},{96,112},{112,96},{1... | collective-permute-start | bytes 786440 | tf_op jit(solution)/shard_map/ppermute | solution.py:71
  37.7 0.7 copy-start.17
  40.8 1.0 copy-start.16
  41.8 1.0 copy-start.18
  42.8 6.9 %copy-start.9 = (bf16[4,64,1536]{2,1,0:T(8,128)(2,1)}, bf16[4,64,1536]{2,1,0:T(8,128)(2,1)S(1)}, u32[]{:S(2)}) copy-start(bf16[4,64,1536]{2,1,0:T(8,128)(2,1)S(1)} %collective-permute-done.5.refs_4_.refs_6_) | copy-start | bytes 2359300
  42.8 5.4 %copy-start.23 = (bf16[2,8192,64]{1,2,0:T(8,128)(2,1)S(1)}, bf16[2,8192,64]{1,2,0:T(8,128)(2,1)}, u32[]{:S(2)}) copy-start(bf16[2,8192,64]{1,2,0:T(8,128)(2,1)} %param.29) | copy-start | bytes 6291460
  45.0 12.7 %collective-permute-start.12 = (bf16[4,64,1536]{2,1,0:T(8,128)(2,1)S(1)}, bf16[4,64,1536]{2,1,0:T(8,128)(2,1)}, u32[]{:S(2)}, u32[]{:S(2)}) collective-permute-start(bf16[4,64,1536]{2,1,0:T(8,128)(2,1)S(1)} %get-tuple-element.19.refs_3_.refs_5_), channel_id=1, source_target_pairs={{0,12},{1,13},{2,14},{3,15},{4,0},{5,1},{6,2},{7,3},{8,4},{9,5},{1... | collective-permute-start | bytes 2359304 | tf_op jit(solution)/shard_map/ppermute | solution.py:67
  49.7 2.8 %copy-start.22 = (bf16[1,8192,64]{1,2,0:T(8,128)(2,1)S(1)}, bf16[1,8192,64]{1,2,0:T(8,128)(2,1)}, u32[]{:S(2)}) copy-start(bf16[1,8192,64]{1,2,0:T(8,128)(2,1)} %get-tuple-element.33) | copy-start | bytes 3145732
  54.3 27.9 %collective-permute-start.11 = (bf16[4,64,1536]{2,1,0:T(8,128)(2,1)S(1)}, bf16[4,64,1536]{2,1,0:T(8,128)(2,1)S(1)}, u32[]{:S(2)}, u32[]{:S(2)}) collective-permute-start(bf16[4,64,1536]{2,1,0:T(8,128)(2,1)S(1)} %get-tuple-element.19.refs_3_.refs_5_), channel_id=1, source_target_pairs={{0,4},{1,5},{2,6},{3,7},{4,8},{5,9},{6,10},{7,11},{8,12},{9,13},{1... | collective-permute-start | bytes 2359304 | tf_op jit(solution)/shard_map/ppermute | solution.py:67
  54.3 21.6 %collective-permute-start.6 = (bf16[4,64,1536]{2,1,0:T(8,128)(2,1)}, bf16[4,64,1536]{2,1,0:T(8,128)(2,1)S(1)}, u32[]{:S(2)}, u32[]{:S(2)}) collective-permute-start(bf16[4,64,1536]{2,1,0:T(8,128)(2,1)} %collective-permute-done.4.refs_3_.refs_5_), channel_id=1, source_target_pairs={{0,4},{1,5},{2,6},{3,7},{4,8},{5,9},{6,10},{7,11},{8,12},{9,13},{1... | collective-permute-start | bytes 2359304 | tf_op jit(solution)/shard_map/ppermute | solution.py:67
  57.7 24.6 %collective-permute-start.13 = (bf16[4,64,1536]{2,1,0:T(8,128)(2,1)}, bf16[4,64,1536]{2,1,0:T(8,128)(2,1)S(1)}, u32[]{:S(2)}, u32[]{:S(2)}) collective-permute-start(bf16[4,64,1536]{2,1,0:T(8,128)(2,1)} %collective-permute-done.12.refs_5_.refs_7_), channel_id=1, source_target_pairs={{0,12},{1,13},{2,14},{3,15},{4,0},{5,1},{6,2},{7,3},{8,4},{9,5},{1... | collective-permute-start | bytes 2359304 | tf_op jit(solution)/shard_map/ppermute | solution.py:67
  61.5 3.4 %copy-start.28 = (s32[8]{0:T(128)S(1)}, s32[8]{0:T(128)}, u32[]{:S(2)}) copy-start(s32[8]{0:T(128)} %param.19) | copy-start | bytes 100
  61.5 4.1 %copy-start.25 = (s32[1024]{0:T(1024)S(1)}, s32[1024]{0:T(1024)}, u32[]{:S(2)}) copy-start(s32[1024]{0:T(1024)} %param.17) | copy-start | bytes 12292
  64.9 11.0 %copy-start.8 = (bf16[4,64,1536]{2,1,0:T(8,128)(2,1)S(1)}, bf16[4,64,1536]{2,1,0:T(8,128)(2,1)}, u32[]{:S(2)}) copy-start(bf16[4,64,1536]{2,1,0:T(8,128)(2,1)} %copy-done.7) | copy-start | bytes 2359300
  64.9 11.0 %copy-start.10 = (bf16[4,64,1536]{2,1,0:T(8,128)(2,1)S(1)}, bf16[4,64,1536]{2,1,0:T(8,128)(2,1)}, u32[]{:S(2)}) copy-start(bf16[4,64,1536]{2,1,0:T(8,128)(2,1)} %copy-done.9) | copy-start | bytes 2359300
  65.6 16.1 %collective-permute-start.15 = (bf16[4,64,1024]{2,1,0:T(8,128)(2,1)}, bf16[4,64,1024]{2,1,0:T(8,128)(2,1)}, u32[]{:S(2)}, u32[]{:S(2)}) collective-permute-start(bf16[4,64,1024]{2,1,0:T(8,128)(2,1)} %get-tuple-element.22.refs_3_), channel_id=1, source_target_pairs={{0,4},{1,5},{2,6},{3,7},{4,8},{5,9},{6,10},{7,11},{8,12},{9,13},{1... | collective-permute-start | bytes 1572872 | tf_op jit(solution)/shard_map/ppermute | solution.py:67
  79.2 3.1 %collective-permute-start.7 = (bf16[8,256,64]{2,1,0:T(8,128)(2,1)S(1)}, bf16[8,256,64]{2,1,0:T(8,128)(2,1)S(1)}, u32[]{:S(2)}, u32[]{:S(2)}) collective-permute-start(bf16[8,256,64]{2,1,0:T(8,128)(2,1)S(1)} %span_attention.1.refs_1_), channel_id=1, source_target_pairs={{0,16},{16,0},{32,48},{48,32},{64,80},{80,64},{96,112},{112,96},{1... | collective-permute-start | bytes 786440 | tf_op jit(solution)/shard_map/ppermute | solution.py:71
  79.4 14.3 %collective-permute-start.16 = (bf16[4,64,1024]{2,1,0:T(8,128)(2,1)}, bf16[4,64,1024]{2,1,0:T(8,128)(2,1)}, u32[]{:S(2)}, u32[]{:S(2)}) collective-permute-start(bf16[4,64,1024]{2,1,0:T(8,128)(2,1)} %get-tuple-element.22.refs_3_), channel_id=1, source_target_pairs={{0,12},{1,13},{2,14},{3,15},{4,0},{5,1},{6,2},{7,3},{8,4},{9,5},{1... | collective-permute-start | bytes 1572872 | tf_op jit(solution)/shard_map/ppermute | solution.py:67
  81.7 12.0 %collective-permute-start.17 = (bf16[4,64,1024]{2,1,0:T(8,128)(2,1)}, bf16[4,64,1024]{2,1,0:T(8,128)(2,1)}, u32[]{:S(2)}, u32[]{:S(2)}) collective-permute-start(bf16[4,64,1024]{2,1,0:T(8,128)(2,1)} %collective-permute-done.15.refs_4_), channel_id=1, source_target_pairs={{0,4},{1,5},{2,6},{3,7},{4,8},{5,9},{6,10},{7,11},{8,12},{9,13},{1... | collective-permute-start | bytes 1572872 | tf_op jit(solution)/shard_map/ppermute | solution.py:67
  82.2 3.2 %copy-start.3 = (bf16[4,64,1536]{2,1,0:T(8,128)(2,1)}, bf16[4,64,1536]{2,1,0:T(8,128)(2,1)S(1)}, u32[]{:S(2)}) copy-start(bf16[4,64,1536]{2,1,0:T(8,128)(2,1)S(1)} %collective-permute-done.11.refs_4_.refs_6_) | copy-start | bytes 2359300
  82.3 3.1 %copy-start.5 = (bf16[4,64,1536]{2,1,0:T(8,128)(2,1)}, bf16[4,64,1536]{2,1,0:T(8,128)(2,1)S(1)}, u32[]{:S(2)}) copy-start(bf16[4,64,1536]{2,1,0:T(8,128)(2,1)S(1)} %collective-permute-done.13.refs_6_.refs_8_) | copy-start | bytes 2359300
  85.4 2.7 %collective-permute-start.14 = (bf16[256,512]{1,0:T(8,128)(2,1)}, bf16[256,512]{1,0:T(8,128)(2,1)}, u32[]{:S(2)}, u32[]{:S(2)}) collective-permute-start(bf16[256,512]{1,0:T(8,128)(2,1)} %context_out.1.refs_3_), channel_id=1, source_target_pairs={{0,16},{16,0},{32,48},{48,32},{64,80},{80,64},{96,112},{112,96},{1... | collective-permute-start | bytes 786440 | tf_op jit(solution)/shard_map/ppermute | solution.py:71
  88.1 1.1 copy-start.4
  89.3 1.1 copy-start.6
  96.1 1.7 collective-permute-start.18
  96.7 12.9 %collective-permute-start.19 = (bf16[16,64,256]{2,1,0:T(8,128)(2,1)S(1)}, bf16[16,64,256]{2,1,0:T(8,128)(2,1)}, u32[]{:S(2)}, u32[]{:S(2)}) collective-permute-start(bf16[16,64,256]{2,1,0:T(8,128)(2,1)S(1)} %all-to-all-done.refs_7_.refs_4_), channel_id=1, source_target_pairs={{0,16},{16,0},{32,48},{48,32},{64,80},{80,64},{96,112},{112,96},{1... | collective-permute-start | bytes 1572872 | tf_op jit(solution)/shard_map/ppermute | solution.py:71
  99.5 28.7 %copy-start.24 = (s32[8,8,8]{2,1,0:T(8,128)S(1)}, s32[8,8,8]{2,1,0:T(8,128)}, u32[]{:S(2)}) copy-start(s32[8,8,8]{2,1,0:T(8,128)} %param.20) | copy-start | bytes 6148
  99.5 20.9 %all-to-all-start.1 = ((bf16[128,8,128]{2,1,0:T(8,128)(2,1)}), bf16[128,8,128]{2,1,0:T(8,128)(2,1)S(1)}, u32[]{:S(2)}, u32[]{:S(2)}) async-start(bf16[128,8,128]{2,1,0:T(8,128)(2,1)} %bitcast.6), calls=%async_computation.1 | async-start | bytes 524288 | tf_op jit(solution)/shard_map/all_to_all | solution.py:612
  109.5 35.7 %copy-start.26 = (f32[128]{0:T(128)S(1)}, f32[128]{0:T(128)}, u32[]{:S(2)}) copy-start(f32[128]{0:T(128)} %iota_convert_fusion) | copy-start | bytes 1540
  109.5 36.1 %copy-start.13 = (f32[8192]{0:T(1024)S(1)}, f32[8192]{0:T(1024)}, u32[]{:S(2)}) copy-start(f32[8192]{0:T(1024)} %param.27) | copy-start | bytes 98308
  120.4 1.6 copy-start.11
  122.0 13.3 %copy-start.27 = (f32[128]{0:T(128)S(1)}, f32[128]{0:T(128)}, u32[]{:S(2)}) copy-start(f32[128]{0:T(128)} %compare_select_fusion.8) | copy-start | bytes 1540
  124.3 6.2 %collective-permute-start.20 = (bf16[128,512]{1,0:T(8,128)(2,1)S(1)}, bf16[128,512]{1,0:T(8,128)(2,1)S(1)}, u32[]{:S(2)}, u32[]{:S(2)}) collective-permute-start(bf16[128,512]{1,0:T(8,128)(2,1)S(1)} %embed.1.refs_1_), channel_id=1, source_target_pairs={{0,1},{1,2},{2,3},{3,0},{4,5},{5,6},{6,7},{7,4},{8,9},{9,10},{10,1... | collective-permute-start | bytes 393224 | tf_op jit(solution)/shard_map/ppermute | solution.py:67
  125.0 6.5 %collective-permute-start.21 = (bf16[128,512]{1,0:T(8,128)(2,1)S(1)}, bf16[128,512]{1,0:T(8,128)(2,1)S(1)}, u32[]{:S(2)}, u32[]{:S(2)}) collective-permute-start(bf16[128,512]{1,0:T(8,128)(2,1)S(1)} %embed.1.refs_1_), channel_id=1, source_target_pairs={{0,3},{1,0},{2,1},{3,2},{4,7},{5,4},{6,5},{7,6},{8,11},{9,8},{10,9... | collective-permute-start | bytes 393224 | tf_op jit(solution)/shard_map/ppermute | solution.py:67
  127.6 6.5 %collective-permute-start.22 = (bf16[128,512]{1,0:T(8,128)(2,1)S(1)}, bf16[128,512]{1,0:T(8,128)(2,1)S(1)}, u32[]{:S(2)}, u32[]{:S(2)}) collective-permute-start(bf16[128,512]{1,0:T(8,128)(2,1)S(1)} %embed.1.refs_1_), channel_id=1, source_target_pairs={{0,2},{1,3},{2,0},{3,1},{4,6},{5,7},{6,4},{7,5},{8,10},{9,11},{10,... | collective-permute-start | bytes 393224 | tf_op jit(solution)/shard_map/ppermute | solution.py:67
  134.6 10.6 %collective-permute-start.23 = (bf16[4,128,512]{2,1,0:T(8,128)(2,1)S(1)}, bf16[4,128,512]{2,1,0:T(8,128)(2,1)}, u32[]{:S(2)}, u32[]{:S(2)}) collective-permute-start(bf16[4,128,512]{2,1,0:T(8,128)(2,1)S(1)} %join_columns.1.refs_1_), channel_id=1, source_target_pairs={{0,4},{1,5},{2,6},{3,7},{4,8},{5,9},{6,10},{7,11},{8,12},{9,13},{1... | collective-permute-start | bytes 1572872 | tf_op jit(solution)/shard_map/ppermute | solution.py:67
  135.4 14.8 %collective-permute-start.25 = (bf16[4,128,512]{2,1,0:T(8,128)(2,1)S(1)}, bf16[4,128,512]{2,1,0:T(8,128)(2,1)}, u32[]{:S(2)}, u32[]{:S(2)}) collective-permute-start(bf16[4,128,512]{2,1,0:T(8,128)(2,1)S(1)} %join_columns.1.refs_1_), channel_id=1, source_target_pairs={{0,12},{1,13},{2,14},{3,15},{4,0},{5,1},{6,2},{7,3},{8,4},{9,5},{1... | collective-permute-start | bytes 1572872 | tf_op jit(solution)/shard_map/ppermute | solution.py:67
  145.2 10.8 %collective-permute-start.24 = (bf16[4,128,512]{2,1,0:T(8,128)(2,1)}, bf16[4,128,512]{2,1,0:T(8,128)(2,1)S(1)}, u32[]{:S(2)}, u32[]{:S(2)}) collective-permute-start(bf16[4,128,512]{2,1,0:T(8,128)(2,1)} %collective-permute-done.23.refs_1_), channel_id=1, source_target_pairs={{0,4},{1,5},{2,6},{3,7},{4,8},{5,9},{6,10},{7,11},{8,12},{9,13},{1... | collective-permute-start | bytes 1572872 | tf_op jit(solution)/shard_map/ppermute | solution.py:67
  145.7 3.4 %copy-start = (bf16[8192,512]{1,0:T(8,128)(2,1)S(1)}, bf16[8192,512]{1,0:T(8,128)(2,1)}, u32[]{:S(2)}) copy-start(bf16[8192,512]{1,0:T(8,128)(2,1)} %refs_3_.7) | copy-start | bytes 25165828
  149.0 8.5 %slice-start = ((s8[8388608]{0:T(1024)(128)(4,1)}), s8[4194304]{0:T(1024)(128)(4,1)S(1)}, s32[]{:S(2)}) async-start(s8[8388608]{0:T(1024)(128)(4,1)} %bitcast.15), calls=%async_computation.3 | async-start | bytes 8388608
  150.2 3.5 %copy-start.1 = (bf16[8192,512]{1,0:T(8,128)(2,1)S(1)}, bf16[8192,512]{1,0:T(8,128)(2,1)}, u32[]{:S(2)}) copy-start(bf16[8192,512]{1,0:T(8,128)(2,1)} %refs_3_.7) | copy-start | bytes 25165828
  153.7 3.9 %slice-start.1 = ((s8[8388608]{0:T(1024)(128)(4,1)}), s8[4194304]{0:T(1024)(128)(4,1)S(1)}, s32[]{:S(2)}) async-start(s8[8388608]{0:T(1024)(128)(4,1)} %bitcast.15), calls=%async_computation.4 | async-start | bytes 8388608
  153.7 8.1 %slice-start.2 = ((s8[8388608]{0:T(1024)(128)(4,1)}), s8[4194304]{0:T(1024)(128)(4,1)S(1)}, s32[]{:S(2)}) async-start(s8[8388608]{0:T(1024)(128)(4,1)} %bitcast.17), calls=%async_computation.5 | async-start | bytes 8388608
  156.1 5.7 %slice-start.3 = ((s8[8388608]{0:T(1024)(128)(4,1)}), s8[4194304]{0:T(1024)(128)(4,1)S(1)}, s32[]{:S(2)}) async-start(s8[8388608]{0:T(1024)(128)(4,1)} %bitcast.17), calls=%async_computation.6 | async-start | bytes 8388608
  157.2 4.6 %collective-permute-start.26 = (bf16[2,128,64]{2,1,0:T(8,128)(2,1)S(1)}, bf16[2,128,64]{2,1,0:T(8,128)(2,1)S(1)}, u32[]{:S(2)}, u32[]{:S(2)}) collective-permute-start(bf16[2,128,64]{2,1,0:T(8,128)(2,1)S(1)} %get-tuple-element.32.mine), channel_id=1, source_target_pairs={{0,1},{1,0},{2,3},{3,2},{4,5},{5,4},{6,7},{7,6},{8,9},{9,8},{10,11... | collective-permute-start | bytes 98312 | tf_op jit(solution)/shard_map/ppermute | solution.py:681
  165.6 1.3 copy-start.2
  167.0 31.5 %all-to-all-start.2 = ((bf16[16,8,8192]{2,1,0:T(8,128)(2,1)}), bf16[16,8,8192]{2,1,0:T(8,128)(2,1)S(1)}, u32[]{:S(2)}, u32[]{:S(2)}) async-start(bf16[16,8,8192]{2,1,0:T(8,128)(2,1)} %bitcast.19), calls=%async_computation.2 | async-start | bytes 4194304 | tf_op jit(solution)/shard_map/all_to_all | solution.py:705

commit v3 on v2

--- a/solution.py
+++ b/solution.py
@@ -113,6 +113,12 @@
     return jnp.dot(left, right, preferred_element_type=jnp.float32)
 
 
+def dot_last(left, right):
+    return lax.dot_general(
+        left, right, (((1,), (1,)), ((), ())), preferred_element_type=jnp.float32
+    )
+
+
 def gelu_exact(values):
     return 0.5 * values * (1.0 + lax.erf(values * (0.5**0.5)))
 
@@ -122,6 +128,11 @@
     for part in range(3):
         start = pl.multiple_of((2 * part + info[16]) * cols, cols)
         out[:, part * cols : (part + 1) * cols] = weight[:, pl.ds(start, cols)]
+
+
+def take_halves(info, qkv, out_weight, up_weight, down_weight, qkv_out, rest_out):
+    take_qkv(info, qkv, qkv_out)
+    take_rest(info, out_weight, up_weight, down_weight, rest_out)
 
 
 def take_rest(info, out_weight, up_weight, down_weight, out):
@@ -160,11 +171,23 @@
         lower[index] = block[:, cols:]
 
 
-def spread_proj(info, weight, out):
-    cols = out.shape[2]
-    for index in range(out.shape[0]):
-        start = pl.multiple_of((2 * index + info[16]) * cols, cols)
-        out[index] = weight[:, pl.ds(start, cols)]
+def deal_columns(info, weight, *outs):
+    core, near = info[16], info[19]
+    cols = outs[0].shape[2]
+    for out, distance in zip(outs, (0, 1, SIDE - 1, 2)):
+        target = lax.rem(near + distance, SIDE)
+        for index in range(SIDE):
+            shard = jnp.where(core == 0, SIDE * index + target, SIDE * target + index)
+            start = pl.multiple_of((2 * shard + core) * cols, cols)
+            out[index] = weight[:, pl.ds(start, cols)]
+
+
+def deal_again(info, own, left, right, opposite, *outs):
+    far = info[20]
+    for out, distance in zip(outs, (0, 1, SIDE - 1, 2)):
+        target = lax.rem(far + distance, SIDE)
+        for index, block in enumerate((own, left, right, opposite)):
+            out[index] = block[target]
 
 
 def both_rows(info, mine, other, pieces_out):
@@ -283,7 +306,7 @@
     out[...] = jnp.broadcast_to(lanes[...].astype(jnp.bfloat16)[:, None], out.shape)
 
 
-def embed(info, arrived, order, proj_in, mine, other, out, lanes):
+def embed(info, arrived, order, proj_in, mine, other, out, lanes, pieces):
     core = info[16]
     lanes[...] = arrived[...].astype(jnp.float32)
     columns = [
@@ -292,10 +315,17 @@
     ]
     arranged = jnp.concatenate(columns, axis=1)
     hidden = gelu_exact(dot32(arranged, proj_in[...])).astype(jnp.bfloat16)
-    units = hidden.shape[1]
-    cols = mine.shape[2]
-    near = dot32(hidden, mine[...].reshape(units, cols))
-    far = dot32(hidden, other[...].reshape(units, cols))
+    units, cols = mine.shape[2:]
+    for index in range(pieces.shape[0]):
+        pieces[index] = hidden[:, index * units : (index + 1) * units]
+    near, far = None, None
+    for at in range(SIDE):
+        act = jnp.concatenate([pieces[info[SIDE * at + step]] for step in range(SIDE)], axis=1)
+        term = dot32(act, mine[at].reshape(SIDE * units, cols))
+        near = term if near is None else near + term
+        act = jnp.concatenate([pieces[info[22 + SIDE * at + step]] for step in range(SIDE)], axis=1)
+        term = dot32(act, other[at].reshape(SIDE * units, cols))
+        far = term if far is None else far + term
     out[:, :cols] = jnp.where(core == 0, near, far).astype(jnp.bfloat16)
     out[:, cols:] = jnp.where(core == 0, far, near).astype(jnp.bfloat16)
 
@@ -315,7 +345,7 @@
             act = (wide * gain[shard]).astype(jnp.bfloat16)
             span = pl.ds(pl.multiple_of(shard * depth, depth), depth)
             q_term = dot32(act, q_weight[span, :])
-            kv_term = dot32(act, kv_weight[span, :])
+            kv_term = dot_last(act, kv_weight[:, span])
             term = jnp.sum(wide * wide, axis=1, keepdims=True)
             queries = q_term if queries is None else queries + q_term
             both = kv_term if both is None else both + kv_term
@@ -343,7 +373,7 @@
         wide = block[step].astype(jnp.float32)
         act = (wide * gain[shard]).astype(jnp.bfloat16)
         span = pl.ds(pl.multiple_of(shard * depth, depth), depth)
-        both += dot32(act, kv_weight[span, :])
+        both += dot_last(act, kv_weight[:, span])
         squares += jnp.sum(wide * wide, axis=1, keepdims=True)
     factor = lax.rsqrt(squares / (depth * SIDE * SIDE) + 1e-05)
     scale[...] = factor
@@ -405,7 +435,7 @@
 def finish(info, terms, *refs):
     own, out = refs[:-1], refs[-1]
     rows, cols = own[0].shape[1:]
-    live = info[18] + lax.broadcasted_iota(jnp.int32, (rows, cols), 0) < info[19]
+    live = info[18] + lax.broadcasted_iota(jnp.int32, (rows, cols), 0) < info[21]
     for at, block in enumerate(own):
         for step in range(SIDE):
             lanes = pl.ds(pl.multiple_of(info[SIDE * at + step] * cols, cols), cols)
@@ -460,8 +490,11 @@
     by_x = SIDE * ((x_index + outer) % SIDE) + (y_index + inside) % SIDE
     by_y = SIDE * ((x_index + inside) % SIDE) + (y_index + outer) % SIDE
     shards = jnp.where(core == 0, by_x, by_y)
-    scalars = jnp.stack([core, tensor_index % 2, tensor_index * own_rows])
-    info = jnp.concatenate([shards, scalars]).astype(jnp.int32)
+    near = jnp.where(core == 0, y_index, x_index)
+    far = jnp.where(core == 0, x_index, y_index)
+    scalars = jnp.stack([core, tensor_index % 2, tensor_index * own_rows, near, far])
+    other_shards = jnp.where(core == 0, by_y, by_x)
+    info = jnp.concatenate([shards, scalars, core[None], other_shards]).astype(jnp.int32)
 
     requests = jnp.arange(req_slot.shape[0])
     dest_slot = jnp.sum(
@@ -480,7 +513,7 @@
         jnp.where(requests[:, None, None] == chosen, block_mask, 0), axis=0
     )
     allowed = visibility(masks, live_count).astype(jnp.float32)
-    live_info = jnp.concatenate([info, live_count[None]]).astype(jnp.int32)
+    live_info = jnp.concatenate([info[:21], live_count[None]]).astype(jnp.int32)
 
     positions = jnp.arange(rows).astype(jnp.float32)
     lane = jnp.arange(HEAD_WIDTH)
@@ -494,34 +527,17 @@
     ).astype(jnp.float32)
 
     own_tokens = span_tokens.reshape(spans * span_size, width)
-    own_qkv = whole_call(
-        take_qkv, "take_qkv", info, [enc_qkv], shape_of((share, 3 * width // 2)), limit=4
-    )
-    share_cols = model_width // tensor_count
-    proj_mine = lax.all_to_all(
-        whole_call(
-            spread_proj,
-            "spread_proj",
-            info,
-            [proj_out],
-            shape_of((tensor_count, proj_out.shape[0], share_cols // 2)),
-            after=[own_qkv],
-        ),
-        "tensor",
-        0,
-        0,
-    )
-    proj_other = to_core(proj_mine)
     units = enc_down.shape[0] // 2
     middle_cols = width // 2 + units * tensor_count
-    own_rest = whole_call(
-        take_rest,
-        "take_rest",
-        info,
-        [enc_out, enc_up, enc_down],
-        shape_of((share, middle_cols + width)),
+    own_qkv, own_rest = whole_call(
+        take_halves,
+        "take_halves",
+        info,
+        [enc_qkv, enc_out, enc_up, enc_down],
+        (shape_of((share, 3 * width // 2)), shape_of((share, middle_cols + width))),
         limit=4,
     )
+    rest_ring = short_relay(own_rest)
     qkv_block = whole_call(
         join_blocks,
         "join_qkv",
@@ -529,7 +545,26 @@
         short_ring(own_qkv),
         shape_of((SIDE, share, 3 * width // 2)),
         limit=6,
-    )
+        after=rest_ring[1:3],
+    )
+    middle_block, lower_block = whole_call(
+        join_rest,
+        "join_rest",
+        info,
+        rest_ring,
+        (shape_of((SIDE, share, middle_cols)), shape_of((SIDE, share, width))),
+        limit=8,
+    )
+    other_tokens = to_core(own_tokens)
+    token_pieces = whole_call(
+        both_rows,
+        "both_rows",
+        info,
+        [own_tokens, other_tokens],
+        shape_of((tensor_count, 2 * spans * span_size, share)),
+    )
+    all_rows = 2 * spans * span_size
+
     def ring(block, relay):
         left = to_ring(block, 2, 1)
         right = to_ring(block, 2, -1)
@@ -537,27 +572,37 @@
         return [block, left, right, opposite]
 
     qkv = ring(qkv_block, 1)
-    middle_block, lower_block = whole_call(
-        join_rest,
-        "join_rest",
-        info,
-        short_relay(own_rest),
-        (shape_of((SIDE, share, middle_cols)), shape_of((SIDE, share, width))),
+    middle_down, _ = lax.optimization_barrier((middle_block, qkv[2]))
+    middle_up, _ = lax.optimization_barrier((middle_block, qkv[3]))
+    right = to_ring(middle_down, 2, -1)
+    middle = [middle_block, to_ring(middle_up, 2, 1), right, to_ring(right, 2, -1)]
+    lower_block, _ = lax.optimization_barrier((lower_block, right))
+    lower = ring(lower_block, 1)
+
+    share_cols = model_width // tensor_count
+    dealt_shape = (SIDE, proj_out.shape[0], share_cols // 2)
+    dealt = whole_call(
+        deal_columns,
+        "deal_columns",
+        info,
+        [proj_out],
+        (shape_of(dealt_shape),) * 4,
         limit=8,
-        after=[*qkv[1:3], proj_mine],
-    )
-    other_tokens = to_core(own_tokens)
-    token_pieces = whole_call(
-        both_rows,
-        "both_rows",
-        info,
-        [own_tokens, other_tokens],
-        shape_of((tensor_count, 2 * spans * span_size, share)),
-    )
-    all_rows = 2 * spans * span_size
-
-    middle = ring(middle_block, -1)
-    lower = ring(lower_block, 1)
+        after=[qkv[1]],
+    )
+    dealt = [dealt[0]] + [
+        to_ring(part, 1, distance) for part, distance in zip(dealt[1:], (1, -1, 2))
+    ]
+    dealt = whole_call(
+        deal_again, "deal_again", info, dealt, (shape_of(dealt_shape),) * 4, limit=8
+    )
+    dealt = [dealt[0]] + [
+        to_ring(part, 2, distance) for part, distance in zip(dealt[1:], (1, -1, 2))
+    ]
+    proj_mine = whole_call(
+        join_blocks, "join_proj", info, dealt, shape_of((SIDE,) + dealt_shape), limit=8
+    )
+    proj_other = to_core(proj_mine)
 
     context = whole_call(
         span_attention,
@@ -619,7 +664,10 @@
         info,
         [arrived, order, proj_in, proj_mine, proj_other],
         shape_of((rows, share_cols)),
-        [pltpu.VMEM((device_count, width // 128, 128), jnp.float32)],
+        [
+            pltpu.VMEM((device_count, width // 128, 128), jnp.float32),
+            pltpu.VMEM((tensor_count, rows, proj_out.shape[0]), jnp.bfloat16),
+        ],
         flops=2 * rows * width * (width + share_cols),
     )
     first_block = whole_call(
@@ -639,7 +687,7 @@
     key_sine = lax.dynamic_slice_in_dim(sine, key_start, kv_cols, 1)
     parts = 8
     gain = norm_gain.reshape(tensor_count, 1, share_cols)
-    kv_pair = jnp.concatenate([key_value_weight[0], key_value_weight[1]], axis=1)
+    kv_pair = key_value_weight.transpose(0, 2, 1).reshape(2 * kv_cols, model_width)
     sums = (
         shape_of((rows, query_cols), jnp.float32),
         shape_of((rows, 2 * kv_cols), jnp.float32),

time: 201 us -> 202 us (level)
  waiting for transfers between devices: 77.9 us -> 85.5 us
  local copies, waits for them, and re-layouts: 25.4 us -> 22.5 us
  Pallas kernels: 34.8 us -> 32 us
  other arithmetic: 9.19 us -> 6.6 us
    ppermute x21 -> x27, waiting for transfers between devices: 36.1 us -> 46.2 us  [to_ring(): return lax.ppermute(value, AXES, ring_pairs(phase, distance))]
    ppermute x21 -> x27, starting transfers between devices: 31.1 us -> 37.8 us  [to_ring(): return lax.ppermute(value, AXES, ring_pairs(phase, distance))]
    all_to_all x1 -> x0, starting transfers between devices: 4.13 us -> none  [local(): lax.all_to_all(whole_call(spread_proj, 'spread_proj', info, [proj_out], s...]
    concatenate x2 -> x0, other arithmetic: 3.48 us -> none  [the longest x1 3.4 us: local(): jnp.concatenate([key_value_weight[0], key_value_weight[1]], axis=1)]
    unnamed x68 -> x56, local copies, waits for them, and re-layouts: 21.2 us -> 17.7 us
    pallas_call x18 -> x19, Pallas kernels: 30.9 us -> 28.1 us  [whole_call(): pl.pallas_call(run, name=name, out_shape=outs, in_specs=[SMEM] + [VMEM] *...]
    all_to_all x1 -> x0, waiting for transfers between devices: 2.39 us -> none  [local(): lax.all_to_all(whole_call(spread_proj, 'spread_proj', info, [proj_out], s...]
  transfers between devices with their start and end apart: 30 -> 35, of which waited for: 17 -> 18; matrix products, arithmetic and copies ran while one was open for 8% -> 5% of each run, Pallas kernels for 11% -> 10%
where the time goes in v3:
time: 202 us; the launch traced here: 201 us
  waiting for transfers between devices  85.5 us (42%)
  starting transfers between devices  53.1 us (26%)
  Pallas kernels  32 us (16%)
  local copies, waits for them, and re-layouts  22.5 us (11%)
  other arithmetic  6.6 us (3%)
    ppermute x27, waiting for transfers between devices, to_ring(): return lax.ppermute(value, AXES, ring_pairs(phase, distance))  46.2 us
    ppermute x27, starting transfers between devices, to_ring(): return lax.ppermute(value, AXES, ring_pairs(phase, distance))  37.8 us
    pallas_call x19, Pallas kernels, whole_call(): pl.pallas_call(run, name=name, out_shape=outs, in_specs=[SMEM] + [VMEM] *...  28.1 us
    all_to_all x1, waiting for transfers between devices, local(): lax.all_to_all(partial.reshape(tensor_count, own_rows, model_width), 'ten...  24.8 us
    unnamed x56, local copies, waits for them, and re-layouts  17.7 us
    all_to_all x1, waiting for transfers between devices, local(): lax.all_to_all(outgoing.reshape(device_count, width // 128, 128), AXES, 0...  10.8 us
    all_to_all x1, starting transfers between devices, local(): lax.all_to_all(outgoing.reshape(device_count, width // 128, 128), AXES, 0...  9 us
    all_to_all x1, starting transfers between devices, local(): lax.all_to_all(partial.reshape(tensor_count, own_rows, model_width), 'ten...  5.14 us
  transfers between devices with their start and end apart: 35, of which 18 were waited for; matrix products, arithmetic and copies ran while one was open for 5% of the time, Pallas kernels for 10%

profile of v3, /device:TPU:0, one launch (start us, length us, event | category | flops | bytes accessed | tf_op | source)
XLA Modules:
  0.0 200.9 jit_solution(14677596374661278710)
XLA Ops:
  1.3 1.0 copy-done.11
  2.3 0.9 copy-done.12
  3.2 0.9 copy-done.13
  4.2 0.9 copy-done.16
  5.1 0.8 take_halves.1
  5.9 1.7 collective-permute-start.4
  7.6 1.6 collective-permute-start.5
  9.6 2.8 %collective-permute-start.2 = (bf16[64,1536]{1,0:T(8,128)(2,1)S(1)}, bf16[64,1536]{1,0:T(8,128)(2,1)S(1)}, u32[]{:S(2)}, u32[]{:S(2)}) collective-permute-start(bf16[64,1536]{1,0:T(8,128)(2,1)S(1)} %get-tuple-element.32.refs_1_), channel_id=1, source_target_pairs={{0,3},{1,0},{2,1},{3,2},{4,7},{5,4},{6,5},{7,6},{8,11},{9,8},{10,9... | collective-permute-start | bytes 589832 | tf_op jit(solution)/shard_map/ppermute | solution.py:67
  12.4 0.9 collective-permute-start.3
  13.3 3.1 %collective-permute-done.1.refs_2_ = bf16[64,1536]{1,0:T(8,128)(2,1)S(1)} collective-permute-done((bf16[64,1536]{1,0:T(8,128)(2,1)S(1)}, bf16[64,1536]{1,0:T(8,128)(2,1)S(1)}, u32[]{:S(2)}, u32[]{:S(2)}) %collective-permute-start.1) | collective-permute-done | bytes 196640 | tf_op jit(solution)/shard_map/ppermute | solution.py:67
  16.8 3.0 %collective-permute-done.3.refs_4_ = bf16[64,1536]{1,0:T(8,128)(2,1)S(1)} collective-permute-done((bf16[64,1536]{1,0:T(8,128)(2,1)S(1)}, bf16[64,1536]{1,0:T(8,128)(2,1)S(1)}, u32[]{:S(2)}, u32[]{:S(2)}) %collective-permute-start.3) | collective-permute-done | bytes 196640 | tf_op jit(solution)/shard_map/ppermute | solution.py:67
  20.4 1.6 collective-permute-start.6
  22.0 1.7 collective-permute-start.7
  23.7 1.9 collective-permute-start.10
  25.6 8.7 %collective-permute-done.10.refs_4_ = bf16[64,2560]{1,0:T(8,128)(2,1)S(1)} collective-permute-done((bf16[64,2560]{1,0:T(8,128)(2,1)S(1)}, bf16[64,2560]{1,0:T(8,128)(2,1)S(1)}, u32[]{:S(2)}, u32[]{:S(2)}) %collective-permute-start.10) | collective-permute-done | bytes 327712 | tf_op jit(solution)/shard_map/ppermute | solution.py:67
  34.3 1.4 join_rest.1
  36.5 3.2 %collective-permute-start.12 = (bf16[4,64,1536]{2,1,0:T(8,128)(2,1)S(1)}, bf16[4,64,1536]{2,1,0:T(8,128)(2,1)S(1)}, u32[]{:S(2)}, u32[]{:S(2)}) collective-permute-start(bf16[4,64,1536]{2,1,0:T(8,128)(2,1)S(1)} %get-tuple-element.36.refs_3_.refs_5_), channel_id=1, source_target_pairs={{0,12},{1,13},{2,14},{3,15},{4,0},{5,1},{6,2},{7,3},{8,4},{9,5},{1... | collective-permute-start | bytes 2359304 | tf_op jit(solution)/shard_map/ppermute | solution.py:67
  39.7 9.3 %collective-permute-done.8.refs_5_ = bf16[4,64,1536]{2,1,0:T(8,128)(2,1)S(1)} collective-permute-done((bf16[4,64,1536]{2,1,0:T(8,128)(2,1)S(1)}, bf16[4,64,1536]{2,1,0:T(8,128)(2,1)S(1)}, u32[]{:S(2)}, u32[]{:S(2)}) %collective-permute-start.8) | collective-permute-done | bytes 786464 | tf_op jit(solution)/shard_map/ppermute | solution.py:67
  49.2 3.7 %collective-permute-start.13 = (bf16[4,64,1536]{2,1,0:T(8,128)(2,1)S(1)}, bf16[4,64,1536]{2,1,0:T(8,128)(2,1)S(1)}, u32[]{:S(2)}, u32[]{:S(2)}) collective-permute-start(bf16[4,64,1536]{2,1,0:T(8,128)(2,1)S(1)} %collective-permute-done.12.refs_5_.refs_7_), channel_id=1, source_target_pairs={{0,12},{1,13},{2,14},{3,15},{4,0},{5,1},{6,2},{7,3},{8,4},{9,5},{1... | collective-permute-start | bytes 2359304 | tf_op jit(solution)/shard_map/ppermute | solution.py:67
  53.6 0.9 collective-permute-done.refs_2_
  54.5 0.9 both_rows.1.refs_1_
  56.0 2.6 %span_attention.1.refs_1_ = bf16[8,256,64]{2,1,0:T(8,128)(2,1)S(1)} custom-call(s32[38]{0:T(128)S(1)} %concatenate.9.refs_0_.info, bf16[16,256,64]{2,1,0:T(8,128)(2,1)S(1)} %both_rows.1.refs_1_, bf16[4,64,1536]{2,1,0:T(8,128)(2,1)S(1)} %join_qkv.1.refs_2_, bf16[4,64,1536]{2,1,0:T(8,128)(2,1)S(1)} %collective-permute-done.6.refs_3_.refs_2_, ...), custom_call_target="tpu_custom_call" | custom-call | flops 805306368 | bytes 3670016 | tf_op jit(solution)/shard_map/span_attention/pallas_call | solution.py:100
  58.9 1.3 select_reduce_fusion.3
  60.3 2.3 %collective-permute-start.16 = (bf16[4,64,1024]{2,1,0:T(8,128)(2,1)}, bf16[4,64,1024]{2,1,0:T(8,128)(2,1)}, u32[]{:S(2)}, u32[]{:S(2)}) collective-permute-start(bf16[4,64,1024]{2,1,0:T(8,128)(2,1)} %get-tuple-element.40.refs_3_), channel_id=1, source_target_pairs={{0,12},{1,13},{2,14},{3,15},{4,0},{5,1},{6,2},{7,3},{8,4},{9,5},{1... | collective-permute-start | bytes 1572872 | tf_op jit(solution)/shard_map/ppermute | solution.py:67
  62.6 5.3 %collective-permute-done.15.refs_4_ = bf16[4,64,1024]{2,1,0:T(8,128)(2,1)} collective-permute-done((bf16[4,64,1024]{2,1,0:T(8,128)(2,1)}, bf16[4,64,1024]{2,1,0:T(8,128)(2,1)}, u32[]{:S(2)}, u32[]{:S(2)}) %collective-permute-start.15) | collective-permute-done | bytes 524320 | tf_op jit(solution)/shard_map/ppermute | solution.py:67
  68.5 1.3 deal_columns.1
  69.8 1.4 collective-permute-start.19
  71.2 1.3 context_out.1.refs_3_
  73.2 1.8 collective-permute-start.20
  75.0 1.0 collective-permute-done.19.refs_2_
  76.6 0.9 collective-permute-start.21
  79.5 1.0 select_reduce_fusion
  80.5 2.9 %collective-permute-done.21.refs_4_ = bf16[4,64,256]{2,1,0:T(8,128)(2,1)} collective-permute-done((bf16[4,64,256]{2,1,0:T(8,128)(2,1)}, bf16[4,64,256]{2,1,0:T(8,128)(2,1)}, u32[]{:S(2)}, u32[]{:S(2)}) %collective-permute-start.21) | collective-permute-done | bytes 131104 | tf_op jit(solution)/shard_map/ppermute | solution.py:67
  83.4 0.9 copy-done.15
  84.3 1.0 deal_again.1
  85.4 3.3 %collective-permute-start.23 = (bf16[4,64,256]{2,1,0:T(8,128)(2,1)S(1)}, bf16[4,64,256]{2,1,0:T(8,128)(2,1)S(1)}, u32[]{:S(2)}, u32[]{:S(2)}) collective-permute-start(bf16[4,64,256]{2,1,0:T(8,128)(2,1)S(1)} %get-tuple-element.49), channel_id=1, source_target_pairs={{0,12},{1,13},{2,14},{3,15},{4,0},{5,1},{6,2},{7,3},{8,4},{9,5},{1... | collective-permute-start | bytes 393224 | tf_op jit(solution)/shard_map/ppermute | solution.py:67
  88.7 1.4 collective-permute-start.24
  90.1 0.9 copy-done.7
  91.1 0.9 copy-done.9
  92.0 2.8 %norm_up.1 = (bf16[256,1024]{1,0:T(8,128)(2,1)S(1)}, bf16[16,256,64]{2,1,0:T(8,128)(2,1)S(1)}) custom-call(s32[38]{0:T(128)S(1)} %concatenate.9.refs_0_.info, bf16[128,1024]{1,0:T(8,128)(2,1)S(1)} %bitcast.28, bf16[128,1024]{1,0:T(8,128)(2,1)S(1)} %copy-done.9, bf16[256,512]{1,0:T(8,128)(2,1)S(1)} %context_out.1.refs_3_, ...), custom_call_target="tpu_custom_call" | custom-call | flops 536870912 | bytes 4194304 | tf_op jit(solution)/shard_map/norm_up/pallas_call | solution.py:100
  94.8 2.3 %down.1 = (f32[128,1024]{1,0:T(8,128)S(1)}, bf16[128,1024]{1,0:T(8,128)(2,1)S(1)}) custom-call(s32[38]{0:T(128)S(1)} %concatenate.9.refs_0_.info, bf16[16,256,64]{2,1,0:T(8,128)(2,1)S(1)} %get-tuple-element.37.refs_1_, bf16[256,1024]{1,0:T(8,128)(2,1)S(1)} %get-tuple-element.38.refs_2_, bf16[4,64,1024]{2,1,0:T(8,128)(2,1)} %get-tuple-element.40.refs_3_, ...), custom_call_target="tpu_custom_call" | custom-call | flops 536870912 | bytes 3145728 | tf_op jit(solution)/shard_map/down/pallas_call | solution.py:100
  99.2 1.7 norm_pool.1
  100.8 9.0 %all-to-all-start = ((bf16[128,8,128]{2,1,0:T(8,128)(2,1)}), bf16[128,8,128]{2,1,0:T(8,128)(2,1)S(1)}, u32[]{:S(2)}, u32[]{:S(2)}) async-start(bf16[128,8,128]{2,1,0:T(8,128)(2,1)} %bitcast.8), calls=%async_computation | async-start | bytes 524288 | tf_op jit(solution)/shard_map/all_to_all | solution.py:657
  109.9 10.8 %all-to-all-done.refs_1_ = bf16[128,8,128]{2,1,0:T(8,128)(2,1)S(1)} async-done(((bf16[128,8,128]{2,1,0:T(8,128)(2,1)}), bf16[128,8,128]{2,1,0:T(8,128)(2,1)S(1)}, u32[]{:S(2)}, u32[]{:S(2)}) %all-to-all-start) | async-done | bytes 262176 | tf_op jit(solution)/shard_map/all_to_all | solution.py:657
  120.7 1.6 copy-done.4
  122.3 2.6 %embed.1.refs_1_ = bf16[128,512]{1,0:T(8,128)(2,1)S(1)} custom-call(s32[38]{0:T(128)S(1)} %concatenate.9.refs_0_.info, bf16[128,8,128]{2,1,0:T(8,128)(2,1)S(1)} %all-to-all-done.refs_1_, bf16[128,128]{1,0:T(8,128)(2,1)S(1)} %fusion.refs_2_, bf16[1024,1024]{1,0:T(8,128)(2,1)S(1)} %copy-done.4, bf16[4,4,64,256]{3,2,1,0:T(8,128)(2,1)S(1)} %join_proj.1.refs_4_, ...), custom_call_target="tpu_custom_call" | custom-call | flops 402653184 | bytes 3440640 | tf_op jit(solution)/shard_map/embed/pallas_call | solution.py:100
  125.6 2.6 %collective-permute-start.27 = (bf16[128,512]{1,0:T(8,128)(2,1)S(1)}, bf16[128,512]{1,0:T(8,128)(2,1)S(1)}, u32[]{:S(2)}, u32[]{:S(2)}) collective-permute-start(bf16[128,512]{1,0:T(8,128)(2,1)S(1)} %embed.1.refs_1_), channel_id=1, source_target_pairs={{0,3},{1,0},{2,1},{3,2},{4,7},{5,4},{6,5},{7,6},{8,11},{9,8},{10,9... | collective-permute-start | bytes 393224 | tf_op jit(solution)/shard_map/ppermute | solution.py:67
  129.0 2.2 %collective-permute-done.26.refs_2_ = bf16[128,512]{1,0:T(8,128)(2,1)S(1)} collective-permute-done((bf16[128,512]{1,0:T(8,128)(2,1)S(1)}, bf16[128,512]{1,0:T(8,128)(2,1)S(1)}, u32[]{:S(2)}, u32[]{:S(2)}) %collective-permute-start.26) | collective-permute-done | bytes 131104 | tf_op jit(solution)/shard_map/ppermute | solution.py:67
  131.2 1.0 collective-permute-done.27.refs_3_
  132.2 2.5 %collective-permute-done.28.refs_4_ = bf16[128,512]{1,0:T(8,128)(2,1)S(1)} collective-permute-done((bf16[128,512]{1,0:T(8,128)(2,1)S(1)}, bf16[128,512]{1,0:T(8,128)(2,1)S(1)}, u32[]{:S(2)}, u32[]{:S(2)}) %collective-permute-start.28) | collective-permute-done | bytes 131104 | tf_op jit(solution)/shard_map/ppermute | solution.py:67
  136.0 2.7 %collective-permute-start.31 = (bf16[4,128,512]{2,1,0:T(8,128)(2,1)S(1)}, bf16[4,128,512]{2,1,0:T(8,128)(2,1)}, u32[]{:S(2)}, u32[]{:S(2)}) collective-permute-start(bf16[4,128,512]{2,1,0:T(8,128)(2,1)S(1)} %join_columns.1.refs_1_), channel_id=1, source_target_pairs={{0,12},{1,13},{2,14},{3,15},{4,0},{5,1},{6,2},{7,3},{8,4},{9,5},{1... | collective-permute-start | bytes 1572872 | tf_op jit(solution)/shard_map/ppermute | solution.py:67
  139.8 6.0 %collective-permute-done.29.refs_1_ = bf16[4,128,512]{2,1,0:T(8,128)(2,1)} collective-permute-done((bf16[4,128,512]{2,1,0:T(8,128)(2,1)S(1)}, bf16[4,128,512]{2,1,0:T(8,128)(2,1)}, u32[]{:S(2)}, u32[]{:S(2)}) %collective-permute-start.29) | collective-permute-done | bytes 524320 | tf_op jit(solution)/shard_map/ppermute | solution.py:67
  146.3 3.4 %copy-done = bf16[8192,512]{1,0:T(8,128)(2,1)S(1)} copy-done((bf16[8192,512]{1,0:T(8,128)(2,1)S(1)}, bf16[8192,512]{1,0:T(8,128)(2,1)}, u32[]{:S(2)}) %copy-start) | copy-done | bytes 8388632
  149.7 1.2 project_own.1
  150.9 3.4 %copy-done.1 = bf16[8192,512]{1,0:T(8,128)(2,1)S(1)} copy-done((bf16[8192,512]{1,0:T(8,128)(2,1)S(1)}, bf16[8192,512]{1,0:T(8,128)(2,1)}, u32[]{:S(2)}) %copy-start.1) | copy-done | bytes 8388632
  154.4 2.5 %project_near.1 = (f32[128,512]{1,0:T(8,128)S(1)}, f32[128,128]{1,0:T(8,128)S(1)}, f32[128,1]{1,0:T(8,128)S(1)}) custom-call(s32[38]{0:T(128)S(1)} %concatenate.9.refs_0_.info, bf16[4,128,512]{2,1,0:T(8,128)(2,1)} %collective-permute-done.29.refs_1_, bf16[4,128,512]{2,1,0:T(8,128)(2,1)} %collective-permute-done.31.refs_2_, f32[16,1,512]{2,1,0:T(1,128)S(1)} %bitcast.30, ...), custom_call_target="tpu_custom_call" | custom-call | flops 671088640 | bytes 11895296 | tf_op jit(solution)/shard_map/project_near/pallas_call | solution.py:100
  156.9 1.2 last_keys.1
  158.5 1.3 last_queries.1.query
  159.8 2.8 %collective-permute-done.32.partner = bf16[2,128,64]{2,1,0:T(8,128)(2,1)S(1)} collective-permute-done((bf16[2,128,64]{2,1,0:T(8,128)(2,1)S(1)}, bf16[2,128,64]{2,1,0:T(8,128)(2,1)S(1)}, u32[]{:S(2)}, u32[]{:S(2)}) %collective-permute-start.32) | collective-permute-done | bytes 32800 | tf_op jit(solution)/shard_map/ppermute | solution.py:729
  162.6 3.9 %attend_out.1 = bf16[128,8192]{1,0:T(8,128)(2,1)S(1)} custom-call(s32[38]{0:T(128)S(1)} %concatenate.9.refs_0_.info, bf16[128,512]{1,0:T(8,128)(2,1)S(1)} %last_queries.1.query, bf16[2,128,64]{2,1,0:T(8,128)(2,1)S(1)} %get-tuple-element.58.mine, bf16[2,128,64]{2,1,0:T(8,128)(2,1)S(1)} %collective-permute-done.32.partner, f32[128,128]{1,0:T(8,128)S(1)} %fusion.3.allowed, ...), custom_call_target="tpu_custom_call" | custom-call | tf_op jit(solution)/shard_map/attend_out/pallas_call | solution.py:740
  166.5 1.3 copy-done.3
  167.8 5.1 %all-to-all-start.1 = ((bf16[16,8,8192]{2,1,0:T(8,128)(2,1)}), bf16[16,8,8192]{2,1,0:T(8,128)(2,1)S(1)}, u32[]{:S(2)}, u32[]{:S(2)}) async-start(bf16[16,8,8192]{2,1,0:T(8,128)(2,1)} %bitcast.25), calls=%async_computation.1 | async-start | bytes 4194304 | tf_op jit(solution)/shard_map/all_to_all | solution.py:753
  174.6 24.8 %all-to-all-done.1.refs_1_ = bf16[16,8,8192]{2,1,0:T(8,128)(2,1)S(1)} async-done(((bf16[16,8,8192]{2,1,0:T(8,128)(2,1)}), bf16[16,8,8192]{2,1,0:T(8,128)(2,1)S(1)}, u32[]{:S(2)}, u32[]{:S(2)}) %all-to-all-start.1) | async-done | bytes 2097184 | tf_op jit(solution)/shard_map/all_to_all | solution.py:753
  199.4 1.5 finish.1
  (130 shorter events, 16.9 us)
Async XLA Ops:
  1.3 1.0 copy-start.11
  2.3 0.9 copy-start.12
  3.2 0.9 copy-start.13
  4.2 0.9 copy-start.16
  5.1 47.8 %copy-start.6 = (bf16[8,16,1024]{2,1,0:T(8,128)(2,1)S(1)}, bf16[8,16,1024]{2,1,0:T(8,128)(2,1)}, u32[]{:S(2)}) copy-start(bf16[8,16,1024]{2,1,0:T(8,128)(2,1)} %param.16) | copy-start | bytes 786436
  5.1 47.8 %copy-start.22 = (s32[8]{0:T(128)S(1)}, s32[8]{0:T(128)}, u32[]{:S(2)}) copy-start(s32[8]{0:T(128)} %param.19) | copy-start | bytes 100
  5.1 48.5 %copy-start.18 = (s32[1024]{0:T(1024)S(1)}, s32[1024]{0:T(1024)}, u32[]{:S(2)}) copy-start(s32[1024]{0:T(1024)} %param.17) | copy-start | bytes 12292
  5.9 13.9 %collective-permute-start.4 = (bf16[64,2560]{1,0:T(8,128)(2,1)S(1)}, bf16[64,2560]{1,0:T(8,128)(2,1)S(1)}, u32[]{:S(2)}, u32[]{:S(2)}) collective-permute-start(bf16[64,2560]{1,0:T(8,128)(2,1)S(1)} %get-tuple-element.33.refs_1_), channel_id=1, source_target_pairs={{0,1},{1,2},{2,3},{3,0},{4,5},{5,6},{6,7},{7,4},{8,9},{9,10},{10,1... | collective-permute-start | bytes 983048 | tf_op jit(solution)/shard_map/ppermute | solution.py:67
  7.6 12.2 %collective-permute-start.5 = (bf16[64,2560]{1,0:T(8,128)(2,1)S(1)}, bf16[64,2560]{1,0:T(8,128)(2,1)S(1)}, u32[]{:S(2)}, u32[]{:S(2)}) collective-permute-start(bf16[64,2560]{1,0:T(8,128)(2,1)S(1)} %get-tuple-element.33.refs_1_), channel_id=1, source_target_pairs={{0,3},{1,0},{2,1},{3,2},{4,7},{5,4},{6,5},{7,6},{8,11},{9,8},{10,9... | collective-permute-start | bytes 983048 | tf_op jit(solution)/shard_map/ppermute | solution.py:67
  9.2 7.2 %collective-permute-start.1 = (bf16[64,1536]{1,0:T(8,128)(2,1)S(1)}, bf16[64,1536]{1,0:T(8,128)(2,1)S(1)}, u32[]{:S(2)}, u32[]{:S(2)}) collective-permute-start(bf16[64,1536]{1,0:T(8,128)(2,1)S(1)} %get-tuple-element.32.refs_1_), channel_id=1, source_target_pairs={{0,1},{1,2},{2,3},{3,0},{4,5},{5,6},{6,7},{7,4},{8,9},{9,10},{10,1... | collective-permute-start | bytes 589832 | tf_op jit(solution)/shard_map/ppermute | solution.py:67
  9.6 7.2 %collective-permute-start.2 = (bf16[64,1536]{1,0:T(8,128)(2,1)S(1)}, bf16[64,1536]{1,0:T(8,128)(2,1)S(1)}, u32[]{:S(2)}, u32[]{:S(2)}) collective-permute-start(bf16[64,1536]{1,0:T(8,128)(2,1)S(1)} %get-tuple-element.32.refs_1_), channel_id=1, source_target_pairs={{0,3},{1,0},{2,1},{3,2},{4,7},{5,4},{6,5},{7,6},{8,11},{9,8},{10,9... | collective-permute-start | bytes 589832 | tf_op jit(solution)/shard_map/ppermute | solution.py:67
  12.4 7.3 %collective-permute-start.3 = (bf16[64,1536]{1,0:T(8,128)(2,1)S(1)}, bf16[64,1536]{1,0:T(8,128)(2,1)S(1)}, u32[]{:S(2)}, u32[]{:S(2)}) collective-permute-start(bf16[64,1536]{1,0:T(8,128)(2,1)S(1)} %get-tuple-element.32.refs_1_), channel_id=1, source_target_pairs={{0,2},{1,3},{2,0},{3,1},{4,6},{5,7},{6,4},{7,5},{8,10},{9,11},{10,... | collective-permute-start | bytes 589832 | tf_op jit(solution)/shard_map/ppermute | solution.py:67
  20.4 15.4 %collective-permute-start.6 = (bf16[4,64,1536]{2,1,0:T(8,128)(2,1)S(1)}, bf16[4,64,1536]{2,1,0:T(8,128)(2,1)S(1)}, u32[]{:S(2)}, u32[]{:S(2)}) collective-permute-start(bf16[4,64,1536]{2,1,0:T(8,128)(2,1)S(1)} %join_qkv.1.refs_2_), channel_id=1, source_target_pairs={{0,4},{1,5},{2,6},{3,7},{4,8},{5,9},{6,10},{7,11},{8,12},{9,13},{1... | collective-permute-start | bytes 2359304 | tf_op jit(solution)/shard_map/ppermute | solution.py:67
  22.0 14.6 %collective-permute-start.7 = (bf16[4,64,1536]{2,1,0:T(8,128)(2,1)S(1)}, bf16[4,64,1536]{2,1,0:T(8,128)(2,1)S(1)}, u32[]{:S(2)}, u32[]{:S(2)}) collective-permute-start(bf16[4,64,1536]{2,1,0:T(8,128)(2,1)S(1)} %join_qkv.1.refs_2_), channel_id=1, source_target_pairs={{0,12},{1,13},{2,14},{3,15},{4,0},{5,1},{6,2},{7,3},{8,4},{9,5},{1... | collective-permute-start | bytes 2359304 | tf_op jit(solution)/shard_map/ppermute | solution.py:67
  23.7 10.6 %collective-permute-start.10 = (bf16[64,2560]{1,0:T(8,128)(2,1)S(1)}, bf16[64,2560]{1,0:T(8,128)(2,1)S(1)}, u32[]{:S(2)}, u32[]{:S(2)}) collective-permute-start(bf16[64,2560]{1,0:T(8,128)(2,1)S(1)} %collective-permute-done.5.refs_6_.refs_3_), channel_id=1, source_target_pairs={{0,3},{1,0},{2,1},{3,2},{4,7},{5,4},{6,5},{7,6},{8,11},{9,8},{10,9... | collective-permute-start | bytes 983048 | tf_op jit(solution)/shard_map/ppermute | solution.py:67
  35.8 13.2 %collective-permute-start.8 = (bf16[4,64,1536]{2,1,0:T(8,128)(2,1)S(1)}, bf16[4,64,1536]{2,1,0:T(8,128)(2,1)S(1)}, u32[]{:S(2)}, u32[]{:S(2)}) collective-permute-start(bf16[4,64,1536]{2,1,0:T(8,128)(2,1)S(1)} %collective-permute-done.6.refs_3_.refs_2_), channel_id=1, source_target_pairs={{0,4},{1,5},{2,6},{3,7},{4,8},{5,9},{6,10},{7,11},{8,12},{9,13},{1... | collective-permute-start | bytes 2359304 | tf_op jit(solution)/shard_map/ppermute | solution.py:67
  36.5 12.7 %collective-permute-start.12 = (bf16[4,64,1536]{2,1,0:T(8,128)(2,1)S(1)}, bf16[4,64,1536]{2,1,0:T(8,128)(2,1)S(1)}, u32[]{:S(2)}, u32[]{:S(2)}) collective-permute-start(bf16[4,64,1536]{2,1,0:T(8,128)(2,1)S(1)} %get-tuple-element.36.refs_3_.refs_5_), channel_id=1, source_target_pairs={{0,12},{1,13},{2,14},{3,15},{4,0},{5,1},{6,2},{7,3},{8,4},{9,5},{1... | collective-permute-start | bytes 2359304 | tf_op jit(solution)/shard_map/ppermute | solution.py:67
  49.0 22.2 %collective-permute-start.11 = (bf16[4,64,1536]{2,1,0:T(8,128)(2,1)S(1)}, bf16[4,64,1536]{2,1,0:T(8,128)(2,1)S(1)}, u32[]{:S(2)}, u32[]{:S(2)}) collective-permute-start(bf16[4,64,1536]{2,1,0:T(8,128)(2,1)S(1)} %get-tuple-element.36.refs_3_.refs_5_), channel_id=1, source_target_pairs={{0,4},{1,5},{2,6},{3,7},{4,8},{5,9},{6,10},{7,11},{8,12},{9,13},{1... | collective-permute-start | bytes 2359304 | tf_op jit(solution)/shard_map/ppermute | solution.py:67
  49.2 22.0 %collective-permute-start.13 = (bf16[4,64,1536]{2,1,0:T(8,128)(2,1)S(1)}, bf16[4,64,1536]{2,1,0:T(8,128)(2,1)S(1)}, u32[]{:S(2)}, u32[]{:S(2)}) collective-permute-start(bf16[4,64,1536]{2,1,0:T(8,128)(2,1)S(1)} %collective-permute-done.12.refs_5_.refs_7_), channel_id=1, source_target_pairs={{0,12},{1,13},{2,14},{3,15},{4,0},{5,1},{6,2},{7,3},{8,4},{9,5},{1... | collective-permute-start | bytes 2359304 | tf_op jit(solution)/shard_map/ppermute | solution.py:67
  52.9 1.5 collective-permute-start
  53.6 14.3 %collective-permute-start.15 = (bf16[4,64,1024]{2,1,0:T(8,128)(2,1)}, bf16[4,64,1024]{2,1,0:T(8,128)(2,1)}, u32[]{:S(2)}, u32[]{:S(2)}) collective-permute-start(bf16[4,64,1024]{2,1,0:T(8,128)(2,1)} %get-tuple-element.40.refs_3_), channel_id=1, source_target_pairs={{0,4},{1,5},{2,6},{3,7},{4,8},{5,9},{6,10},{7,11},{8,12},{9,13},{1... | collective-permute-start | bytes 1572872 | tf_op jit(solution)/shard_map/ppermute | solution.py:67
  55.3 0.7 copy-start.8
  56.0 2.8 %copy-start.23 = (s32[8]{0:T(128)S(1)}, s32[8]{0:T(128)}, u32[]{:S(2)}) copy-start(s32[8]{0:T(128)} %param.18) | copy-start | bytes 100
  56.0 12.4 %copy-start.5 = (bf16[64,8192]{1,0:T(8,128)(2,1)S(1)}, bf16[64,8192]{1,0:T(8,128)(2,1)}, u32[]{:S(2)}) copy-start(bf16[64,8192]{1,0:T(8,128)(2,1)} %refs_1_.3) | copy-start | bytes 3145732
  58.7 11.1 %collective-permute-start.9 = (bf16[8,256,64]{2,1,0:T(8,128)(2,1)S(1)}, bf16[8,256,64]{2,1,0:T(8,128)(2,1)S(1)}, u32[]{:S(2)}, u32[]{:S(2)}) collective-permute-start(bf16[8,256,64]{2,1,0:T(8,128)(2,1)S(1)} %span_attention.1.refs_1_), channel_id=1, source_target_pairs={{0,16},{16,0},{32,48},{48,32},{64,80},{80,64},{96,112},{112,96},{1... | collective-permute-start | bytes 786440 | tf_op jit(solution)/shard_map/ppermute | solution.py:71
  60.3 34.6 %collective-permute-start.16 = (bf16[4,64,1024]{2,1,0:T(8,128)(2,1)}, bf16[4,64,1024]{2,1,0:T(8,128)(2,1)}, u32[]{:S(2)}, u32[]{:S(2)}) collective-permute-start(bf16[4,64,1024]{2,1,0:T(8,128)(2,1)} %get-tuple-element.40.refs_3_), channel_id=1, source_target_pairs={{0,12},{1,13},{2,14},{3,15},{4,0},{5,1},{6,2},{7,3},{8,4},{9,5},{1... | collective-permute-start | bytes 1572872 | tf_op jit(solution)/shard_map/ppermute | solution.py:67
  67.9 26.9 %collective-permute-start.17 = (bf16[4,64,1024]{2,1,0:T(8,128)(2,1)}, bf16[4,64,1024]{2,1,0:T(8,128)(2,1)}, u32[]{:S(2)}, u32[]{:S(2)}) collective-permute-start(bf16[4,64,1024]{2,1,0:T(8,128)(2,1)} %collective-permute-done.15.refs_4_), channel_id=1, source_target_pairs={{0,4},{1,5},{2,6},{3,7},{4,8},{5,9},{6,10},{7,11},{8,12},{9,13},{1... | collective-permute-start | bytes 1572872 | tf_op jit(solution)/shard_map/ppermute | solution.py:67
  69.8 6.2 %collective-permute-start.19 = (bf16[4,64,256]{2,1,0:T(8,128)(2,1)S(1)}, bf16[4,64,256]{2,1,0:T(8,128)(2,1)S(1)}, u32[]{:S(2)}, u32[]{:S(2)}) collective-permute-start(bf16[4,64,256]{2,1,0:T(8,128)(2,1)S(1)} %get-tuple-element.44), channel_id=1, source_target_pairs={{0,1},{1,2},{2,3},{3,0},{4,5},{5,6},{6,7},{7,4},{8,9},{9,10},{10,1... | collective-permute-start | bytes 393224 | tf_op jit(solution)/shard_map/ppermute | solution.py:67
  72.5 16.2 %collective-permute-start.14 = (bf16[256,512]{1,0:T(8,128)(2,1)S(1)}, bf16[256,512]{1,0:T(8,128)(2,1)}, u32[]{:S(2)}, u32[]{:S(2)}) collective-permute-start(bf16[256,512]{1,0:T(8,128)(2,1)S(1)} %context_out.1.refs_3_), channel_id=1, source_target_pairs={{0,16},{16,0},{32,48},{48,32},{64,80},{80,64},{96,112},{112,96},{1... | collective-permute-start | bytes 786440 | tf_op jit(solution)/shard_map/ppermute | solution.py:71
  73.2 7.3 %collective-permute-start.20 = (bf16[4,64,256]{2,1,0:T(8,128)(2,1)}, bf16[4,64,256]{2,1,0:T(8,128)(2,1)}, u32[]{:S(2)}, u32[]{:S(2)}) collective-permute-start(bf16[4,64,256]{2,1,0:T(8,128)(2,1)} %get-tuple-element.45), channel_id=1, source_target_pairs={{0,3},{1,0},{2,1},{3,2},{4,7},{5,4},{6,5},{7,6},{8,11},{9,8},{10,9... | collective-permute-start | bytes 393224 | tf_op jit(solution)/shard_map/ppermute | solution.py:67
  76.0 0.6 copy-start.14
  76.6 6.8 %collective-permute-start.21 = (bf16[4,64,256]{2,1,0:T(8,128)(2,1)}, bf16[4,64,256]{2,1,0:T(8,128)(2,1)}, u32[]{:S(2)}, u32[]{:S(2)}) collective-permute-start(bf16[4,64,256]{2,1,0:T(8,128)(2,1)} %get-tuple-element.46), channel_id=1, source_target_pairs={{0,2},{1,3},{2,0},{3,1},{4,6},{5,7},{6,4},{7,5},{8,10},{9,11},{10,... | collective-permute-start | bytes 393224 | tf_op jit(solution)/shard_map/ppermute | solution.py:67
  83.4 0.9 copy-start.15
  85.3 12.6 %collective-permute-start.22 = (bf16[4,64,256]{2,1,0:T(8,128)(2,1)S(1)}, bf16[4,64,256]{2,1,0:T(8,128)(2,1)S(1)}, u32[]{:S(2)}, u32[]{:S(2)}) collective-permute-start(bf16[4,64,256]{2,1,0:T(8,128)(2,1)S(1)} %get-tuple-element.48), channel_id=1, source_target_pairs={{0,4},{1,5},{2,6},{3,7},{4,8},{5,9},{6,10},{7,11},{8,12},{9,13},{1... | collective-permute-start | bytes 393224 | tf_op jit(solution)/shard_map/ppermute | solution.py:67
  85.4 12.6 %collective-permute-start.23 = (bf16[4,64,256]{2,1,0:T(8,128)(2,1)S(1)}, bf16[4,64,256]{2,1,0:T(8,128)(2,1)S(1)}, u32[]{:S(2)}, u32[]{:S(2)}) collective-permute-start(bf16[4,64,256]{2,1,0:T(8,128)(2,1)S(1)} %get-tuple-element.49), channel_id=1, source_target_pairs={{0,12},{1,13},{2,14},{3,15},{4,0},{5,1},{6,2},{7,3},{8,4},{9,5},{1... | collective-permute-start | bytes 393224 | tf_op jit(solution)/shard_map/ppermute | solution.py:67
  88.7 9.3 %collective-permute-start.24 = (bf16[4,64,256]{2,1,0:T(8,128)(2,1)S(1)}, bf16[4,64,256]{2,1,0:T(8,128)(2,1)S(1)}, u32[]{:S(2)}, u32[]{:S(2)}) collective-permute-start(bf16[4,64,256]{2,1,0:T(8,128)(2,1)S(1)} %get-tuple-element.50), channel_id=1, source_target_pairs={{0,8},{1,9},{2,10},{3,11},{4,12},{5,13},{6,14},{7,15},{8,0},{9,1},... | collective-permute-start | bytes 393224 | tf_op jit(solution)/shard_map/ppermute | solution.py:67
  90.1 0.9 copy-start.7
  91.1 0.9 copy-start.9
  97.2 2.0 collective-permute-start.18
  98.6 11.3 %collective-permute-start.25 = (bf16[4,4,64,256]{3,2,1,0:T(8,128)(2,1)S(1)}, bf16[4,4,64,256]{3,2,1,0:T(8,128)(2,1)}, u32[]{:S(2)}, u32[]{:S(2)}) collective-permute-start(bf16[4,4,64,256]{3,2,1,0:T(8,128)(2,1)S(1)} %join_proj.1.refs_4_), channel_id=1, source_target_pairs={{0,16},{16,0},{32,48},{48,32},{64,80},{80,64},{96,112},{112,96},{1... | collective-permute-start | bytes 1572872 | tf_op jit(solution)/shard_map/ppermute | solution.py:71
  100.8 28.0 %copy-start.17 = (s32[8,8,8]{2,1,0:T(8,128)S(1)}, s32[8,8,8]{2,1,0:T(8,128)}, u32[]{:S(2)}) copy-start(s32[8,8,8]{2,1,0:T(8,128)} %param.20) | copy-start | bytes 6148
  100.8 19.9 %all-to-all-start = ((bf16[128,8,128]{2,1,0:T(8,128)(2,1)}), bf16[128,8,128]{2,1,0:T(8,128)(2,1)S(1)}, u32[]{:S(2)}, u32[]{:S(2)}) async-start(bf16[128,8,128]{2,1,0:T(8,128)(2,1)} %bitcast.8), calls=%async_computation | async-start | bytes 524288 | tf_op jit(solution)/shard_map/all_to_all | solution.py:657
  109.9 36.0 %copy-start.19 = (f32[128]{0:T(128)S(1)}, f32[128]{0:T(128)}, u32[]{:S(2)}) copy-start(f32[128]{0:T(128)} %fusion.15) | copy-start | bytes 1540
  109.9 36.4 %copy-start.10 = (f32[8192]{0:T(1024)S(1)}, f32[8192]{0:T(1024)}, u32[]{:S(2)}) copy-start(f32[8192]{0:T(1024)} %param.27) | copy-start | bytes 98308
  109.9 36.4 %copy-start.2 = (bf16[2,8192,64]{1,2,0:T(8,128)(2,1)S(1)}, bf16[2,8192,64]{1,2,0:T(8,128)(2,1)}, u32[]{:S(2)}) copy-start(bf16[2,8192,64]{1,2,0:T(8,128)(2,1)} %param.29) | copy-start | bytes 6291460
  120.7 1.6 copy-start.4
  122.3 13.6 %copy-start.21 = (f32[128]{0:T(128)S(1)}, f32[128]{0:T(128)}, u32[]{:S(2)}) copy-start(f32[128]{0:T(128)} %compare_select_fusion.8) | copy-start | bytes 1540
  122.3 23.5 %copy-start.20 = (f32[128]{0:T(128)S(1)}, f32[128]{0:T(128)}, u32[]{:S(2)}) copy-start(f32[128]{0:T(128)} %iota_convert_fusion) | copy-start | bytes 1540
  124.9 6.2 %collective-permute-start.26 = (bf16[128,512]{1,0:T(8,128)(2,1)S(1)}, bf16[128,512]{1,0:T(8,128)(2,1)S(1)}, u32[]{:S(2)}, u32[]{:S(2)}) collective-permute-start(bf16[128,512]{1,0:T(8,128)(2,1)S(1)} %embed.1.refs_1_), channel_id=1, source_target_pairs={{0,1},{1,2},{2,3},{3,0},{4,5},{5,6},{6,7},{7,4},{8,9},{9,10},{10,1... | collective-permute-start | bytes 393224 | tf_op jit(solution)/shard_map/ppermute | solution.py:67
  125.6 6.5 %collective-permute-start.27 = (bf16[128,512]{1,0:T(8,128)(2,1)S(1)}, bf16[128,512]{1,0:T(8,128)(2,1)S(1)}, u32[]{:S(2)}, u32[]{:S(2)}) collective-permute-start(bf16[128,512]{1,0:T(8,128)(2,1)S(1)} %embed.1.refs_1_), channel_id=1, source_target_pairs={{0,3},{1,0},{2,1},{3,2},{4,7},{5,4},{6,5},{7,6},{8,11},{9,8},{10,9... | collective-permute-start | bytes 393224 | tf_op jit(solution)/shard_map/ppermute | solution.py:67
  128.2 6.5 %collective-permute-start.28 = (bf16[128,512]{1,0:T(8,128)(2,1)S(1)}, bf16[128,512]{1,0:T(8,128)(2,1)S(1)}, u32[]{:S(2)}, u32[]{:S(2)}) collective-permute-start(bf16[128,512]{1,0:T(8,128)(2,1)S(1)} %embed.1.refs_1_), channel_id=1, source_target_pairs={{0,2},{1,3},{2,0},{3,1},{4,6},{5,7},{6,4},{7,5},{8,10},{9,11},{10,... | collective-permute-start | bytes 393224 | tf_op jit(solution)/shard_map/ppermute | solution.py:67
  135.3 10.6 %collective-permute-start.29 = (bf16[4,128,512]{2,1,0:T(8,128)(2,1)S(1)}, bf16[4,128,512]{2,1,0:T(8,128)(2,1)}, u32[]{:S(2)}, u32[]{:S(2)}) collective-permute-start(bf16[4,128,512]{2,1,0:T(8,128)(2,1)S(1)} %join_columns.1.refs_1_), channel_id=1, source_target_pairs={{0,4},{1,5},{2,6},{3,7},{4,8},{5,9},{6,10},{7,11},{8,12},{9,13},{1... | collective-permute-start | bytes 1572872 | tf_op jit(solution)/shard_map/ppermute | solution.py:67
  136.0 14.9 %collective-permute-start.31 = (bf16[4,128,512]{2,1,0:T(8,128)(2,1)S(1)}, bf16[4,128,512]{2,1,0:T(8,128)(2,1)}, u32[]{:S(2)}, u32[]{:S(2)}) collective-permute-start(bf16[4,128,512]{2,1,0:T(8,128)(2,1)S(1)} %join_columns.1.refs_1_), channel_id=1, source_target_pairs={{0,12},{1,13},{2,14},{3,15},{4,0},{5,1},{6,2},{7,3},{8,4},{9,5},{1... | collective-permute-start | bytes 1572872 | tf_op jit(solution)/shard_map/ppermute | solution.py:67
  145.9 11.0 %collective-permute-start.30 = (bf16[4,128,512]{2,1,0:T(8,128)(2,1)}, bf16[4,128,512]{2,1,0:T(8,128)(2,1)S(1)}, u32[]{:S(2)}, u32[]{:S(2)}) collective-permute-start(bf16[4,128,512]{2,1,0:T(8,128)(2,1)} %collective-permute-done.29.refs_1_), channel_id=1, source_target_pairs={{0,4},{1,5},{2,6},{3,7},{4,8},{5,9},{6,10},{7,11},{8,12},{9,13},{1... | collective-permute-start | bytes 1572872 | tf_op jit(solution)/shard_map/ppermute | solution.py:67
  146.3 3.4 %copy-start = (bf16[8192,512]{1,0:T(8,128)(2,1)S(1)}, bf16[8192,512]{1,0:T(8,128)(2,1)}, u32[]{:S(2)}) copy-start(bf16[8192,512]{1,0:T(8,128)(2,1)} %refs_3_.7) | copy-start | bytes 25165828
  149.7 8.8 %slice-start = ((s8[8388608]{0:T(1024)(128)(4,1)}), s8[4194304]{0:T(1024)(128)(4,1)S(1)}, s32[]{:S(2)}) async-start(s8[8388608]{0:T(1024)(128)(4,1)} %bitcast.18), calls=%async_computation.2 | async-start | bytes 8388608
  150.9 3.4 %copy-start.1 = (bf16[8192,512]{1,0:T(8,128)(2,1)S(1)}, bf16[8192,512]{1,0:T(8,128)(2,1)}, u32[]{:S(2)}) copy-start(bf16[8192,512]{1,0:T(8,128)(2,1)} %refs_3_.7) | copy-start | bytes 25165828
  154.3 4.1 %slice-start.1 = ((s8[8388608]{0:T(1024)(128)(4,1)}), s8[4194304]{0:T(1024)(128)(4,1)S(1)}, s32[]{:S(2)}) async-start(s8[8388608]{0:T(1024)(128)(4,1)} %bitcast.18), calls=%async_computation.3 | async-start | bytes 8388608
  154.3 8.3 %slice-start.2 = ((s8[8388608]{0:T(1024)(128)(4,1)}), s8[4194304]{0:T(1024)(128)(4,1)S(1)}, s32[]{:S(2)}) async-start(s8[8388608]{0:T(1024)(128)(4,1)} %bitcast.23), calls=%async_computation.4 | async-start | bytes 8388608
  156.9 5.8 %slice-start.3 = ((s8[8388608]{0:T(1024)(128)(4,1)}), s8[4194304]{0:T(1024)(128)(4,1)S(1)}, s32[]{:S(2)}) async-start(s8[8388608]{0:T(1024)(128)(4,1)} %bitcast.23), calls=%async_computation.5 | async-start | bytes 8388608
  158.0 4.6 %collective-permute-start.32 = (bf16[2,128,64]{2,1,0:T(8,128)(2,1)S(1)}, bf16[2,128,64]{2,1,0:T(8,128)(2,1)S(1)}, u32[]{:S(2)}, u32[]{:S(2)}) collective-permute-start(bf16[2,128,64]{2,1,0:T(8,128)(2,1)S(1)} %get-tuple-element.58.mine), channel_id=1, source_target_pairs={{0,1},{1,0},{2,3},{3,2},{4,5},{5,4},{6,7},{7,6},{8,9},{9,8},{10,11... | collective-permute-start | bytes 98312 | tf_op jit(solution)/shard_map/ppermute | solution.py:729
  166.5 1.3 copy-start.3
  167.8 31.6 %all-to-all-start.1 = ((bf16[16,8,8192]{2,1,0:T(8,128)(2,1)}), bf16[16,8,8192]{2,1,0:T(8,128)(2,1)S(1)}, u32[]{:S(2)}, u32[]{:S(2)}) async-start(bf16[16,8,8192]{2,1,0:T(8,128)(2,1)} %bitcast.25), calls=%async_computation.1 | async-start | bytes 4194304 | tf_op jit(solution)/shard_map/all_to_all | solution.py:753

commit v4 on v3

--- a/solution.py
+++ b/solution.py
@@ -83,6 +83,7 @@
 
 VMEM = pl.BlockSpec(memory_space=pltpu.VMEM)
 SMEM = pl.BlockSpec(memory_space=pltpu.SMEM)
+ANYWHERE = pl.BlockSpec(memory_space=pl.ANY)
 MIB = 2**20
 
 
@@ -90,8 +91,8 @@
     return jax.ShapeDtypeStruct(shape, dtype)
 
 
-def whole_call(body, name, info, arrays, outs, scratch=(), limit=12, flops=0, out_space=pltpu.VMEM, after=()):
-    count = len(arrays)
+def whole_call(body, name, info, arrays, outs, scratch=(), limit=12, flops=0, far=(), after=()):
+    count = len(arrays) + len(far)
 
     def run(*refs):
         body(*refs[: 1 + count], *refs[1 + count + len(after) :])
@@ -101,12 +102,12 @@
         run,
         name=name,
         out_shape=outs,
-        in_specs=[SMEM] + [VMEM] * count + [pl.BlockSpec(memory_space=pl.ANY)] * len(after),
-        out_specs=jax.tree.map(lambda _: pl.BlockSpec(memory_space=out_space), outs),
+        in_specs=[SMEM] + [VMEM] * len(arrays) + [ANYWHERE] * (len(far) + len(after)),
+        out_specs=jax.tree.map(lambda _: VMEM, outs),
         scratch_shapes=list(scratch),
         compiler_params=pltpu.CompilerParams(vmem_limit_bytes=limit * MIB),
         cost_estimate=pl.CostEstimate(flops=flops, bytes_accessed=moved, transcendentals=0),
-    )(info, *arrays, *after)
+    )(info, *arrays, *far, *after)
 
 
 def dot32(left, right):
@@ -164,11 +165,14 @@
         out[index] = block[...]
 
 
-def join_rest(info, own, left, right, opposite, middle, lower):
-    cols = middle.shape[2]
+def join_middle(info, own, left, right, opposite, out):
     for index, block in enumerate((own, left, right, opposite)):
-        middle[index] = block[:, :cols]
-        lower[index] = block[:, cols:]
+        out[index] = block[:, : out.shape[2]]
+
+
+def join_lower(info, own, left, right, opposite, out):
+    for index, block in enumerate((own, left, right, opposite)):
+        out[index] = block[:, block.shape[1] - out.shape[2] :]
 
 
 def deal_columns(info, weight, *outs):
@@ -219,10 +223,13 @@
     return [(power / total).astype(jnp.bfloat16) for power, total in zip(powers, sums)]
 
 
-def span_attention(info, pieces, w0, w1, w2, w3, context, mixed):
-    cols = w0.shape[2]
-    third = cols // 3
-    mixed[...] = ring_dot(info, pieces, (w0, w1, w2, w3), 0, cols).astype(jnp.bfloat16)
+def span_qkv(info, pieces, w0, w1, w2, w3, mixed, mark):
+    mixed[...] = ring_dot(info, pieces, (w0, w1, w2, w3), 0, w0.shape[2]).astype(jnp.bfloat16)
+    mark[...] = jnp.zeros_like(mark)
+
+
+def span_attention(info, mixed, context):
+    third = mixed.shape[1] // 3
     size = context.shape[2]
     half = mixed.shape[0] // 2
     span = 16
@@ -248,25 +255,25 @@
         context[head, rows, :] = dot32(prob, value).astype(jnp.bfloat16)
 
 
-def context_out(info, mine, other, w0, w1, w2, w3, attended, pieces):
+def context_out(info, mine, other, tokens, w0, w1, w2, w3, attended, pieces):
     heads = mine.shape[0]
     core = info[16]
     pieces[pl.ds(core * heads, heads)] = mine[...]
     pieces[pl.ds((1 - core) * heads, heads)] = other[...]
     cols = attended.shape[1]
-    attended[...] = ring_dot(info, pieces, (w0, w1, w2, w3), 0, cols).astype(jnp.bfloat16)
-
-
-def norm_up(info, near_rows, far_rows, mine, other, w0, w1, w2, w3, first_out, inner, pieces, rows):
+    residual = jnp.concatenate([tokens[core * heads + index] for index in range(heads)], axis=1)
+    total = ring_dot(info, pieces, (w0, w1, w2, w3), 0, cols)
+    attended[...] = (residual.astype(jnp.float32) + total).astype(jnp.bfloat16)
+
+
+def norm_up(info, mine, other, w0, w1, w2, w3, first_out, inner, pieces):
     core = info[16]
     cols = mine.shape[1]
-    half, width = near_rows.shape
-    rows[pl.ds(pl.multiple_of(core * half, half), half), :] = near_rows[...]
-    rows[pl.ds(pl.multiple_of((1 - core) * half, half), half), :] = far_rows[...]
+    width = 2 * cols
     near = mine[...].astype(jnp.float32)
     far = other[...].astype(jnp.float32)
-    low = rows[:, :cols].astype(jnp.float32) + jnp.where(core == 0, near, far)
-    high = rows[:, cols:].astype(jnp.float32) + jnp.where(core == 0, far, near)
+    low = jnp.where(core == 0, near, far)
+    high = jnp.where(core == 0, far, near)
     mean = (jnp.sum(low, 1, keepdims=True) + jnp.sum(high, 1, keepdims=True)) / width
     low, high = low - mean, high - mean
     var = (jnp.sum(low * low, 1, keepdims=True) + jnp.sum(high * high, 1, keepdims=True)) / width
@@ -330,26 +337,40 @@
     out[:, cols:] = jnp.where(core == 0, far, near).astype(jnp.bfloat16)
 
 
+def shard_rows(info, weight, buffer, sems, at, step, slot):
+    depth = buffer.shape[1]
+    start = pl.multiple_of(info[SIDE * at + step] * depth, depth)
+    return pltpu.make_async_copy(
+        weight.at[pl.ds(start, depth), :], buffer.at[slot], sems.at[slot]
+    )
+
+
 def project(info, *refs, starts, count):
     blocks, refs = refs[:count], refs[count:]
-    gain, q_weight, kv_weight = refs[:3]
-    before = refs[3:6] if len(refs) > 6 else None
-    q_total, kv_total, square = refs[-3:]
+    gain, kv_weight = refs[:2]
+    before = refs[2:5] if len(refs) > 8 else None
+    q_weight, q_total, kv_total, square, buffer, sems = refs[-6:]
     depth = blocks[0].shape[2]
-    queries, both = None, None
-    squares = None
-    for at, block in zip(starts, blocks):
-        for step in range(SIDE):
-            shard = info[SIDE * at + step]
-            wide = block[step].astype(jnp.float32)
-            act = (wide * gain[shard]).astype(jnp.bfloat16)
-            span = pl.ds(pl.multiple_of(shard * depth, depth), depth)
-            q_term = dot32(act, q_weight[span, :])
-            kv_term = dot_last(act, kv_weight[:, span])
-            term = jnp.sum(wide * wide, axis=1, keepdims=True)
-            queries = q_term if queries is None else queries + q_term
-            both = kv_term if both is None else both + kv_term
-            squares = term if squares is None else squares + term
+    places = [(at, step) for at in starts for step in range(SIDE)]
+    copies = [
+        shard_rows(info, q_weight, buffer, sems, at, step, slot)
+        for slot, (at, step) in enumerate(places)
+    ]
+    for copy in copies:
+        copy.start()
+    queries, both, squares = None, None, None
+    for slot, (at, step) in enumerate(places):
+        shard = info[SIDE * at + step]
+        wide = blocks[slot // SIDE][step].astype(jnp.float32)
+        act = (wide * gain[shard]).astype(jnp.bfloat16)
+        span = pl.ds(pl.multiple_of(shard * depth, depth), depth)
+        kv_term = dot_last(act, kv_weight[:, span])
+        term = jnp.sum(wide * wide, axis=1, keepdims=True)
+        copies[slot].wait()
+        q_term = dot32(act, buffer[slot])
+        queries = q_term if queries is None else queries + q_term
+        both = kv_term if both is None else both + kv_term
+        squares = term if squares is None else squares + term
     if before is not None:
         queries, both, squares = queries + before[0][...], both + before[1][...], squares + before[2][...]
     q_total[...] = queries
@@ -383,28 +404,34 @@
     out[1] = both[:, cols:].astype(jnp.bfloat16)
 
 
-def last_queries(info, block, gain, q_weight, q_before, scale, cosine, sine, swap, out):
-    depth = block.shape[2]
+def last_queries(
+    info, block, gain, q_before, scale, cosine, sine, swap, q_weight, out, buffer, sems
+):
+    copies = [shard_rows(info, q_weight, buffer, sems, 3, step, step) for step in range(SIDE)]
+    for copy in copies:
+        copy.start()
     total = q_before[...]
     for step in range(SIDE):
         shard = info[SIDE * 3 + step]
         act = (block[step].astype(jnp.float32) * gain[shard]).astype(jnp.bfloat16)
-        span = pl.ds(pl.multiple_of(shard * depth, depth), depth)
-        total += dot32(act, q_weight[span, :])
+        copies[step].wait()
+        total += dot32(act, buffer[step])
     for head in range(out.shape[1] // HEAD_WIDTH):
         lanes = slice(head * HEAD_WIDTH, (head + 1) * HEAD_WIDTH)
         query = total[:, lanes] * scale[...]
         out[:, lanes] = turn(query, cosine[...], sine[...], swap[...]).astype(jnp.bfloat16)
 
 
-def attend_out(info, query, mine, partner, allowed, weight, out, context, result, out_sems):
-    parts = out_sems.shape[0]
-    step = weight.shape[1] // parts
-
-    def store(part):
+def attend_out(info, query, mine, partner, allowed, deal, weight_hbm, *refs):
+    outs, context, weight, sems = refs[:4], refs[4], refs[5], refs[6]
+    step = weight.shape[1] // sems.shape[0]
+
+    def fetch(part):
         span = pl.ds(part * step, step)
-        return pltpu.make_async_copy(result.at[:, span], out.at[:, span], out_sems.at[part])
-
+        return pltpu.make_async_copy(weight_hbm.at[:, span], weight.at[:, span], sems.at[part])
+
+    for part in range(sems.shape[0]):
+        fetch(part).start()
     odd = info[17] == 1
     own = mine[...].astype(jnp.float32)
     far = partner[...].astype(jnp.float32)
@@ -424,23 +451,41 @@
     ]
     for lanes, prob in zip(heads, masked_softmax(scores, allowed[...] > 0, HEAD_WIDTH)):
         context[:, lanes] = dot32(prob, value).astype(jnp.bfloat16)
-    for part in range(parts):
-        span = slice(part * step, (part + 1) * step)
-        result[:, span] = dot32(context[...], weight[:, span]).astype(jnp.bfloat16)
-        store(part).start()
-    for part in range(parts):
-        store(part).wait()
-
-
-def finish(info, terms, *refs):
+    dealt = dot32(deal[...], context[...]).astype(jnp.bfloat16)
+    rows = outs[0].shape[0]
+    for part in range(sems.shape[0]):
+        start = part * step
+        fetch(part).wait()
+        result = dot32(dealt, weight[:, start : start + step])
+        for index, out in enumerate(outs):
+            piece = result[index * rows : (index + 1) * rows]
+            out[:, start : start + step] = piece.astype(jnp.bfloat16)
+
+
+def add_ring(info, own, left, right, opposite, kept, *sent):
+    rows = kept.shape[0]
+    step = 1024
+    for start in range(0, own.shape[1], step):
+        lanes = slice(start, start + step)
+        total = own[:, lanes].astype(jnp.float32)
+        for block in (left, right, opposite):
+            total = total + block[:, lanes].astype(jnp.float32)
+        kept[:, lanes] = total[:rows]
+        for index, out in enumerate(sent):
+            piece = total[(index + 1) * rows : (index + 2) * rows]
+            out[:, lanes] = piece.astype(jnp.bfloat16)
+
+
+def finish(info, kept, left, right, opposite, *refs):
     own, out = refs[:-1], refs[-1]
     rows, cols = own[0].shape[1:]
     live = info[18] + lax.broadcasted_iota(jnp.int32, (rows, cols), 0) < info[21]
     for at, block in enumerate(own):
         for step in range(SIDE):
             lanes = pl.ds(pl.multiple_of(info[SIDE * at + step] * cols, cols), cols)
-            total = jnp.sum(terms[:, :, lanes].astype(jnp.float32), axis=0)
-            total = total + block[step].astype(jnp.float32)
+            total = kept[:, lanes] + block[step].astype(jnp.float32)
+            for term in (left, right, opposite):
+                total = total + term[:, lanes].astype(jnp.float32)
             out[:, lanes] = jnp.where(live, total, 0.0).astype(jnp.bfloat16)
 
 
@@ -496,6 +541,14 @@
     other_shards = jnp.where(core == 0, by_y, by_x)
     info = jnp.concatenate([shards, scalars, core[None], other_shards]).astype(jnp.int32)
 
+    ahead = jnp.array([0, 1, SIDE - 1, 2])
+    outer, inside = jnp.repeat(ahead, SIDE), jnp.tile(ahead, SIDE)
+    owner_x = SIDE * ((x_index + outer) % SIDE) + (y_index + inside) % SIDE
+    owner_y = SIDE * ((x_index + inside) % SIDE) + (y_index + outer) % SIDE
+    owners = jnp.where(core == 0, owner_x, owner_y)
+    from_row = (owners[:, None] * own_rows + jnp.arange(own_rows)[None, :]).reshape(-1)
+    deal = (from_row[:, None] == jnp.arange(rows)[None, :]).astype(jnp.bfloat16)
+
     requests = jnp.arange(req_slot.shape[0])
     dest_slot = jnp.sum(
         jnp.where(enc_dest[:, None] // SPAN_LIMIT == requests[None, :], req_slot[None, :], 0), axis=1
@@ -527,6 +580,14 @@
     ).astype(jnp.float32)
 
     own_tokens = span_tokens.reshape(spans * span_size, width)
+    other_tokens = to_core(own_tokens)
+    token_pieces = whole_call(
+        both_rows,
+        "both_rows",
+        info,
+        [own_tokens, other_tokens],
+        shape_of((tensor_count, 2 * spans * span_size, share)),
+    )
     units = enc_down.shape[0] // 2
     middle_cols = width // 2 + units * tensor_count
     own_qkv, own_rest = whole_call(
@@ -535,7 +596,7 @@
         info,
         [enc_qkv, enc_out, enc_up, enc_down],
         (shape_of((share, 3 * width // 2)), shape_of((share, middle_cols + width))),
-        limit=4,
+        limit=60,
     )
     rest_ring = short_relay(own_rest)
     qkv_block = whole_call(
@@ -547,37 +608,9 @@
         limit=6,
         after=rest_ring[1:3],
     )
-    middle_block, lower_block = whole_call(
-        join_rest,
-        "join_rest",
-        info,
-        rest_ring,
-        (shape_of((SIDE, share, middle_cols)), shape_of((SIDE, share, width))),
-        limit=8,
-    )
-    other_tokens = to_core(own_tokens)
-    token_pieces = whole_call(
-        both_rows,
-        "both_rows",
-        info,
-        [own_tokens, other_tokens],
-        shape_of((tensor_count, 2 * spans * span_size, share)),
-    )
     all_rows = 2 * spans * span_size
 
-    def ring(block, relay):
-        left = to_ring(block, 2, 1)
-        right = to_ring(block, 2, -1)
-        opposite = to_ring(left, 2, 1) if relay == 1 else to_ring(right, 2, -1)
-        return [block, left, right, opposite]
-
-    qkv = ring(qkv_block, 1)
-    middle_down, _ = lax.optimization_barrier((middle_block, qkv[2]))
-    middle_up, _ = lax.optimization_barrier((middle_block, qkv[3]))
-    right = to_ring(middle_down, 2, -1)
-    middle = [middle_block, to_ring(middle_up, 2, 1), right, to_ring(right, 2, -1)]
-    lower_block, _ = lax.optimization_barrier((lower_block, right))
-    lower = ring(lower_block, 1)
+    qkv = [qkv_block] + [to_ring(qkv_block, 2, distance) for distance in (1, -1, 2)]
 
     share_cols = model_width // tensor_count
     dealt_shape = (SIDE, proj_out.shape[0], share_cols // 2)
@@ -588,11 +621,12 @@
         [proj_out],
         (shape_of(dealt_shape),) * 4,
         limit=8,
-        after=[qkv[1]],
+        after=[qkv_block],
     )
     dealt = [dealt[0]] + [
         to_ring(part, 1, distance) for part, distance in zip(dealt[1:], (1, -1, 2))
     ]
+
     dealt = whole_call(
         deal_again, "deal_again", info, dealt, (shape_of(dealt_shape),) * 4, limit=8
     )
@@ -603,21 +637,51 @@
         join_blocks, "join_proj", info, dealt, shape_of((SIDE,) + dealt_shape), limit=8
     )
     proj_other = to_core(proj_mine)
+
+    mixed, mark = whole_call(
+        span_qkv,
+        "span_qkv",
+        info,
+        [token_pieces, *qkv],
+        (shape_of((all_rows, 3 * width // 2)), shape_of((8, 128), jnp.float32)),
+        flops=2 * all_rows * width * 3 * width // 2,
+        after=[proj_mine, *rest_ring],
+    )
+    middle_block = whole_call(
+        join_middle,
+        "join_middle",
+        info,
+        rest_ring,
+        shape_of((SIDE, share, middle_cols)),
+        limit=8,
+        after=[mark],
+    )
+    right = to_ring(middle_block, 2, -1)
+    middle = [middle_block, to_ring(middle_block, 2, 1), right, to_ring(right, 2, -1)]
+    lower_block = whole_call(
+        join_lower,
+        "join_lower",
+        info,
+        rest_ring,
+        shape_of((SIDE, share, width)),
+        limit=8,
+        after=[right],
+    )
+    left = to_ring(lower_block, 2, 1)
+    lower = [lower_block, left, to_ring(lower_block, 2, -1), to_ring(left, 2, 1)]
 
     context = whole_call(
         span_attention,
         "span_attention",
         info,
-        [token_pieces, *qkv],
+        [mixed],
         shape_of((tensor_count // 2, all_rows, share)),
-        [pltpu.VMEM((all_rows, 3 * width // 2), jnp.bfloat16)],
-        flops=2 * all_rows * width * 3 * width // 2,
     )
     attended = whole_call(
         context_out,
         "context_out",
         info,
-        [context, to_core(context), *middle],
+        [context, to_core(context), token_pieces, *middle],
         shape_of((all_rows, width // 2)),
         [pltpu.VMEM((tensor_count, all_rows, share), jnp.bfloat16)],
         flops=2 * all_rows * width * width // 2,
@@ -626,12 +690,9 @@
         norm_up,
         "norm_up",
         info,
-        [own_tokens, other_tokens, attended, to_core(attended), *middle],
+        [attended, to_core(attended), *middle],
         (shape_of((all_rows, width)), shape_of((tensor_count, all_rows, units))),
-        [
-            pltpu.VMEM((tensor_count, all_rows, share), jnp.bfloat16),
-            pltpu.VMEM((all_rows, width), jnp.bfloat16),
-        ],
+        [pltpu.VMEM((tensor_count, all_rows, share), jnp.bfloat16)],
         flops=2 * all_rows * width * width,
     )
     kept, sent = whole_call(
@@ -678,14 +739,13 @@
         shape_of((SIDE, rows, share_cols)),
         limit=4,
     )
-    embedded = ring(first_block, 1)
-
+    near_left = to_ring(first_block, 2, 1)
+    near_right = to_ring(first_block, 2, -1)
     query_cols = q_weight.shape[1]
     kv_cols = key_value_weight.shape[2]
     key_start = tensor_index * kv_cols % HEAD_WIDTH
     key_cosine = lax.dynamic_slice_in_dim(cosine, key_start, kv_cols, 1)
     key_sine = lax.dynamic_slice_in_dim(sine, key_start, kv_cols, 1)
-    parts = 8
     gain = norm_gain.reshape(tensor_count, 1, share_cols)
     kv_pair = key_value_weight.transpose(0, 2, 1).reshape(2 * kv_cols, model_width)
     sums = (
@@ -698,16 +758,30 @@
         functools.partial(project, starts=(0,), count=1),
         "project_own",
         info,
-        [embedded[0], gain, q_weight, kv_pair],
+        [first_block, gain, kv_pair],
         sums,
+        [
+            pltpu.VMEM((SIDE, share_cols, query_cols), jnp.bfloat16),
+            pltpu.SemaphoreType.DMA((SIDE,)),
+        ],
+        limit=56,
+        far=[q_weight],
         flops=block_flops,
     )
+    relayed, _ = lax.optimization_barrier((near_left, totals[2]))
+    embedded = [first_block, relayed, near_right, to_ring(relayed, 2, 1)]
     totals = whole_call(
         functools.partial(project, starts=(1, 2), count=2),
         "project_near",
         info,
-        [embedded[1], embedded[2], gain, q_weight, kv_pair, *totals],
+        [embedded[1], embedded[2], gain, kv_pair, *totals],
         sums,
+        [
+            pltpu.VMEM((2 * SIDE, share_cols, query_cols), jnp.bfloat16),
+            pltpu.SemaphoreType.DMA((2 * SIDE,)),
+        ],
+        limit=56,
+        far=[q_weight],
         flops=2 * block_flops,
     )
     own_kv, scale = whole_call(
@@ -733,31 +807,52 @@
         last_queries,
         "last_queries",
         info,
-        [embedded[3], gain, q_weight, totals[0], scale, cosine, sine, swap],
+        [embedded[3], gain, totals[0], scale, cosine, sine, swap],
         shape_of((rows, query_cols)),
+        [
+            pltpu.VMEM((SIDE, share_cols, query_cols), jnp.bfloat16),
+            pltpu.SemaphoreType.DMA((SIDE,)),
+        ],
+        limit=56,
+        far=[q_weight],
         flops=block_flops,
     )
-    partial = pl.pallas_call(
+    partial = whole_call(
         attend_out,
-        name="attend_out",
-        out_shape=shape_of((rows, model_width)),
-        in_specs=[SMEM, VMEM, VMEM, VMEM, VMEM, VMEM],
-        out_specs=pl.BlockSpec(memory_space=pltpu.HBM),
-        scratch_shapes=[
+        "attend_out",
+        info,
+        [query, own_kv, partner_kv, allowed, deal],
+        (shape_of((rows // SIDE, model_width)),) * 4,
+        [
             pltpu.VMEM((rows, query_cols), jnp.bfloat16),
-            pltpu.VMEM((rows, model_width), jnp.bfloat16),
-            pltpu.SemaphoreType.DMA((parts,)),
+            pltpu.VMEM((query_cols, model_width), jnp.bfloat16),
+            pltpu.SemaphoreType.DMA((8,)),
         ],
-        compiler_params=pltpu.CompilerParams(vmem_limit_bytes=16 * MIB),
-    )(info, query, own_kv, partner_kv, allowed, out_weight)
-    terms = lax.all_to_all(
-        partial.reshape(tensor_count, own_rows, model_width), "tensor", 0, 0
-    )
+        limit=56,
+        far=[out_weight],
+        flops=2 * rows * model_width * query_cols,
+    )
+    arrived_sums = [
+        to_ring(part, 2, distance) for part, distance in zip(partial[1:], (1, -1, 2))
+    ]
+    kept_sum, *sent_sums = whole_call(
+        add_ring,
+        "add_ring",
+        info,
+        [partial[0], *arrived_sums],
+        (shape_of((own_rows, model_width), jnp.float32),)
+        + (shape_of((own_rows, model_width)),) * 3,
+    )
+    terms = [to_ring(part, 1, distance) for part, distance in zip(sent_sums, (1, -1, 2))]
     own_embedded = [
         lax.dynamic_slice_in_dim(block, tensor_index * own_rows, own_rows, 1) for block in embedded
     ]
     return whole_call(
-        finish, "finish", live_info, [terms, *own_embedded], shape_of((own_rows, model_width))
+        finish,
+        "finish",
+        live_info,
+        [kept_sum, *terms, *own_embedded],
+        shape_of((own_rows, model_width)),
     )
 
 

time: 202 us -> 217 us (1.074)
  Pallas kernels: 32 us -> 45.5 us
  starting transfers between devices: 53.1 us -> 57.7 us
  waiting for transfers between devices: 85.5 us -> 82.4 us
    all_to_all x1 -> x0, waiting for transfers between devices: 24.8 us -> none  [local(): lax.all_to_all(partial.reshape(tensor_count, own_rows, model_width), 'ten...]
    ppermute x27 -> x33, waiting for transfers between devices: 46.2 us -> 69.2 us  [to_ring(): return lax.ppermute(value, AXES, ring_pairs(phase, distance))]
    pallas_call x19 -> x23, Pallas kernels: 28.1 us -> 45.5 us  [whole_call(): pl.pallas_call(run, name=name, out_shape=outs, in_specs=[SMEM] + [VMEM] *...]
    ppermute x27 -> x33, starting transfers between devices: 37.8 us -> 48 us  [to_ring(): return lax.ppermute(value, AXES, ring_pairs(phase, distance))]
    all_to_all x1 -> x0, starting transfers between devices: 5.14 us -> none  [local(): lax.all_to_all(partial.reshape(tensor_count, own_rows, model_width), 'ten...]
    pallas_call x1 -> x0, Pallas kernels: 3.88 us -> none  [local(): pl.pallas_call(attend_out, name='attend_out', out_shape=shape_of((rows, m...]
    ppermute x1, waiting for transfers between devices: 2.81 us -> 0.01 us  [local(): lax.ppermute(own_kv, 'tensor', [(index, index ^ 1) for index in range(ten...]
    unnamed x56 -> x80, local copies, waits for them, and re-layouts: 17.7 us -> 17.5 us
  transfers between devices with their start and end apart: 35 -> 40, of which waited for: 18 -> 24; matrix products, arithmetic and copies ran while one was open for 5% -> 4% of each run, Pallas kernels for 10% -> 12%
where the time goes in v4:
time: 217 us; the launch traced here: 215 us
  waiting for transfers between devices  82.4 us (38%)
  starting transfers between devices  57.7 us (27%)
  Pallas kernels  45.5 us (21%)
  local copies, waits for them, and re-layouts  22.9 us (11%)
  other arithmetic  5.52 us (3%)
    ppermute x33, waiting for transfers between devices, to_ring(): return lax.ppermute(value, AXES, ring_pairs(phase, distance))  69.2 us
    ppermute x33, starting transfers between devices, to_ring(): return lax.ppermute(value, AXES, ring_pairs(phase, distance))  48 us
    pallas_call x23, Pallas kernels, whole_call(): pl.pallas_call(run, name=name, out_shape=outs, in_specs=[SMEM] + [VMEM] *...  45.5 us
    unnamed x80, local copies, waits for them, and re-layouts  17.5 us
    all_to_all x1, waiting for transfers between devices, local(): lax.all_to_all(outgoing.reshape(device_count, width // 128, 128), AXES, 0...  10.8 us
    all_to_all x1, starting transfers between devices, local(): lax.all_to_all(outgoing.reshape(device_count, width // 128, 128), AXES, 0...  8.96 us
  transfers between devices with their start and end apart: 40, of which 24 were waited for; matrix products, arithmetic and copies ran while one was open for 4% of the time, Pallas kernels for 12%

profile of v4, /device:TPU:0, one launch (start us, length us, event | category | flops | bytes accessed | tf_op | source)
XLA Modules:
  0.0 215.5 jit_solution(13757879531940525880)
XLA Ops:
  1.9 2.3 %take_halves.1 = (bf16[64,1536]{1,0:T(8,128)(2,1)}, bf16[64,2560]{1,0:T(8,128)(2,1)}) custom-call(s32[38]{0:T(128)} %concatenate.9.refs_0_, bf16[64,3072]{1,0:T(8,128)(2,1)} %refs_1_.2, bf16[64,1024]{1,0:T(8,128)(2,1)} %refs_2_.1, bf16[64,2048]{1,0:T(8,128)(2,1)} %refs_3_.2, bf16[128,1024]{1,0:T(8,128)(2,1)} %refs_4_.2), custom_call_target="tpu_custom_call" | custom-call | bytes 1048576 | tf_op jit(solution)/shard_map/take_halves/pallas_call | solution.py:101
  4.1 1.7 collective-permute-start.4
  5.8 1.6 collective-permute-start.5
  7.8 2.8 %collective-permute-start.2 = (bf16[64,1536]{1,0:T(8,128)(2,1)}, bf16[64,1536]{1,0:T(8,128)(2,1)S(1)}, u32[]{:S(2)}, u32[]{:S(2)}) collective-permute-start(bf16[64,1536]{1,0:T(8,128)(2,1)} %get-tuple-element.38.refs_1_), channel_id=1, source_target_pairs={{0,3},{1,0},{2,1},{3,2},{4,7},{5,4},{6,5},{7,6},{8,11},{9,8},{10,9... | collective-permute-start | bytes 589832 | tf_op jit(solution)/shard_map/ppermute | solution.py:67
  11.5 3.3 %collective-permute-done.1.refs_2_ = bf16[64,1536]{1,0:T(8,128)(2,1)S(1)} collective-permute-done((bf16[64,1536]{1,0:T(8,128)(2,1)}, bf16[64,1536]{1,0:T(8,128)(2,1)S(1)}, u32[]{:S(2)}, u32[]{:S(2)}) %collective-permute-start.1) | collective-permute-done | bytes 196640 | tf_op jit(solution)/shard_map/ppermute | solution.py:67
  15.2 3.0 %collective-permute-done.3.refs_4_ = bf16[64,1536]{1,0:T(8,128)(2,1)S(1)} collective-permute-done((bf16[64,1536]{1,0:T(8,128)(2,1)}, bf16[64,1536]{1,0:T(8,128)(2,1)S(1)}, u32[]{:S(2)}, u32[]{:S(2)}) %collective-permute-start.3) | collective-permute-done | bytes 196640 | tf_op jit(solution)/shard_map/ppermute | solution.py:67
  20.3 1.6 collective-permute-start.6
  21.9 1.7 collective-permute-start.7
  23.6 1.8 collective-permute-start.8
  25.4 1.2 copy-done.15
  27.9 1.5 collective-permute-start.9
  29.4 1.8 collective-permute-start.10
  31.2 4.6 %collective-permute-done.9.refs_2_ = bf16[4,64,256]{2,1,0:T(8,128)(2,1)S(1)} collective-permute-done((bf16[4,64,256]{2,1,0:T(8,128)(2,1)S(1)}, bf16[4,64,256]{2,1,0:T(8,128)(2,1)S(1)}, u32[]{:S(2)}, u32[]{:S(2)}) %collective-permute-start.9) | collective-permute-done | bytes 131104 | tf_op jit(solution)/shard_map/ppermute | solution.py:67
  35.8 4.8 %collective-permute-done.10.refs_3_ = bf16[4,64,256]{2,1,0:T(8,128)(2,1)S(1)} collective-permute-done((bf16[4,64,256]{2,1,0:T(8,128)(2,1)S(1)}, bf16[4,64,256]{2,1,0:T(8,128)(2,1)S(1)}, u32[]{:S(2)}, u32[]{:S(2)}) %collective-permute-start.10) | collective-permute-done | bytes 131104 | tf_op jit(solution)/shard_map/ppermute | solution.py:67
  40.6 2.3 %collective-permute-start.11 = (bf16[4,64,256]{2,1,0:T(8,128)(2,1)S(1)}, bf16[4,64,256]{2,1,0:T(8,128)(2,1)S(1)}, u32[]{:S(2)}, u32[]{:S(2)}) collective-permute-start(bf16[4,64,256]{2,1,0:T(8,128)(2,1)S(1)} %get-tuple-element.43), channel_id=1, source_target_pairs={{0,2},{1,3},{2,0},{3,1},{4,6},{5,7},{6,4},{7,5},{8,10},{9,11},{10,... | collective-permute-start | bytes 393224 | tf_op jit(solution)/shard_map/ppermute | solution.py:67
  42.9 4.2 %collective-permute-done.11.refs_4_ = bf16[4,64,256]{2,1,0:T(8,128)(2,1)S(1)} collective-permute-done((bf16[4,64,256]{2,1,0:T(8,128)(2,1)S(1)}, bf16[4,64,256]{2,1,0:T(8,128)(2,1)S(1)}, u32[]{:S(2)}, u32[]{:S(2)}) %collective-permute-start.11) | collective-permute-done | bytes 131104 | tf_op jit(solution)/shard_map/ppermute | solution.py:67
  47.7 1.3 collective-permute-start.12
  48.9 3.6 %collective-permute-start.15 = (bf16[64,2560]{1,0:T(8,128)(2,1)S(1)}, bf16[64,2560]{1,0:T(8,128)(2,1)S(1)}, u32[]{:S(2)}, u32[]{:S(2)}) collective-permute-start(bf16[64,2560]{1,0:T(8,128)(2,1)S(1)} %collective-permute-done.5.refs_6_.refs_9_.refs_3_), channel_id=1, source_target_pairs={{0,3},{1,0},{2,1},{3,2},{4,7},{5,4},{6,5},{7,6},{8,11},{9,8},{10,9... | collective-permute-start | bytes 983048 | tf_op jit(solution)/shard_map/ppermute | solution.py:67
  52.5 1.4 collective-permute-done.12.refs_2_
  54.8 4.1 %collective-permute-done.13.refs_3_ = bf16[4,64,256]{2,1,0:T(8,128)(2,1)S(1)} collective-permute-done((bf16[4,64,256]{2,1,0:T(8,128)(2,1)S(1)}, bf16[4,64,256]{2,1,0:T(8,128)(2,1)S(1)}, u32[]{:S(2)}, u32[]{:S(2)}) %collective-permute-start.13) | collective-permute-done | bytes 131104 | tf_op jit(solution)/shard_map/ppermute | solution.py:67
  62.2 3.1 %collective-permute-done.14.refs_4_ = bf16[4,64,256]{2,1,0:T(8,128)(2,1)S(1)} collective-permute-done((bf16[4,64,256]{2,1,0:T(8,128)(2,1)S(1)}, bf16[4,64,256]{2,1,0:T(8,128)(2,1)S(1)}, u32[]{:S(2)}, u32[]{:S(2)}) %collective-permute-start.14) | collective-permute-done | bytes 131104 | tf_op jit(solution)/shard_map/ppermute | solution.py:67
  66.0 1.2 copy-done.7
  67.2 1.6 span_qkv.1
  69.7 2.1 collective-permute-start.18
  73.2 8.5 %collective-permute-done.18.refs_6_.refs_5_ = bf16[4,64,1536]{2,1,0:T(8,128)(2,1)S(1)} collective-permute-done((bf16[4,64,1536]{2,1,0:T(8,128)(2,1)S(1)}, bf16[4,64,1536]{2,1,0:T(8,128)(2,1)S(1)}, u32[]{:S(2)}, u32[]{:S(2)}) %collective-permute-start.18) | collective-permute-done | bytes 786464 | tf_op jit(solution)/shard_map/ppermute | solution.py:67
  81.7 3.3 %collective-permute-start.19 = (bf16[4,64,1536]{2,1,0:T(8,128)(2,1)S(1)}, bf16[4,64,1536]{2,1,0:T(8,128)(2,1)S(1)}, u32[]{:S(2)}, u32[]{:S(2)}) collective-permute-start(bf16[4,64,1536]{2,1,0:T(8,128)(2,1)S(1)} %collective-permute-done.18.refs_6_.refs_5_), channel_id=1, source_target_pairs={{0,12},{1,13},{2,14},{3,15},{4,0},{5,1},{6,2},{7,3},{8,4},{9,5},{1... | collective-permute-start | bytes 2359304 | tf_op jit(solution)/shard_map/ppermute | solution.py:67
  87.6 1.4 join_lower.1.refs_3_
  89.1 1.2 copy-done.17
  90.3 2.0 span_attention.1.refs_1_
  92.4 3.3 %collective-permute-start.22 = (bf16[4,64,1024]{2,1,0:T(8,128)(2,1)}, bf16[4,64,1024]{2,1,0:T(8,128)(2,1)}, u32[]{:S(2)}, u32[]{:S(2)}) collective-permute-start(bf16[4,64,1024]{2,1,0:T(8,128)(2,1)} %join_lower.1.refs_3_), channel_id=1, source_target_pairs={{0,12},{1,13},{2,14},{3,15},{4,0},{5,1},{6,2},{7,3},{8,4},{9,5},{1... | collective-permute-start | bytes 1572872 | tf_op jit(solution)/shard_map/ppermute | solution.py:67
  95.6 4.1 %collective-permute-done.21.refs_4_ = bf16[4,64,1024]{2,1,0:T(8,128)(2,1)} collective-permute-done((bf16[4,64,1024]{2,1,0:T(8,128)(2,1)}, bf16[4,64,1024]{2,1,0:T(8,128)(2,1)}, u32[]{:S(2)}, u32[]{:S(2)}) %collective-permute-start.21) | collective-permute-done | bytes 524320 | tf_op jit(solution)/shard_map/ppermute | solution.py:67
  99.9 1.3 context_out.1.refs_1_
  101.4 1.4 collective-permute-done.20.refs_2_
  102.8 1.1 copy-done.4
  103.9 1.1 copy-done.6
  105.0 2.3 %norm_up.1 = (bf16[256,1024]{1,0:T(8,128)(2,1)S(1)}, bf16[16,256,64]{2,1,0:T(8,128)(2,1)S(1)}) custom-call(s32[38]{0:T(128)S(1)} %copy-done.23, bf16[256,512]{1,0:T(8,128)(2,1)S(1)} %context_out.1.refs_1_, bf16[256,512]{1,0:T(8,128)(2,1)S(1)} %collective-permute-done.20.refs_2_, bf16[4,64,1536]{2,1,0:T(8,128)(2,1)S(1)} %join_middle.1.refs_4_.refs_3_, ...), custom_call_target="tpu_custom_call" | custom-call | flops 536870912 | bytes 3670016 | tf_op jit(solution)/shard_map/norm_up/pallas_call | solution.py:101
  107.4 3.0 %collective-permute-done.23.refs_6_ = bf16[4,64,1024]{2,1,0:T(8,128)(2,1)} collective-permute-done((bf16[4,64,1024]{2,1,0:T(8,128)(2,1)}, bf16[4,64,1024]{2,1,0:T(8,128)(2,1)}, u32[]{:S(2)}, u32[]{:S(2)}) %collective-permute-start.23) | collective-permute-done | bytes 524320 | tf_op jit(solution)/shard_map/ppermute | solution.py:67
  110.4 2.3 %down.1 = (f32[128,1024]{1,0:T(8,128)S(1)}, bf16[128,1024]{1,0:T(8,128)(2,1)S(1)}) custom-call(s32[38]{0:T(128)S(1)} %copy-done.23, bf16[16,256,64]{2,1,0:T(8,128)(2,1)S(1)} %get-tuple-element.50.refs_1_, bf16[256,1024]{1,0:T(8,128)(2,1)S(1)} %get-tuple-element.51.refs_2_, bf16[4,64,1024]{2,1,0:T(8,128)(2,1)} %join_lower.1.refs_3_, ...), custom_call_target="tpu_custom_call" | custom-call | flops 536870912 | bytes 3145728 | tf_op jit(solution)/shard_map/down/pallas_call | solution.py:101
  114.4 1.7 norm_pool.1
  116.1 9.0 %all-to-all-start = ((bf16[128,8,128]{2,1,0:T(8,128)(2,1)}), bf16[128,8,128]{2,1,0:T(8,128)(2,1)S(1)}, u32[]{:S(2)}, u32[]{:S(2)}) async-start(bf16[128,8,128]{2,1,0:T(8,128)(2,1)} %bitcast.8), calls=%async_computation | async-start | bytes 524288 | tf_op jit(solution)/shard_map/all_to_all | solution.py:718
  125.1 10.8 %all-to-all-done.refs_1_ = bf16[128,8,128]{2,1,0:T(8,128)(2,1)S(1)} async-done(((bf16[128,8,128]{2,1,0:T(8,128)(2,1)}), bf16[128,8,128]{2,1,0:T(8,128)(2,1)S(1)}, u32[]{:S(2)}, u32[]{:S(2)}) %all-to-all-start) | async-done | bytes 262176 | tf_op jit(solution)/shard_map/all_to_all | solution.py:718
  135.9 1.6 copy-done.14
  137.5 2.1 embed.1.refs_1_
  140.3 2.6 %collective-permute-start.27 = (bf16[128,512]{1,0:T(8,128)(2,1)S(1)}, bf16[128,512]{1,0:T(8,128)(2,1)S(1)}, u32[]{:S(2)}, u32[]{:S(2)}) collective-permute-start(bf16[128,512]{1,0:T(8,128)(2,1)S(1)} %embed.1.refs_1_), channel_id=1, source_target_pairs={{0,3},{1,0},{2,1},{3,2},{4,7},{5,4},{6,5},{7,6},{8,11},{9,8},{10,9... | collective-permute-start | bytes 393224 | tf_op jit(solution)/shard_map/ppermute | solution.py:67
  142.9 1.3 select_reduce_fusion.3
  144.2 1.7 collective-permute-done.26.refs_2_
  145.8 1.0 collective-permute-done.27.refs_3_
  146.8 2.5 %collective-permute-done.28.refs_4_ = bf16[128,512]{1,0:T(8,128)(2,1)S(1)} collective-permute-done((bf16[128,512]{1,0:T(8,128)(2,1)S(1)}, bf16[128,512]{1,0:T(8,128)(2,1)S(1)}, u32[]{:S(2)}, u32[]{:S(2)}) %collective-permute-start.28) | collective-permute-done | bytes 131104 | tf_op jit(solution)/shard_map/ppermute | solution.py:67
  151.0 2.7 %collective-permute-start.31 = (bf16[4,128,512]{2,1,0:T(8,128)(2,1)S(1)}, bf16[4,128,512]{2,1,0:T(8,128)(2,1)}, u32[]{:S(2)}, u32[]{:S(2)}) collective-permute-start(bf16[4,128,512]{2,1,0:T(8,128)(2,1)S(1)} %join_columns.1.refs_1_), channel_id=1, source_target_pairs={{0,12},{1,13},{2,14},{3,15},{4,0},{5,1},{6,2},{7,3},{8,4},{9,5},{1... | collective-permute-start | bytes 1572872 | tf_op jit(solution)/shard_map/ppermute | solution.py:67
  153.8 4.7 %project_own.1 = (f32[128,512]{1,0:T(8,128)}, f32[128,128]{1,0:T(8,128)}, f32[128,1]{1,0:T(8,128)}) custom-call(s32[38]{0:T(128)} %concatenate.9.refs_0_, bf16[4,128,512]{2,1,0:T(8,128)(2,1)} %copy-done.13, f32[16,1,512]{2,1,0:T(1,128)} %bitcast.20, bf16[128,8192]{1,0:T(8,128)(2,1)} %bitcast.17, bf16[8192,512]{1,0:T(8,128)(2,1)} %refs_8_.3), custom_call_target="tpu_custom_call" | custom-call | flops 335544320 | bytes 2654208 | tf_op jit(solution)/shard_map/project_own/pallas_call | solution.py:101
  158.5 2.0 collective-permute-done.29.refs_1_
  162.5 6.0 %project_near.1 = (f32[128,512]{1,0:T(8,128)}, f32[128,128]{1,0:T(8,128)}, f32[128,1]{1,0:T(8,128)}) custom-call(s32[38]{0:T(128)} %concatenate.9.refs_0_, bf16[4,128,512]{2,1,0:T(8,128)(2,1)} %collective-permute-done.29.refs_1_, bf16[4,128,512]{2,1,0:T(8,128)(2,1)} %collective-permute-done.31.refs_2_, f32[16,1,512]{2,1,0:T(1,128)} %bitcast.21, ...), custom_call_target="tpu_custom_call" | custom-call | flops 671088640 | bytes 3506688 | tf_op jit(solution)/shard_map/project_near/pallas_call | solution.py:101
  168.6 2.6 %collective-permute-done.30.refs_1_ = bf16[4,128,512]{2,1,0:T(8,128)(2,1)S(1)} collective-permute-done((bf16[4,128,512]{2,1,0:T(8,128)(2,1)}, bf16[4,128,512]{2,1,0:T(8,128)(2,1)S(1)}, u32[]{:S(2)}, u32[]{:S(2)}) %collective-permute-start.30) | collective-permute-done | bytes 524320 | tf_op jit(solution)/shard_map/ppermute | solution.py:67
  172.9 1.2 last_keys.1
  175.4 4.0 %last_queries.1.refs_1_ = bf16[128,512]{1,0:T(8,128)(2,1)} custom-call(s32[38]{0:T(128)} %concatenate.9.refs_0_, bf16[4,128,512]{2,1,0:T(8,128)(2,1)} %copy-done.12, f32[16,1,512]{2,1,0:T(1,128)} %bitcast.22, f32[128,512]{1,0:T(8,128)} %get-tuple-element.58.refs_3_, f32[128,1]{1,0:T(8,128)} %copy-done.29, f32[128,128]{1,0:T(8,128)} %copy-done.33, ...), custom_call_target="tpu_custom_call" | custom-call | flops 335544320 | bytes 1016320 | tf_op jit(solution)/shard_map/last_queries/pallas_call | solution.py:101
  180.0 6.2 %attend_out.1 = (bf16[32,8192]{1,0:T(8,128)(2,1)}, bf16[32,8192]{1,0:T(8,128)(2,1)}, bf16[32,8192]{1,0:T(8,128)(2,1)}, bf16[32,8192]{1,0:T(8,128)(2,1)}) custom-call(s32[38]{0:T(128)} %concatenate.9.refs_0_, bf16[128,512]{1,0:T(8,128)(2,1)} %last_queries.1.refs_1_, bf16[2,128,64]{2,1,0:T(8,128)(2,1)} %copy-done.28, bf16[2,128,64]{2,1,0:T(8,128)(2,1)} %copy-done.35, ...), custom_call_target="tpu_custom_call" | custom-call | flops 1073741824 | bytes 294912 | tf_op jit(solution)/shard_map/attend_out/pallas_call | solution.py:101
  186.4 3.2 %collective-permute-start.34 = (bf16[32,8192]{1,0:T(8,128)(2,1)}, bf16[32,8192]{1,0:T(8,128)(2,1)S(1)}, u32[]{:S(2)}, u32[]{:S(2)}) collective-permute-start(bf16[32,8192]{1,0:T(8,128)(2,1)} %get-tuple-element.65), channel_id=1, source_target_pairs={{0,12},{1,13},{2,14},{3,15},{4,0},{5,1},{6,2},{7,3},{8,4},{9,5},{1... | collective-permute-start | bytes 1572872 | tf_op jit(solution)/shard_map/ppermute | solution.py:67
  191.2 11.4 %collective-permute-done.33.refs_2_ = bf16[32,8192]{1,0:T(8,128)(2,1)S(1)} collective-permute-done((bf16[32,8192]{1,0:T(8,128)(2,1)}, bf16[32,8192]{1,0:T(8,128)(2,1)S(1)}, u32[]{:S(2)}, u32[]{:S(2)}) %collective-permute-start.33) | collective-permute-done | bytes 524320 | tf_op jit(solution)/shard_map/ppermute | solution.py:67
  202.6 1.0 copy-done.19
  204.4 2.1 collective-permute-start.36
  206.5 1.2 collective-permute-start.37
  207.7 1.4 collective-permute-start.38
  211.5 2.7 %collective-permute-done.38.refs_4_ = bf16[8,8192]{1,0:T(8,128)(2,1)S(1)} collective-permute-done((bf16[8,8192]{1,0:T(8,128)(2,1)S(1)}, bf16[8,8192]{1,0:T(8,128)(2,1)S(1)}, u32[]{:S(2)}, u32[]{:S(2)}) %collective-permute-start.38) | collective-permute-done | bytes 131104 | tf_op jit(solution)/shard_map/ppermute | solution.py:67
  214.2 1.3 finish.1
  (177 shorter events, 31.6 us)
Async XLA Ops:
  0.0 71.8 %copy-start.37 = (s32[1024]{0:T(1024)S(1)}, s32[1024]{0:T(1024)}, u32[]{:S(2)}) copy-start(s32[1024]{0:T(1024)} %param.18) | copy-start | bytes 12292
  0.0 71.8 %copy-start.38 = (s32[8]{0:T(128)S(1)}, s32[8]{0:T(128)}, u32[]{:S(2)}) copy-start(s32[8]{0:T(128)} %param.20) | copy-start | bytes 100
  1.9 83.8 %copy-start.23 = (s32[38]{0:T(128)S(1)}, s32[38]{0:T(128)}, u32[]{:S(2)}) copy-start(s32[38]{0:T(128)} %concatenate.9.refs_0_) | copy-start | bytes 460
  4.1 64.7 %copy-start.8 = (bf16[64,2560]{1,0:T(8,128)(2,1)S(1)}, bf16[64,2560]{1,0:T(8,128)(2,1)}, u32[]{:S(2)}) copy-start(bf16[64,2560]{1,0:T(8,128)(2,1)} %get-tuple-element.39.refs_7_.refs_1_) | copy-start | bytes 983044
  4.1 14.0 %collective-permute-start.4 = (bf16[64,2560]{1,0:T(8,128)(2,1)}, bf16[64,2560]{1,0:T(8,128)(2,1)S(1)}, u32[]{:S(2)}, u32[]{:S(2)}) collective-permute-start(bf16[64,2560]{1,0:T(8,128)(2,1)} %get-tuple-element.39.refs_7_.refs_1_), channel_id=1, source_target_pairs={{0,1},{1,2},{2,3},{3,0},{4,5},{5,6},{6,7},{7,4},{8,9},{9,10},{10,1... | collective-permute-start | bytes 983048 | tf_op jit(solution)/shard_map/ppermute | solution.py:67
  5.8 12.4 %collective-permute-start.5 = (bf16[64,2560]{1,0:T(8,128)(2,1)}, bf16[64,2560]{1,0:T(8,128)(2,1)S(1)}, u32[]{:S(2)}, u32[]{:S(2)}) collective-permute-start(bf16[64,2560]{1,0:T(8,128)(2,1)} %get-tuple-element.39.refs_7_.refs_1_), channel_id=1, source_target_pairs={{0,3},{1,0},{2,1},{3,2},{4,7},{5,4},{6,5},{7,6},{8,11},{9,8},{10,9... | collective-permute-start | bytes 983048 | tf_op jit(solution)/shard_map/ppermute | solution.py:67
  7.4 7.4 %collective-permute-start.1 = (bf16[64,1536]{1,0:T(8,128)(2,1)}, bf16[64,1536]{1,0:T(8,128)(2,1)S(1)}, u32[]{:S(2)}, u32[]{:S(2)}) collective-permute-start(bf16[64,1536]{1,0:T(8,128)(2,1)} %get-tuple-element.38.refs_1_), channel_id=1, source_target_pairs={{0,1},{1,2},{2,3},{3,0},{4,5},{5,6},{6,7},{7,4},{8,9},{9,10},{10,1... | collective-permute-start | bytes 589832 | tf_op jit(solution)/shard_map/ppermute | solution.py:67
  7.8 7.4 %collective-permute-start.2 = (bf16[64,1536]{1,0:T(8,128)(2,1)}, bf16[64,1536]{1,0:T(8,128)(2,1)S(1)}, u32[]{:S(2)}, u32[]{:S(2)}) collective-permute-start(bf16[64,1536]{1,0:T(8,128)(2,1)} %get-tuple-element.38.refs_1_), channel_id=1, source_target_pairs={{0,3},{1,0},{2,1},{3,2},{4,7},{5,4},{6,5},{7,6},{8,11},{9,8},{10,9... | collective-permute-start | bytes 589832 | tf_op jit(solution)/shard_map/ppermute | solution.py:67
  10.6 7.6 %collective-permute-start.3 = (bf16[64,1536]{1,0:T(8,128)(2,1)}, bf16[64,1536]{1,0:T(8,128)(2,1)S(1)}, u32[]{:S(2)}, u32[]{:S(2)}) collective-permute-start(bf16[64,1536]{1,0:T(8,128)(2,1)} %get-tuple-element.38.refs_1_), channel_id=1, source_target_pairs={{0,2},{1,3},{2,0},{3,1},{4,6},{5,7},{6,4},{7,5},{8,10},{9,11},{10,... | collective-permute-start | bytes 589832 | tf_op jit(solution)/shard_map/ppermute | solution.py:67
  19.7 69.3 %copy-start.36 = (s32[8,8,8]{2,1,0:T(8,128)S(1)}, s32[8,8,8]{2,1,0:T(8,128)}, u32[]{:S(2)}) copy-start(s32[8,8,8]{2,1,0:T(8,128)} %param.21) | copy-start | bytes 6148
  20.3 45.7 %collective-permute-start.6 = (bf16[4,64,1536]{2,1,0:T(8,128)(2,1)S(1)}, bf16[4,64,1536]{2,1,0:T(8,128)(2,1)S(1)}, u32[]{:S(2)}, u32[]{:S(2)}) collective-permute-start(bf16[4,64,1536]{2,1,0:T(8,128)(2,1)S(1)} %join_qkv.1.refs_2_), channel_id=1, source_target_pairs={{0,4},{1,5},{2,6},{3,7},{4,8},{5,9},{6,10},{7,11},{8,12},{9,13},{1... | collective-permute-start | bytes 2359304 | tf_op jit(solution)/shard_map/ppermute | solution.py:67
  21.9 44.1 %collective-permute-start.7 = (bf16[4,64,1536]{2,1,0:T(8,128)(2,1)S(1)}, bf16[4,64,1536]{2,1,0:T(8,128)(2,1)S(1)}, u32[]{:S(2)}, u32[]{:S(2)}) collective-permute-start(bf16[4,64,1536]{2,1,0:T(8,128)(2,1)S(1)} %join_qkv.1.refs_2_), channel_id=1, source_target_pairs={{0,12},{1,13},{2,14},{3,15},{4,0},{5,1},{6,2},{7,3},{8,4},{9,5},{1... | collective-permute-start | bytes 2359304 | tf_op jit(solution)/shard_map/ppermute | solution.py:67
  23.6 42.4 %collective-permute-start.8 = (bf16[4,64,1536]{2,1,0:T(8,128)(2,1)S(1)}, bf16[4,64,1536]{2,1,0:T(8,128)(2,1)S(1)}, u32[]{:S(2)}, u32[]{:S(2)}) collective-permute-start(bf16[4,64,1536]{2,1,0:T(8,128)(2,1)S(1)} %join_qkv.1.refs_2_), channel_id=1, source_target_pairs={{0,8},{1,9},{2,10},{3,11},{4,12},{5,13},{6,14},{7,15},{8,0},{9,1},... | collective-permute-start | bytes 2359304 | tf_op jit(solution)/shard_map/ppermute | solution.py:67
  25.4 1.2 copy-start.15
  27.9 7.9 %collective-permute-start.9 = (bf16[4,64,256]{2,1,0:T(8,128)(2,1)S(1)}, bf16[4,64,256]{2,1,0:T(8,128)(2,1)S(1)}, u32[]{:S(2)}, u32[]{:S(2)}) collective-permute-start(bf16[4,64,256]{2,1,0:T(8,128)(2,1)S(1)} %get-tuple-element.41), channel_id=1, source_target_pairs={{0,1},{1,2},{2,3},{3,0},{4,5},{5,6},{6,7},{7,4},{8,9},{9,10},{10,1... | collective-permute-start | bytes 393224 | tf_op jit(solution)/shard_map/ppermute | solution.py:67
  29.4 11.2 %collective-permute-start.10 = (bf16[4,64,256]{2,1,0:T(8,128)(2,1)S(1)}, bf16[4,64,256]{2,1,0:T(8,128)(2,1)S(1)}, u32[]{:S(2)}, u32[]{:S(2)}) collective-permute-start(bf16[4,64,256]{2,1,0:T(8,128)(2,1)S(1)} %get-tuple-element.42), channel_id=1, source_target_pairs={{0,3},{1,0},{2,1},{3,2},{4,7},{5,4},{6,5},{7,6},{8,11},{9,8},{10,9... | collective-permute-start | bytes 393224 | tf_op jit(solution)/shard_map/ppermute | solution.py:67
  35.8 13.1 %collective-permute-start = (bf16[128,1024]{1,0:T(8,128)(2,1)}, bf16[128,1024]{1,0:T(8,128)(2,1)S(1)}, u32[]{:S(2)}, u32[]{:S(2)}) collective-permute-start(bf16[128,1024]{1,0:T(8,128)(2,1)} %bitcast.24), channel_id=1, source_target_pairs={{0,16},{16,0},{32,48},{48,32},{64,80},{80,64},{96,112},{112,96},{1... | collective-permute-start | bytes 786440 | tf_op jit(solution)/shard_map/ppermute | solution.py:71
  40.6 6.5 %collective-permute-start.11 = (bf16[4,64,256]{2,1,0:T(8,128)(2,1)S(1)}, bf16[4,64,256]{2,1,0:T(8,128)(2,1)S(1)}, u32[]{:S(2)}, u32[]{:S(2)}) collective-permute-start(bf16[4,64,256]{2,1,0:T(8,128)(2,1)S(1)} %get-tuple-element.43), channel_id=1, source_target_pairs={{0,2},{1,3},{2,0},{3,1},{4,6},{5,7},{6,4},{7,5},{8,10},{9,11},{10,... | collective-permute-start | bytes 393224 | tf_op jit(solution)/shard_map/ppermute | solution.py:67
  47.7 6.2 %collective-permute-start.12 = (bf16[4,64,256]{2,1,0:T(8,128)(2,1)S(1)}, bf16[4,64,256]{2,1,0:T(8,128)(2,1)S(1)}, u32[]{:S(2)}, u32[]{:S(2)}) collective-permute-start(bf16[4,64,256]{2,1,0:T(8,128)(2,1)S(1)} %get-tuple-element.45), channel_id=1, source_target_pairs={{0,4},{1,5},{2,6},{3,7},{4,8},{5,9},{6,10},{7,11},{8,12},{9,13},{1... | collective-permute-start | bytes 393224 | tf_op jit(solution)/shard_map/ppermute | solution.py:67
  48.9 17.0 %collective-permute-start.15 = (bf16[64,2560]{1,0:T(8,128)(2,1)S(1)}, bf16[64,2560]{1,0:T(8,128)(2,1)S(1)}, u32[]{:S(2)}, u32[]{:S(2)}) collective-permute-start(bf16[64,2560]{1,0:T(8,128)(2,1)S(1)} %collective-permute-done.5.refs_6_.refs_9_.refs_3_), channel_id=1, source_target_pairs={{0,3},{1,0},{2,1},{3,2},{4,7},{5,4},{6,5},{7,6},{8,11},{9,8},{10,9... | collective-permute-start | bytes 983048 | tf_op jit(solution)/shard_map/ppermute | solution.py:67
  53.9 5.0 %collective-permute-start.13 = (bf16[4,64,256]{2,1,0:T(8,128)(2,1)S(1)}, bf16[4,64,256]{2,1,0:T(8,128)(2,1)S(1)}, u32[]{:S(2)}, u32[]{:S(2)}) collective-permute-start(bf16[4,64,256]{2,1,0:T(8,128)(2,1)S(1)} %get-tuple-element.46), channel_id=1, source_target_pairs={{0,12},{1,13},{2,14},{3,15},{4,0},{5,1},{6,2},{7,3},{8,4},{9,5},{1... | collective-permute-start | bytes 393224 | tf_op jit(solution)/shard_map/ppermute | solution.py:67
  58.9 6.5 %collective-permute-start.14 = (bf16[4,64,256]{2,1,0:T(8,128)(2,1)S(1)}, bf16[4,64,256]{2,1,0:T(8,128)(2,1)S(1)}, u32[]{:S(2)}, u32[]{:S(2)}) collective-permute-start(bf16[4,64,256]{2,1,0:T(8,128)(2,1)S(1)} %get-tuple-element.47), channel_id=1, source_target_pairs={{0,8},{1,9},{2,10},{3,11},{4,12},{5,13},{6,14},{7,15},{8,0},{9,1},... | collective-permute-start | bytes 393224 | tf_op jit(solution)/shard_map/ppermute | solution.py:67
  65.9 2.9 %copy-start.1 = (bf16[4,4,64,256]{3,2,1,0:T(8,128)(2,1)}, bf16[4,4,64,256]{3,2,1,0:T(8,128)(2,1)S(1)}, u32[]{:S(2)}) copy-start(bf16[4,4,64,256]{3,2,1,0:T(8,128)(2,1)S(1)} %join_proj.1.refs_6_.refs_4_) | copy-start | bytes 1572868
  66.0 2.9 %copy-start.10 = (bf16[64,2560]{1,0:T(8,128)(2,1)}, bf16[64,2560]{1,0:T(8,128)(2,1)S(1)}, u32[]{:S(2)}) copy-start(bf16[64,2560]{1,0:T(8,128)(2,1)S(1)} %collective-permute-done.15.refs_10_.refs_4_) | copy-start | bytes 983044
  66.0 1.2 copy-start.7
  69.7 12.0 %collective-permute-start.18 = (bf16[4,64,1536]{2,1,0:T(8,128)(2,1)S(1)}, bf16[4,64,1536]{2,1,0:T(8,128)(2,1)S(1)}, u32[]{:S(2)}, u32[]{:S(2)}) collective-permute-start(bf16[4,64,1536]{2,1,0:T(8,128)(2,1)S(1)} %join_middle.1.refs_4_.refs_3_), channel_id=1, source_target_pairs={{0,12},{1,13},{2,14},{3,15},{4,0},{5,1},{6,2},{7,3},{8,4},{9,5},{1... | collective-permute-start | bytes 2359304 | tf_op jit(solution)/shard_map/ppermute | solution.py:67
  73.2 26.6 %collective-permute-start.17 = (bf16[4,64,1536]{2,1,0:T(8,128)(2,1)S(1)}, bf16[4,64,1536]{2,1,0:T(8,128)(2,1)S(1)}, u32[]{:S(2)}, u32[]{:S(2)}) collective-permute-start(bf16[4,64,1536]{2,1,0:T(8,128)(2,1)S(1)} %join_middle.1.refs_4_.refs_3_), channel_id=1, source_target_pairs={{0,4},{1,5},{2,6},{3,7},{4,8},{5,9},{6,10},{7,11},{8,12},{9,13},{1... | collective-permute-start | bytes 2359304 | tf_op jit(solution)/shard_map/ppermute | solution.py:67
  81.7 18.1 %collective-permute-start.19 = (bf16[4,64,1536]{2,1,0:T(8,128)(2,1)S(1)}, bf16[4,64,1536]{2,1,0:T(8,128)(2,1)S(1)}, u32[]{:S(2)}, u32[]{:S(2)}) collective-permute-start(bf16[4,64,1536]{2,1,0:T(8,128)(2,1)S(1)} %collective-permute-done.18.refs_6_.refs_5_), channel_id=1, source_target_pairs={{0,12},{1,13},{2,14},{3,15},{4,0},{5,1},{6,2},{7,3},{8,4},{9,5},{1... | collective-permute-start | bytes 2359304 | tf_op jit(solution)/shard_map/ppermute | solution.py:67
  89.0 23.9 %copy-start.2 = (bf16[4,4,64,256]{3,2,1,0:T(8,128)(2,1)S(1)}, bf16[4,4,64,256]{3,2,1,0:T(8,128)(2,1)}, u32[]{:S(2)}) copy-start(bf16[4,4,64,256]{3,2,1,0:T(8,128)(2,1)} %copy-done.1) | copy-start | bytes 1572868
  89.0 10.7 %collective-permute-start.21 = (bf16[4,64,1024]{2,1,0:T(8,128)(2,1)}, bf16[4,64,1024]{2,1,0:T(8,128)(2,1)}, u32[]{:S(2)}, u32[]{:S(2)}) collective-permute-start(bf16[4,64,1024]{2,1,0:T(8,128)(2,1)} %join_lower.1.refs_3_), channel_id=1, source_target_pairs={{0,4},{1,5},{2,6},{3,7},{4,8},{5,9},{6,10},{7,11},{8,12},{9,13},{1... | collective-permute-start | bytes 1572872 | tf_op jit(solution)/shard_map/ppermute | solution.py:67
  92.3 7.5 %collective-permute-start.16 = (bf16[8,256,64]{2,1,0:T(8,128)(2,1)S(1)}, bf16[8,256,64]{2,1,0:T(8,128)(2,1)S(1)}, u32[]{:S(2)}, u32[]{:S(2)}) collective-permute-start(bf16[8,256,64]{2,1,0:T(8,128)(2,1)S(1)} %span_attention.1.refs_1_), channel_id=1, source_target_pairs={{0,16},{16,0},{32,48},{48,32},{64,80},{80,64},{96,112},{112,96},{1... | collective-permute-start | bytes 786440 | tf_op jit(solution)/shard_map/ppermute | solution.py:71
  92.4 15.0 %collective-permute-start.22 = (bf16[4,64,1024]{2,1,0:T(8,128)(2,1)}, bf16[4,64,1024]{2,1,0:T(8,128)(2,1)}, u32[]{:S(2)}, u32[]{:S(2)}) collective-permute-start(bf16[4,64,1024]{2,1,0:T(8,128)(2,1)} %join_lower.1.refs_3_), channel_id=1, source_target_pairs={{0,12},{1,13},{2,14},{3,15},{4,0},{5,1},{6,2},{7,3},{8,4},{9,5},{1... | collective-permute-start | bytes 1572872 | tf_op jit(solution)/shard_map/ppermute | solution.py:67
  99.7 10.7 %collective-permute-start.23 = (bf16[4,64,1024]{2,1,0:T(8,128)(2,1)}, bf16[4,64,1024]{2,1,0:T(8,128)(2,1)}, u32[]{:S(2)}, u32[]{:S(2)}) collective-permute-start(bf16[4,64,1024]{2,1,0:T(8,128)(2,1)} %collective-permute-done.21.refs_4_), channel_id=1, source_target_pairs={{0,4},{1,5},{2,6},{3,7},{4,8},{5,9},{6,10},{7,11},{8,12},{9,13},{1... | collective-permute-start | bytes 1572872 | tf_op jit(solution)/shard_map/ppermute | solution.py:67
  99.8 43.1 %copy-start.39 = (s32[8]{0:T(128)S(1)}, s32[8]{0:T(128)}, u32[]{:S(2)}) copy-start(s32[8]{0:T(128)} %param.19) | copy-start | bytes 100
  99.8 1.3 copy-start.3
  99.8 1.4 copy-start.5
  101.2 1.6 collective-permute-start.20
  112.7 1.6 collective-permute-start.24
  112.9 12.2 %collective-permute-start.25 = (bf16[4,4,64,256]{3,2,1,0:T(8,128)(2,1)S(1)}, bf16[4,4,64,256]{3,2,1,0:T(8,128)(2,1)S(1)}, u32[]{:S(2)}, u32[]{:S(2)}) collective-permute-start(bf16[4,4,64,256]{3,2,1,0:T(8,128)(2,1)S(1)} %copy-done.2), channel_id=1, source_target_pairs={{0,16},{16,0},{32,48},{48,32},{64,80},{80,64},{96,112},{112,96},{1... | collective-permute-start | bytes 1572872 | tf_op jit(solution)/shard_map/ppermute | solution.py:71
  116.1 19.9 %all-to-all-start = ((bf16[128,8,128]{2,1,0:T(8,128)(2,1)}), bf16[128,8,128]{2,1,0:T(8,128)(2,1)S(1)}, u32[]{:S(2)}, u32[]{:S(2)}) async-start(bf16[128,8,128]{2,1,0:T(8,128)(2,1)} %bitcast.8), calls=%async_computation | async-start | bytes 524288 | tf_op jit(solution)/shard_map/all_to_all | solution.py:718
  135.9 1.6 copy-start.14
  139.6 6.2 %collective-permute-start.26 = (bf16[128,512]{1,0:T(8,128)(2,1)S(1)}, bf16[128,512]{1,0:T(8,128)(2,1)S(1)}, u32[]{:S(2)}, u32[]{:S(2)}) collective-permute-start(bf16[128,512]{1,0:T(8,128)(2,1)S(1)} %embed.1.refs_1_), channel_id=1, source_target_pairs={{0,1},{1,2},{2,3},{3,0},{4,5},{5,6},{6,7},{7,4},{8,9},{9,10},{10,1... | collective-permute-start | bytes 393224 | tf_op jit(solution)/shard_map/ppermute | solution.py:67
  140.3 6.5 %collective-permute-start.27 = (bf16[128,512]{1,0:T(8,128)(2,1)S(1)}, bf16[128,512]{1,0:T(8,128)(2,1)S(1)}, u32[]{:S(2)}, u32[]{:S(2)}) collective-permute-start(bf16[128,512]{1,0:T(8,128)(2,1)S(1)} %embed.1.refs_1_), channel_id=1, source_target_pairs={{0,3},{1,0},{2,1},{3,2},{4,7},{5,4},{6,5},{7,6},{8,11},{9,8},{10,9... | collective-permute-start | bytes 393224 | tf_op jit(solution)/shard_map/ppermute | solution.py:67
  142.9 6.5 %collective-permute-start.28 = (bf16[128,512]{1,0:T(8,128)(2,1)S(1)}, bf16[128,512]{1,0:T(8,128)(2,1)S(1)}, u32[]{:S(2)}, u32[]{:S(2)}) collective-permute-start(bf16[128,512]{1,0:T(8,128)(2,1)S(1)} %embed.1.refs_1_), channel_id=1, source_target_pairs={{0,2},{1,3},{2,0},{3,1},{4,6},{5,7},{6,4},{7,5},{8,10},{9,11},{10,... | collective-permute-start | bytes 393224 | tf_op jit(solution)/shard_map/ppermute | solution.py:67
  149.9 3.8 %copy-start.13 = (bf16[4,128,512]{2,1,0:T(8,128)(2,1)}, bf16[4,128,512]{2,1,0:T(8,128)(2,1)S(1)}, u32[]{:S(2)}) copy-start(bf16[4,128,512]{2,1,0:T(8,128)(2,1)S(1)} %join_columns.1.refs_1_) | copy-start | bytes 1572868
  149.9 10.6 %collective-permute-start.29 = (bf16[4,128,512]{2,1,0:T(8,128)(2,1)S(1)}, bf16[4,128,512]{2,1,0:T(8,128)(2,1)}, u32[]{:S(2)}, u32[]{:S(2)}) collective-permute-start(bf16[4,128,512]{2,1,0:T(8,128)(2,1)S(1)} %join_columns.1.refs_1_), channel_id=1, source_target_pairs={{0,4},{1,5},{2,6},{3,7},{4,8},{5,9},{6,10},{7,11},{8,12},{9,13},{1... | collective-permute-start | bytes 1572872 | tf_op jit(solution)/shard_map/ppermute | solution.py:67
  150.7 17.8 %copy-start.34 = (f32[128,128]{1,0:T(8,128)}, f32[128,128]{1,0:T(8,128)S(1)}, u32[]{:S(2)}) copy-start(f32[128,128]{1,0:T(8,128)S(1)} %fusion.1.refs_7_) | copy-start | bytes 196612
  151.0 17.5 %copy-start.32 = (f32[128,128]{1,0:T(8,128)}, f32[128,128]{1,0:T(8,128)S(1)}, u32[]{:S(2)}) copy-start(f32[128,128]{1,0:T(8,128)S(1)} %get-tuple-element.76.refs_6_) | copy-start | bytes 196612
  151.0 17.5 %copy-start.33 = (f32[128,128]{1,0:T(8,128)}, f32[128,128]{1,0:T(8,128)S(1)}, u32[]{:S(2)}) copy-start(f32[128,128]{1,0:T(8,128)S(1)} %get-tuple-element.77.refs_5_) | copy-start | bytes 196612
  151.0 11.4 %collective-permute-start.31 = (bf16[4,128,512]{2,1,0:T(8,128)(2,1)S(1)}, bf16[4,128,512]{2,1,0:T(8,128)(2,1)}, u32[]{:S(2)}, u32[]{:S(2)}) collective-permute-start(bf16[4,128,512]{2,1,0:T(8,128)(2,1)S(1)} %join_columns.1.refs_1_), channel_id=1, source_target_pairs={{0,12},{1,13},{2,14},{3,15},{4,0},{5,1},{6,2},{7,3},{8,4},{9,5},{1... | collective-permute-start | bytes 1572872 | tf_op jit(solution)/shard_map/ppermute | solution.py:67
  158.5 12.7 %copy-start = (bf16[2,8192,64]{1,2,0:T(8,128)(2,1)S(1)}, bf16[2,8192,64]{1,2,0:T(8,128)(2,1)}, u32[]{:S(2)}) copy-start(bf16[2,8192,64]{1,2,0:T(8,128)(2,1)} %param.30) | copy-start | bytes 6291460
  158.5 12.6 %copy-start.18 = (f32[8192]{0:T(1024)S(1)}, f32[8192]{0:T(1024)}, u32[]{:S(2)}) copy-start(f32[8192]{0:T(1024)} %param.28) | copy-start | bytes 98308
  158.5 12.6 %copy-start.24 = (s32[38]{0:T(128)S(1)}, s32[38]{0:T(128)}, u32[]{:S(2)}) copy-start(s32[38]{0:T(128)} %concatenate.9.refs_0_) | copy-start | bytes 460
  160.5 10.6 %collective-permute-start.30 = (bf16[4,128,512]{2,1,0:T(8,128)(2,1)}, bf16[4,128,512]{2,1,0:T(8,128)(2,1)S(1)}, u32[]{:S(2)}, u32[]{:S(2)}) collective-permute-start(bf16[4,128,512]{2,1,0:T(8,128)(2,1)} %collective-permute-done.29.refs_1_), channel_id=1, source_target_pairs={{0,4},{1,5},{2,6},{3,7},{4,8},{5,9},{6,10},{7,11},{8,12},{9,13},{1... | collective-permute-start | bytes 1572872 | tf_op jit(solution)/shard_map/ppermute | solution.py:67
  171.1 4.3 %copy-start.12 = (bf16[4,128,512]{2,1,0:T(8,128)(2,1)}, bf16[4,128,512]{2,1,0:T(8,128)(2,1)S(1)}, u32[]{:S(2)}) copy-start(bf16[4,128,512]{2,1,0:T(8,128)(2,1)S(1)} %collective-permute-done.30.refs_1_) | copy-start | bytes 1572868
  174.7 4.7 %copy-start.28 = (bf16[2,128,64]{2,1,0:T(8,128)(2,1)}, bf16[2,128,64]{2,1,0:T(8,128)(2,1)S(1)}, u32[]{:S(2)}) copy-start(bf16[2,128,64]{2,1,0:T(8,128)(2,1)S(1)} %get-tuple-element.62.refs_2_) | copy-start | bytes 98308
  174.7 4.7 %collective-permute-start.32 = (bf16[2,128,64]{2,1,0:T(8,128)(2,1)S(1)}, bf16[2,128,64]{2,1,0:T(8,128)(2,1)S(1)}, u32[]{:S(2)}, u32[]{:S(2)}) collective-permute-start(bf16[2,128,64]{2,1,0:T(8,128)(2,1)S(1)} %get-tuple-element.62.refs_2_), channel_id=1, source_target_pairs={{0,1},{1,0},{2,3},{3,2},{4,5},{5,4},{6,7},{7,6},{8,9},{9,8},{10,11... | collective-permute-start | bytes 98312 | tf_op jit(solution)/shard_map/ppermute | solution.py:803
  175.4 27.2 %copy-start.25 = (s32[38]{0:T(128)S(1)}, s32[38]{0:T(128)}, u32[]{:S(2)}) copy-start(s32[38]{0:T(128)} %concatenate.9.refs_0_) | copy-start | bytes 460
  186.3 16.3 %collective-permute-start.33 = (bf16[32,8192]{1,0:T(8,128)(2,1)}, bf16[32,8192]{1,0:T(8,128)(2,1)S(1)}, u32[]{:S(2)}, u32[]{:S(2)}) collective-permute-start(bf16[32,8192]{1,0:T(8,128)(2,1)} %get-tuple-element.64), channel_id=1, source_target_pairs={{0,4},{1,5},{2,6},{3,7},{4,8},{5,9},{6,10},{7,11},{8,12},{9,13},{1... | collective-permute-start | bytes 1572872 | tf_op jit(solution)/shard_map/ppermute | solution.py:67
  186.4 16.2 %collective-permute-start.34 = (bf16[32,8192]{1,0:T(8,128)(2,1)}, bf16[32,8192]{1,0:T(8,128)(2,1)S(1)}, u32[]{:S(2)}, u32[]{:S(2)}) collective-permute-start(bf16[32,8192]{1,0:T(8,128)(2,1)} %get-tuple-element.65), channel_id=1, source_target_pairs={{0,12},{1,13},{2,14},{3,15},{4,0},{5,1},{6,2},{7,3},{8,4},{9,5},{1... | collective-permute-start | bytes 1572872 | tf_op jit(solution)/shard_map/ppermute | solution.py:67
  189.6 13.0 %collective-permute-start.35 = (bf16[32,8192]{1,0:T(8,128)(2,1)}, bf16[32,8192]{1,0:T(8,128)(2,1)S(1)}, u32[]{:S(2)}, u32[]{:S(2)}) collective-permute-start(bf16[32,8192]{1,0:T(8,128)(2,1)} %get-tuple-element.66), channel_id=1, source_target_pairs={{0,8},{1,9},{2,10},{3,11},{4,12},{5,13},{6,14},{7,15},{8,0},{9,1},... | collective-permute-start | bytes 1572872 | tf_op jit(solution)/shard_map/ppermute | solution.py:67
  204.4 6.2 %collective-permute-start.36 = (bf16[8,8192]{1,0:T(8,128)(2,1)S(1)}, bf16[8,8192]{1,0:T(8,128)(2,1)S(1)}, u32[]{:S(2)}, u32[]{:S(2)}) collective-permute-start(bf16[8,8192]{1,0:T(8,128)(2,1)S(1)} %get-tuple-element.68), channel_id=1, source_target_pairs={{0,1},{1,2},{2,3},{3,0},{4,5},{5,6},{6,7},{7,4},{8,9},{9,10},{10,1... | collective-permute-start | bytes 393224 | tf_op jit(solution)/shard_map/ppermute | solution.py:67
  206.5 5.0 %collective-permute-start.37 = (bf16[8,8192]{1,0:T(8,128)(2,1)S(1)}, bf16[8,8192]{1,0:T(8,128)(2,1)S(1)}, u32[]{:S(2)}, u32[]{:S(2)}) collective-permute-start(bf16[8,8192]{1,0:T(8,128)(2,1)S(1)} %get-tuple-element.69), channel_id=1, source_target_pairs={{0,3},{1,0},{2,1},{3,2},{4,7},{5,4},{6,5},{7,6},{8,11},{9,8},{10,9... | collective-permute-start | bytes 393224 | tf_op jit(solution)/shard_map/ppermute | solution.py:67
  207.7 6.5 %collective-permute-start.38 = (bf16[8,8192]{1,0:T(8,128)(2,1)S(1)}, bf16[8,8192]{1,0:T(8,128)(2,1)S(1)}, u32[]{:S(2)}, u32[]{:S(2)}) collective-permute-start(bf16[8,8192]{1,0:T(8,128)(2,1)S(1)} %get-tuple-element.70), channel_id=1, source_target_pairs={{0,2},{1,3},{2,0},{3,1},{4,6},{5,7},{6,4},{7,5},{8,10},{9,11},{10,... | collective-permute-start | bytes 393224 | tf_op jit(solution)/shard_map/ppermute | solution.py:67
  (16 other events, 14.1 us)

commit v5 on v4

--- a/solution.py
+++ b/solution.py
@@ -131,18 +131,12 @@
         out[:, part * cols : (part + 1) * cols] = weight[:, pl.ds(start, cols)]
 
 
-def take_halves(info, qkv, out_weight, up_weight, down_weight, qkv_out, rest_out):
-    take_qkv(info, qkv, qkv_out)
-    take_rest(info, out_weight, up_weight, down_weight, rest_out)
-
-
-def take_rest(info, out_weight, up_weight, down_weight, out):
-    core = info[16]
+def take_rest(info, out_weight, up_weight, down_weight, proj, up_out, down_out, kept, beyond):
+    core, near = info[16], info[19]
     rows, width = out_weight.shape
     cols = width // 2
     units = down_weight.shape[0] // 2
-    out[:, :cols] = out_weight[:, pl.ds(pl.multiple_of(core * cols, cols), cols)]
-    at = cols
+    pieces = [out_weight[:, pl.ds(pl.multiple_of(core * cols, cols), cols)]]
     for pair in range(up_weight.shape[1] // (4 * units)):
         halves = []
         for step in range(2):
@@ -154,10 +148,20 @@
                     up_weight[:, low + units : low + 2 * units].astype(jnp.float32),
                 )
             )
-        piece = jnp.concatenate(halves, axis=1).astype(jnp.bfloat16)
-        out[:, at : at + 2 * units] = piece
-        at += 2 * units
-    out[:, at:] = down_weight[pl.ds(pl.multiple_of(core * units, units), units), :]
+        pieces.append(jnp.concatenate(halves, axis=1).astype(jnp.bfloat16))
+    pieces.append(down_weight[pl.ds(pl.multiple_of(core * units, units), units), :])
+    at = 0
+    for piece in pieces:
+        for out in (up_out, down_out):
+            out[:, at : at + piece.shape[1]] = piece
+        at += piece.shape[1]
+    block = kept.shape[1] // SIDE
+    for out, start, distance in ((kept, 0, 0), (up_out, at, 1), (down_out, at, SIDE - 1), (beyond, 0, 2)):
+        target = lax.rem(near + distance, SIDE)
+        for index in range(SIDE):
+            shard = jnp.where(core == 0, SIDE * index + target, SIDE * target + index)
+            source = pl.multiple_of((2 * shard + core) * block, block)
+            out[:, start + index * block : start + (index + 1) * block] = proj[:, pl.ds(source, block)]
 
 
 def join_blocks(info, own, left, right, opposite, out):
@@ -170,28 +174,32 @@
         out[index] = block[:, : out.shape[2]]
 
 
-def join_lower(info, own, left, right, opposite, out):
-    for index, block in enumerate((own, left, right, opposite)):
-        out[index] = block[:, block.shape[1] - out.shape[2] :]
-
-
-def deal_columns(info, weight, *outs):
-    core, near = info[16], info[19]
-    cols = outs[0].shape[2]
-    for out, distance in zip(outs, (0, 1, SIDE - 1, 2)):
-        target = lax.rem(near + distance, SIDE)
-        for index in range(SIDE):
-            shard = jnp.where(core == 0, SIDE * index + target, SIDE * target + index)
-            start = pl.multiple_of((2 * shard + core) * cols, cols)
-            out[index] = weight[:, pl.ds(start, cols)]
-
-
-def deal_again(info, own, left, right, opposite, *outs):
+def join_lower(info, own, left, right, opposite, kept, beyond, up_out, down_out, far_kept, far_beyond):
     far = info[20]
-    for out, distance in zip(outs, (0, 1, SIDE - 1, 2)):
-        target = lax.rem(far + distance, SIDE)
-        for index, block in enumerate((own, left, right, opposite)):
-            out[index] = block[target]
+    block = far_kept.shape[2]
+    width = up_out.shape[2] - block
+    start = own.shape[1] - kept.shape[1] - width
+    for index, part in enumerate((own, left, right, opposite)):
+        for out in (up_out, down_out):
+            out[index, :, :width] = part[:, start : start + width]
+        columns, first = (part, start + width) if index in (1, 2) else (kept, 0)
+        if index == 3:
+            columns = beyond
+        for out, at, distance in (
+            (far_kept, 0, 0),
+            (up_out, width, 1),
+            (down_out, width, SIDE - 1),
+            (far_beyond, 0, 2),
+        ):
+            target = lax.rem(far + distance, SIDE)
+            source = pl.multiple_of(first + target * block, 128)
+            out[index, :, at : at + block] = columns[:, pl.ds(source, block)]
+
+
+def join_proj(info, own, left, right, opposite, out):
+    block = own.shape[2]
+    for index, part in enumerate((own, left, right, opposite)):
+        out[index] = part[:, :, part.shape[2] - block :]
 
 
 def both_rows(info, mine, other, pieces_out):
@@ -223,9 +231,8 @@
     return [(power / total).astype(jnp.bfloat16) for power, total in zip(powers, sums)]
 
 
-def span_qkv(info, pieces, w0, w1, w2, w3, mixed, mark):
+def span_qkv(info, pieces, w0, w1, w2, w3, mixed):
     mixed[...] = ring_dot(info, pieces, (w0, w1, w2, w3), 0, w0.shape[2]).astype(jnp.bfloat16)
-    mark[...] = jnp.zeros_like(mark)
 
 
 def span_attention(info, mixed, context):
@@ -292,7 +299,7 @@
 
 def down(info, inner, first_out, w0, w1, w2, w3, kept, sent, total):
     core = info[16]
-    total[...] = ring_dot(info, inner, (w0, w1, w2, w3), 0, w0.shape[2])
+    total[...] = ring_dot(info, inner, (w0, w1, w2, w3), 0, total.shape[1])
     half = kept.shape[0]
     rows = pl.ds(pl.multiple_of(core * half, half), half)
     kept[...] = total[rows, :] + first_out[rows, :].astype(jnp.float32)
@@ -337,40 +344,26 @@
     out[:, cols:] = jnp.where(core == 0, far, near).astype(jnp.bfloat16)
 
 
-def shard_rows(info, weight, buffer, sems, at, step, slot):
-    depth = buffer.shape[1]
-    start = pl.multiple_of(info[SIDE * at + step] * depth, depth)
-    return pltpu.make_async_copy(
-        weight.at[pl.ds(start, depth), :], buffer.at[slot], sems.at[slot]
-    )
-
-
 def project(info, *refs, starts, count):
     blocks, refs = refs[:count], refs[count:]
-    gain, kv_weight = refs[:2]
-    before = refs[2:5] if len(refs) > 8 else None
-    q_weight, q_total, kv_total, square, buffer, sems = refs[-6:]
+    gain, q_weight, kv_weight = refs[:3]
+    before = refs[3:6] if len(refs) > 6 else None
+    q_total, kv_total, square = refs[-3:]
     depth = blocks[0].shape[2]
-    places = [(at, step) for at in starts for step in range(SIDE)]
-    copies = [
-        shard_rows(info, q_weight, buffer, sems, at, step, slot)
-        for slot, (at, step) in enumerate(places)
-    ]
-    for copy in copies:
-        copy.start()
-    queries, both, squares = None, None, None
-    for slot, (at, step) in enumerate(places):
-        shard = info[SIDE * at + step]
-        wide = blocks[slot // SIDE][step].astype(jnp.float32)
-        act = (wide * gain[shard]).astype(jnp.bfloat16)
-        span = pl.ds(pl.multiple_of(shard * depth, depth), depth)
-        kv_term = dot_last(act, kv_weight[:, span])
-        term = jnp.sum(wide * wide, axis=1, keepdims=True)
-        copies[slot].wait()
-        q_term = dot32(act, buffer[slot])
-        queries = q_term if queries is None else queries + q_term
-        both = kv_term if both is None else both + kv_term
-        squares = term if squares is None else squares + term
+    queries, both = None, None
+    squares = None
+    for at, block in zip(starts, blocks):
+        for step in range(SIDE):
+            shard = info[SIDE * at + step]
+            wide = block[step].astype(jnp.float32)
+            act = (wide * gain[shard]).astype(jnp.bfloat16)
+            span = pl.ds(pl.multiple_of(shard * depth, depth), depth)
+            q_term = dot32(act, q_weight[span, :])
+            kv_term = dot_last(act, kv_weight[:, span])
+            term = jnp.sum(wide * wide, axis=1, keepdims=True)
+            queries = q_term if queries is None else queries + q_term
+            both = kv_term if both is None else both + kv_term
+            squares = term if squares is None else squares + term
     if before is not None:
         queries, both, squares = queries + before[0][...], both + before[1][...], squares + before[2][...]
     q_total[...] = queries
@@ -404,34 +397,22 @@
     out[1] = both[:, cols:].astype(jnp.bfloat16)
 
 
-def last_queries(
-    info, block, gain, q_before, scale, cosine, sine, swap, q_weight, out, buffer, sems
-):
-    copies = [shard_rows(info, q_weight, buffer, sems, 3, step, step) for step in range(SIDE)]
-    for copy in copies:
-        copy.start()
+def last_queries(info, block, gain, q_weight, q_before, scale, cosine, sine, swap, out):
+    depth = block.shape[2]
     total = q_before[...]
     for step in range(SIDE):
         shard = info[SIDE * 3 + step]
         act = (block[step].astype(jnp.float32) * gain[shard]).astype(jnp.bfloat16)
-        copies[step].wait()
-        total += dot32(act, buffer[step])
+        span = pl.ds(pl.multiple_of(shard * depth, depth), depth)
+        total += dot32(act, q_weight[span, :])
     for head in range(out.shape[1] // HEAD_WIDTH):
         lanes = slice(head * HEAD_WIDTH, (head + 1) * HEAD_WIDTH)
         query = total[:, lanes] * scale[...]
         out[:, lanes] = turn(query, cosine[...], sine[...], swap[...]).astype(jnp.bfloat16)
 
 
-def attend_out(info, query, mine, partner, allowed, deal, weight_hbm, *refs):
-    outs, context, weight, sems = refs[:4], refs[4], refs[5], refs[6]
-    step = weight.shape[1] // sems.shape[0]
-
-    def fetch(part):
-        span = pl.ds(part * step, step)
-        return pltpu.make_async_copy(weight_hbm.at[:, span], weight.at[:, span], sems.at[part])
-
-    for part in range(sems.shape[0]):
-        fetch(part).start()
+def attend_out(info, query, mine, partner, allowed, deal, weight, *refs):
+    outs, context = refs[:4], refs[4]
     odd = info[17] == 1
     own = mine[...].astype(jnp.float32)
     far = partner[...].astype(jnp.float32)
@@ -453,9 +434,8 @@
         context[:, lanes] = dot32(prob, value).astype(jnp.bfloat16)
     dealt = dot32(deal[...], context[...]).astype(jnp.bfloat16)
     rows = outs[0].shape[0]
-    for part in range(sems.shape[0]):
-        start = part * step
-        fetch(part).wait()
+    step = weight.shape[1] // 8
+    for start in range(0, weight.shape[1], step):
         result = dot32(dealt, weight[:, start : start + step])
         for index, out in enumerate(outs):
             piece = result[index * rows : (index + 1) * rows]
@@ -590,20 +570,31 @@
     )
     units = enc_down.shape[0] // 2
     middle_cols = width // 2 + units * tensor_count
-    own_qkv, own_rest = whole_call(
-        take_halves,
-        "take_halves",
-        info,
-        [enc_qkv, enc_out, enc_up, enc_down],
-        (shape_of((share, 3 * width // 2)), shape_of((share, middle_cols + width))),
+    share_cols = model_width // tensor_count
+    half_cols = share_cols // 2
+    rest_shape = shape_of((share, middle_cols + width + SIDE * half_cols))
+    dealt_shape = shape_of((share, SIDE * half_cols))
+    own_qkv = whole_call(
+        take_qkv, "take_qkv", info, [enc_qkv], shape_of((share, 3 * width // 2)), limit=4
+    )
+    rest_up, rest_down, kept_cols, beyond_cols = whole_call(
+        take_rest,
+        "take_rest",
+        info,
+        [enc_out, enc_up, enc_down, proj_out],
+        (rest_shape, rest_shape, dealt_shape, dealt_shape),
         limit=60,
-    )
-    rest_ring = short_relay(own_rest)
+        after=[own_qkv],
+    )
+    qkv_ring = short_ring(own_qkv)
+    rest_right = to_ring(rest_down, 1, -1)
+    rest_ring = [rest_up, to_ring(rest_up, 1, 1), rest_right, to_ring(rest_right, 1, -1)]
+    beyond_cols = to_ring(beyond_cols, 1, 2)
     qkv_block = whole_call(
         join_blocks,
         "join_qkv",
         info,
-        short_ring(own_qkv),
+        qkv_ring,
         shape_of((SIDE, share, 3 * width // 2)),
         limit=6,
         after=rest_ring[1:3],
@@ -611,41 +602,20 @@
     all_rows = 2 * spans * span_size
 
     qkv = [qkv_block] + [to_ring(qkv_block, 2, distance) for distance in (1, -1, 2)]
-
-    share_cols = model_width // tensor_count
-    dealt_shape = (SIDE, proj_out.shape[0], share_cols // 2)
-    dealt = whole_call(
-        deal_columns,
-        "deal_columns",
-        info,
-        [proj_out],
-        (shape_of(dealt_shape),) * 4,
-        limit=8,
-        after=[qkv_block],
-    )
-    dealt = [dealt[0]] + [
-        to_ring(part, 1, distance) for part, distance in zip(dealt[1:], (1, -1, 2))
-    ]
-
-    dealt = whole_call(
-        deal_again, "deal_again", info, dealt, (shape_of(dealt_shape),) * 4, limit=8
-    )
-    dealt = [dealt[0]] + [
-        to_ring(part, 2, distance) for part, distance in zip(dealt[1:], (1, -1, 2))
-    ]
-    proj_mine = whole_call(
-        join_blocks, "join_proj", info, dealt, shape_of((SIDE,) + dealt_shape), limit=8
-    )
-    proj_other = to_core(proj_mine)
-
-    mixed, mark = whole_call(
+    mixed = whole_call(
         span_qkv,
         "span_qkv",
         info,
         [token_pieces, *qkv],
-        (shape_of((all_rows, 3 * width // 2)), shape_of((8, 128), jnp.float32)),
+        shape_of((all_rows, 3 * width // 2)),
         flops=2 * all_rows * width * 3 * width // 2,
-        after=[proj_mine, *rest_ring],
+    )
+    context = whole_call(
+        span_attention,
+        "span_attention",
+        info,
+        [mixed],
+        shape_of((tensor_count // 2, all_rows, share)),
     )
     middle_block = whole_call(
         join_middle,
@@ -654,29 +624,24 @@
         rest_ring,
         shape_of((SIDE, share, middle_cols)),
         limit=8,
-        after=[mark],
+        after=[mixed],
     )
     right = to_ring(middle_block, 2, -1)
     middle = [middle_block, to_ring(middle_block, 2, 1), right, to_ring(right, 2, -1)]
-    lower_block = whole_call(
+    lower_shape = shape_of((SIDE, share, width + half_cols))
+    far_shape = shape_of((SIDE, share, half_cols))
+    lower_up, lower_down, far_kept, far_beyond = whole_call(
         join_lower,
         "join_lower",
         info,
-        rest_ring,
-        shape_of((SIDE, share, width)),
+        [*rest_ring, kept_cols, beyond_cols],
+        (lower_shape, lower_shape, far_shape, far_shape),
         limit=8,
-        after=[right],
-    )
-    left = to_ring(lower_block, 2, 1)
-    lower = [lower_block, left, to_ring(lower_block, 2, -1), to_ring(left, 2, 1)]
-
-    context = whole_call(
-        span_attention,
-        "span_attention",
-        info,
-        [mixed],
-        shape_of((tensor_count // 2, all_rows, share)),
-    )
+        after=[context, *middle[1:3]],
+    )
+    lower_left = to_ring(lower_up, 2, 1)
+    lower = [lower_up, lower_left, to_ring(lower_down, 2, -1), to_ring(lower_left, 2, 1)]
+    far_beyond = to_ring(far_beyond, 2, 2)
     attended = whole_call(
         context_out,
         "context_out",
@@ -719,6 +684,16 @@
         outgoing.reshape(device_count, width // 128, 128), AXES, 0, 0
     )
 
+    proj_mine = whole_call(
+        join_proj,
+        "join_proj",
+        info,
+        [far_kept, lower[1], lower[2], far_beyond],
+        shape_of((SIDE, SIDE, share, half_cols)),
+        limit=8,
+        after=[outgoing],
+    )
+    proj_other = to_core(proj_mine)
     own_cols = whole_call(
         embed,
         "embed",
@@ -758,30 +733,17 @@
         functools.partial(project, starts=(0,), count=1),
         "project_own",
         info,
-        [first_block, gain, kv_pair],
+        [first_block, gain, q_weight, kv_pair],
         sums,
-        [
-            pltpu.VMEM((SIDE, share_cols, query_cols), jnp.bfloat16),
-            pltpu.SemaphoreType.DMA((SIDE,)),
-        ],
-        limit=56,
-        far=[q_weight],
         flops=block_flops,
     )
-    relayed, _ = lax.optimization_barrier((near_left, totals[2]))
-    embedded = [first_block, relayed, near_right, to_ring(relayed, 2, 1)]
+    embedded = [first_block, near_left, near_right, to_ring(near_left, 2, 1)]
     totals = whole_call(
         functools.partial(project, starts=(1, 2), count=2),
         "project_near",
         info,
-        [embedded[1], embedded[2], gain, kv_pair, *totals],
+        [embedded[1], embedded[2], gain, q_weight, kv_pair, *totals],
         sums,
-        [
-            pltpu.VMEM((2 * SIDE, share_cols, query_cols), jnp.bfloat16),
-            pltpu.SemaphoreType.DMA((2 * SIDE,)),
-        ],
-        limit=56,
-        far=[q_weight],
         flops=2 * block_flops,
     )
     own_kv, scale = whole_call(
@@ -807,29 +769,17 @@
         last_queries,
         "last_queries",
         info,
-        [embedded[3], gain, totals[0], scale, cosine, sine, swap],
+        [embedded[3], gain, q_weight, totals[0], scale, cosine, sine, swap],
         shape_of((rows, query_cols)),
-        [
-            pltpu.VMEM((SIDE, share_cols, query_cols), jnp.bfloat16),
-            pltpu.SemaphoreType.DMA((SIDE,)),
-        ],
-        limit=56,
-        far=[q_weight],
         flops=block_flops,
     )
     partial = whole_call(
         attend_out,
         "attend_out",
         info,
-        [query, own_kv, partner_kv, allowed, deal],
+        [query, own_kv, partner_kv, allowed, deal, out_weight],
         (shape_of((rows // SIDE, model_width)),) * 4,
-        [
-            pltpu.VMEM((rows, query_cols), jnp.bfloat16),
-            pltpu.VMEM((query_cols, model_width), jnp.bfloat16),
-            pltpu.SemaphoreType.DMA((8,)),
-        ],
-        limit=56,
-        far=[out_weight],
+        [pltpu.VMEM((rows, query_cols), jnp.bfloat16)],
         flops=2 * rows * model_width * query_cols,
     )
     arrived_sums = [

time: 217 us -> 200 us (0.922)
  Pallas kernels: 45.5 us -> 35.9 us
  starting transfers between devices: 57.7 us -> 50.2 us
  local copies, waits for them, and re-layouts: 22.9 us -> 19.9 us
  waiting for transfers between devices: 82.4 us -> 85.3 us
    pallas_call x23 -> x22, Pallas kernels: 45.5 us -> 35.9 us  [whole_call(): pl.pallas_call(run, name=name, out_shape=outs, in_specs=[SMEM] + [VMEM] *...]
    ppermute x33 -> x29, starting transfers between devices: 48 us -> 40.6 us  [to_ring(): return lax.ppermute(value, AXES, ring_pairs(phase, distance))]
    ppermute x1, waiting for transfers between devices: 0.01 us -> 2.77 us  [local(): lax.ppermute(own_kv, 'tensor', [(index, index ^ 1) for index in range(ten...]
    unnamed x80 -> x62, local copies, waits for them, and re-layouts: 17.5 us -> 16.5 us
    ppermute x33 -> x29, waiting for transfers between devices: 69.2 us -> 69.2 us  [to_ring(): return lax.ppermute(value, AXES, ring_pairs(phase, distance))]
  transfers between devices with their start and end apart: 40 -> 36, of which waited for: 24 -> 24; matrix products, arithmetic and copies ran while one was open for 4% -> 4% of each run, Pallas kernels for 12% -> 8%
where the time goes in v5:
time: 200 us; the launch traced here: 199 us
  waiting for transfers between devices  85.3 us (43%)
  starting transfers between devices  50.2 us (25%)
  Pallas kernels  35.9 us (18%)
  local copies, waits for them, and re-layouts  19.9 us (10%)
  other arithmetic  6.76 us (3%)
    ppermute x29, waiting for transfers between devices, to_ring(): return lax.ppermute(value, AXES, ring_pairs(phase, distance))  69.2 us
    ppermute x29, starting transfers between devices, to_ring(): return lax.ppermute(value, AXES, ring_pairs(phase, distance))  40.6 us
    pallas_call x22, Pallas kernels, whole_call(): pl.pallas_call(run, name=name, out_shape=outs, in_specs=[SMEM] + [VMEM] *...  35.9 us
    unnamed x62, local copies, waits for them, and re-layouts  16.5 us
    all_to_all x1, waiting for transfers between devices, local(): lax.all_to_all(outgoing.reshape(device_count, width // 128, 128), AXES, 0...  10.8 us
    all_to_all x1, starting transfers between devices, local(): lax.all_to_all(outgoing.reshape(device_count, width // 128, 128), AXES, 0...  8.84 us
  transfers between devices with their start and end apart: 36, of which 24 were waited for; matrix products, arithmetic and copies ran while one was open for 4% of the time, Pallas kernels for 8%

profile of v5, /device:TPU:0, one launch (start us, length us, event | category | flops | bytes accessed | tf_op | source)
XLA Modules:
  0.0 199.3 jit_solution(10001326132575998369)
XLA Ops:
  1.3 1.0 copy-done.12
  3.6 2.8 %take_rest.1 = (bf16[64,3584]{1,0:T(8,128)(2,1)}, bf16[64,3584]{1,0:T(8,128)(2,1)}, bf16[64,1024]{1,0:T(8,128)(2,1)}, bf16[64,1024]{1,0:T(8,128)(2,1)}) custom-call(s32[38]{0:T(128)} %copy-done.14, bf16[64,1024]{1,0:T(8,128)(2,1)} %refs_1_.3, bf16[64,2048]{1,0:T(8,128)(2,1)} %refs_2_.1, bf16[128,1024]{1,0:T(8,128)(2,1)} %refs_3_.4, ...), custom_call_target="tpu_custom_call" | custom-call | bytes 1703936 | tf_op jit(solution)/shard_map/take_rest/pallas_call | solution.py:101
  6.3 1.7 collective-permute-start.4
  8.0 1.6 collective-permute-start.5
  10.0 2.8 %collective-permute-start.2 = (bf16[64,1536]{1,0:T(8,128)(2,1)}, bf16[64,1536]{1,0:T(8,128)(2,1)S(1)}, u32[]{:S(2)}, u32[]{:S(2)}) collective-permute-start(bf16[64,1536]{1,0:T(8,128)(2,1)} %copy-done.9), channel_id=1, source_target_pairs={{0,3},{1,0},{2,1},{3,2},{4,7},{5,4},{6,5},{7,6},{8,11},{9,8},{10,9... | collective-permute-start | bytes 589832 | tf_op jit(solution)/shard_map/ppermute | solution.py:67
  13.7 4.7 %collective-permute-done.1.refs_2_ = bf16[64,1536]{1,0:T(8,128)(2,1)S(1)} collective-permute-done((bf16[64,1536]{1,0:T(8,128)(2,1)}, bf16[64,1536]{1,0:T(8,128)(2,1)S(1)}, u32[]{:S(2)}, u32[]{:S(2)}) %collective-permute-start.1) | collective-permute-done | bytes 196640 | tf_op jit(solution)/shard_map/ppermute | solution.py:67
  18.8 3.0 %collective-permute-done.3.refs_4_ = bf16[64,1536]{1,0:T(8,128)(2,1)S(1)} collective-permute-done((bf16[64,1536]{1,0:T(8,128)(2,1)}, bf16[64,1536]{1,0:T(8,128)(2,1)S(1)}, u32[]{:S(2)}, u32[]{:S(2)}) %collective-permute-start.3) | collective-permute-done | bytes 196640 | tf_op jit(solution)/shard_map/ppermute | solution.py:67
  24.0 1.6 collective-permute-start.6
  25.5 1.7 collective-permute-start.7
  27.3 1.8 collective-permute-start.8
  29.1 2.0 %collective-permute-start.10 = (bf16[64,3584]{1,0:T(8,128)(2,1)S(1)}, bf16[64,3584]{1,0:T(8,128)(2,1)S(1)}, u32[]{:S(2)}, u32[]{:S(2)}) collective-permute-start(bf16[64,3584]{1,0:T(8,128)(2,1)S(1)} %collective-permute-done.5.refs_6_.refs_3_), channel_id=1, source_target_pairs={{0,3},{1,0},{2,1},{3,2},{4,7},{5,4},{6,5},{7,6},{8,11},{9,8},{10,9... | collective-permute-start | bytes 1376264 | tf_op jit(solution)/shard_map/ppermute | solution.py:67
  31.1 1.7 collective-permute-done.refs_2_
  35.3 1.9 collective-permute-done.6.refs_3_
  37.2 12.9 %collective-permute-done.7.refs_4_ = bf16[4,64,1536]{2,1,0:T(8,128)(2,1)S(1)} collective-permute-done((bf16[4,64,1536]{2,1,0:T(8,128)(2,1)S(1)}, bf16[4,64,1536]{2,1,0:T(8,128)(2,1)S(1)}, u32[]{:S(2)}, u32[]{:S(2)}) %collective-permute-start.7) | collective-permute-done | bytes 786464 | tf_op jit(solution)/shard_map/ppermute | solution.py:67
  50.2 1.6 span_qkv.1.refs_1_.refs_5_
  52.4 2.3 %collective-permute-start.11 = (bf16[4,64,1536]{2,1,0:T(8,128)(2,1)S(1)}, bf16[4,64,1536]{2,1,0:T(8,128)(2,1)S(1)}, u32[]{:S(2)}, u32[]{:S(2)}) collective-permute-start(bf16[4,64,1536]{2,1,0:T(8,128)(2,1)S(1)} %join_middle.1.refs_4_.refs_3_), channel_id=1, source_target_pairs={{0,4},{1,5},{2,6},{3,7},{4,8},{5,9},{6,10},{7,11},{8,12},{9,13},{1... | collective-permute-start | bytes 2359304 | tf_op jit(solution)/shard_map/ppermute | solution.py:67
  54.6 1.6 collective-permute-start.12
  57.0 2.0 %span_attention.1.refs_1_.refs_7_ = bf16[8,256,64]{2,1,0:T(8,128)(2,1)S(1)} custom-call(s32[38]{0:T(128)S(1)} %copy-done.16, bf16[256,1536]{1,0:T(8,128)(2,1)S(1)} %span_qkv.1.refs_1_.refs_5_), custom_call_target="tpu_custom_call" | custom-call | bytes 786432 | tf_op jit(solution)/shard_map/span_attention/pallas_call | solution.py:101
  59.0 5.2 %collective-permute-done.15.refs_6_ = bf16[64,1024]{1,0:T(8,128)(2,1)S(1)} collective-permute-done((bf16[64,1024]{1,0:T(8,128)(2,1)S(1)}, bf16[64,1024]{1,0:T(8,128)(2,1)S(1)}, u32[]{:S(2)}, u32[]{:S(2)}) %collective-permute-start.15) | collective-permute-done | bytes 131104 | tf_op jit(solution)/shard_map/ppermute | solution.py:67
  64.1 2.6 %collective-permute-done.11.refs_5_.refs_4_.refs_8_ = bf16[4,64,1536]{2,1,0:T(8,128)(2,1)S(1)} collective-permute-done((bf16[4,64,1536]{2,1,0:T(8,128)(2,1)S(1)}, bf16[4,64,1536]{2,1,0:T(8,128)(2,1)S(1)}, u32[]{:S(2)}, u32[]{:S(2)}) %collective-permute-start.11) | collective-permute-done | bytes 786464 | tf_op jit(solution)/shard_map/ppermute | solution.py:67
  66.8 1.5 join_lower.1
  69.2 1.4 collective-permute-start.16
  70.9 1.9 collective-permute-start.13
  73.4 1.4 collective-permute-start.17
  74.9 6.4 %collective-permute-done.16.refs_4_.refs_2_ = bf16[4,64,1280]{2,1,0:T(8,128)(2,1)} collective-permute-done((bf16[4,64,1280]{2,1,0:T(8,128)(2,1)}, bf16[4,64,1280]{2,1,0:T(8,128)(2,1)}, u32[]{:S(2)}, u32[]{:S(2)}) %collective-permute-start.16) | collective-permute-done | bytes 655392 | tf_op jit(solution)/shard_map/ppermute | solution.py:67
  81.5 1.3 fusion.22
  83.3 1.1 copy-done.6
  84.4 2.0 %context_out.1.refs_1_ = bf16[256,512]{1,0:T(8,128)(2,1)S(1)} custom-call(s32[38]{0:T(128)S(1)} %copy-done.17, bf16[8,256,64]{2,1,0:T(8,128)(2,1)S(1)} %span_attention.1.refs_1_.refs_7_, bf16[8,256,64]{2,1,0:T(8,128)(2,1)} %collective-permute-done.9.refs_2_, bf16[16,256,64]{2,1,0:T(8,128)(2,1)S(1)} %both_rows.1.refs_1_.refs_3_, ...), custom_call_target="tpu_custom_call" | custom-call | flops 268435456 | bytes 4194304 | tf_op jit(solution)/shard_map/context_out/pallas_call | solution.py:101
  88.3 1.1 copy-done.4
  89.4 2.9 %norm_up.1 = (bf16[256,1024]{1,0:T(8,128)(2,1)S(1)}, bf16[16,256,64]{2,1,0:T(8,128)(2,1)S(1)}) custom-call(s32[38]{0:T(128)S(1)} %copy-done.17, bf16[256,512]{1,0:T(8,128)(2,1)S(1)} %context_out.1.refs_1_, bf16[256,512]{1,0:T(8,128)(2,1)S(1)} %collective-permute-done.14.refs_2_, bf16[4,64,1536]{2,1,0:T(8,128)(2,1)S(1)} %copy-done.6, ...), custom_call_target="tpu_custom_call" | custom-call | flops 536870912 | bytes 3670016 | tf_op jit(solution)/shard_map/norm_up/pallas_call | solution.py:101
  92.4 1.0 collective-permute-done.18.refs_6_
  93.4 2.5 %down.1 = (f32[128,1024]{1,0:T(8,128)S(1)}, bf16[128,1024]{1,0:T(8,128)(2,1)S(1)}) custom-call(s32[38]{0:T(128)S(1)} %copy-done.17, bf16[16,256,64]{2,1,0:T(8,128)(2,1)S(1)} %get-tuple-element.35.refs_1_, bf16[256,1024]{1,0:T(8,128)(2,1)S(1)} %get-tuple-element.36.refs_2_, bf16[4,64,1280]{2,1,0:T(8,128)(2,1)} %get-tuple-element.39.refs_3_, ...), custom_call_target="tpu_custom_call" | custom-call | flops 536870912 | bytes 3670016 | tf_op jit(solution)/shard_map/down/pallas_call | solution.py:101
  96.0 2.0 collective-permute-start.20
  98.0 1.9 select_reduce_fusion.3
  99.9 1.7 norm_pool.1.refs_5_
  101.6 1.2 collective-permute-done.20.refs_4_
  102.8 1.3 join_proj.1.refs_4_
  104.3 8.8 %all-to-all-start = ((bf16[128,8,128]{2,1,0:T(8,128)(2,1)}), bf16[128,8,128]{2,1,0:T(8,128)(2,1)S(1)}, u32[]{:S(2)}, u32[]{:S(2)}) async-start(bf16[128,8,128]{2,1,0:T(8,128)(2,1)} %bitcast.8), calls=%async_computation | async-start | bytes 524288 | tf_op jit(solution)/shard_map/all_to_all | solution.py:683
  113.2 10.8 %all-to-all-done.refs_1_ = bf16[128,8,128]{2,1,0:T(8,128)(2,1)S(1)} async-done(((bf16[128,8,128]{2,1,0:T(8,128)(2,1)}), bf16[128,8,128]{2,1,0:T(8,128)(2,1)S(1)}, u32[]{:S(2)}, u32[]{:S(2)}) %all-to-all-start) | async-done | bytes 262176 | tf_op jit(solution)/shard_map/all_to_all | solution.py:683
  124.0 1.6 copy-done.7
  125.6 2.6 %embed.1.refs_1_ = bf16[128,512]{1,0:T(8,128)(2,1)S(1)} custom-call(s32[38]{0:T(128)S(1)} %copy-done.17, bf16[128,8,128]{2,1,0:T(8,128)(2,1)S(1)} %all-to-all-done.refs_1_, bf16[128,128]{1,0:T(8,128)(2,1)S(1)} %fusion.refs_2_, bf16[1024,1024]{1,0:T(8,128)(2,1)S(1)} %copy-done.7, bf16[4,4,64,256]{3,2,1,0:T(8,128)(2,1)S(1)} %join_proj.1.refs_4_, ...), custom_call_target="tpu_custom_call" | custom-call | flops 402653184 | bytes 3440640 | tf_op jit(solution)/shard_map/embed/pallas_call | solution.py:101
  128.9 2.6 %collective-permute-start.23 = (bf16[128,512]{1,0:T(8,128)(2,1)S(1)}, bf16[128,512]{1,0:T(8,128)(2,1)S(1)}, u32[]{:S(2)}, u32[]{:S(2)}) collective-permute-start(bf16[128,512]{1,0:T(8,128)(2,1)S(1)} %embed.1.refs_1_), channel_id=1, source_target_pairs={{0,3},{1,0},{2,1},{3,2},{4,7},{5,4},{6,5},{7,6},{8,11},{9,8},{10,9... | collective-permute-start | bytes 393224 | tf_op jit(solution)/shard_map/ppermute | solution.py:67
  132.2 2.2 %collective-permute-done.22.refs_2_ = bf16[128,512]{1,0:T(8,128)(2,1)S(1)} collective-permute-done((bf16[128,512]{1,0:T(8,128)(2,1)S(1)}, bf16[128,512]{1,0:T(8,128)(2,1)S(1)}, u32[]{:S(2)}, u32[]{:S(2)}) %collective-permute-start.22) | collective-permute-done | bytes 131104 | tf_op jit(solution)/shard_map/ppermute | solution.py:67
  134.4 1.0 collective-permute-done.23.refs_3_
  135.4 2.5 %collective-permute-done.24.refs_4_ = bf16[128,512]{1,0:T(8,128)(2,1)S(1)} collective-permute-done((bf16[128,512]{1,0:T(8,128)(2,1)S(1)}, bf16[128,512]{1,0:T(8,128)(2,1)S(1)}, u32[]{:S(2)}, u32[]{:S(2)}) %collective-permute-start.24) | collective-permute-done | bytes 131104 | tf_op jit(solution)/shard_map/ppermute | solution.py:67
  139.5 2.7 %collective-permute-start.27 = (bf16[4,128,512]{2,1,0:T(8,128)(2,1)S(1)}, bf16[4,128,512]{2,1,0:T(8,128)(2,1)}, u32[]{:S(2)}, u32[]{:S(2)}) collective-permute-start(bf16[4,128,512]{2,1,0:T(8,128)(2,1)S(1)} %join_columns.1.refs_1_), channel_id=1, source_target_pairs={{0,12},{1,13},{2,14},{3,15},{4,0},{5,1},{6,2},{7,3},{8,4},{9,5},{1... | collective-permute-start | bytes 1572872 | tf_op jit(solution)/shard_map/ppermute | solution.py:67
  143.3 5.8 %collective-permute-done.25.refs_1_ = bf16[4,128,512]{2,1,0:T(8,128)(2,1)} collective-permute-done((bf16[4,128,512]{2,1,0:T(8,128)(2,1)S(1)}, bf16[4,128,512]{2,1,0:T(8,128)(2,1)}, u32[]{:S(2)}, u32[]{:S(2)}) %collective-permute-start.25) | collective-permute-done | bytes 524320 | tf_op jit(solution)/shard_map/ppermute | solution.py:67
  149.3 3.4 %copy-done = bf16[8192,512]{1,0:T(8,128)(2,1)S(1)} copy-done((bf16[8192,512]{1,0:T(8,128)(2,1)S(1)}, bf16[8192,512]{1,0:T(8,128)(2,1)}, u32[]{:S(2)}) %copy-start) | copy-done | bytes 8388632
  152.7 1.2 project_own.1
  153.9 3.4 %copy-done.1 = bf16[8192,512]{1,0:T(8,128)(2,1)S(1)} copy-done((bf16[8192,512]{1,0:T(8,128)(2,1)S(1)}, bf16[8192,512]{1,0:T(8,128)(2,1)}, u32[]{:S(2)}) %copy-start.1) | copy-done | bytes 8388632
  157.4 2.5 %project_near.1 = (f32[128,512]{1,0:T(8,128)S(1)}, f32[128,128]{1,0:T(8,128)S(1)}, f32[128,1]{1,0:T(8,128)S(1)}) custom-call(s32[38]{0:T(128)S(1)} %copy-done.17, bf16[4,128,512]{2,1,0:T(8,128)(2,1)} %collective-permute-done.25.refs_1_, bf16[4,128,512]{2,1,0:T(8,128)(2,1)} %collective-permute-done.27.refs_2_, f32[16,1,512]{2,1,0:T(1,128)S(1)} %bitcast.25, ...), custom_call_target="tpu_custom_call" | custom-call | flops 671088640 | bytes 11895296 | tf_op jit(solution)/shard_map/project_near/pallas_call | solution.py:101
  159.9 1.2 last_keys.1
  161.5 1.3 last_queries.1.refs_1_
  162.8 2.8 %collective-permute-done.28.refs_3_ = bf16[2,128,64]{2,1,0:T(8,128)(2,1)S(1)} collective-permute-done((bf16[2,128,64]{2,1,0:T(8,128)(2,1)S(1)}, bf16[2,128,64]{2,1,0:T(8,128)(2,1)S(1)}, u32[]{:S(2)}, u32[]{:S(2)}) %collective-permute-start.28) | collective-permute-done | bytes 32800 | tf_op jit(solution)/shard_map/ppermute | solution.py:765
  165.6 3.6 %attend_out.1 = (bf16[32,8192]{1,0:T(8,128)(2,1)S(1)}, bf16[32,8192]{1,0:T(8,128)(2,1)}, bf16[32,8192]{1,0:T(8,128)(2,1)}, bf16[32,8192]{1,0:T(8,128)(2,1)}) custom-call(s32[38]{0:T(128)S(1)} %copy-done.17, bf16[128,512]{1,0:T(8,128)(2,1)S(1)} %last_queries.1.refs_1_, bf16[2,128,64]{2,1,0:T(8,128)(2,1)S(1)} %get-tuple-element.52.refs_2_, ...), custom_call_target="tpu_custom_call" | custom-call | flops 1073741824 | bytes 8683520 | tf_op jit(solution)/shard_map/attend_out/pallas_call | solution.py:101
  169.2 3.2 %collective-permute-start.30 = (bf16[32,8192]{1,0:T(8,128)(2,1)}, bf16[32,8192]{1,0:T(8,128)(2,1)S(1)}, u32[]{:S(2)}, u32[]{:S(2)}) collective-permute-start(bf16[32,8192]{1,0:T(8,128)(2,1)} %get-tuple-element.55), channel_id=1, source_target_pairs={{0,12},{1,13},{2,14},{3,15},{4,0},{5,1},{6,2},{7,3},{8,4},{9,5},{1... | collective-permute-start | bytes 1572872 | tf_op jit(solution)/shard_map/ppermute | solution.py:67
  172.5 1.5 collective-permute-start.31
  174.8 5.0 %collective-permute-done.29.refs_2_ = bf16[32,8192]{1,0:T(8,128)(2,1)S(1)} collective-permute-done((bf16[32,8192]{1,0:T(8,128)(2,1)}, bf16[32,8192]{1,0:T(8,128)(2,1)S(1)}, u32[]{:S(2)}, u32[]{:S(2)}) %collective-permute-start.29) | collective-permute-done | bytes 524320 | tf_op jit(solution)/shard_map/ppermute | solution.py:67
  179.8 5.3 %collective-permute-done.30.refs_3_ = bf16[32,8192]{1,0:T(8,128)(2,1)S(1)} collective-permute-done((bf16[32,8192]{1,0:T(8,128)(2,1)}, bf16[32,8192]{1,0:T(8,128)(2,1)S(1)}, u32[]{:S(2)}, u32[]{:S(2)}) %collective-permute-start.30) | collective-permute-done | bytes 524320 | tf_op jit(solution)/shard_map/ppermute | solution.py:67
  185.1 2.3 %collective-permute-done.31.refs_4_ = bf16[32,8192]{1,0:T(8,128)(2,1)S(1)} collective-permute-done((bf16[32,8192]{1,0:T(8,128)(2,1)}, bf16[32,8192]{1,0:T(8,128)(2,1)S(1)}, u32[]{:S(2)}, u32[]{:S(2)}) %collective-permute-start.31) | collective-permute-done | bytes 524320 | tf_op jit(solution)/shard_map/ppermute | solution.py:67
  188.3 3.2 %collective-permute-start.33 = (bf16[8,8192]{1,0:T(8,128)(2,1)S(1)}, bf16[8,8192]{1,0:T(8,128)(2,1)S(1)}, u32[]{:S(2)}, u32[]{:S(2)}) collective-permute-start(bf16[8,8192]{1,0:T(8,128)(2,1)S(1)} %get-tuple-element.59), channel_id=1, source_target_pairs={{0,3},{1,0},{2,1},{3,2},{4,7},{5,4},{6,5},{7,6},{8,11},{9,8},{10,9... | collective-permute-start | bytes 393224 | tf_op jit(solution)/shard_map/ppermute | solution.py:67
  192.3 2.2 %collective-permute-done.32.refs_2_ = bf16[8,8192]{1,0:T(8,128)(2,1)S(1)} collective-permute-done((bf16[8,8192]{1,0:T(8,128)(2,1)S(1)}, bf16[8,8192]{1,0:T(8,128)(2,1)S(1)}, u32[]{:S(2)}, u32[]{:S(2)}) %collective-permute-start.32) | collective-permute-done | bytes 131104 | tf_op jit(solution)/shard_map/ppermute | solution.py:67
  195.4 2.5 %collective-permute-done.34.refs_4_ = bf16[8,8192]{1,0:T(8,128)(2,1)S(1)} collective-permute-done((bf16[8,8192]{1,0:T(8,128)(2,1)S(1)}, bf16[8,8192]{1,0:T(8,128)(2,1)S(1)}, u32[]{:S(2)}, u32[]{:S(2)}) %collective-permute-start.34) | collective-permute-done | bytes 131104 | tf_op jit(solution)/shard_map/ppermute | solution.py:67
  198.0 1.3 finish.1
  (152 shorter events, 22.5 us)
Async XLA Ops:
  1.2 65.6 %copy-start.22 = (s32[16]{0:T(128)}, s32[16]{0:T(128)S(1)}, u32[]{:S(2)}) copy-start(s32[16]{0:T(128)S(1)} %broadcast_select_fusion.2) | copy-start | bytes 196
  1.3 1.0 copy-start.12
  2.9 0.7 copy-start.9
  3.6 67.0 %copy-start.24 = (s32[1024]{0:T(1024)S(1)}, s32[1024]{0:T(1024)}, u32[]{:S(2)}) copy-start(s32[1024]{0:T(1024)} %param.18) | copy-start | bytes 12292
  3.6 67.0 %copy-start.25 = (s32[8]{0:T(128)S(1)}, s32[8]{0:T(128)}, u32[]{:S(2)}) copy-start(s32[8]{0:T(128)} %param.20) | copy-start | bytes 100
  6.3 45.4 %copy-start.8 = (bf16[64,3584]{1,0:T(8,128)(2,1)S(1)}, bf16[64,3584]{1,0:T(8,128)(2,1)}, u32[]{:S(2)}) copy-start(bf16[64,3584]{1,0:T(8,128)(2,1)} %get-tuple-element.33.refs_1_) | copy-start | bytes 1376260
  6.3 15.4 %collective-permute-start.4 = (bf16[64,3584]{1,0:T(8,128)(2,1)}, bf16[64,3584]{1,0:T(8,128)(2,1)S(1)}, u32[]{:S(2)}, u32[]{:S(2)}) collective-permute-start(bf16[64,3584]{1,0:T(8,128)(2,1)} %get-tuple-element.33.refs_1_), channel_id=1, source_target_pairs={{0,1},{1,2},{2,3},{3,0},{4,5},{5,6},{6,7},{7,4},{8,9},{9,10},{10,1... | collective-permute-start | bytes 1376264 | tf_op jit(solution)/shard_map/ppermute | solution.py:67
  8.0 13.8 %collective-permute-start.5 = (bf16[64,3584]{1,0:T(8,128)(2,1)}, bf16[64,3584]{1,0:T(8,128)(2,1)S(1)}, u32[]{:S(2)}, u32[]{:S(2)}) collective-permute-start(bf16[64,3584]{1,0:T(8,128)(2,1)} %get-tuple-element.34), channel_id=1, source_target_pairs={{0,3},{1,0},{2,1},{3,2},{4,7},{5,4},{6,5},{7,6},{8,11},{9,8},{10,9... | collective-permute-start | bytes 1376264 | tf_op jit(solution)/shard_map/ppermute | solution.py:67
  9.6 8.8 %collective-permute-start.1 = (bf16[64,1536]{1,0:T(8,128)(2,1)}, bf16[64,1536]{1,0:T(8,128)(2,1)S(1)}, u32[]{:S(2)}, u32[]{:S(2)}) collective-permute-start(bf16[64,1536]{1,0:T(8,128)(2,1)} %copy-done.9), channel_id=1, source_target_pairs={{0,1},{1,2},{2,3},{3,0},{4,5},{5,6},{6,7},{7,4},{8,9},{9,10},{10,1... | collective-permute-start | bytes 589832 | tf_op jit(solution)/shard_map/ppermute | solution.py:67
  10.0 8.8 %collective-permute-start.2 = (bf16[64,1536]{1,0:T(8,128)(2,1)}, bf16[64,1536]{1,0:T(8,128)(2,1)S(1)}, u32[]{:S(2)}, u32[]{:S(2)}) collective-permute-start(bf16[64,1536]{1,0:T(8,128)(2,1)} %copy-done.9), channel_id=1, source_target_pairs={{0,3},{1,0},{2,1},{3,2},{4,7},{5,4},{6,5},{7,6},{8,11},{9,8},{10,9... | collective-permute-start | bytes 589832 | tf_op jit(solution)/shard_map/ppermute | solution.py:67
  12.8 9.0 %collective-permute-start.3 = (bf16[64,1536]{1,0:T(8,128)(2,1)}, bf16[64,1536]{1,0:T(8,128)(2,1)S(1)}, u32[]{:S(2)}, u32[]{:S(2)}) collective-permute-start(bf16[64,1536]{1,0:T(8,128)(2,1)} %copy-done.9), channel_id=1, source_target_pairs={{0,2},{1,3},{2,0},{3,1},{4,6},{5,7},{6,4},{7,5},{8,10},{9,11},{10,... | collective-permute-start | bytes 589832 | tf_op jit(solution)/shard_map/ppermute | solution.py:67
  21.8 0.9 copy-start.10
  23.4 32.8 %copy-start.26 = (bf16[64,1024]{1,0:T(8,128)(2,1)S(1)}, bf16[64,1024]{1,0:T(8,128)(2,1)}, u32[]{:S(2)}) copy-start(bf16[64,1024]{1,0:T(8,128)(2,1)} %get-tuple-element.38) | copy-start | bytes 393220
  23.4 43.4 %copy-start.17 = (s32[38]{0:T(128)S(1)}, s32[38]{0:T(128)}, u32[]{:S(2)}) copy-start(s32[38]{0:T(128)} %copy-done.14) | copy-start | bytes 460
  23.4 43.4 %copy-start.18 = (bf16[64,1024]{1,0:T(8,128)(2,1)S(1)}, bf16[64,1024]{1,0:T(8,128)(2,1)}, u32[]{:S(2)}) copy-start(bf16[64,1024]{1,0:T(8,128)(2,1)} %get-tuple-element.37.refs_5_) | copy-start | bytes 393220
  24.0 13.3 %collective-permute-start.6 = (bf16[4,64,1536]{2,1,0:T(8,128)(2,1)S(1)}, bf16[4,64,1536]{2,1,0:T(8,128)(2,1)S(1)}, u32[]{:S(2)}, u32[]{:S(2)}) collective-permute-start(bf16[4,64,1536]{2,1,0:T(8,128)(2,1)S(1)} %join_qkv.1.refs_2_), channel_id=1, source_target_pairs={{0,4},{1,5},{2,6},{3,7},{4,8},{5,9},{6,10},{7,11},{8,12},{9,13},{1... | collective-permute-start | bytes 2359304 | tf_op jit(solution)/shard_map/ppermute | solution.py:67
  25.5 24.6 %collective-permute-start.7 = (bf16[4,64,1536]{2,1,0:T(8,128)(2,1)S(1)}, bf16[4,64,1536]{2,1,0:T(8,128)(2,1)S(1)}, u32[]{:S(2)}, u32[]{:S(2)}) collective-permute-start(bf16[4,64,1536]{2,1,0:T(8,128)(2,1)S(1)} %join_qkv.1.refs_2_), channel_id=1, source_target_pairs={{0,12},{1,13},{2,14},{3,15},{4,0},{5,1},{6,2},{7,3},{8,4},{9,5},{1... | collective-permute-start | bytes 2359304 | tf_op jit(solution)/shard_map/ppermute | solution.py:67
  27.3 22.9 %collective-permute-start.8 = (bf16[4,64,1536]{2,1,0:T(8,128)(2,1)S(1)}, bf16[4,64,1536]{2,1,0:T(8,128)(2,1)S(1)}, u32[]{:S(2)}, u32[]{:S(2)}) collective-permute-start(bf16[4,64,1536]{2,1,0:T(8,128)(2,1)S(1)} %join_qkv.1.refs_2_), channel_id=1, source_target_pairs={{0,8},{1,9},{2,10},{3,11},{4,12},{5,13},{6,14},{7,15},{8,0},{9,1},... | collective-permute-start | bytes 2359304 | tf_op jit(solution)/shard_map/ppermute | solution.py:67
  29.1 22.7 %collective-permute-start.10 = (bf16[64,3584]{1,0:T(8,128)(2,1)S(1)}, bf16[64,3584]{1,0:T(8,128)(2,1)S(1)}, u32[]{:S(2)}, u32[]{:S(2)}) collective-permute-start(bf16[64,3584]{1,0:T(8,128)(2,1)S(1)} %collective-permute-done.5.refs_6_.refs_3_), channel_id=1, source_target_pairs={{0,3},{1,0},{2,1},{3,2},{4,7},{5,4},{6,5},{7,6},{8,11},{9,8},{10,9... | collective-permute-start | bytes 1376264 | tf_op jit(solution)/shard_map/ppermute | solution.py:67
  31.1 1.7 collective-permute-start
  32.8 1.0 copy-start.13
  52.4 14.4 %copy-start.5 = (bf16[4,64,1536]{2,1,0:T(8,128)(2,1)}, bf16[4,64,1536]{2,1,0:T(8,128)(2,1)S(1)}, u32[]{:S(2)}) copy-start(bf16[4,64,1536]{2,1,0:T(8,128)(2,1)S(1)} %join_middle.1.refs_4_.refs_3_) | copy-start | bytes 2359300
  52.4 14.4 %collective-permute-start.11 = (bf16[4,64,1536]{2,1,0:T(8,128)(2,1)S(1)}, bf16[4,64,1536]{2,1,0:T(8,128)(2,1)S(1)}, u32[]{:S(2)}, u32[]{:S(2)}) collective-permute-start(bf16[4,64,1536]{2,1,0:T(8,128)(2,1)S(1)} %join_middle.1.refs_4_.refs_3_), channel_id=1, source_target_pairs={{0,4},{1,5},{2,6},{3,7},{4,8},{5,9},{6,10},{7,11},{8,12},{9,13},{1... | collective-permute-start | bytes 2359304 | tf_op jit(solution)/shard_map/ppermute | solution.py:67
  54.6 12.1 %collective-permute-start.12 = (bf16[4,64,1536]{2,1,0:T(8,128)(2,1)S(1)}, bf16[4,64,1536]{2,1,0:T(8,128)(2,1)S(1)}, u32[]{:S(2)}, u32[]{:S(2)}) collective-permute-start(bf16[4,64,1536]{2,1,0:T(8,128)(2,1)S(1)} %join_middle.1.refs_4_.refs_3_), channel_id=1, source_target_pairs={{0,12},{1,13},{2,14},{3,15},{4,0},{5,1},{6,2},{7,3},{8,4},{9,5},{1... | collective-permute-start | bytes 2359304 | tf_op jit(solution)/shard_map/ppermute | solution.py:67
  56.2 7.9 %collective-permute-start.15 = (bf16[64,1024]{1,0:T(8,128)(2,1)S(1)}, bf16[64,1024]{1,0:T(8,128)(2,1)S(1)}, u32[]{:S(2)}, u32[]{:S(2)}) collective-permute-start(bf16[64,1024]{1,0:T(8,128)(2,1)S(1)} %copy-done.26), channel_id=1, source_target_pairs={{0,2},{1,3},{2,0},{3,1},{4,6},{5,7},{6,4},{7,5},{8,10},{9,11},{10,... | collective-permute-start | bytes 393224 | tf_op jit(solution)/shard_map/ppermute | solution.py:67
  66.8 20.0 %copy-start.3 = (bf16[4,64,1536]{2,1,0:T(8,128)(2,1)}, bf16[4,64,1536]{2,1,0:T(8,128)(2,1)S(1)}, u32[]{:S(2)}) copy-start(bf16[4,64,1536]{2,1,0:T(8,128)(2,1)S(1)} %collective-permute-done.12.refs_6_.refs_5_.refs_9_) | copy-start | bytes 2359300
  68.3 0.9 copy-start.19
  69.2 17.7 %copy-start.20 = (bf16[4,64,256]{2,1,0:T(8,128)(2,1)}, bf16[4,64,256]{2,1,0:T(8,128)(2,1)S(1)}, u32[]{:S(2)}) copy-start(bf16[4,64,256]{2,1,0:T(8,128)(2,1)S(1)} %get-tuple-element.44) | copy-start | bytes 393220
  69.2 12.1 %collective-permute-start.16 = (bf16[4,64,1280]{2,1,0:T(8,128)(2,1)}, bf16[4,64,1280]{2,1,0:T(8,128)(2,1)}, u32[]{:S(2)}, u32[]{:S(2)}) collective-permute-start(bf16[4,64,1280]{2,1,0:T(8,128)(2,1)} %get-tuple-element.39.refs_3_), channel_id=1, source_target_pairs={{0,4},{1,5},{2,6},{3,7},{4,8},{5,9},{6,10},{7,11},{8,12},{9,13},{1... | collective-permute-start | bytes 1966088 | tf_op jit(solution)/shard_map/ppermute | solution.py:67
  70.9 12.4 %collective-permute-start.13 = (bf16[4,64,1536]{2,1,0:T(8,128)(2,1)S(1)}, bf16[4,64,1536]{2,1,0:T(8,128)(2,1)}, u32[]{:S(2)}, u32[]{:S(2)}) collective-permute-start(bf16[4,64,1536]{2,1,0:T(8,128)(2,1)S(1)} %collective-permute-done.12.refs_6_.refs_5_.refs_9_), channel_id=1, source_target_pairs={{0,12},{1,13},{2,14},{3,15},{4,0},{5,1},{6,2},{7,3},{8,4},{9,5},{1... | collective-permute-start | bytes 2359304 | tf_op jit(solution)/shard_map/ppermute | solution.py:67
  73.4 9.9 %collective-permute-start.9 = (bf16[8,256,64]{2,1,0:T(8,128)(2,1)S(1)}, bf16[8,256,64]{2,1,0:T(8,128)(2,1)}, u32[]{:S(2)}, u32[]{:S(2)}) collective-permute-start(bf16[8,256,64]{2,1,0:T(8,128)(2,1)S(1)} %span_attention.1.refs_1_.refs_7_), channel_id=1, source_target_pairs={{0,16},{16,0},{32,48},{48,32},{64,80},{80,64},{96,112},{112,96},{1... | collective-permute-start | bytes 786440 | tf_op jit(solution)/shard_map/ppermute | solution.py:71
  73.4 18.9 %collective-permute-start.17 = (bf16[4,64,1280]{2,1,0:T(8,128)(2,1)}, bf16[4,64,1280]{2,1,0:T(8,128)(2,1)}, u32[]{:S(2)}, u32[]{:S(2)}) collective-permute-start(bf16[4,64,1280]{2,1,0:T(8,128)(2,1)} %copy-done.19), channel_id=1, source_target_pairs={{0,12},{1,13},{2,14},{3,15},{4,0},{5,1},{6,2},{7,3},{8,4},{9,5},{1... | collective-permute-start | bytes 1966088 | tf_op jit(solution)/shard_map/ppermute | solution.py:67
  81.3 12.1 %collective-permute-start.18 = (bf16[4,64,1280]{2,1,0:T(8,128)(2,1)}, bf16[4,64,1280]{2,1,0:T(8,128)(2,1)}, u32[]{:S(2)}, u32[]{:S(2)}) collective-permute-start(bf16[4,64,1280]{2,1,0:T(8,128)(2,1)} %collective-permute-done.16.refs_4_.refs_2_), channel_id=1, source_target_pairs={{0,4},{1,5},{2,6},{3,7},{4,8},{5,9},{6,10},{7,11},{8,12},{9,13},{1... | collective-permute-start | bytes 1966088 | tf_op jit(solution)/shard_map/ppermute | solution.py:67
  83.3 1.1 copy-start.6
  86.5 45.6 %copy-start.21 = (s32[8,8,8]{2,1,0:T(8,128)S(1)}, s32[8,8,8]{2,1,0:T(8,128)}, u32[]{:S(2)}) copy-start(s32[8,8,8]{2,1,0:T(8,128)} %param.21) | copy-start | bytes 6148
  86.5 1.8 collective-permute-start.14
  87.5 61.8 %copy-start.2 = (bf16[2,8192,64]{1,2,0:T(8,128)(2,1)S(1)}, bf16[2,8192,64]{1,2,0:T(8,128)(2,1)}, u32[]{:S(2)}) copy-start(bf16[2,8192,64]{1,2,0:T(8,128)(2,1)} %param.30) | copy-start | bytes 6291460
  88.3 1.1 copy-start.4
  89.4 59.9 %copy-start.11 = (f32[8192]{0:T(1024)S(1)}, f32[8192]{0:T(1024)}, u32[]{:S(2)}) copy-start(f32[8192]{0:T(1024)} %param.28) | copy-start | bytes 98308
  95.9 4.0 %collective-permute-start.19 = (bf16[128,1024]{1,0:T(8,128)(2,1)S(1)}, bf16[128,1024]{1,0:T(8,128)(2,1)S(1)}, u32[]{:S(2)}, u32[]{:S(2)}) collective-permute-start(bf16[128,1024]{1,0:T(8,128)(2,1)S(1)} %get-tuple-element.42), channel_id=1, source_target_pairs={{0,16},{16,0},{32,48},{48,32},{64,80},{80,64},{96,112},{112,96},{1... | collective-permute-start | bytes 786440 | tf_op jit(solution)/shard_map/ppermute | solution.py:71
  96.0 6.8 %collective-permute-start.20 = (bf16[4,64,256]{2,1,0:T(8,128)(2,1)}, bf16[4,64,256]{2,1,0:T(8,128)(2,1)S(1)}, u32[]{:S(2)}, u32[]{:S(2)}) collective-permute-start(bf16[4,64,256]{2,1,0:T(8,128)(2,1)} %copy-done.20), channel_id=1, source_target_pairs={{0,8},{1,9},{2,10},{3,11},{4,12},{5,13},{6,14},{7,15},{8,0},{9,1},... | collective-permute-start | bytes 393224 | tf_op jit(solution)/shard_map/ppermute | solution.py:67
  104.1 19.9 %collective-permute-start.21 = (bf16[4,4,64,256]{3,2,1,0:T(8,128)(2,1)S(1)}, bf16[4,4,64,256]{3,2,1,0:T(8,128)(2,1)}, u32[]{:S(2)}, u32[]{:S(2)}) collective-permute-start(bf16[4,4,64,256]{3,2,1,0:T(8,128)(2,1)S(1)} %join_proj.1.refs_4_), channel_id=1, source_target_pairs={{0,16},{16,0},{32,48},{48,32},{64,80},{80,64},{96,112},{112,96},{1... | collective-permute-start | bytes 1572872 | tf_op jit(solution)/shard_map/ppermute | solution.py:71
  104.3 19.7 %all-to-all-start = ((bf16[128,8,128]{2,1,0:T(8,128)(2,1)}), bf16[128,8,128]{2,1,0:T(8,128)(2,1)S(1)}, u32[]{:S(2)}, u32[]{:S(2)}) async-start(bf16[128,8,128]{2,1,0:T(8,128)(2,1)} %bitcast.8), calls=%async_computation | async-start | bytes 524288 | tf_op jit(solution)/shard_map/all_to_all | solution.py:683
  124.0 1.6 copy-start.7
  128.2 6.2 %collective-permute-start.22 = (bf16[128,512]{1,0:T(8,128)(2,1)S(1)}, bf16[128,512]{1,0:T(8,128)(2,1)S(1)}, u32[]{:S(2)}, u32[]{:S(2)}) collective-permute-start(bf16[128,512]{1,0:T(8,128)(2,1)S(1)} %embed.1.refs_1_), channel_id=1, source_target_pairs={{0,1},{1,2},{2,3},{3,0},{4,5},{5,6},{6,7},{7,4},{8,9},{9,10},{10,1... | collective-permute-start | bytes 393224 | tf_op jit(solution)/shard_map/ppermute | solution.py:67
  128.9 6.5 %collective-permute-start.23 = (bf16[128,512]{1,0:T(8,128)(2,1)S(1)}, bf16[128,512]{1,0:T(8,128)(2,1)S(1)}, u32[]{:S(2)}, u32[]{:S(2)}) collective-permute-start(bf16[128,512]{1,0:T(8,128)(2,1)S(1)} %embed.1.refs_1_), channel_id=1, source_target_pairs={{0,3},{1,0},{2,1},{3,2},{4,7},{5,4},{6,5},{7,6},{8,11},{9,8},{10,9... | collective-permute-start | bytes 393224 | tf_op jit(solution)/shard_map/ppermute | solution.py:67
  131.5 6.5 %collective-permute-start.24 = (bf16[128,512]{1,0:T(8,128)(2,1)S(1)}, bf16[128,512]{1,0:T(8,128)(2,1)S(1)}, u32[]{:S(2)}, u32[]{:S(2)}) collective-permute-start(bf16[128,512]{1,0:T(8,128)(2,1)S(1)} %embed.1.refs_1_), channel_id=1, source_target_pairs={{0,2},{1,3},{2,0},{3,1},{4,6},{5,7},{6,4},{7,5},{8,10},{9,11},{10,... | collective-permute-start | bytes 393224 | tf_op jit(solution)/shard_map/ppermute | solution.py:67
  138.5 10.6 %collective-permute-start.25 = (bf16[4,128,512]{2,1,0:T(8,128)(2,1)S(1)}, bf16[4,128,512]{2,1,0:T(8,128)(2,1)}, u32[]{:S(2)}, u32[]{:S(2)}) collective-permute-start(bf16[4,128,512]{2,1,0:T(8,128)(2,1)S(1)} %join_columns.1.refs_1_), channel_id=1, source_target_pairs={{0,4},{1,5},{2,6},{3,7},{4,8},{5,9},{6,10},{7,11},{8,12},{9,13},{1... | collective-permute-start | bytes 1572872 | tf_op jit(solution)/shard_map/ppermute | solution.py:67
  139.5 14.4 %collective-permute-start.27 = (bf16[4,128,512]{2,1,0:T(8,128)(2,1)S(1)}, bf16[4,128,512]{2,1,0:T(8,128)(2,1)}, u32[]{:S(2)}, u32[]{:S(2)}) collective-permute-start(bf16[4,128,512]{2,1,0:T(8,128)(2,1)S(1)} %join_columns.1.refs_1_), channel_id=1, source_target_pairs={{0,12},{1,13},{2,14},{3,15},{4,0},{5,1},{6,2},{7,3},{8,4},{9,5},{1... | collective-permute-start | bytes 1572872 | tf_op jit(solution)/shard_map/ppermute | solution.py:67
  149.1 10.8 %collective-permute-start.26 = (bf16[4,128,512]{2,1,0:T(8,128)(2,1)}, bf16[4,128,512]{2,1,0:T(8,128)(2,1)S(1)}, u32[]{:S(2)}, u32[]{:S(2)}) collective-permute-start(bf16[4,128,512]{2,1,0:T(8,128)(2,1)} %collective-permute-done.25.refs_1_), channel_id=1, source_target_pairs={{0,4},{1,5},{2,6},{3,7},{4,8},{5,9},{6,10},{7,11},{8,12},{9,13},{1... | collective-permute-start | bytes 1572872 | tf_op jit(solution)/shard_map/ppermute | solution.py:67
  149.3 3.4 %copy-start = (bf16[8192,512]{1,0:T(8,128)(2,1)S(1)}, bf16[8192,512]{1,0:T(8,128)(2,1)}, u32[]{:S(2)}) copy-start(bf16[8192,512]{1,0:T(8,128)(2,1)} %refs_3_.7) | copy-start | bytes 25165828
  152.7 8.7 %slice-start = ((s8[8388608]{0:T(1024)(128)(4,1)}), s8[4194304]{0:T(1024)(128)(4,1)S(1)}, s32[]{:S(2)}) async-start(s8[8388608]{0:T(1024)(128)(4,1)} %bitcast.17), calls=%async_computation.1 | async-start | bytes 8388608
  153.9 3.4 %copy-start.1 = (bf16[8192,512]{1,0:T(8,128)(2,1)S(1)}, bf16[8192,512]{1,0:T(8,128)(2,1)}, u32[]{:S(2)}) copy-start(bf16[8192,512]{1,0:T(8,128)(2,1)} %refs_3_.7) | copy-start | bytes 25165828
  157.4 4.1 %slice-start.1 = ((s8[8388608]{0:T(1024)(128)(4,1)}), s8[4194304]{0:T(1024)(128)(4,1)S(1)}, s32[]{:S(2)}) async-start(s8[8388608]{0:T(1024)(128)(4,1)} %bitcast.17), calls=%async_computation.2 | async-start | bytes 8388608
  157.4 8.3 %slice-start.2 = ((s8[8388608]{0:T(1024)(128)(4,1)}), s8[4194304]{0:T(1024)(128)(4,1)S(1)}, s32[]{:S(2)}) async-start(s8[8388608]{0:T(1024)(128)(4,1)} %bitcast.22), calls=%async_computation.3 | async-start | bytes 8388608
  159.9 5.8 %slice-start.3 = ((s8[8388608]{0:T(1024)(128)(4,1)}), s8[4194304]{0:T(1024)(128)(4,1)S(1)}, s32[]{:S(2)}) async-start(s8[8388608]{0:T(1024)(128)(4,1)} %bitcast.22), calls=%async_computation.4 | async-start | bytes 8388608
  161.0 4.6 %collective-permute-start.28 = (bf16[2,128,64]{2,1,0:T(8,128)(2,1)S(1)}, bf16[2,128,64]{2,1,0:T(8,128)(2,1)S(1)}, u32[]{:S(2)}, u32[]{:S(2)}) collective-permute-start(bf16[2,128,64]{2,1,0:T(8,128)(2,1)S(1)} %get-tuple-element.52.refs_2_), channel_id=1, source_target_pairs={{0,1},{1,0},{2,3},{3,2},{4,5},{5,4},{6,7},{7,6},{8,9},{9,8},{10,11... | collective-permute-start | bytes 98312 | tf_op jit(solution)/shard_map/ppermute | solution.py:765
  161.5 12.5 %copy-start.23 = (s32[16]{0:T(128)S(1)}, s32[16]{0:T(128)}, u32[]{:S(2)}) copy-start(s32[16]{0:T(128)} %copy-done.22) | copy-start | bytes 196
  169.2 10.6 %collective-permute-start.29 = (bf16[32,8192]{1,0:T(8,128)(2,1)}, bf16[32,8192]{1,0:T(8,128)(2,1)S(1)}, u32[]{:S(2)}, u32[]{:S(2)}) collective-permute-start(bf16[32,8192]{1,0:T(8,128)(2,1)} %get-tuple-element.54), channel_id=1, source_target_pairs={{0,4},{1,5},{2,6},{3,7},{4,8},{5,9},{6,10},{7,11},{8,12},{9,13},{1... | collective-permute-start | bytes 1572872 | tf_op jit(solution)/shard_map/ppermute | solution.py:67
  169.2 15.9 %collective-permute-start.30 = (bf16[32,8192]{1,0:T(8,128)(2,1)}, bf16[32,8192]{1,0:T(8,128)(2,1)S(1)}, u32[]{:S(2)}, u32[]{:S(2)}) collective-permute-start(bf16[32,8192]{1,0:T(8,128)(2,1)} %get-tuple-element.55), channel_id=1, source_target_pairs={{0,12},{1,13},{2,14},{3,15},{4,0},{5,1},{6,2},{7,3},{8,4},{9,5},{1... | collective-permute-start | bytes 1572872 | tf_op jit(solution)/shard_map/ppermute | solution.py:67
  172.5 14.9 %collective-permute-start.31 = (bf16[32,8192]{1,0:T(8,128)(2,1)}, bf16[32,8192]{1,0:T(8,128)(2,1)S(1)}, u32[]{:S(2)}, u32[]{:S(2)}) collective-permute-start(bf16[32,8192]{1,0:T(8,128)(2,1)} %get-tuple-element.56), channel_id=1, source_target_pairs={{0,8},{1,9},{2,10},{3,11},{4,12},{5,13},{6,14},{7,15},{8,0},{9,1},... | collective-permute-start | bytes 1572872 | tf_op jit(solution)/shard_map/ppermute | solution.py:67
  188.2 6.2 %collective-permute-start.32 = (bf16[8,8192]{1,0:T(8,128)(2,1)S(1)}, bf16[8,8192]{1,0:T(8,128)(2,1)S(1)}, u32[]{:S(2)}, u32[]{:S(2)}) collective-permute-start(bf16[8,8192]{1,0:T(8,128)(2,1)S(1)} %get-tuple-element.58), channel_id=1, source_target_pairs={{0,1},{1,2},{2,3},{3,0},{4,5},{5,6},{6,7},{7,4},{8,9},{9,10},{10,1... | collective-permute-start | bytes 393224 | tf_op jit(solution)/shard_map/ppermute | solution.py:67
  188.3 7.1 %collective-permute-start.33 = (bf16[8,8192]{1,0:T(8,128)(2,1)S(1)}, bf16[8,8192]{1,0:T(8,128)(2,1)S(1)}, u32[]{:S(2)}, u32[]{:S(2)}) collective-permute-start(bf16[8,8192]{1,0:T(8,128)(2,1)S(1)} %get-tuple-element.59), channel_id=1, source_target_pairs={{0,3},{1,0},{2,1},{3,2},{4,7},{5,4},{6,5},{7,6},{8,11},{9,8},{10,9... | collective-permute-start | bytes 393224 | tf_op jit(solution)/shard_map/ppermute | solution.py:67
  191.5 6.5 %collective-permute-start.34 = (bf16[8,8192]{1,0:T(8,128)(2,1)S(1)}, bf16[8,8192]{1,0:T(8,128)(2,1)S(1)}, u32[]{:S(2)}, u32[]{:S(2)}) collective-permute-start(bf16[8,8192]{1,0:T(8,128)(2,1)S(1)} %get-tuple-element.60), channel_id=1, source_target_pairs={{0,2},{1,3},{2,0},{3,1},{4,6},{5,7},{6,4},{7,5},{8,10},{9,11},{10,... | collective-permute-start | bytes 393224 | tf_op jit(solution)/shard_map/ppermute | solution.py:67
  (3 other events, 1.9 us)

commit v6 on v5

--- a/solution.py
+++ b/solution.py
@@ -231,12 +231,10 @@
     return [(power / total).astype(jnp.bfloat16) for power, total in zip(powers, sums)]
 
 
-def span_qkv(info, pieces, w0, w1, w2, w3, mixed):
-    mixed[...] = ring_dot(info, pieces, (w0, w1, w2, w3), 0, w0.shape[2]).astype(jnp.bfloat16)
-
-
-def span_attention(info, mixed, context):
-    third = mixed.shape[1] // 3
+def span_attention(info, pieces, w0, w1, w2, w3, context, mixed):
+    cols = w0.shape[2]
+    third = cols // 3
+    mixed[...] = ring_dot(info, pieces, (w0, w1, w2, w3), 0, cols).astype(jnp.bfloat16)
     size = context.shape[2]
     half = mixed.shape[0] // 2
     span = 16
@@ -587,8 +585,8 @@
         after=[own_qkv],
     )
     qkv_ring = short_ring(own_qkv)
-    rest_right = to_ring(rest_down, 1, -1)
-    rest_ring = [rest_up, to_ring(rest_up, 1, 1), rest_right, to_ring(rest_right, 1, -1)]
+    rest_left = to_ring(rest_up, 1, 1)
+    rest_ring = [rest_up, rest_left, to_ring(rest_down, 1, -1), to_ring(rest_left, 1, 1)]
     beyond_cols = to_ring(beyond_cols, 1, 2)
     qkv_block = whole_call(
         join_blocks,
@@ -597,37 +595,31 @@
         qkv_ring,
         shape_of((SIDE, share, 3 * width // 2)),
         limit=6,
-        after=rest_ring[1:3],
     )
     all_rows = 2 * spans * span_size
 
-    qkv = [qkv_block] + [to_ring(qkv_block, 2, distance) for distance in (1, -1, 2)]
-    mixed = whole_call(
-        span_qkv,
-        "span_qkv",
-        info,
-        [token_pieces, *qkv],
-        shape_of((all_rows, 3 * width // 2)),
-        flops=2 * all_rows * width * 3 * width // 2,
-    )
+    qkv_right = to_ring(qkv_block, 2, -1)
+    qkv = [qkv_block, to_ring(qkv_block, 2, 1), qkv_right, to_ring(qkv_right, 2, -1)]
+    middle_block = whole_call(
+        join_middle,
+        "join_middle",
+        info,
+        rest_ring,
+        shape_of((SIDE, share, middle_cols)),
+        limit=8,
+        after=[*qkv[1:3], token_pieces],
+    )
+    left = to_ring(middle_block, 2, 1)
+    middle = [middle_block, left, to_ring(middle_block, 2, -1), to_ring(left, 2, 1)]
     context = whole_call(
         span_attention,
         "span_attention",
         info,
-        [mixed],
+        [token_pieces, *qkv],
         shape_of((tensor_count // 2, all_rows, share)),
-    )
-    middle_block = whole_call(
-        join_middle,
-        "join_middle",
-        info,
-        rest_ring,
-        shape_of((SIDE, share, middle_cols)),
-        limit=8,
-        after=[mixed],
-    )
-    right = to_ring(middle_block, 2, -1)
-    middle = [middle_block, to_ring(middle_block, 2, 1), right, to_ring(right, 2, -1)]
+        [pltpu.VMEM((all_rows, 3 * width // 2), jnp.bfloat16)],
+        flops=2 * all_rows * width * 3 * width // 2,
+    )
     lower_shape = shape_of((SIDE, share, width + half_cols))
     far_shape = shape_of((SIDE, share, half_cols))
     lower_up, lower_down, far_kept, far_beyond = whole_call(
@@ -637,7 +629,7 @@
         [*rest_ring, kept_cols, beyond_cols],
         (lower_shape, lower_shape, far_shape, far_shape),
         limit=8,
-        after=[context, *middle[1:3]],
+        after=[context],
     )
     lower_left = to_ring(lower_up, 2, 1)
     lower = [lower_up, lower_left, to_ring(lower_down, 2, -1), to_ring(lower_left, 2, 1)]

time: 200 us -> 193 us (0.965)
  waiting for transfers between devices: 85.3 us -> 77.4 us
  starting transfers between devices: 50.2 us -> 43.5 us
  other arithmetic: 6.76 us -> 11.7 us
  local copies, waits for them, and re-layouts: 19.9 us -> 22.6 us
    ppermute x29, waiting for transfers between devices: 69.2 us -> 62.4 us  [to_ring(): return lax.ppermute(value, AXES, ring_pairs(phase, distance))]
    ppermute x29, starting transfers between devices: 40.6 us -> 34.7 us  [to_ring(): return lax.ppermute(value, AXES, ring_pairs(phase, distance))]
    pallas_call x22 -> x21, Pallas kernels: 35.9 us -> 35.6 us  [whole_call(): pl.pallas_call(run, name=name, out_shape=outs, in_specs=[SMEM] + [VMEM] *...]
    unnamed x62 -> x60, local copies, waits for them, and re-layouts: 16.5 us -> 16.2 us
  transfers between devices with their start and end apart: 36 -> 36, of which waited for: 24 -> 24; matrix products, arithmetic and copies ran while one was open for 4% -> 8% of each run, Pallas kernels for 8% -> 11%
where the time goes in v6:
time: 193 us; the launch traced here: 192 us
  waiting for transfers between devices  77.4 us (40%)
  starting transfers between devices  43.5 us (23%)
  Pallas kernels  35.6 us (18%)
  local copies, waits for them, and re-layouts  22.6 us (12%)
  other arithmetic  11.7 us (6%)
    ppermute x29, waiting for transfers between devices, to_ring(): return lax.ppermute(value, AXES, ring_pairs(phase, distance))  62.4 us
    pallas_call x21, Pallas kernels, whole_call(): pl.pallas_call(run, name=name, out_shape=outs, in_specs=[SMEM] + [VMEM] *...  35.6 us
    ppermute x29, starting transfers between devices, to_ring(): return lax.ppermute(value, AXES, ring_pairs(phase, distance))  34.7 us
    unnamed x60, local copies, waits for them, and re-layouts  16.2 us
    all_to_all x1, waiting for transfers between devices, local(): lax.all_to_all(outgoing.reshape(device_count, width // 128, 128), AXES, 0...  10.2 us
    all_to_all x1, starting transfers between devices, local(): lax.all_to_all(outgoing.reshape(device_count, width // 128, 128), AXES, 0...  7.86 us
  transfers between devices with their start and end apart: 36, of which 24 were waited for; matrix products, arithmetic and copies ran while one was open for 8% of the time, Pallas kernels for 11%

profile of v6, /device:TPU:0, one launch (start us, length us, event | category | flops | bytes accessed | tf_op | source)
XLA Modules:
  0.0 192.0 jit_solution(1495127068846776250)
XLA Ops:
  0.0 1.2 broadcast_add_fusion.2
  1.9 1.0 copy-done.10
  3.5 1.7 collective-permute-start.1
  5.2 1.6 collective-permute-start.2
  6.8 2.1 %collective-permute-start.3 = (bf16[64,1536]{1,0:T(8,128)(2,1)S(1)}, bf16[64,1536]{1,0:T(8,128)(2,1)S(1)}, u32[]{:S(2)}, u32[]{:S(2)}) collective-permute-start(bf16[64,1536]{1,0:T(8,128)(2,1)S(1)} %take_qkv.1.refs_1_.refs_5_), channel_id=1, source_target_pairs={{0,2},{1,3},{2,0},{3,1},{4,6},{5,7},{6,4},{7,5},{8,10},{9,11},{10,... | collective-permute-start | bytes 589832 | tf_op jit(solution)/shard_map/ppermute | solution.py:67
  8.8 1.6 collective-permute-done.1.refs_2_
  10.9 3.1 %collective-permute-done.3.refs_4_ = bf16[64,1536]{1,0:T(8,128)(2,1)S(1)} collective-permute-done((bf16[64,1536]{1,0:T(8,128)(2,1)S(1)}, bf16[64,1536]{1,0:T(8,128)(2,1)S(1)}, u32[]{:S(2)}, u32[]{:S(2)}) %collective-permute-start.3) | collective-permute-done | bytes 196640 | tf_op jit(solution)/shard_map/ppermute | solution.py:67
  14.6 2.9 %collective-permute-start.5 = (bf16[4,64,1536]{2,1,0:T(8,128)(2,1)S(1)}, bf16[4,64,1536]{2,1,0:T(8,128)(2,1)}, u32[]{:S(2)}, u32[]{:S(2)}) collective-permute-start(bf16[4,64,1536]{2,1,0:T(8,128)(2,1)S(1)} %join_qkv.1.refs_2_), channel_id=1, source_target_pairs={{0,12},{1,13},{2,14},{3,15},{4,0},{5,1},{6,2},{7,3},{8,4},{9,5},{1... | collective-permute-start | bytes 2359304 | tf_op jit(solution)/shard_map/ppermute | solution.py:67
  17.5 2.7 %take_rest.1 = (bf16[64,3584]{1,0:T(8,128)(2,1)}, bf16[64,3584]{1,0:T(8,128)(2,1)}, bf16[64,1024]{1,0:T(8,128)(2,1)}, bf16[64,1024]{1,0:T(8,128)(2,1)}) custom-call(s32[38]{0:T(128)} %copy-done.12, bf16[64,1024]{1,0:T(8,128)(2,1)} %refs_1_.3, bf16[64,2048]{1,0:T(8,128)(2,1)} %refs_2_.1, bf16[128,1024]{1,0:T(8,128)(2,1)} %refs_3_.4, ...), custom_call_target="tpu_custom_call" | custom-call | bytes 1703936 | tf_op jit(solution)/shard_map/take_rest/pallas_call | solution.py:101
  20.2 1.2 collective-permute-start.8
  21.4 2.0 %collective-permute-start.9 = (bf16[64,3584]{1,0:T(8,128)(2,1)}, bf16[64,3584]{1,0:T(8,128)(2,1)S(1)}, u32[]{:S(2)}, u32[]{:S(2)}) collective-permute-start(bf16[64,3584]{1,0:T(8,128)(2,1)} %get-tuple-element.34), channel_id=1, source_target_pairs={{0,3},{1,0},{2,1},{3,2},{4,7},{5,4},{6,5},{7,6},{8,11},{9,8},{10,9... | collective-permute-start | bytes 1376264 | tf_op jit(solution)/shard_map/ppermute | solution.py:67
  23.4 11.6 %collective-permute-done.8.refs_2_ = bf16[64,3584]{1,0:T(8,128)(2,1)S(1)} collective-permute-done((bf16[64,3584]{1,0:T(8,128)(2,1)}, bf16[64,3584]{1,0:T(8,128)(2,1)S(1)}, u32[]{:S(2)}, u32[]{:S(2)}) %collective-permute-start.8) | collective-permute-done | bytes 458784 | tf_op jit(solution)/shard_map/ppermute | solution.py:67
  35.9 1.7 collective-permute-done.refs_2_
  37.7 0.9 copy-done.11
  39.2 0.9 both_rows.1.refs_1_.refs_7_.refs_3_
  40.1 4.6 %collective-permute-done.10.refs_4_ = bf16[64,3584]{1,0:T(8,128)(2,1)S(1)} collective-permute-done((bf16[64,3584]{1,0:T(8,128)(2,1)S(1)}, bf16[64,3584]{1,0:T(8,128)(2,1)S(1)}, u32[]{:S(2)}, u32[]{:S(2)}) %collective-permute-start.10) | collective-permute-done | bytes 458784 | tf_op jit(solution)/shard_map/ppermute | solution.py:67
  44.8 1.0 copy-done.6
  46.6 2.1 %collective-permute-done.6.refs_5_ = bf16[4,64,1536]{2,1,0:T(8,128)(2,1)S(1)} collective-permute-done((bf16[4,64,1536]{2,1,0:T(8,128)(2,1)}, bf16[4,64,1536]{2,1,0:T(8,128)(2,1)S(1)}, u32[]{:S(2)}, u32[]{:S(2)}) %collective-permute-start.6) | collective-permute-done | bytes 786464 | tf_op jit(solution)/shard_map/ppermute | solution.py:67
  48.7 1.1 copy-done.4
  49.8 3.2 %span_attention.1.refs_1_.refs_7_ = bf16[8,256,64]{2,1,0:T(8,128)(2,1)S(1)} custom-call(s32[38]{0:T(128)S(1)} %copy-done.13, bf16[16,256,64]{2,1,0:T(8,128)(2,1)S(1)} %both_rows.1.refs_1_.refs_7_.refs_3_, bf16[4,64,1536]{2,1,0:T(8,128)(2,1)S(1)} %copy-done.4, bf16[4,64,1536]{2,1,0:T(8,128)(2,1)S(1)} %collective-permute-done.4.refs_3_.refs_5_, ...), custom_call_target="tpu_custom_call" | custom-call | flops 805306368 | bytes 3670016 | tf_op jit(solution)/shard_map/span_attention/pallas_call | solution.py:101
  53.1 1.6 collective-permute-done.15.refs_6_
  54.7 1.5 join_lower.1
  58.6 2.7 %collective-permute-start.12 = (bf16[4,64,1536]{2,1,0:T(8,128)(2,1)S(1)}, bf16[4,64,1536]{2,1,0:T(8,128)(2,1)}, u32[]{:S(2)}, u32[]{:S(2)}) collective-permute-start(bf16[4,64,1536]{2,1,0:T(8,128)(2,1)S(1)} %join_middle.1.refs_4_.refs_3_), channel_id=1, source_target_pairs={{0,12},{1,13},{2,14},{3,15},{4,0},{5,1},{6,2},{7,3},{8,4},{9,5},{1... | collective-permute-start | bytes 2359304 | tf_op jit(solution)/shard_map/ppermute | solution.py:67
  62.0 3.3 %collective-permute-start.17 = (bf16[4,64,1280]{2,1,0:T(8,128)(2,1)}, bf16[4,64,1280]{2,1,0:T(8,128)(2,1)}, u32[]{:S(2)}, u32[]{:S(2)}) collective-permute-start(bf16[4,64,1280]{2,1,0:T(8,128)(2,1)} %copy-done.19), channel_id=1, source_target_pairs={{0,12},{1,13},{2,14},{3,15},{4,0},{5,1},{6,2},{7,3},{8,4},{9,5},{1... | collective-permute-start | bytes 1966088 | tf_op jit(solution)/shard_map/ppermute | solution.py:67
  65.3 4.5 %collective-permute-done.16.refs_4_.refs_2_ = bf16[4,64,1280]{2,1,0:T(8,128)(2,1)S(1)} collective-permute-done((bf16[4,64,1280]{2,1,0:T(8,128)(2,1)}, bf16[4,64,1280]{2,1,0:T(8,128)(2,1)S(1)}, u32[]{:S(2)}, u32[]{:S(2)}) %collective-permute-start.16) | collective-permute-done | bytes 655392 | tf_op jit(solution)/shard_map/ppermute | solution.py:67
  69.7 1.3 fusion.22
  75.2 3.0 %collective-permute-done.13.refs_7_.refs_6_ = bf16[4,64,1536]{2,1,0:T(8,128)(2,1)} collective-permute-done((bf16[4,64,1536]{2,1,0:T(8,128)(2,1)}, bf16[4,64,1536]{2,1,0:T(8,128)(2,1)}, u32[]{:S(2)}, u32[]{:S(2)}) %collective-permute-start.13) | collective-permute-done | bytes 786464 | tf_op jit(solution)/shard_map/ppermute | solution.py:67
  78.3 2.3 %context_out.1.refs_1_ = bf16[256,512]{1,0:T(8,128)(2,1)S(1)} custom-call(s32[38]{0:T(128)S(1)} %copy-done.14, bf16[8,256,64]{2,1,0:T(8,128)(2,1)S(1)} %span_attention.1.refs_1_.refs_7_, bf16[8,256,64]{2,1,0:T(8,128)(2,1)S(1)} %collective-permute-done.7.refs_2_, bf16[16,256,64]{2,1,0:T(8,128)(2,1)S(1)} %both_rows.1.refs_1_.refs_7_.refs_3_, ...), custom_call_target="tpu_custom_call" | custom-call | flops 268435456 | bytes 4194304 | tf_op jit(solution)/shard_map/context_out/pallas_call | solution.py:101
  80.9 1.2 fusion.refs_2_
  82.4 3.5 %norm_up.1 = (bf16[256,1024]{1,0:T(8,128)(2,1)S(1)}, bf16[16,256,64]{2,1,0:T(8,128)(2,1)S(1)}) custom-call(s32[38]{0:T(128)S(1)} %copy-done.14, bf16[256,512]{1,0:T(8,128)(2,1)S(1)} %context_out.1.refs_1_, bf16[256,512]{1,0:T(8,128)(2,1)S(1)} %collective-permute-done.14.refs_2_, bf16[4,64,1536]{2,1,0:T(8,128)(2,1)S(1)} %join_middle.1.refs_4_.refs_3_, ...), custom_call_target="tpu_custom_call" | custom-call | flops 536870912 | bytes 3670016 | tf_op jit(solution)/shard_map/norm_up/pallas_call | solution.py:101
  86.0 2.3 %down.1 = (f32[128,1024]{1,0:T(8,128)S(1)}, bf16[128,1024]{1,0:T(8,128)(2,1)S(1)}) custom-call(s32[38]{0:T(128)S(1)} %copy-done.14, bf16[16,256,64]{2,1,0:T(8,128)(2,1)S(1)} %get-tuple-element.35.refs_1_, bf16[256,1024]{1,0:T(8,128)(2,1)S(1)} %get-tuple-element.36.refs_2_, bf16[4,64,1280]{2,1,0:T(8,128)(2,1)} %get-tuple-element.39.refs_3_, ...), custom_call_target="tpu_custom_call" | custom-call | flops 536870912 | bytes 3670016 | tf_op jit(solution)/shard_map/down/pallas_call | solution.py:101
  90.5 2.0 %select_reduce_fusion.3 = s32[]{:T(128)} fusion(s32[8]{0:T(128)} %param.19, s32[]{:T(128)} %fusion.22), kind=kLoop, calls=%fused_computation.100 | loop fusion | flops 23 | bytes 40 | tf_op jit(solution)/shard_map/reduce_sum | solution.py:542
  92.5 1.7 norm_pool.1.refs_5_
  94.2 1.4 collective-permute-done.20.refs_4_
  95.6 1.1 join_proj.1.refs_4_
  96.9 7.9 %all-to-all-start = ((bf16[128,8,128]{2,1,0:T(8,128)(2,1)}), bf16[128,8,128]{2,1,0:T(8,128)(2,1)S(1)}, u32[]{:S(2)}, u32[]{:S(2)}) async-start(bf16[128,8,128]{2,1,0:T(8,128)(2,1)} %bitcast.8), calls=%async_computation | async-start | bytes 524288 | tf_op jit(solution)/shard_map/all_to_all | solution.py:675
  105.5 10.2 %all-to-all-done.refs_1_ = bf16[128,8,128]{2,1,0:T(8,128)(2,1)S(1)} async-done(((bf16[128,8,128]{2,1,0:T(8,128)(2,1)}), bf16[128,8,128]{2,1,0:T(8,128)(2,1)S(1)}, u32[]{:S(2)}, u32[]{:S(2)}) %all-to-all-start) | async-done | bytes 262176 | tf_op jit(solution)/shard_map/all_to_all | solution.py:675
  115.7 1.6 copy-done.5
  118.0 2.1 %embed.1.refs_1_ = bf16[128,512]{1,0:T(8,128)(2,1)S(1)} custom-call(s32[38]{0:T(128)S(1)} %copy-done.14, bf16[128,8,128]{2,1,0:T(8,128)(2,1)S(1)} %all-to-all-done.refs_1_, bf16[128,128]{1,0:T(8,128)(2,1)S(1)} %copy-done.15, bf16[1024,1024]{1,0:T(8,128)(2,1)S(1)} %copy-done.5, bf16[4,4,64,256]{3,2,1,0:T(8,128)(2,1)S(1)} %join_proj.1.refs_4_, ...), custom_call_target="tpu_custom_call" | custom-call | flops 402653184 | bytes 3440640 | tf_op jit(solution)/shard_map/embed/pallas_call | solution.py:101
  120.8 2.6 %collective-permute-start.23 = (bf16[128,512]{1,0:T(8,128)(2,1)S(1)}, bf16[128,512]{1,0:T(8,128)(2,1)S(1)}, u32[]{:S(2)}, u32[]{:S(2)}) collective-permute-start(bf16[128,512]{1,0:T(8,128)(2,1)S(1)} %embed.1.refs_1_), channel_id=1, source_target_pairs={{0,3},{1,0},{2,1},{3,2},{4,7},{5,4},{6,5},{7,6},{8,11},{9,8},{10,9... | collective-permute-start | bytes 393224 | tf_op jit(solution)/shard_map/ppermute | solution.py:67
  124.9 1.4 collective-permute-done.22.refs_2_
  126.3 1.0 collective-permute-done.23.refs_3_
  127.3 2.5 %collective-permute-done.24.refs_4_ = bf16[128,512]{1,0:T(8,128)(2,1)S(1)} collective-permute-done((bf16[128,512]{1,0:T(8,128)(2,1)S(1)}, bf16[128,512]{1,0:T(8,128)(2,1)S(1)}, u32[]{:S(2)}, u32[]{:S(2)}) %collective-permute-start.24) | collective-permute-done | bytes 131104 | tf_op jit(solution)/shard_map/ppermute | solution.py:67
  131.1 1.0 multiply_sine_fusion
  132.1 2.7 %collective-permute-start.27 = (bf16[4,128,512]{2,1,0:T(8,128)(2,1)S(1)}, bf16[4,128,512]{2,1,0:T(8,128)(2,1)}, u32[]{:S(2)}, u32[]{:S(2)}) collective-permute-start(bf16[4,128,512]{2,1,0:T(8,128)(2,1)S(1)} %join_columns.1.refs_1_), channel_id=1, source_target_pairs={{0,12},{1,13},{2,14},{3,15},{4,0},{5,1},{6,2},{7,3},{8,4},{9,5},{1... | collective-permute-start | bytes 1572872 | tf_op jit(solution)/shard_map/ppermute | solution.py:67
  136.0 5.0 %collective-permute-done.25.refs_1_ = bf16[4,128,512]{2,1,0:T(8,128)(2,1)} collective-permute-done((bf16[4,128,512]{2,1,0:T(8,128)(2,1)S(1)}, bf16[4,128,512]{2,1,0:T(8,128)(2,1)}, u32[]{:S(2)}, u32[]{:S(2)}) %collective-permute-start.25) | collective-permute-done | bytes 524320 | tf_op jit(solution)/shard_map/ppermute | solution.py:67
  141.2 3.4 %copy-done = bf16[8192,512]{1,0:T(8,128)(2,1)S(1)} copy-done((bf16[8192,512]{1,0:T(8,128)(2,1)S(1)}, bf16[8192,512]{1,0:T(8,128)(2,1)}, u32[]{:S(2)}) %copy-start) | copy-done | bytes 8388632
  145.4 1.2 project_own.1
  146.6 3.4 %copy-done.1 = bf16[8192,512]{1,0:T(8,128)(2,1)S(1)} copy-done((bf16[8192,512]{1,0:T(8,128)(2,1)S(1)}, bf16[8192,512]{1,0:T(8,128)(2,1)}, u32[]{:S(2)}) %copy-start.1) | copy-done | bytes 8388632
  150.0 2.5 %project_near.1 = (f32[128,512]{1,0:T(8,128)S(1)}, f32[128,128]{1,0:T(8,128)S(1)}, f32[128,1]{1,0:T(8,128)S(1)}) custom-call(s32[38]{0:T(128)S(1)} %copy-done.14, bf16[4,128,512]{2,1,0:T(8,128)(2,1)} %collective-permute-done.25.refs_1_, bf16[4,128,512]{2,1,0:T(8,128)(2,1)} %collective-permute-done.27.refs_2_, f32[16,1,512]{2,1,0:T(1,128)S(1)} %bitcast.25, ...), custom_call_target="tpu_custom_call" | custom-call | flops 671088640 | bytes 11895296 | tf_op jit(solution)/shard_map/project_near/pallas_call | solution.py:101
  152.5 1.2 last_keys.1
  154.1 1.3 last_queries.1.refs_1_
  155.5 2.8 %collective-permute-done.28.refs_3_ = bf16[2,128,64]{2,1,0:T(8,128)(2,1)S(1)} collective-permute-done((bf16[2,128,64]{2,1,0:T(8,128)(2,1)S(1)}, bf16[2,128,64]{2,1,0:T(8,128)(2,1)S(1)}, u32[]{:S(2)}, u32[]{:S(2)}) %collective-permute-start.28) | collective-permute-done | bytes 32800 | tf_op jit(solution)/shard_map/ppermute | solution.py:757
  158.3 3.6 %attend_out.1 = (bf16[32,8192]{1,0:T(8,128)(2,1)S(1)}, bf16[32,8192]{1,0:T(8,128)(2,1)}, bf16[32,8192]{1,0:T(8,128)(2,1)}, bf16[32,8192]{1,0:T(8,128)(2,1)}) custom-call(s32[38]{0:T(128)S(1)} %copy-done.14, bf16[128,512]{1,0:T(8,128)(2,1)S(1)} %last_queries.1.refs_1_, bf16[2,128,64]{2,1,0:T(8,128)(2,1)S(1)} %get-tuple-element.52.refs_2_, ...), custom_call_target="tpu_custom_call" | custom-call | flops 1073741824 | bytes 8683520 | tf_op jit(solution)/shard_map/attend_out/pallas_call | solution.py:101
  161.9 3.2 %collective-permute-start.30 = (bf16[32,8192]{1,0:T(8,128)(2,1)}, bf16[32,8192]{1,0:T(8,128)(2,1)S(1)}, u32[]{:S(2)}, u32[]{:S(2)}) collective-permute-start(bf16[32,8192]{1,0:T(8,128)(2,1)} %get-tuple-element.55), channel_id=1, source_target_pairs={{0,12},{1,13},{2,14},{3,15},{4,0},{5,1},{6,2},{7,3},{8,4},{9,5},{1... | collective-permute-start | bytes 1572872 | tf_op jit(solution)/shard_map/ppermute | solution.py:67
  165.1 1.5 collective-permute-start.31
  167.5 5.0 %collective-permute-done.29.refs_2_ = bf16[32,8192]{1,0:T(8,128)(2,1)S(1)} collective-permute-done((bf16[32,8192]{1,0:T(8,128)(2,1)}, bf16[32,8192]{1,0:T(8,128)(2,1)S(1)}, u32[]{:S(2)}, u32[]{:S(2)}) %collective-permute-start.29) | collective-permute-done | bytes 524320 | tf_op jit(solution)/shard_map/ppermute | solution.py:67
  172.5 5.3 %collective-permute-done.30.refs_3_ = bf16[32,8192]{1,0:T(8,128)(2,1)S(1)} collective-permute-done((bf16[32,8192]{1,0:T(8,128)(2,1)}, bf16[32,8192]{1,0:T(8,128)(2,1)S(1)}, u32[]{:S(2)}, u32[]{:S(2)}) %collective-permute-start.30) | collective-permute-done | bytes 524320 | tf_op jit(solution)/shard_map/ppermute | solution.py:67
  177.8 2.3 %collective-permute-done.31.refs_4_ = bf16[32,8192]{1,0:T(8,128)(2,1)S(1)} collective-permute-done((bf16[32,8192]{1,0:T(8,128)(2,1)}, bf16[32,8192]{1,0:T(8,128)(2,1)S(1)}, u32[]{:S(2)}, u32[]{:S(2)}) %collective-permute-start.31) | collective-permute-done | bytes 524320 | tf_op jit(solution)/shard_map/ppermute | solution.py:67
  181.0 3.2 %collective-permute-start.33 = (bf16[8,8192]{1,0:T(8,128)(2,1)S(1)}, bf16[8,8192]{1,0:T(8,128)(2,1)S(1)}, u32[]{:S(2)}, u32[]{:S(2)}) collective-permute-start(bf16[8,8192]{1,0:T(8,128)(2,1)S(1)} %get-tuple-element.59), channel_id=1, source_target_pairs={{0,3},{1,0},{2,1},{3,2},{4,7},{5,4},{6,5},{7,6},{8,11},{9,8},{10,9... | collective-permute-start | bytes 393224 | tf_op jit(solution)/shard_map/ppermute | solution.py:67
  185.0 2.2 %collective-permute-done.32.refs_2_ = bf16[8,8192]{1,0:T(8,128)(2,1)S(1)} collective-permute-done((bf16[8,8192]{1,0:T(8,128)(2,1)S(1)}, bf16[8,8192]{1,0:T(8,128)(2,1)S(1)}, u32[]{:S(2)}, u32[]{:S(2)}) %collective-permute-start.32) | collective-permute-done | bytes 131104 | tf_op jit(solution)/shard_map/ppermute | solution.py:67
  187.1 1.0 collective-permute-done.33.refs_3_
  188.1 2.5 %collective-permute-done.34.refs_4_ = bf16[8,8192]{1,0:T(8,128)(2,1)S(1)} collective-permute-done((bf16[8,8192]{1,0:T(8,128)(2,1)S(1)}, bf16[8,8192]{1,0:T(8,128)(2,1)S(1)}, u32[]{:S(2)}, u32[]{:S(2)}) %collective-permute-start.34) | collective-permute-done | bytes 131104 | tf_op jit(solution)/shard_map/ppermute | solution.py:67
  190.7 1.3 finish.1
  (149 shorter events, 23.8 us)
Async XLA Ops:
  1.8 54.4 %copy-start.22 = (s32[16]{0:T(128)}, s32[16]{0:T(128)S(1)}, u32[]{:S(2)}) copy-start(s32[16]{0:T(128)S(1)} %broadcast_select_fusion.2) | copy-start | bytes 196
  1.9 1.0 copy-start.10
  2.9 14.6 %copy-start.12 = (s32[38]{0:T(128)}, s32[38]{0:T(128)S(1)}, u32[]{:S(2)}) copy-start(s32[38]{0:T(128)S(1)} %concatenate.9.refs_0_) | copy-start | bytes 460
  3.4 14.0 %copy-start.8 = (bf16[64,1536]{1,0:T(8,128)(2,1)}, bf16[64,1536]{1,0:T(8,128)(2,1)S(1)}, u32[]{:S(2)}) copy-start(bf16[64,1536]{1,0:T(8,128)(2,1)S(1)} %take_qkv.1.refs_1_.refs_5_) | copy-start | bytes 589828
  3.5 6.9 %collective-permute-start.1 = (bf16[64,1536]{1,0:T(8,128)(2,1)S(1)}, bf16[64,1536]{1,0:T(8,128)(2,1)S(1)}, u32[]{:S(2)}, u32[]{:S(2)}) collective-permute-start(bf16[64,1536]{1,0:T(8,128)(2,1)S(1)} %take_qkv.1.refs_1_.refs_5_), channel_id=1, source_target_pairs={{0,1},{1,2},{2,3},{3,0},{4,5},{5,6},{6,7},{7,4},{8,9},{9,10},{10,1... | collective-permute-start | bytes 589832 | tf_op jit(solution)/shard_map/ppermute | solution.py:67
  5.2 5.7 %collective-permute-start.2 = (bf16[64,1536]{1,0:T(8,128)(2,1)S(1)}, bf16[64,1536]{1,0:T(8,128)(2,1)S(1)}, u32[]{:S(2)}, u32[]{:S(2)}) collective-permute-start(bf16[64,1536]{1,0:T(8,128)(2,1)S(1)} %take_qkv.1.refs_1_.refs_5_), channel_id=1, source_target_pairs={{0,3},{1,0},{2,1},{3,2},{4,7},{5,4},{6,5},{7,6},{8,11},{9,8},{10,9... | collective-permute-start | bytes 589832 | tf_op jit(solution)/shard_map/ppermute | solution.py:67
  6.8 7.2 %collective-permute-start.3 = (bf16[64,1536]{1,0:T(8,128)(2,1)S(1)}, bf16[64,1536]{1,0:T(8,128)(2,1)S(1)}, u32[]{:S(2)}, u32[]{:S(2)}) collective-permute-start(bf16[64,1536]{1,0:T(8,128)(2,1)S(1)} %take_qkv.1.refs_1_.refs_5_), channel_id=1, source_target_pairs={{0,2},{1,3},{2,0},{3,1},{4,6},{5,7},{6,4},{7,5},{8,10},{9,11},{10,... | collective-permute-start | bytes 589832 | tf_op jit(solution)/shard_map/ppermute | solution.py:67
  14.5 32.0 %copy-start.3 = (bf16[4,64,1536]{2,1,0:T(8,128)(2,1)}, bf16[4,64,1536]{2,1,0:T(8,128)(2,1)S(1)}, u32[]{:S(2)}) copy-start(bf16[4,64,1536]{2,1,0:T(8,128)(2,1)S(1)} %join_qkv.1.refs_2_) | copy-start | bytes 2359300
  14.5 43.8 %copy-start.24 = (s32[1024]{0:T(1024)S(1)}, s32[1024]{0:T(1024)}, u32[]{:S(2)}) copy-start(s32[1024]{0:T(1024)} %param.18) | copy-start | bytes 12292
  14.6 43.8 %copy-start.25 = (s32[8]{0:T(128)S(1)}, s32[8]{0:T(128)}, u32[]{:S(2)}) copy-start(s32[8]{0:T(128)} %param.20) | copy-start | bytes 100
  14.6 20.5 %collective-permute-start.5 = (bf16[4,64,1536]{2,1,0:T(8,128)(2,1)S(1)}, bf16[4,64,1536]{2,1,0:T(8,128)(2,1)}, u32[]{:S(2)}, u32[]{:S(2)}) collective-permute-start(bf16[4,64,1536]{2,1,0:T(8,128)(2,1)S(1)} %join_qkv.1.refs_2_), channel_id=1, source_target_pairs={{0,12},{1,13},{2,14},{3,15},{4,0},{5,1},{6,2},{7,3},{8,4},{9,5},{1... | collective-permute-start | bytes 2359304 | tf_op jit(solution)/shard_map/ppermute | solution.py:67
  20.2 34.5 %copy-start.7 = (bf16[64,3584]{1,0:T(8,128)(2,1)S(1)}, bf16[64,3584]{1,0:T(8,128)(2,1)}, u32[]{:S(2)}) copy-start(bf16[64,3584]{1,0:T(8,128)(2,1)} %get-tuple-element.33.refs_1_) | copy-start | bytes 1376260
  20.2 14.9 %collective-permute-start.8 = (bf16[64,3584]{1,0:T(8,128)(2,1)}, bf16[64,3584]{1,0:T(8,128)(2,1)S(1)}, u32[]{:S(2)}, u32[]{:S(2)}) collective-permute-start(bf16[64,3584]{1,0:T(8,128)(2,1)} %get-tuple-element.33.refs_1_), channel_id=1, source_target_pairs={{0,1},{1,2},{2,3},{3,0},{4,5},{5,6},{6,7},{7,4},{8,9},{9,10},{10,1... | collective-permute-start | bytes 1376264 | tf_op jit(solution)/shard_map/ppermute | solution.py:67
  21.4 23.3 %collective-permute-start.4 = (bf16[4,64,1536]{2,1,0:T(8,128)(2,1)S(1)}, bf16[4,64,1536]{2,1,0:T(8,128)(2,1)S(1)}, u32[]{:S(2)}, u32[]{:S(2)}) collective-permute-start(bf16[4,64,1536]{2,1,0:T(8,128)(2,1)S(1)} %join_qkv.1.refs_2_), channel_id=1, source_target_pairs={{0,4},{1,5},{2,6},{3,7},{4,8},{5,9},{6,10},{7,11},{8,12},{9,13},{1... | collective-permute-start | bytes 2359304 | tf_op jit(solution)/shard_map/ppermute | solution.py:67
  21.4 18.7 %collective-permute-start.9 = (bf16[64,3584]{1,0:T(8,128)(2,1)}, bf16[64,3584]{1,0:T(8,128)(2,1)S(1)}, u32[]{:S(2)}, u32[]{:S(2)}) collective-permute-start(bf16[64,3584]{1,0:T(8,128)(2,1)} %get-tuple-element.34), channel_id=1, source_target_pairs={{0,3},{1,0},{2,1},{3,2},{4,7},{5,4},{6,5},{7,6},{8,11},{9,8},{10,9... | collective-permute-start | bytes 1376264 | tf_op jit(solution)/shard_map/ppermute | solution.py:67
  35.1 9.7 %collective-permute-start.10 = (bf16[64,3584]{1,0:T(8,128)(2,1)S(1)}, bf16[64,3584]{1,0:T(8,128)(2,1)S(1)}, u32[]{:S(2)}, u32[]{:S(2)}) collective-permute-start(bf16[64,3584]{1,0:T(8,128)(2,1)S(1)} %collective-permute-done.8.refs_2_), channel_id=1, source_target_pairs={{0,1},{1,2},{2,3},{3,0},{4,5},{5,6},{6,7},{7,4},{8,9},{9,10},{10,1... | collective-permute-start | bytes 1376264 | tf_op jit(solution)/shard_map/ppermute | solution.py:67
  35.1 13.6 %collective-permute-start.6 = (bf16[4,64,1536]{2,1,0:T(8,128)(2,1)}, bf16[4,64,1536]{2,1,0:T(8,128)(2,1)S(1)}, u32[]{:S(2)}, u32[]{:S(2)}) collective-permute-start(bf16[4,64,1536]{2,1,0:T(8,128)(2,1)} %collective-permute-done.5.refs_4_.refs_6_), channel_id=1, source_target_pairs={{0,12},{1,13},{2,14},{3,15},{4,0},{5,1},{6,2},{7,3},{8,4},{9,5},{1... | collective-permute-start | bytes 2359304 | tf_op jit(solution)/shard_map/ppermute | solution.py:67
  35.9 1.7 collective-permute-start
  37.7 1.0 copy-start.11
  39.2 15.5 %copy-start.14 = (s32[38]{0:T(128)S(1)}, s32[38]{0:T(128)}, u32[]{:S(2)}) copy-start(s32[38]{0:T(128)} %copy-done.12) | copy-start | bytes 460
  39.2 15.5 %copy-start.18 = (bf16[64,1024]{1,0:T(8,128)(2,1)S(1)}, bf16[64,1024]{1,0:T(8,128)(2,1)}, u32[]{:S(2)}) copy-start(bf16[64,1024]{1,0:T(8,128)(2,1)} %get-tuple-element.37.refs_5_) | copy-start | bytes 393220
  44.8 1.0 copy-start.6
  46.4 14.9 %collective-permute-start.11 = (bf16[4,64,1536]{2,1,0:T(8,128)(2,1)S(1)}, bf16[4,64,1536]{2,1,0:T(8,128)(2,1)}, u32[]{:S(2)}, u32[]{:S(2)}) collective-permute-start(bf16[4,64,1536]{2,1,0:T(8,128)(2,1)S(1)} %join_middle.1.refs_4_.refs_3_), channel_id=1, source_target_pairs={{0,4},{1,5},{2,6},{3,7},{4,8},{5,9},{6,10},{7,11},{8,12},{9,13},{1... | collective-permute-start | bytes 2359304 | tf_op jit(solution)/shard_map/ppermute | solution.py:67
  46.5 8.2 %collective-permute-start.15 = (bf16[64,1024]{1,0:T(8,128)(2,1)}, bf16[64,1024]{1,0:T(8,128)(2,1)S(1)}, u32[]{:S(2)}, u32[]{:S(2)}) collective-permute-start(bf16[64,1024]{1,0:T(8,128)(2,1)} %get-tuple-element.38), channel_id=1, source_target_pairs={{0,2},{1,3},{2,0},{3,1},{4,6},{5,7},{6,4},{7,5},{8,10},{9,11},{10,... | collective-permute-start | bytes 393224 | tf_op jit(solution)/shard_map/ppermute | solution.py:67
  48.7 1.1 copy-start.4
  56.9 0.9 copy-start.19
  57.7 4.2 %copy-start.20 = (bf16[4,64,256]{2,1,0:T(8,128)(2,1)}, bf16[4,64,256]{2,1,0:T(8,128)(2,1)S(1)}, u32[]{:S(2)}) copy-start(bf16[4,64,256]{2,1,0:T(8,128)(2,1)S(1)} %get-tuple-element.44) | copy-start | bytes 393220
  57.7 12.0 %collective-permute-start.16 = (bf16[4,64,1280]{2,1,0:T(8,128)(2,1)}, bf16[4,64,1280]{2,1,0:T(8,128)(2,1)S(1)}, u32[]{:S(2)}, u32[]{:S(2)}) collective-permute-start(bf16[4,64,1280]{2,1,0:T(8,128)(2,1)} %get-tuple-element.39.refs_3_), channel_id=1, source_target_pairs={{0,4},{1,5},{2,6},{3,7},{4,8},{5,9},{6,10},{7,11},{8,12},{9,13},{1... | collective-permute-start | bytes 1966088 | tf_op jit(solution)/shard_map/ppermute | solution.py:67
  58.6 16.6 %collective-permute-start.12 = (bf16[4,64,1536]{2,1,0:T(8,128)(2,1)S(1)}, bf16[4,64,1536]{2,1,0:T(8,128)(2,1)}, u32[]{:S(2)}, u32[]{:S(2)}) collective-permute-start(bf16[4,64,1536]{2,1,0:T(8,128)(2,1)S(1)} %join_middle.1.refs_4_.refs_3_), channel_id=1, source_target_pairs={{0,12},{1,13},{2,14},{3,15},{4,0},{5,1},{6,2},{7,3},{8,4},{9,5},{1... | collective-permute-start | bytes 2359304 | tf_op jit(solution)/shard_map/ppermute | solution.py:67
  61.3 16.9 %collective-permute-start.13 = (bf16[4,64,1536]{2,1,0:T(8,128)(2,1)}, bf16[4,64,1536]{2,1,0:T(8,128)(2,1)}, u32[]{:S(2)}, u32[]{:S(2)}) collective-permute-start(bf16[4,64,1536]{2,1,0:T(8,128)(2,1)} %collective-permute-done.11.refs_5_.refs_4_), channel_id=1, source_target_pairs={{0,4},{1,5},{2,6},{3,7},{4,8},{5,9},{6,10},{7,11},{8,12},{9,13},{1... | collective-permute-start | bytes 2359304 | tf_op jit(solution)/shard_map/ppermute | solution.py:67
  62.0 13.3 %collective-permute-start.7 = (bf16[8,256,64]{2,1,0:T(8,128)(2,1)S(1)}, bf16[8,256,64]{2,1,0:T(8,128)(2,1)S(1)}, u32[]{:S(2)}, u32[]{:S(2)}) collective-permute-start(bf16[8,256,64]{2,1,0:T(8,128)(2,1)S(1)} %span_attention.1.refs_1_.refs_7_), channel_id=1, source_target_pairs={{0,16},{16,0},{32,48},{48,32},{64,80},{80,64},{96,112},{112,96},{1... | collective-permute-start | bytes 786440 | tf_op jit(solution)/shard_map/ppermute | solution.py:71
  62.0 24.0 %collective-permute-start.17 = (bf16[4,64,1280]{2,1,0:T(8,128)(2,1)}, bf16[4,64,1280]{2,1,0:T(8,128)(2,1)}, u32[]{:S(2)}, u32[]{:S(2)}) collective-permute-start(bf16[4,64,1280]{2,1,0:T(8,128)(2,1)} %copy-done.19), channel_id=1, source_target_pairs={{0,12},{1,13},{2,14},{3,15},{4,0},{5,1},{6,2},{7,3},{8,4},{9,5},{1... | collective-permute-start | bytes 1966088 | tf_op jit(solution)/shard_map/ppermute | solution.py:67
  69.7 16.2 %collective-permute-start.18 = (bf16[4,64,1280]{2,1,0:T(8,128)(2,1)S(1)}, bf16[4,64,1280]{2,1,0:T(8,128)(2,1)}, u32[]{:S(2)}, u32[]{:S(2)}) collective-permute-start(bf16[4,64,1280]{2,1,0:T(8,128)(2,1)S(1)} %collective-permute-done.16.refs_4_.refs_2_), channel_id=1, source_target_pairs={{0,4},{1,5},{2,6},{3,7},{4,8},{5,9},{6,10},{7,11},{8,12},{9,13},{1... | collective-permute-start | bytes 1966088 | tf_op jit(solution)/shard_map/ppermute | solution.py:67
  74.5 14.7 %copy-start.21 = (bf16[4,64,256]{2,1,0:T(8,128)(2,1)S(1)}, bf16[4,64,256]{2,1,0:T(8,128)(2,1)}, u32[]{:S(2)}) copy-start(bf16[4,64,256]{2,1,0:T(8,128)(2,1)} %copy-done.20) | copy-start | bytes 393220
  74.5 21.1 %copy-start.17 = (bf16[4,64,256]{2,1,0:T(8,128)(2,1)S(1)}, bf16[4,64,256]{2,1,0:T(8,128)(2,1)}, u32[]{:S(2)}) copy-start(bf16[4,64,256]{2,1,0:T(8,128)(2,1)} %copy-done.16) | copy-start | bytes 393220
  80.6 1.8 collective-permute-start.14
  82.1 59.1 %copy-start.2 = (bf16[2,8192,64]{1,2,0:T(8,128)(2,1)S(1)}, bf16[2,8192,64]{1,2,0:T(8,128)(2,1)}, u32[]{:S(2)}) copy-start(bf16[2,8192,64]{1,2,0:T(8,128)(2,1)} %param.30) | copy-start | bytes 6291460
  88.3 4.2 %collective-permute-start.19 = (bf16[128,1024]{1,0:T(8,128)(2,1)S(1)}, bf16[128,1024]{1,0:T(8,128)(2,1)S(1)}, u32[]{:S(2)}, u32[]{:S(2)}) collective-permute-start(bf16[128,1024]{1,0:T(8,128)(2,1)S(1)} %get-tuple-element.42), channel_id=1, source_target_pairs={{0,16},{16,0},{32,48},{48,32},{64,80},{80,64},{96,112},{112,96},{1... | collective-permute-start | bytes 786440 | tf_op jit(solution)/shard_map/ppermute | solution.py:71
  89.1 6.5 %collective-permute-start.20 = (bf16[4,64,256]{2,1,0:T(8,128)(2,1)S(1)}, bf16[4,64,256]{2,1,0:T(8,128)(2,1)S(1)}, u32[]{:S(2)}, u32[]{:S(2)}) collective-permute-start(bf16[4,64,256]{2,1,0:T(8,128)(2,1)S(1)} %copy-done.21), channel_id=1, source_target_pairs={{0,8},{1,9},{2,10},{3,11},{4,12},{5,13},{6,14},{7,15},{8,0},{9,1},... | collective-permute-start | bytes 393224 | tf_op jit(solution)/shard_map/ppermute | solution.py:67
  96.7 18.9 %collective-permute-start.21 = (bf16[4,4,64,256]{3,2,1,0:T(8,128)(2,1)S(1)}, bf16[4,4,64,256]{3,2,1,0:T(8,128)(2,1)S(1)}, u32[]{:S(2)}, u32[]{:S(2)}) collective-permute-start(bf16[4,4,64,256]{3,2,1,0:T(8,128)(2,1)S(1)} %join_proj.1.refs_4_), channel_id=1, source_target_pairs={{0,16},{16,0},{32,48},{48,32},{64,80},{80,64},{96,112},{112,96},{1... | collective-permute-start | bytes 1572872 | tf_op jit(solution)/shard_map/ppermute | solution.py:71
  96.9 18.7 %all-to-all-start = ((bf16[128,8,128]{2,1,0:T(8,128)(2,1)}), bf16[128,8,128]{2,1,0:T(8,128)(2,1)S(1)}, u32[]{:S(2)}, u32[]{:S(2)}) async-start(bf16[128,8,128]{2,1,0:T(8,128)(2,1)} %bitcast.8), calls=%async_computation | async-start | bytes 524288 | tf_op jit(solution)/shard_map/all_to_all | solution.py:675
  115.7 1.6 copy-start.5
  117.3 0.8 copy-start.15
  120.1 6.2 %collective-permute-start.22 = (bf16[128,512]{1,0:T(8,128)(2,1)S(1)}, bf16[128,512]{1,0:T(8,128)(2,1)S(1)}, u32[]{:S(2)}, u32[]{:S(2)}) collective-permute-start(bf16[128,512]{1,0:T(8,128)(2,1)S(1)} %embed.1.refs_1_), channel_id=1, source_target_pairs={{0,1},{1,2},{2,3},{3,0},{4,5},{5,6},{6,7},{7,4},{8,9},{9,10},{10,1... | collective-permute-start | bytes 393224 | tf_op jit(solution)/shard_map/ppermute | solution.py:67
  120.8 6.5 %collective-permute-start.23 = (bf16[128,512]{1,0:T(8,128)(2,1)S(1)}, bf16[128,512]{1,0:T(8,128)(2,1)S(1)}, u32[]{:S(2)}, u32[]{:S(2)}) collective-permute-start(bf16[128,512]{1,0:T(8,128)(2,1)S(1)} %embed.1.refs_1_), channel_id=1, source_target_pairs={{0,3},{1,0},{2,1},{3,2},{4,7},{5,4},{6,5},{7,6},{8,11},{9,8},{10,9... | collective-permute-start | bytes 393224 | tf_op jit(solution)/shard_map/ppermute | solution.py:67
  123.4 6.5 %collective-permute-start.24 = (bf16[128,512]{1,0:T(8,128)(2,1)S(1)}, bf16[128,512]{1,0:T(8,128)(2,1)S(1)}, u32[]{:S(2)}, u32[]{:S(2)}) collective-permute-start(bf16[128,512]{1,0:T(8,128)(2,1)S(1)} %embed.1.refs_1_), channel_id=1, source_target_pairs={{0,2},{1,3},{2,0},{3,1},{4,6},{5,7},{6,4},{7,5},{8,10},{9,11},{10,... | collective-permute-start | bytes 393224 | tf_op jit(solution)/shard_map/ppermute | solution.py:67
  130.4 10.6 %collective-permute-start.25 = (bf16[4,128,512]{2,1,0:T(8,128)(2,1)S(1)}, bf16[4,128,512]{2,1,0:T(8,128)(2,1)}, u32[]{:S(2)}, u32[]{:S(2)}) collective-permute-start(bf16[4,128,512]{2,1,0:T(8,128)(2,1)S(1)} %join_columns.1.refs_1_), channel_id=1, source_target_pairs={{0,4},{1,5},{2,6},{3,7},{4,8},{5,9},{6,10},{7,11},{8,12},{9,13},{1... | collective-permute-start | bytes 1572872 | tf_op jit(solution)/shard_map/ppermute | solution.py:67
  132.1 14.5 %collective-permute-start.27 = (bf16[4,128,512]{2,1,0:T(8,128)(2,1)S(1)}, bf16[4,128,512]{2,1,0:T(8,128)(2,1)}, u32[]{:S(2)}, u32[]{:S(2)}) collective-permute-start(bf16[4,128,512]{2,1,0:T(8,128)(2,1)S(1)} %join_columns.1.refs_1_), channel_id=1, source_target_pairs={{0,12},{1,13},{2,14},{3,15},{4,0},{5,1},{6,2},{7,3},{8,4},{9,5},{1... | collective-permute-start | bytes 1572872 | tf_op jit(solution)/shard_map/ppermute | solution.py:67
  141.0 11.5 %collective-permute-start.26 = (bf16[4,128,512]{2,1,0:T(8,128)(2,1)}, bf16[4,128,512]{2,1,0:T(8,128)(2,1)S(1)}, u32[]{:S(2)}, u32[]{:S(2)}) collective-permute-start(bf16[4,128,512]{2,1,0:T(8,128)(2,1)} %collective-permute-done.25.refs_1_), channel_id=1, source_target_pairs={{0,4},{1,5},{2,6},{3,7},{4,8},{5,9},{6,10},{7,11},{8,12},{9,13},{1... | collective-permute-start | bytes 1572872 | tf_op jit(solution)/shard_map/ppermute | solution.py:67
  141.2 3.4 %copy-start = (bf16[8192,512]{1,0:T(8,128)(2,1)S(1)}, bf16[8192,512]{1,0:T(8,128)(2,1)}, u32[]{:S(2)}) copy-start(bf16[8192,512]{1,0:T(8,128)(2,1)} %refs_3_.7) | copy-start | bytes 25165828
  144.6 0.8 copy-start.9
  145.4 8.7 %slice-start = ((s8[8388608]{0:T(1024)(128)(4,1)}), s8[4194304]{0:T(1024)(128)(4,1)S(1)}, s32[]{:S(2)}) async-start(s8[8388608]{0:T(1024)(128)(4,1)} %bitcast.17), calls=%async_computation.1 | async-start | bytes 8388608
  146.6 3.4 %copy-start.1 = (bf16[8192,512]{1,0:T(8,128)(2,1)S(1)}, bf16[8192,512]{1,0:T(8,128)(2,1)}, u32[]{:S(2)}) copy-start(bf16[8192,512]{1,0:T(8,128)(2,1)} %refs_3_.7) | copy-start | bytes 25165828
  150.0 4.1 %slice-start.1 = ((s8[8388608]{0:T(1024)(128)(4,1)}), s8[4194304]{0:T(1024)(128)(4,1)S(1)}, s32[]{:S(2)}) async-start(s8[8388608]{0:T(1024)(128)(4,1)} %bitcast.17), calls=%async_computation.2 | async-start | bytes 8388608
  150.0 8.3 %slice-start.2 = ((s8[8388608]{0:T(1024)(128)(4,1)}), s8[4194304]{0:T(1024)(128)(4,1)S(1)}, s32[]{:S(2)}) async-start(s8[8388608]{0:T(1024)(128)(4,1)} %bitcast.22), calls=%async_computation.3 | async-start | bytes 8388608
  152.5 5.8 %slice-start.3 = ((s8[8388608]{0:T(1024)(128)(4,1)}), s8[4194304]{0:T(1024)(128)(4,1)S(1)}, s32[]{:S(2)}) async-start(s8[8388608]{0:T(1024)(128)(4,1)} %bitcast.22), calls=%async_computation.4 | async-start | bytes 8388608
  153.7 4.6 %collective-permute-start.28 = (bf16[2,128,64]{2,1,0:T(8,128)(2,1)S(1)}, bf16[2,128,64]{2,1,0:T(8,128)(2,1)S(1)}, u32[]{:S(2)}, u32[]{:S(2)}) collective-permute-start(bf16[2,128,64]{2,1,0:T(8,128)(2,1)S(1)} %get-tuple-element.52.refs_2_), channel_id=1, source_target_pairs={{0,1},{1,0},{2,3},{3,2},{4,5},{5,4},{6,7},{7,6},{8,9},{9,8},{10,11... | collective-permute-start | bytes 98312 | tf_op jit(solution)/shard_map/ppermute | solution.py:757
  154.1 12.5 %copy-start.23 = (s32[16]{0:T(128)S(1)}, s32[16]{0:T(128)}, u32[]{:S(2)}) copy-start(s32[16]{0:T(128)} %copy-done.22) | copy-start | bytes 196
  161.9 10.6 %collective-permute-start.29 = (bf16[32,8192]{1,0:T(8,128)(2,1)}, bf16[32,8192]{1,0:T(8,128)(2,1)S(1)}, u32[]{:S(2)}, u32[]{:S(2)}) collective-permute-start(bf16[32,8192]{1,0:T(8,128)(2,1)} %get-tuple-element.54), channel_id=1, source_target_pairs={{0,4},{1,5},{2,6},{3,7},{4,8},{5,9},{6,10},{7,11},{8,12},{9,13},{1... | collective-permute-start | bytes 1572872 | tf_op jit(solution)/shard_map/ppermute | solution.py:67
  161.9 15.9 %collective-permute-start.30 = (bf16[32,8192]{1,0:T(8,128)(2,1)}, bf16[32,8192]{1,0:T(8,128)(2,1)S(1)}, u32[]{:S(2)}, u32[]{:S(2)}) collective-permute-start(bf16[32,8192]{1,0:T(8,128)(2,1)} %get-tuple-element.55), channel_id=1, source_target_pairs={{0,12},{1,13},{2,14},{3,15},{4,0},{5,1},{6,2},{7,3},{8,4},{9,5},{1... | collective-permute-start | bytes 1572872 | tf_op jit(solution)/shard_map/ppermute | solution.py:67
  165.1 14.9 %collective-permute-start.31 = (bf16[32,8192]{1,0:T(8,128)(2,1)}, bf16[32,8192]{1,0:T(8,128)(2,1)S(1)}, u32[]{:S(2)}, u32[]{:S(2)}) collective-permute-start(bf16[32,8192]{1,0:T(8,128)(2,1)} %get-tuple-element.56), channel_id=1, source_target_pairs={{0,8},{1,9},{2,10},{3,11},{4,12},{5,13},{6,14},{7,15},{8,0},{9,1},... | collective-permute-start | bytes 1572872 | tf_op jit(solution)/shard_map/ppermute | solution.py:67
  180.9 6.2 %collective-permute-start.32 = (bf16[8,8192]{1,0:T(8,128)(2,1)S(1)}, bf16[8,8192]{1,0:T(8,128)(2,1)S(1)}, u32[]{:S(2)}, u32[]{:S(2)}) collective-permute-start(bf16[8,8192]{1,0:T(8,128)(2,1)S(1)} %get-tuple-element.58), channel_id=1, source_target_pairs={{0,1},{1,2},{2,3},{3,0},{4,5},{5,6},{6,7},{7,4},{8,9},{9,10},{10,1... | collective-permute-start | bytes 393224 | tf_op jit(solution)/shard_map/ppermute | solution.py:67
  181.0 7.1 %collective-permute-start.33 = (bf16[8,8192]{1,0:T(8,128)(2,1)S(1)}, bf16[8,8192]{1,0:T(8,128)(2,1)S(1)}, u32[]{:S(2)}, u32[]{:S(2)}) collective-permute-start(bf16[8,8192]{1,0:T(8,128)(2,1)S(1)} %get-tuple-element.59), channel_id=1, source_target_pairs={{0,3},{1,0},{2,1},{3,2},{4,7},{5,4},{6,5},{7,6},{8,11},{9,8},{10,9... | collective-permute-start | bytes 393224 | tf_op jit(solution)/shard_map/ppermute | solution.py:67
  184.2 6.5 %collective-permute-start.34 = (bf16[8,8192]{1,0:T(8,128)(2,1)S(1)}, bf16[8,8192]{1,0:T(8,128)(2,1)S(1)}, u32[]{:S(2)}, u32[]{:S(2)}) collective-permute-start(bf16[8,8192]{1,0:T(8,128)(2,1)S(1)} %get-tuple-element.60), channel_id=1, source_target_pairs={{0,2},{1,3},{2,0},{3,1},{4,6},{5,7},{6,4},{7,5},{8,10},{9,11},{10,... | collective-permute-start | bytes 393224 | tf_op jit(solution)/shard_map/ppermute | solution.py:67
  (2 other events, 1.3 us)

commit v7 on v6

--- a/solution.py
+++ b/solution.py
@@ -557,6 +557,12 @@
         (lane[:, None] ^ 1) == lane[None, :], jnp.where(lane[None, :] % 2 == 0, -1.0, 1.0), 0.0
     ).astype(jnp.float32)
 
+    kv_cols = key_value_weight.shape[2]
+    key_start = tensor_index * kv_cols % HEAD_WIDTH
+    key_cosine = lax.dynamic_slice_in_dim(cosine, key_start, kv_cols, 1)
+    key_sine = lax.dynamic_slice_in_dim(sine, key_start, kv_cols, 1)
+    early = [pick, order, deal, allowed, cosine, sine, key_cosine, key_sine, swap]
+
     own_tokens = span_tokens.reshape(spans * span_size, width)
     other_tokens = to_core(own_tokens)
     token_pieces = whole_call(
@@ -607,7 +613,7 @@
         rest_ring,
         shape_of((SIDE, share, middle_cols)),
         limit=8,
-        after=[*qkv[1:3], token_pieces],
+        after=[*qkv[1:3], token_pieces, *early],
     )
     left = to_ring(middle_block, 2, 1)
     middle = [middle_block, left, to_ring(middle_block, 2, -1), to_ring(left, 2, 1)]
@@ -629,10 +635,10 @@
         [*rest_ring, kept_cols, beyond_cols],
         (lower_shape, lower_shape, far_shape, far_shape),
         limit=8,
-        after=[context],
-    )
-    lower_left = to_ring(lower_up, 2, 1)
-    lower = [lower_up, lower_left, to_ring(lower_down, 2, -1), to_ring(lower_left, 2, 1)]
+        after=[context, left],
+    )
+    lower_right = to_ring(lower_down, 2, -1)
+    lower = [lower_up, to_ring(lower_up, 2, 1), lower_right, to_ring(lower_right, 2, -1)]
     far_beyond = to_ring(far_beyond, 2, 2)
     attended = whole_call(
         context_out,
@@ -652,6 +658,15 @@
         [pltpu.VMEM((tensor_count, all_rows, share), jnp.bfloat16)],
         flops=2 * all_rows * width * width,
     )
+    proj_mine = whole_call(
+        join_proj,
+        "join_proj",
+        info,
+        [far_kept, lower[1], lower[2], far_beyond],
+        shape_of((SIDE, SIDE, share, half_cols)),
+        limit=8,
+    )
+    proj_other = to_core(proj_mine)
     kept, sent = whole_call(
         down,
         "down",
@@ -663,6 +678,7 @@
         ),
         [pltpu.VMEM((all_rows, width), jnp.float32)],
         flops=2 * all_rows * width * width,
+        after=[proj_mine],
     )
     outgoing = whole_call(
         norm_pool,
@@ -676,16 +692,6 @@
         outgoing.reshape(device_count, width // 128, 128), AXES, 0, 0
     )
 
-    proj_mine = whole_call(
-        join_proj,
-        "join_proj",
-        info,
-        [far_kept, lower[1], lower[2], far_beyond],
-        shape_of((SIDE, SIDE, share, half_cols)),
-        limit=8,
-        after=[outgoing],
-    )
-    proj_other = to_core(proj_mine)
     own_cols = whole_call(
         embed,
         "embed",
@@ -710,9 +716,6 @@
     near_right = to_ring(first_block, 2, -1)
     query_cols = q_weight.shape[1]
     kv_cols = key_value_weight.shape[2]
-    key_start = tensor_index * kv_cols % HEAD_WIDTH
-    key_cosine = lax.dynamic_slice_in_dim(cosine, key_start, kv_cols, 1)
-    key_sine = lax.dynamic_slice_in_dim(sine, key_start, kv_cols, 1)
     gain = norm_gain.reshape(tensor_count, 1, share_cols)
     kv_pair = key_value_weight.transpose(0, 2, 1).reshape(2 * kv_cols, model_width)
     sums = (
@@ -729,7 +732,8 @@
         sums,
         flops=block_flops,
     )
-    embedded = [first_block, near_left, near_right, to_ring(near_left, 2, 1)]
+    relayed, _ = lax.optimization_barrier((near_left, totals[2]))
+    embedded = [first_block, relayed, near_right, to_ring(relayed, 2, 1)]
     totals = whole_call(
         functools.partial(project, starts=(1, 2), count=2),
         "project_near",

time: 193 us -> 198 us (1.026)
  waiting for transfers between devices: 77.4 us -> 84.8 us
  Pallas kernels: 35.6 us -> 31.8 us
  other arithmetic: 11.7 us -> 9.27 us
    ppermute x29, waiting for transfers between devices: 62.4 us -> 69.9 us  [to_ring(): return lax.ppermute(value, AXES, ring_pairs(phase, distance))]
    pallas_call x21, Pallas kernels: 35.6 us -> 31.8 us  [whole_call(): pl.pallas_call(run, name=name, out_shape=outs, in_specs=[SMEM] + [VMEM] *...]
    unnamed x60 -> x66, local copies, waits for them, and re-layouts: 16.2 us -> 18.5 us
  transfers between devices with their start and end apart: 36 -> 36, of which waited for: 24 -> 20; matrix products, arithmetic and copies ran while one was open for 8% -> 6% of each run, Pallas kernels for 11% -> 10%
where the time goes in v7:
time: 198 us; the launch traced here: 196 us
  waiting for transfers between devices  84.8 us (43%)
  starting transfers between devices  45.2 us (23%)
  Pallas kernels  31.8 us (16%)
  local copies, waits for them, and re-layouts  23.2 us (12%)
  other arithmetic  9.27 us (5%)
    ppermute x29, waiting for transfers between devices, to_ring(): return lax.ppermute(value, AXES, ring_pairs(phase, distance))  69.9 us
    ppermute x29, starting transfers between devices, to_ring(): return lax.ppermute(value, AXES, ring_pairs(phase, distance))  35.1 us
    pallas_call x21, Pallas kernels, whole_call(): pl.pallas_call(run, name=name, out_shape=outs, in_specs=[SMEM] + [VMEM] *...  31.8 us
    unnamed x66, local copies, waits for them, and re-layouts  18.5 us
    all_to_all x1, waiting for transfers between devices, local(): lax.all_to_all(outgoing.reshape(device_count, width // 128, 128), AXES, 0...  10.9 us
    all_to_all x1, starting transfers between devices, local(): lax.all_to_all(outgoing.reshape(device_count, width // 128, 128), AXES, 0...  9.13 us
  transfers between devices with their start and end apart: 36, of which 20 were waited for; matrix products, arithmetic and copies ran while one was open for 6% of the time, Pallas kernels for 10%

profile of v7, /device:TPU:0, one launch (start us, length us, event | category | flops | bytes accessed | tf_op | source)
XLA Modules:
  0.0 195.6 jit_solution(17434759957824173321)
XLA Ops:
  1.3 1.0 copy-done.16
  2.9 1.7 collective-permute-start.1
  4.6 1.6 collective-permute-start.2
  6.2 2.1 %collective-permute-start.3 = (bf16[64,1536]{1,0:T(8,128)(2,1)S(1)}, bf16[64,1536]{1,0:T(8,128)(2,1)S(1)}, u32[]{:S(2)}, u32[]{:S(2)}) collective-permute-start(bf16[64,1536]{1,0:T(8,128)(2,1)S(1)} %take_qkv.1.refs_1_.refs_5_), channel_id=1, source_target_pairs={{0,2},{1,3},{2,0},{3,1},{4,6},{5,7},{6,4},{7,5},{8,10},{9,11},{10,... | collective-permute-start | bytes 589832 | tf_op jit(solution)/shard_map/ppermute | solution.py:67
  8.3 2.7 %take_rest.1 = (bf16[64,3584]{1,0:T(8,128)(2,1)}, bf16[64,3584]{1,0:T(8,128)(2,1)}, bf16[64,1024]{1,0:T(8,128)(2,1)}, bf16[64,1024]{1,0:T(8,128)(2,1)}) custom-call(s32[38]{0:T(128)} %copy-done.22, bf16[64,1024]{1,0:T(8,128)(2,1)} %refs_1_.3, bf16[64,2048]{1,0:T(8,128)(2,1)} %refs_2_.1, bf16[128,1024]{1,0:T(8,128)(2,1)} %refs_3_.4, ...), custom_call_target="tpu_custom_call" | custom-call | bytes 1703936 | tf_op jit(solution)/shard_map/take_rest/pallas_call | solution.py:101
  11.8 1.3 fusion.22
  13.7 1.9 select_reduce_fusion.3
  17.2 0.8 select_reduce_fusion.1
  20.7 2.6 %collective-permute-start.9 = (bf16[64,3584]{1,0:T(8,128)(2,1)}, bf16[64,3584]{1,0:T(8,128)(2,1)}, u32[]{:S(2)}, u32[]{:S(2)}) collective-permute-start(bf16[64,3584]{1,0:T(8,128)(2,1)} %get-tuple-element.35), channel_id=1, source_target_pairs={{0,3},{1,0},{2,1},{3,2},{4,7},{5,4},{6,5},{7,6},{8,11},{9,8},{10,9... | collective-permute-start | bytes 1376264 | tf_op jit(solution)/shard_map/ppermute | solution.py:67
  23.4 0.9 copy-done.7
  25.6 1.6 collective-permute-start.4
  27.1 1.7 collective-permute-start.5
  29.6 1.3 fusion.1.refs_10_.refs_5_
  31.6 7.5 %collective-permute-done.5.refs_4_.refs_6_ = bf16[4,64,1536]{2,1,0:T(8,128)(2,1)S(1)} collective-permute-done((bf16[4,64,1536]{2,1,0:T(8,128)(2,1)S(1)}, bf16[4,64,1536]{2,1,0:T(8,128)(2,1)S(1)}, u32[]{:S(2)}, u32[]{:S(2)}) %collective-permute-start.5) | collective-permute-done | bytes 786464 | tf_op jit(solution)/shard_map/ppermute | solution.py:67
  39.1 3.0 %collective-permute-start.6 = (bf16[4,64,1536]{2,1,0:T(8,128)(2,1)S(1)}, bf16[4,64,1536]{2,1,0:T(8,128)(2,1)S(1)}, u32[]{:S(2)}, u32[]{:S(2)}) collective-permute-start(bf16[4,64,1536]{2,1,0:T(8,128)(2,1)S(1)} %collective-permute-done.5.refs_4_.refs_6_), channel_id=1, source_target_pairs={{0,12},{1,13},{2,14},{3,15},{4,0},{5,1},{6,2},{7,3},{8,4},{9,5},{1... | collective-permute-start | bytes 2359304 | tf_op jit(solution)/shard_map/ppermute | solution.py:67
  42.2 1.0 copy-done.21
  43.9 1.3 both_rows.1.refs_1_.refs_7_.refs_3_
  45.3 1.0 copy-done.4
  48.5 1.2 join_middle.1.refs_4_.refs_3_
  49.8 0.9 collective-permute-start.15
  50.6 1.0 collective-permute-done.6.refs_5_
  51.6 2.6 %span_attention.1.refs_1_.refs_7_ = bf16[8,256,64]{2,1,0:T(8,128)(2,1)S(1)} custom-call(s32[38]{0:T(128)S(1)} %copy-done.26, bf16[16,256,64]{2,1,0:T(8,128)(2,1)S(1)} %both_rows.1.refs_1_.refs_7_.refs_3_, bf16[4,64,1536]{2,1,0:T(8,128)(2,1)S(1)} %join_qkv.1.refs_2_, bf16[4,64,1536]{2,1,0:T(8,128)(2,1)S(1)} %collective-permute-done.4.refs_3_.refs_5_, ...), custom_call_target="tpu_custom_call" | custom-call | flops 805306368 | bytes 3670016 | tf_op jit(solution)/shard_map/span_attention/pallas_call | solution.py:101
  54.2 3.8 %collective-permute-done.15.refs_6_ = bf16[64,1024]{1,0:T(8,128)(2,1)S(1)} collective-permute-done((bf16[64,1024]{1,0:T(8,128)(2,1)}, bf16[64,1024]{1,0:T(8,128)(2,1)S(1)}, u32[]{:S(2)}, u32[]{:S(2)}) %collective-permute-start.15) | collective-permute-done | bytes 131104 | tf_op jit(solution)/shard_map/ppermute | solution.py:67
  58.0 5.9 %collective-permute-done.11.refs_5_.refs_4_.refs_8_ = bf16[4,64,1536]{2,1,0:T(8,128)(2,1)S(1)} collective-permute-done((bf16[4,64,1536]{2,1,0:T(8,128)(2,1)S(1)}, bf16[4,64,1536]{2,1,0:T(8,128)(2,1)S(1)}, u32[]{:S(2)}, u32[]{:S(2)}) %collective-permute-start.11) | collective-permute-done | bytes 786464 | tf_op jit(solution)/shard_map/ppermute | solution.py:67
  63.9 1.3 join_lower.1
  65.7 1.7 collective-permute-start.13
  67.3 1.9 collective-permute-start.16
  69.3 6.5 %collective-permute-done.17.refs_3_.refs_5_ = bf16[4,64,1280]{2,1,0:T(8,128)(2,1)S(1)} collective-permute-done((bf16[4,64,1280]{2,1,0:T(8,128)(2,1)S(1)}, bf16[4,64,1280]{2,1,0:T(8,128)(2,1)S(1)}, u32[]{:S(2)}, u32[]{:S(2)}) %collective-permute-start.17) | collective-permute-done | bytes 655392 | tf_op jit(solution)/shard_map/ppermute | solution.py:67
  75.8 1.2 collective-permute-start.18
  77.0 7.2 %collective-permute-done.12.refs_6_.refs_5_ = bf16[4,64,1536]{2,1,0:T(8,128)(2,1)S(1)} collective-permute-done((bf16[4,64,1536]{2,1,0:T(8,128)(2,1)S(1)}, bf16[4,64,1536]{2,1,0:T(8,128)(2,1)S(1)}, u32[]{:S(2)}, u32[]{:S(2)}) %collective-permute-start.12) | collective-permute-done | bytes 786464 | tf_op jit(solution)/shard_map/ppermute | solution.py:67
  84.2 1.3 context_out.1.refs_1_
  86.3 5.9 %collective-permute-done.19.refs_4_ = bf16[4,64,256]{2,1,0:T(8,128)(2,1)S(1)} collective-permute-done((bf16[4,64,256]{2,1,0:T(8,128)(2,1)S(1)}, bf16[4,64,256]{2,1,0:T(8,128)(2,1)S(1)}, u32[]{:S(2)}, u32[]{:S(2)}) %collective-permute-start.19) | collective-permute-done | bytes 131104 | tf_op jit(solution)/shard_map/ppermute | solution.py:67
  93.1 2.3 %norm_up.1 = (bf16[256,1024]{1,0:T(8,128)(2,1)S(1)}, bf16[16,256,64]{2,1,0:T(8,128)(2,1)S(1)}) custom-call(s32[38]{0:T(128)S(1)} %copy-done.26, bf16[256,512]{1,0:T(8,128)(2,1)S(1)} %context_out.1.refs_1_, bf16[256,512]{1,0:T(8,128)(2,1)S(1)} %collective-permute-done.14.refs_2_, bf16[4,64,1536]{2,1,0:T(8,128)(2,1)S(1)} %join_middle.1.refs_4_.refs_3_, ...), custom_call_target="tpu_custom_call" | custom-call | flops 536870912 | bytes 3670016 | tf_op jit(solution)/shard_map/norm_up/pallas_call | solution.py:101
  95.4 1.4 down.1
  97.3 1.2 collective-permute-done.20.refs_2_
  98.5 1.7 norm_pool.1
  100.2 9.1 %all-to-all-start = ((bf16[128,8,128]{2,1,0:T(8,128)(2,1)}), bf16[128,8,128]{2,1,0:T(8,128)(2,1)S(1)}, u32[]{:S(2)}, u32[]{:S(2)}) async-start(bf16[128,8,128]{2,1,0:T(8,128)(2,1)} %bitcast.9), calls=%async_computation | async-start | bytes 524288 | tf_op jit(solution)/shard_map/all_to_all | solution.py:691
  109.3 10.9 %all-to-all-done.refs_1_ = bf16[128,8,128]{2,1,0:T(8,128)(2,1)S(1)} async-done(((bf16[128,8,128]{2,1,0:T(8,128)(2,1)}), bf16[128,8,128]{2,1,0:T(8,128)(2,1)S(1)}, u32[]{:S(2)}, u32[]{:S(2)}) %all-to-all-start) | async-done | bytes 262176 | tf_op jit(solution)/shard_map/all_to_all | solution.py:691
  120.2 1.6 copy-done.3
  122.6 2.6 %embed.1.refs_1_ = bf16[128,512]{1,0:T(8,128)(2,1)S(1)} custom-call(s32[38]{0:T(128)S(1)} %copy-done.26, bf16[128,8,128]{2,1,0:T(8,128)(2,1)S(1)} %all-to-all-done.refs_1_, bf16[128,128]{1,0:T(8,128)(2,1)S(1)} %copy-done.18, bf16[1024,1024]{1,0:T(8,128)(2,1)S(1)} %copy-done.3, bf16[4,4,64,256]{3,2,1,0:T(8,128)(2,1)S(1)} %join_proj.1.refs_7_.refs_4_, ...), custom_call_target="tpu_custom_call" | custom-call | flops 402653184 | bytes 3440640 | tf_op jit(solution)/shard_map/embed/pallas_call | solution.py:101
  125.9 2.6 %collective-permute-start.23 = (bf16[128,512]{1,0:T(8,128)(2,1)S(1)}, bf16[128,512]{1,0:T(8,128)(2,1)S(1)}, u32[]{:S(2)}, u32[]{:S(2)}) collective-permute-start(bf16[128,512]{1,0:T(8,128)(2,1)S(1)} %embed.1.refs_1_), channel_id=1, source_target_pairs={{0,3},{1,0},{2,1},{3,2},{4,7},{5,4},{6,5},{7,6},{8,11},{9,8},{10,9... | collective-permute-start | bytes 393224 | tf_op jit(solution)/shard_map/ppermute | solution.py:67
  128.5 2.9 %collective-permute-done.22.refs_2_ = bf16[128,512]{1,0:T(8,128)(2,1)S(1)} collective-permute-done((bf16[128,512]{1,0:T(8,128)(2,1)S(1)}, bf16[128,512]{1,0:T(8,128)(2,1)S(1)}, u32[]{:S(2)}, u32[]{:S(2)}) %collective-permute-start.22) | collective-permute-done | bytes 131104 | tf_op jit(solution)/shard_map/ppermute | solution.py:67
  131.4 1.0 collective-permute-done.23.refs_3_
  132.4 2.5 %collective-permute-done.24.refs_4_ = bf16[128,512]{1,0:T(8,128)(2,1)S(1)} collective-permute-done((bf16[128,512]{1,0:T(8,128)(2,1)S(1)}, bf16[128,512]{1,0:T(8,128)(2,1)S(1)}, u32[]{:S(2)}, u32[]{:S(2)}) %collective-permute-start.24) | collective-permute-done | bytes 131104 | tf_op jit(solution)/shard_map/ppermute | solution.py:67
  136.2 2.7 %collective-permute-start.27 = (bf16[4,128,512]{2,1,0:T(8,128)(2,1)S(1)}, bf16[4,128,512]{2,1,0:T(8,128)(2,1)S(1)}, u32[]{:S(2)}, u32[]{:S(2)}) collective-permute-start(bf16[4,128,512]{2,1,0:T(8,128)(2,1)S(1)} %join_columns.1.refs_1_), channel_id=1, source_target_pairs={{0,12},{1,13},{2,14},{3,15},{4,0},{5,1},{6,2},{7,3},{8,4},{9,5},{1... | collective-permute-start | bytes 1572872 | tf_op jit(solution)/shard_map/ppermute | solution.py:67
  138.8 3.4 %copy-done = bf16[8192,512]{1,0:T(8,128)(2,1)S(1)} copy-done((bf16[8192,512]{1,0:T(8,128)(2,1)S(1)}, bf16[8192,512]{1,0:T(8,128)(2,1)}, u32[]{:S(2)}) %copy-start) | copy-done | bytes 8388632
  143.0 1.2 project_own.1
  144.2 1.8 collective-permute-done.25.refs_1_
  146.0 3.7 %copy-done.1 = bf16[8192,512]{1,0:T(8,128)(2,1)S(1)} copy-done((bf16[8192,512]{1,0:T(8,128)(2,1)S(1)}, bf16[8192,512]{1,0:T(8,128)(2,1)}, u32[]{:S(2)}) %copy-start.1) | copy-done | bytes 8388632
  150.5 1.7 project_near.1
  152.2 4.2 %collective-permute-done.26.refs_1_ = bf16[4,128,512]{2,1,0:T(8,128)(2,1)S(1)} collective-permute-done((bf16[4,128,512]{2,1,0:T(8,128)(2,1)S(1)}, bf16[4,128,512]{2,1,0:T(8,128)(2,1)S(1)}, u32[]{:S(2)}, u32[]{:S(2)}) %collective-permute-start.26) | collective-permute-done | bytes 524320 | tf_op jit(solution)/shard_map/ppermute | solution.py:67
  156.4 1.2 last_keys.1
  157.7 1.3 last_queries.1.refs_1_
  159.0 2.9 %collective-permute-done.28.refs_3_ = bf16[2,128,64]{2,1,0:T(8,128)(2,1)S(1)} collective-permute-done((bf16[2,128,64]{2,1,0:T(8,128)(2,1)S(1)}, bf16[2,128,64]{2,1,0:T(8,128)(2,1)S(1)}, u32[]{:S(2)}, u32[]{:S(2)}) %collective-permute-start.28) | collective-permute-done | bytes 32800 | tf_op jit(solution)/shard_map/ppermute | solution.py:761
  161.9 3.6 %attend_out.1 = (bf16[32,8192]{1,0:T(8,128)(2,1)S(1)}, bf16[32,8192]{1,0:T(8,128)(2,1)}, bf16[32,8192]{1,0:T(8,128)(2,1)}, bf16[32,8192]{1,0:T(8,128)(2,1)}) custom-call(s32[38]{0:T(128)S(1)} %copy-done.26, bf16[128,512]{1,0:T(8,128)(2,1)S(1)} %last_queries.1.refs_1_, bf16[2,128,64]{2,1,0:T(8,128)(2,1)S(1)} %get-tuple-element.54.refs_2_, ...), custom_call_target="tpu_custom_call" | custom-call | flops 1073741824 | bytes 8683520 | tf_op jit(solution)/shard_map/attend_out/pallas_call | solution.py:101
  165.6 3.2 %collective-permute-start.30 = (bf16[32,8192]{1,0:T(8,128)(2,1)}, bf16[32,8192]{1,0:T(8,128)(2,1)S(1)}, u32[]{:S(2)}, u32[]{:S(2)}) collective-permute-start(bf16[32,8192]{1,0:T(8,128)(2,1)} %get-tuple-element.57), channel_id=1, source_target_pairs={{0,12},{1,13},{2,14},{3,15},{4,0},{5,1},{6,2},{7,3},{8,4},{9,5},{1... | collective-permute-start | bytes 1572872 | tf_op jit(solution)/shard_map/ppermute | solution.py:67
  169.7 13.1 %collective-permute-done.29.refs_2_ = bf16[32,8192]{1,0:T(8,128)(2,1)S(1)} collective-permute-done((bf16[32,8192]{1,0:T(8,128)(2,1)}, bf16[32,8192]{1,0:T(8,128)(2,1)S(1)}, u32[]{:S(2)}, u32[]{:S(2)}) %collective-permute-start.29) | collective-permute-done | bytes 524320 | tf_op jit(solution)/shard_map/ppermute | solution.py:67
  182.7 0.9 collective-permute-done.30.refs_3_
  183.7 0.8 add_ring.1
  184.6 3.2 %collective-permute-start.33 = (bf16[8,8192]{1,0:T(8,128)(2,1)S(1)}, bf16[8,8192]{1,0:T(8,128)(2,1)S(1)}, u32[]{:S(2)}, u32[]{:S(2)}) collective-permute-start(bf16[8,8192]{1,0:T(8,128)(2,1)S(1)} %get-tuple-element.61), channel_id=1, source_target_pairs={{0,3},{1,0},{2,1},{3,2},{4,7},{5,4},{6,5},{7,6},{8,11},{9,8},{10,9... | collective-permute-start | bytes 393224 | tf_op jit(solution)/shard_map/ppermute | solution.py:67
  188.6 2.2 %collective-permute-done.32.refs_2_ = bf16[8,8192]{1,0:T(8,128)(2,1)S(1)} collective-permute-done((bf16[8,8192]{1,0:T(8,128)(2,1)S(1)}, bf16[8,8192]{1,0:T(8,128)(2,1)S(1)}, u32[]{:S(2)}, u32[]{:S(2)}) %collective-permute-start.32) | collective-permute-done | bytes 131104 | tf_op jit(solution)/shard_map/ppermute | solution.py:67
  190.7 1.0 collective-permute-done.33.refs_3_
  191.7 2.5 %collective-permute-done.34.refs_4_ = bf16[8,8192]{1,0:T(8,128)(2,1)S(1)} collective-permute-done((bf16[8,8192]{1,0:T(8,128)(2,1)S(1)}, bf16[8,8192]{1,0:T(8,128)(2,1)S(1)}, u32[]{:S(2)}, u32[]{:S(2)}) %collective-permute-start.34) | collective-permute-done | bytes 131104 | tf_op jit(solution)/shard_map/ppermute | solution.py:67
  194.3 1.3 finish.1
  (154 shorter events, 21.3 us)
Async XLA Ops:
  1.3 1.0 copy-start.16
  2.3 6.0 %copy-start.22 = (s32[38]{0:T(128)}, s32[38]{0:T(128)S(1)}, u32[]{:S(2)}) copy-start(s32[38]{0:T(128)S(1)} %concatenate.9.refs_0_) | copy-start | bytes 460
  2.9 5.4 %copy-start.6 = (bf16[64,1536]{1,0:T(8,128)(2,1)}, bf16[64,1536]{1,0:T(8,128)(2,1)S(1)}, u32[]{:S(2)}) copy-start(bf16[64,1536]{1,0:T(8,128)(2,1)S(1)} %take_qkv.1.refs_1_.refs_5_) | copy-start | bytes 589828
  2.9 17.9 %collective-permute-start.1 = (bf16[64,1536]{1,0:T(8,128)(2,1)S(1)}, bf16[64,1536]{1,0:T(8,128)(2,1)S(1)}, u32[]{:S(2)}, u32[]{:S(2)}) collective-permute-start(bf16[64,1536]{1,0:T(8,128)(2,1)S(1)} %take_qkv.1.refs_1_.refs_5_), channel_id=1, source_target_pairs={{0,1},{1,2},{2,3},{3,0},{4,5},{5,6},{6,7},{7,4},{8,9},{9,10},{10,1... | collective-permute-start | bytes 589832 | tf_op jit(solution)/shard_map/ppermute | solution.py:67
  4.6 18.8 %collective-permute-start.2 = (bf16[64,1536]{1,0:T(8,128)(2,1)S(1)}, bf16[64,1536]{1,0:T(8,128)(2,1)S(1)}, u32[]{:S(2)}, u32[]{:S(2)}) collective-permute-start(bf16[64,1536]{1,0:T(8,128)(2,1)S(1)} %take_qkv.1.refs_1_.refs_5_), channel_id=1, source_target_pairs={{0,3},{1,0},{2,1},{3,2},{4,7},{5,4},{6,5},{7,6},{8,11},{9,8},{10,9... | collective-permute-start | bytes 589832 | tf_op jit(solution)/shard_map/ppermute | solution.py:67
  6.2 17.2 %collective-permute-start.3 = (bf16[64,1536]{1,0:T(8,128)(2,1)S(1)}, bf16[64,1536]{1,0:T(8,128)(2,1)S(1)}, u32[]{:S(2)}, u32[]{:S(2)}) collective-permute-start(bf16[64,1536]{1,0:T(8,128)(2,1)S(1)} %take_qkv.1.refs_1_.refs_5_), channel_id=1, source_target_pairs={{0,2},{1,3},{2,0},{3,1},{4,6},{5,7},{6,4},{7,5},{8,10},{9,11},{10,... | collective-permute-start | bytes 589832 | tf_op jit(solution)/shard_map/ppermute | solution.py:67
  8.2 34.0 %collective-permute-start = (bf16[128,1024]{1,0:T(8,128)(2,1)}, bf16[128,1024]{1,0:T(8,128)(2,1)}, u32[]{:S(2)}, u32[]{:S(2)}) collective-permute-start(bf16[128,1024]{1,0:T(8,128)(2,1)} %bitcast.28), channel_id=1, source_target_pairs={{0,16},{16,0},{32,48},{48,32},{64,80},{80,64},{96,112},{112,96},{1... | collective-permute-start | bytes 786440 | tf_op jit(solution)/shard_map/ppermute | solution.py:71
  11.0 40.6 %copy-start.26 = (s32[38]{0:T(128)S(1)}, s32[38]{0:T(128)}, u32[]{:S(2)}) copy-start(s32[38]{0:T(128)} %copy-done.22) | copy-start | bytes 460
  11.0 52.9 %copy-start.5 = (bf16[64,3584]{1,0:T(8,128)(2,1)S(1)}, bf16[64,3584]{1,0:T(8,128)(2,1)}, u32[]{:S(2)}) copy-start(bf16[64,3584]{1,0:T(8,128)(2,1)} %get-tuple-element.34.refs_1_) | copy-start | bytes 1376260
  11.0 18.6 %collective-permute-start.8 = (bf16[64,3584]{1,0:T(8,128)(2,1)}, bf16[64,3584]{1,0:T(8,128)(2,1)S(1)}, u32[]{:S(2)}, u32[]{:S(2)}) collective-permute-start(bf16[64,3584]{1,0:T(8,128)(2,1)} %get-tuple-element.34.refs_1_), channel_id=1, source_target_pairs={{0,1},{1,2},{2,3},{3,0},{4,5},{5,6},{6,7},{7,4},{8,9},{9,10},{10,1... | collective-permute-start | bytes 1376264 | tf_op jit(solution)/shard_map/ppermute | solution.py:67
  17.1 2.0 %copy-start.28 = (s32[128,8]{1,0:T(8,128)}, s32[128,8]{1,0:T(8,128)S(1)}, u32[]{:S(2)}) copy-start(s32[128,8]{1,0:T(8,128)S(1)} %reshape.230) | copy-start | bytes 12292
  20.7 24.5 %collective-permute-start.9 = (bf16[64,3584]{1,0:T(8,128)(2,1)}, bf16[64,3584]{1,0:T(8,128)(2,1)}, u32[]{:S(2)}, u32[]{:S(2)}) collective-permute-start(bf16[64,3584]{1,0:T(8,128)(2,1)} %get-tuple-element.35), channel_id=1, source_target_pairs={{0,3},{1,0},{2,1},{3,2},{4,7},{5,4},{6,5},{7,6},{8,11},{9,8},{10,9... | collective-permute-start | bytes 1376264 | tf_op jit(solution)/shard_map/ppermute | solution.py:67
  23.4 0.9 copy-start.7
  25.6 19.6 %collective-permute-start.4 = (bf16[4,64,1536]{2,1,0:T(8,128)(2,1)S(1)}, bf16[4,64,1536]{2,1,0:T(8,128)(2,1)S(1)}, u32[]{:S(2)}, u32[]{:S(2)}) collective-permute-start(bf16[4,64,1536]{2,1,0:T(8,128)(2,1)S(1)} %join_qkv.1.refs_2_), channel_id=1, source_target_pairs={{0,4},{1,5},{2,6},{3,7},{4,8},{5,9},{6,10},{7,11},{8,12},{9,13},{1... | collective-permute-start | bytes 2359304 | tf_op jit(solution)/shard_map/ppermute | solution.py:67
  27.1 12.0 %collective-permute-start.5 = (bf16[4,64,1536]{2,1,0:T(8,128)(2,1)S(1)}, bf16[4,64,1536]{2,1,0:T(8,128)(2,1)S(1)}, u32[]{:S(2)}, u32[]{:S(2)}) collective-permute-start(bf16[4,64,1536]{2,1,0:T(8,128)(2,1)S(1)} %join_qkv.1.refs_2_), channel_id=1, source_target_pairs={{0,12},{1,13},{2,14},{3,15},{4,0},{5,1},{6,2},{7,3},{8,4},{9,5},{1... | collective-permute-start | bytes 2359304 | tf_op jit(solution)/shard_map/ppermute | solution.py:67
  29.6 15.6 %collective-permute-start.10 = (bf16[64,3584]{1,0:T(8,128)(2,1)S(1)}, bf16[64,3584]{1,0:T(8,128)(2,1)}, u32[]{:S(2)}, u32[]{:S(2)}) collective-permute-start(bf16[64,3584]{1,0:T(8,128)(2,1)S(1)} %collective-permute-done.8.refs_2_), channel_id=1, source_target_pairs={{0,1},{1,2},{2,3},{3,0},{4,5},{5,6},{6,7},{7,4},{8,9},{9,10},{10,1... | collective-permute-start | bytes 1376264 | tf_op jit(solution)/shard_map/ppermute | solution.py:67
  30.9 33.0 %copy-start.27 = (bf16[64,1024]{1,0:T(8,128)(2,1)S(1)}, bf16[64,1024]{1,0:T(8,128)(2,1)}, u32[]{:S(2)}) copy-start(bf16[64,1024]{1,0:T(8,128)(2,1)} %get-tuple-element.38.refs_5_) | copy-start | bytes 393220
  39.1 12.5 %collective-permute-start.6 = (bf16[4,64,1536]{2,1,0:T(8,128)(2,1)S(1)}, bf16[4,64,1536]{2,1,0:T(8,128)(2,1)S(1)}, u32[]{:S(2)}, u32[]{:S(2)}) collective-permute-start(bf16[4,64,1536]{2,1,0:T(8,128)(2,1)S(1)} %collective-permute-done.5.refs_4_.refs_6_), channel_id=1, source_target_pairs={{0,12},{1,13},{2,14},{3,15},{4,0},{5,1},{6,2},{7,3},{8,4},{9,5},{1... | collective-permute-start | bytes 2359304 | tf_op jit(solution)/shard_map/ppermute | solution.py:67
  42.2 3.0 %copy-start.10 = (f32[128,64]{1,0:T(8,128)}, f32[128,64]{1,0:T(8,128)S(1)}, u32[]{:S(2)}) copy-start(f32[128,64]{1,0:T(8,128)S(1)} %get-tuple-element.76.refs_15_.refs_7_) | copy-start | bytes 98308
  42.2 3.0 %copy-start.12 = (f32[128,64]{1,0:T(8,128)}, f32[128,64]{1,0:T(8,128)S(1)}, u32[]{:S(2)}) copy-start(f32[128,64]{1,0:T(8,128)S(1)} %get-tuple-element.77.refs_14_.refs_6_) | copy-start | bytes 98308
  42.2 1.0 copy-start.21
  45.2 1.0 copy-start.4
  46.3 0.8 copy-start.17
  47.0 0.8 copy-start.19
  49.7 14.2 %collective-permute-start.11 = (bf16[4,64,1536]{2,1,0:T(8,128)(2,1)S(1)}, bf16[4,64,1536]{2,1,0:T(8,128)(2,1)S(1)}, u32[]{:S(2)}, u32[]{:S(2)}) collective-permute-start(bf16[4,64,1536]{2,1,0:T(8,128)(2,1)S(1)} %join_middle.1.refs_4_.refs_3_), channel_id=1, source_target_pairs={{0,4},{1,5},{2,6},{3,7},{4,8},{5,9},{6,10},{7,11},{8,12},{9,13},{1... | collective-permute-start | bytes 2359304 | tf_op jit(solution)/shard_map/ppermute | solution.py:67
  49.8 8.2 %collective-permute-start.15 = (bf16[64,1024]{1,0:T(8,128)(2,1)}, bf16[64,1024]{1,0:T(8,128)(2,1)S(1)}, u32[]{:S(2)}, u32[]{:S(2)}) collective-permute-start(bf16[64,1024]{1,0:T(8,128)(2,1)} %get-tuple-element.39), channel_id=1, source_target_pairs={{0,2},{1,3},{2,0},{3,1},{4,6},{5,7},{6,4},{7,5},{8,10},{9,11},{10,... | collective-permute-start | bytes 393224 | tf_op jit(solution)/shard_map/ppermute | solution.py:67
  65.1 10.7 %collective-permute-start.17 = (bf16[4,64,1280]{2,1,0:T(8,128)(2,1)S(1)}, bf16[4,64,1280]{2,1,0:T(8,128)(2,1)S(1)}, u32[]{:S(2)}, u32[]{:S(2)}) collective-permute-start(bf16[4,64,1280]{2,1,0:T(8,128)(2,1)S(1)} %get-tuple-element.41), channel_id=1, source_target_pairs={{0,12},{1,13},{2,14},{3,15},{4,0},{5,1},{6,2},{7,3},{8,4},{9,5},{1... | collective-permute-start | bytes 1966088 | tf_op jit(solution)/shard_map/ppermute | solution.py:67
  65.2 19.0 %collective-permute-start.12 = (bf16[4,64,1536]{2,1,0:T(8,128)(2,1)S(1)}, bf16[4,64,1536]{2,1,0:T(8,128)(2,1)S(1)}, u32[]{:S(2)}, u32[]{:S(2)}) collective-permute-start(bf16[4,64,1536]{2,1,0:T(8,128)(2,1)S(1)} %join_middle.1.refs_4_.refs_3_), channel_id=1, source_target_pairs={{0,12},{1,13},{2,14},{3,15},{4,0},{5,1},{6,2},{7,3},{8,4},{9,5},{1... | collective-permute-start | bytes 2359304 | tf_op jit(solution)/shard_map/ppermute | solution.py:67
  65.7 18.6 %collective-permute-start.13 = (bf16[4,64,1536]{2,1,0:T(8,128)(2,1)S(1)}, bf16[4,64,1536]{2,1,0:T(8,128)(2,1)S(1)}, u32[]{:S(2)}, u32[]{:S(2)}) collective-permute-start(bf16[4,64,1536]{2,1,0:T(8,128)(2,1)S(1)} %collective-permute-done.11.refs_5_.refs_4_.refs_8_), channel_id=1, source_target_pairs={{0,4},{1,5},{2,6},{3,7},{4,8},{5,9},{6,10},{7,11},{8,12},{9,13},{1... | collective-permute-start | bytes 2359304 | tf_op jit(solution)/shard_map/ppermute | solution.py:67
  67.3 24.9 %collective-permute-start.16 = (bf16[4,64,1280]{2,1,0:T(8,128)(2,1)S(1)}, bf16[4,64,1280]{2,1,0:T(8,128)(2,1)S(1)}, u32[]{:S(2)}, u32[]{:S(2)}) collective-permute-start(bf16[4,64,1280]{2,1,0:T(8,128)(2,1)S(1)} %get-tuple-element.40.refs_3_), channel_id=1, source_target_pairs={{0,4},{1,5},{2,6},{3,7},{4,8},{5,9},{6,10},{7,11},{8,12},{9,13},{1... | collective-permute-start | bytes 1966088 | tf_op jit(solution)/shard_map/ppermute | solution.py:67
  75.8 19.6 %collective-permute-start.18 = (bf16[4,64,1280]{2,1,0:T(8,128)(2,1)S(1)}, bf16[4,64,1280]{2,1,0:T(8,128)(2,1)S(1)}, u32[]{:S(2)}, u32[]{:S(2)}) collective-permute-start(bf16[4,64,1280]{2,1,0:T(8,128)(2,1)S(1)} %collective-permute-done.17.refs_3_.refs_5_), channel_id=1, source_target_pairs={{0,12},{1,13},{2,14},{3,15},{4,0},{5,1},{6,2},{7,3},{8,4},{9,5},{1... | collective-permute-start | bytes 1966088 | tf_op jit(solution)/shard_map/ppermute | solution.py:67
  77.0 7.2 %collective-permute-start.7 = (bf16[8,256,64]{2,1,0:T(8,128)(2,1)S(1)}, bf16[8,256,64]{2,1,0:T(8,128)(2,1)S(1)}, u32[]{:S(2)}, u32[]{:S(2)}) collective-permute-start(bf16[8,256,64]{2,1,0:T(8,128)(2,1)S(1)} %span_attention.1.refs_1_.refs_7_), channel_id=1, source_target_pairs={{0,16},{16,0},{32,48},{48,32},{64,80},{80,64},{96,112},{112,96},{1... | collective-permute-start | bytes 786440 | tf_op jit(solution)/shard_map/ppermute | solution.py:71
  85.5 53.3 %copy-start.2 = (bf16[2,8192,64]{1,2,0:T(8,128)(2,1)S(1)}, bf16[2,8192,64]{1,2,0:T(8,128)(2,1)}, u32[]{:S(2)}) copy-start(bf16[2,8192,64]{1,2,0:T(8,128)(2,1)} %param.30) | copy-start | bytes 6291460
  85.5 7.5 %collective-permute-start.14 = (bf16[256,512]{1,0:T(8,128)(2,1)S(1)}, bf16[256,512]{1,0:T(8,128)(2,1)S(1)}, u32[]{:S(2)}, u32[]{:S(2)}) collective-permute-start(bf16[256,512]{1,0:T(8,128)(2,1)S(1)} %context_out.1.refs_1_), channel_id=1, source_target_pairs={{0,16},{16,0},{32,48},{48,32},{64,80},{80,64},{96,112},{112,96},{1... | collective-permute-start | bytes 786440 | tf_op jit(solution)/shard_map/ppermute | solution.py:71
  85.6 6.6 %collective-permute-start.19 = (bf16[4,64,256]{2,1,0:T(8,128)(2,1)S(1)}, bf16[4,64,256]{2,1,0:T(8,128)(2,1)S(1)}, u32[]{:S(2)}, u32[]{:S(2)}) collective-permute-start(bf16[4,64,256]{2,1,0:T(8,128)(2,1)S(1)} %get-tuple-element.43), channel_id=1, source_target_pairs={{0,8},{1,9},{2,10},{3,11},{4,12},{5,13},{6,14},{7,15},{8,0},{9,1},... | collective-permute-start | bytes 393224 | tf_op jit(solution)/shard_map/ppermute | solution.py:67
  92.8 16.6 %collective-permute-start.21 = (bf16[4,4,64,256]{3,2,1,0:T(8,128)(2,1)S(1)}, bf16[4,4,64,256]{3,2,1,0:T(8,128)(2,1)}, u32[]{:S(2)}, u32[]{:S(2)}) collective-permute-start(bf16[4,4,64,256]{3,2,1,0:T(8,128)(2,1)S(1)} %join_proj.1.refs_7_.refs_4_), channel_id=1, source_target_pairs={{0,16},{16,0},{32,48},{48,32},{64,80},{80,64},{96,112},{112,96},{1... | collective-permute-start | bytes 1572872 | tf_op jit(solution)/shard_map/ppermute | solution.py:71
  96.8 1.7 collective-permute-start.20
  100.2 20.0 %all-to-all-start = ((bf16[128,8,128]{2,1,0:T(8,128)(2,1)}), bf16[128,8,128]{2,1,0:T(8,128)(2,1)S(1)}, u32[]{:S(2)}, u32[]{:S(2)}) async-start(bf16[128,8,128]{2,1,0:T(8,128)(2,1)} %bitcast.9), calls=%async_computation | async-start | bytes 524288 | tf_op jit(solution)/shard_map/all_to_all | solution.py:691
  120.2 1.6 copy-start.3
  125.1 6.2 %collective-permute-start.22 = (bf16[128,512]{1,0:T(8,128)(2,1)S(1)}, bf16[128,512]{1,0:T(8,128)(2,1)S(1)}, u32[]{:S(2)}, u32[]{:S(2)}) collective-permute-start(bf16[128,512]{1,0:T(8,128)(2,1)S(1)} %embed.1.refs_1_), channel_id=1, source_target_pairs={{0,1},{1,2},{2,3},{3,0},{4,5},{5,6},{6,7},{7,4},{8,9},{9,10},{10,1... | collective-permute-start | bytes 393224 | tf_op jit(solution)/shard_map/ppermute | solution.py:67
  125.9 6.5 %collective-permute-start.23 = (bf16[128,512]{1,0:T(8,128)(2,1)S(1)}, bf16[128,512]{1,0:T(8,128)(2,1)S(1)}, u32[]{:S(2)}, u32[]{:S(2)}) collective-permute-start(bf16[128,512]{1,0:T(8,128)(2,1)S(1)} %embed.1.refs_1_), channel_id=1, source_target_pairs={{0,3},{1,0},{2,1},{3,2},{4,7},{5,4},{6,5},{7,6},{8,11},{9,8},{10,9... | collective-permute-start | bytes 393224 | tf_op jit(solution)/shard_map/ppermute | solution.py:67
  128.5 6.5 %collective-permute-start.24 = (bf16[128,512]{1,0:T(8,128)(2,1)S(1)}, bf16[128,512]{1,0:T(8,128)(2,1)S(1)}, u32[]{:S(2)}, u32[]{:S(2)}) collective-permute-start(bf16[128,512]{1,0:T(8,128)(2,1)S(1)} %embed.1.refs_1_), channel_id=1, source_target_pairs={{0,2},{1,3},{2,0},{3,1},{4,6},{5,7},{6,4},{7,5},{8,10},{9,11},{10,... | collective-permute-start | bytes 393224 | tf_op jit(solution)/shard_map/ppermute | solution.py:67
  135.5 10.5 %collective-permute-start.25 = (bf16[4,128,512]{2,1,0:T(8,128)(2,1)S(1)}, bf16[4,128,512]{2,1,0:T(8,128)(2,1)S(1)}, u32[]{:S(2)}, u32[]{:S(2)}) collective-permute-start(bf16[4,128,512]{2,1,0:T(8,128)(2,1)S(1)} %join_columns.1.refs_1_), channel_id=1, source_target_pairs={{0,4},{1,5},{2,6},{3,7},{4,8},{5,9},{6,10},{7,11},{8,12},{9,13},{1... | collective-permute-start | bytes 1572872 | tf_op jit(solution)/shard_map/ppermute | solution.py:67
  136.2 9.8 %collective-permute-start.27 = (bf16[4,128,512]{2,1,0:T(8,128)(2,1)S(1)}, bf16[4,128,512]{2,1,0:T(8,128)(2,1)S(1)}, u32[]{:S(2)}, u32[]{:S(2)}) collective-permute-start(bf16[4,128,512]{2,1,0:T(8,128)(2,1)S(1)} %join_columns.1.refs_1_), channel_id=1, source_target_pairs={{0,12},{1,13},{2,14},{3,15},{4,0},{5,1},{6,2},{7,3},{8,4},{9,5},{1... | collective-permute-start | bytes 1572872 | tf_op jit(solution)/shard_map/ppermute | solution.py:67
  138.8 3.4 %copy-start = (bf16[8192,512]{1,0:T(8,128)(2,1)S(1)}, bf16[8192,512]{1,0:T(8,128)(2,1)}, u32[]{:S(2)}) copy-start(bf16[8192,512]{1,0:T(8,128)(2,1)} %refs_3_.7) | copy-start | bytes 25165828
  142.2 0.8 copy-start.14
  143.0 13.4 %copy-start.13 = (f32[128,64]{1,0:T(8,128)S(1)}, f32[128,64]{1,0:T(8,128)}, u32[]{:S(2)}) copy-start(f32[128,64]{1,0:T(8,128)} %copy-done.12) | copy-start | bytes 98308
  143.0 14.7 %slice-start = ((s8[8388608]{0:T(1024)(128)(4,1)}), s8[4194304]{0:T(1024)(128)(4,1)S(1)}, s32[]{:S(2)}) async-start(s8[8388608]{0:T(1024)(128)(4,1)} %bitcast.17), calls=%async_computation.1 | async-start | bytes 8388608
  144.1 12.2 %copy-start.11 = (f32[128,64]{1,0:T(8,128)S(1)}, f32[128,64]{1,0:T(8,128)}, u32[]{:S(2)}) copy-start(f32[128,64]{1,0:T(8,128)} %copy-done.10) | copy-start | bytes 98308
  146.0 13.1 %copy-start.9 = (bf16[4,128,512]{2,1,0:T(8,128)(2,1)}, bf16[4,128,512]{2,1,0:T(8,128)(2,1)S(1)}, u32[]{:S(2)}) copy-start(bf16[4,128,512]{2,1,0:T(8,128)(2,1)S(1)} %collective-permute-done.25.refs_1_) | copy-start | bytes 1572868
  146.0 10.4 %collective-permute-start.26 = (bf16[4,128,512]{2,1,0:T(8,128)(2,1)S(1)}, bf16[4,128,512]{2,1,0:T(8,128)(2,1)S(1)}, u32[]{:S(2)}, u32[]{:S(2)}) collective-permute-start(bf16[4,128,512]{2,1,0:T(8,128)(2,1)S(1)} %collective-permute-done.25.refs_1_), channel_id=1, source_target_pairs={{0,4},{1,5},{2,6},{3,7},{4,8},{5,9},{6,10},{7,11},{8,12},{9,13},{1... | collective-permute-start | bytes 1572872 | tf_op jit(solution)/shard_map/ppermute | solution.py:67
  146.0 11.6 %copy-start.8 = (bf16[4,128,512]{2,1,0:T(8,128)(2,1)}, bf16[4,128,512]{2,1,0:T(8,128)(2,1)S(1)}, u32[]{:S(2)}) copy-start(bf16[4,128,512]{2,1,0:T(8,128)(2,1)S(1)} %collective-permute-done.27.refs_2_) | copy-start | bytes 1572868
  146.0 3.7 %copy-start.1 = (bf16[8192,512]{1,0:T(8,128)(2,1)S(1)}, bf16[8192,512]{1,0:T(8,128)(2,1)}, u32[]{:S(2)}) copy-start(bf16[8192,512]{1,0:T(8,128)(2,1)} %refs_3_.7) | copy-start | bytes 25165828
  150.5 7.1 %slice-start.1 = ((s8[8388608]{0:T(1024)(128)(4,1)}), s8[4194304]{0:T(1024)(128)(4,1)S(1)}, s32[]{:S(2)}) async-start(s8[8388608]{0:T(1024)(128)(4,1)} %bitcast.17), calls=%async_computation.2 | async-start | bytes 8388608
  150.5 11.4 %slice-start.2 = ((s8[8388608]{0:T(1024)(128)(4,1)}), s8[4194304]{0:T(1024)(128)(4,1)S(1)}, s32[]{:S(2)}) async-start(s8[8388608]{0:T(1024)(128)(4,1)} %bitcast.22), calls=%async_computation.3 | async-start | bytes 8388608
  152.2 9.7 %copy-start.20 = (bf16[128,128]{1,0:T(8,128)(2,1)S(1)}, bf16[128,128]{1,0:T(8,128)(2,1)}, u32[]{:S(2)}) copy-start(bf16[128,128]{1,0:T(8,128)(2,1)} %fusion.1.refs_10_.refs_5_) | copy-start | bytes 98308
  156.4 5.5 %slice-start.3 = ((s8[8388608]{0:T(1024)(128)(4,1)}), s8[4194304]{0:T(1024)(128)(4,1)S(1)}, s32[]{:S(2)}) async-start(s8[8388608]{0:T(1024)(128)(4,1)} %bitcast.22), calls=%async_computation.4 | async-start | bytes 8388608
  157.6 4.3 %collective-permute-start.28 = (bf16[2,128,64]{2,1,0:T(8,128)(2,1)S(1)}, bf16[2,128,64]{2,1,0:T(8,128)(2,1)S(1)}, u32[]{:S(2)}, u32[]{:S(2)}) collective-permute-start(bf16[2,128,64]{2,1,0:T(8,128)(2,1)S(1)} %get-tuple-element.54.refs_2_), channel_id=1, source_target_pairs={{0,1},{1,0},{2,3},{3,2},{4,5},{5,4},{6,7},{7,6},{8,9},{9,8},{10,11... | collective-permute-start | bytes 98312 | tf_op jit(solution)/shard_map/ppermute | solution.py:761
  165.6 17.2 %collective-permute-start.29 = (bf16[32,8192]{1,0:T(8,128)(2,1)}, bf16[32,8192]{1,0:T(8,128)(2,1)S(1)}, u32[]{:S(2)}, u32[]{:S(2)}) collective-permute-start(bf16[32,8192]{1,0:T(8,128)(2,1)} %get-tuple-element.56), channel_id=1, source_target_pairs={{0,4},{1,5},{2,6},{3,7},{4,8},{5,9},{6,10},{7,11},{8,12},{9,13},{1... | collective-permute-start | bytes 1572872 | tf_op jit(solution)/shard_map/ppermute | solution.py:67
  165.6 18.1 %collective-permute-start.30 = (bf16[32,8192]{1,0:T(8,128)(2,1)}, bf16[32,8192]{1,0:T(8,128)(2,1)S(1)}, u32[]{:S(2)}, u32[]{:S(2)}) collective-permute-start(bf16[32,8192]{1,0:T(8,128)(2,1)} %get-tuple-element.57), channel_id=1, source_target_pairs={{0,12},{1,13},{2,14},{3,15},{4,0},{5,1},{6,2},{7,3},{8,4},{9,5},{1... | collective-permute-start | bytes 1572872 | tf_op jit(solution)/shard_map/ppermute | solution.py:67
  168.8 14.9 %collective-permute-start.31 = (bf16[32,8192]{1,0:T(8,128)(2,1)}, bf16[32,8192]{1,0:T(8,128)(2,1)S(1)}, u32[]{:S(2)}, u32[]{:S(2)}) collective-permute-start(bf16[32,8192]{1,0:T(8,128)(2,1)} %get-tuple-element.58), channel_id=1, source_target_pairs={{0,8},{1,9},{2,10},{3,11},{4,12},{5,13},{6,14},{7,15},{8,0},{9,1},... | collective-permute-start | bytes 1572872 | tf_op jit(solution)/shard_map/ppermute | solution.py:67
  184.5 6.2 %collective-permute-start.32 = (bf16[8,8192]{1,0:T(8,128)(2,1)S(1)}, bf16[8,8192]{1,0:T(8,128)(2,1)S(1)}, u32[]{:S(2)}, u32[]{:S(2)}) collective-permute-start(bf16[8,8192]{1,0:T(8,128)(2,1)S(1)} %get-tuple-element.60), channel_id=1, source_target_pairs={{0,1},{1,2},{2,3},{3,0},{4,5},{5,6},{6,7},{7,4},{8,9},{9,10},{10,1... | collective-permute-start | bytes 393224 | tf_op jit(solution)/shard_map/ppermute | solution.py:67
  184.6 7.1 %collective-permute-start.33 = (bf16[8,8192]{1,0:T(8,128)(2,1)S(1)}, bf16[8,8192]{1,0:T(8,128)(2,1)S(1)}, u32[]{:S(2)}, u32[]{:S(2)}) collective-permute-start(bf16[8,8192]{1,0:T(8,128)(2,1)S(1)} %get-tuple-element.61), channel_id=1, source_target_pairs={{0,3},{1,0},{2,1},{3,2},{4,7},{5,4},{6,5},{7,6},{8,11},{9,8},{10,9... | collective-permute-start | bytes 393224 | tf_op jit(solution)/shard_map/ppermute | solution.py:67
  187.8 6.5 %collective-permute-start.34 = (bf16[8,8192]{1,0:T(8,128)(2,1)S(1)}, bf16[8,8192]{1,0:T(8,128)(2,1)S(1)}, u32[]{:S(2)}, u32[]{:S(2)}) collective-permute-start(bf16[8,8192]{1,0:T(8,128)(2,1)S(1)} %get-tuple-element.62), channel_id=1, source_target_pairs={{0,2},{1,3},{2,0},{3,1},{4,6},{5,7},{6,4},{7,5},{8,10},{9,11},{10,... | collective-permute-start | bytes 393224 | tf_op jit(solution)/shard_map/ppermute | solution.py:67
  (5 other events, 3.6 us)

commit v8 on v7

--- a/solution.py
+++ b/solution.py
@@ -613,7 +613,7 @@
         rest_ring,
         shape_of((SIDE, share, middle_cols)),
         limit=8,
-        after=[*qkv[1:3], token_pieces, *early],
+        after=[*qkv[1:3], token_pieces],
     )
     left = to_ring(middle_block, 2, 1)
     middle = [middle_block, left, to_ring(middle_block, 2, -1), to_ring(left, 2, 1)]
@@ -635,7 +635,7 @@
         [*rest_ring, kept_cols, beyond_cols],
         (lower_shape, lower_shape, far_shape, far_shape),
         limit=8,
-        after=[context, left],
+        after=[context, *middle[1:3]],
     )
     lower_right = to_ring(lower_down, 2, -1)
     lower = [lower_up, to_ring(lower_up, 2, 1), lower_right, to_ring(lower_right, 2, -1)]
@@ -648,6 +648,7 @@
         shape_of((all_rows, width // 2)),
         [pltpu.VMEM((tensor_count, all_rows, share), jnp.bfloat16)],
         flops=2 * all_rows * width * width // 2,
+        after=[far_beyond],
     )
     first_out, inner = whole_call(
         norm_up,

time: 198 us -> 208 us (1.051)
  waiting for transfers between devices: 84.8 us -> 64.2 us
  local copies, waits for them, and re-layouts: 23.2 us -> 39.9 us
  starting transfers between devices: 45.2 us -> 53.1 us
  Pallas kernels: 31.8 us -> 35.5 us
  other arithmetic: 9.27 us -> 12.4 us
    ppermute x29, waiting for transfers between devices: 69.9 us -> 52.9 us  [to_ring(): return lax.ppermute(value, AXES, ring_pairs(phase, distance))]
    unnamed x66 -> x68, local copies, waits for them, and re-layouts: 18.5 us -> 29.5 us
    ppermute x29, starting transfers between devices: 35.1 us -> 43.2 us  [to_ring(): return lax.ppermute(value, AXES, ring_pairs(phase, distance))]
    pallas_call x21, Pallas kernels: 31.8 us -> 35.5 us  [whole_call(): pl.pallas_call(run, name=name, out_shape=outs, in_specs=[SMEM] + [VMEM] *...]
    ppermute x1, waiting for transfers between devices: 2.86 us -> 0.01 us  [local(): lax.ppermute(own_kv, 'tensor', [(index, index ^ 1) for index in range(ten...]
    gt x3, local copies, waits for them, and re-layouts: 0.3 us -> 2.72 us  [visibility(): expanded = jnp.repeat(jnp.repeat(masks, CPP, axis=0), CPP, axis=1) > 0]
  transfers between devices with their start and end apart: 36 -> 36, of which waited for: 20 -> 21; matrix products, arithmetic and copies ran while one was open for 6% -> 10% of each run, Pallas kernels for 10% -> 10%
where the time goes in v8:
time: 208 us; the launch traced here: 206 us
  waiting for transfers between devices  64.2 us (31%)
  starting transfers between devices  53.1 us (26%)
  local copies, waits for them, and re-layouts  39.9 us (19%)
  Pallas kernels  35.5 us (17%)
  other arithmetic  12.4 us (6%)
    ppermute x29, waiting for transfers between devices, to_ring(): return lax.ppermute(value, AXES, ring_pairs(phase, distance))  52.9 us
    ppermute x29, starting transfers between devices, to_ring(): return lax.ppermute(value, AXES, ring_pairs(phase, distance))  43.2 us
    pallas_call x21, Pallas kernels, whole_call(): pl.pallas_call(run, name=name, out_shape=outs, in_specs=[SMEM] + [VMEM] *...  35.5 us
    unnamed x68, local copies, waits for them, and re-layouts  29.5 us
    all_to_all x1, waiting for transfers between devices, local(): lax.all_to_all(outgoing.reshape(device_count, width // 128, 128), AXES, 0...  10.8 us
    all_to_all x1, starting transfers between devices, local(): lax.all_to_all(outgoing.reshape(device_count, width // 128, 128), AXES, 0...  8.9 us
  transfers between devices with their start and end apart: 36, of which 21 were waited for; matrix products, arithmetic and copies ran while one was open for 10% of the time, Pallas kernels for 10%

profile of v8, /device:TPU:0, one launch (start us, length us, event | category | flops | bytes accessed | tf_op | source)
XLA Modules:
  0.0 206.2 jit_solution(15492639138821195016)
XLA Ops:
  1.3 1.0 copy-done.17
  2.9 1.7 collective-permute-start.1
  4.6 1.6 collective-permute-start.2
  6.2 2.1 %collective-permute-start.3 = (bf16[64,1536]{1,0:T(8,128)(2,1)S(1)}, bf16[64,1536]{1,0:T(8,128)(2,1)S(1)}, u32[]{:S(2)}, u32[]{:S(2)}) collective-permute-start(bf16[64,1536]{1,0:T(8,128)(2,1)S(1)} %take_qkv.1.refs_1_.refs_5_), channel_id=1, source_target_pairs={{0,2},{1,3},{2,0},{3,1},{4,6},{5,7},{6,4},{7,5},{8,10},{9,11},{10,... | collective-permute-start | bytes 589832 | tf_op jit(solution)/shard_map/ppermute | solution.py:67
  8.3 2.8 %take_rest.1 = (bf16[64,3584]{1,0:T(8,128)(2,1)}, bf16[64,3584]{1,0:T(8,128)(2,1)}, bf16[64,1024]{1,0:T(8,128)(2,1)}, bf16[64,1024]{1,0:T(8,128)(2,1)}) custom-call(s32[38]{0:T(128)} %copy-done.21, bf16[64,1024]{1,0:T(8,128)(2,1)} %refs_1_.3, bf16[64,2048]{1,0:T(8,128)(2,1)} %refs_2_.1, bf16[128,1024]{1,0:T(8,128)(2,1)} %refs_3_.4, ...), custom_call_target="tpu_custom_call" | custom-call | bytes 1703936 | tf_op jit(solution)/shard_map/take_rest/pallas_call | solution.py:101
  11.7 1.6 collective-permute-done.3.refs_4_
  15.5 2.9 %collective-permute-start.5 = (bf16[4,64,1536]{2,1,0:T(8,128)(2,1)S(1)}, bf16[4,64,1536]{2,1,0:T(8,128)(2,1)S(1)}, u32[]{:S(2)}, u32[]{:S(2)}) collective-permute-start(bf16[4,64,1536]{2,1,0:T(8,128)(2,1)S(1)} %join_qkv.1.refs_2_), channel_id=1, source_target_pairs={{0,12},{1,13},{2,14},{3,15},{4,0},{5,1},{6,2},{7,3},{8,4},{9,5},{1... | collective-permute-start | bytes 2359304 | tf_op jit(solution)/shard_map/ppermute | solution.py:67
  18.4 1.8 collective-permute-start.9
  21.1 11.5 %collective-permute-done.5.refs_4_.refs_6_ = bf16[4,64,1536]{2,1,0:T(8,128)(2,1)S(1)} collective-permute-done((bf16[4,64,1536]{2,1,0:T(8,128)(2,1)S(1)}, bf16[4,64,1536]{2,1,0:T(8,128)(2,1)S(1)}, u32[]{:S(2)}, u32[]{:S(2)}) %collective-permute-start.5) | collective-permute-done | bytes 786464 | tf_op jit(solution)/shard_map/ppermute | solution.py:67
  32.6 3.7 %collective-permute-start.6 = (bf16[4,64,1536]{2,1,0:T(8,128)(2,1)S(1)}, bf16[4,64,1536]{2,1,0:T(8,128)(2,1)S(1)}, u32[]{:S(2)}, u32[]{:S(2)}) collective-permute-start(bf16[4,64,1536]{2,1,0:T(8,128)(2,1)S(1)} %collective-permute-done.5.refs_4_.refs_6_), channel_id=1, source_target_pairs={{0,12},{1,13},{2,14},{3,15},{4,0},{5,1},{6,2},{7,3},{8,4},{9,5},{1... | collective-permute-start | bytes 2359304 | tf_op jit(solution)/shard_map/ppermute | solution.py:67
  38.7 1.0 copy-done.11
  41.0 3.2 %collective-permute-start.12 = (bf16[4,64,1536]{2,1,0:T(8,128)(2,1)S(1)}, bf16[4,64,1536]{2,1,0:T(8,128)(2,1)S(1)}, u32[]{:S(2)}, u32[]{:S(2)}) collective-permute-start(bf16[4,64,1536]{2,1,0:T(8,128)(2,1)S(1)} %join_middle.1.refs_4_.refs_3_), channel_id=1, source_target_pairs={{0,12},{1,13},{2,14},{3,15},{4,0},{5,1},{6,2},{7,3},{8,4},{9,5},{1... | collective-permute-start | bytes 2359304 | tf_op jit(solution)/shard_map/ppermute | solution.py:67
  44.3 1.8 collective-permute-start.14
  47.2 2.6 %span_attention.1.refs_7_.refs_1_ = bf16[8,256,64]{2,1,0:T(8,128)(2,1)S(1)} custom-call(s32[38]{0:T(128)S(1)} %copy-done.25, bf16[16,256,64]{2,1,0:T(8,128)(2,1)S(1)} %both_rows.1.refs_1_.refs_7_.refs_3_, bf16[4,64,1536]{2,1,0:T(8,128)(2,1)S(1)} %join_qkv.1.refs_2_, bf16[4,64,1536]{2,1,0:T(8,128)(2,1)S(1)} %collective-permute-done.4.refs_3_.refs_5_, ...), custom_call_target="tpu_custom_call" | custom-call | flops 805306368 | bytes 3670016 | tf_op jit(solution)/shard_map/span_attention/pallas_call | solution.py:101
  49.8 1.0 collective-permute-done.14.refs_6_
  50.8 4.4 %collective-permute-done.11.refs_8_.refs_5_.refs_4_ = bf16[4,64,1536]{2,1,0:T(8,128)(2,1)S(1)} collective-permute-done((bf16[4,64,1536]{2,1,0:T(8,128)(2,1)S(1)}, bf16[4,64,1536]{2,1,0:T(8,128)(2,1)S(1)}, u32[]{:S(2)}, u32[]{:S(2)}) %collective-permute-start.11) | collective-permute-done | bytes 786464 | tf_op jit(solution)/shard_map/ppermute | solution.py:67
  55.6 1.5 join_lower.1
  58.0 3.7 %collective-permute-start.18 = (bf16[4,64,1280]{2,1,0:T(8,128)(2,1)}, bf16[4,64,1280]{2,1,0:T(8,128)(2,1)}, u32[]{:S(2)}, u32[]{:S(2)}) collective-permute-start(bf16[4,64,1280]{2,1,0:T(8,128)(2,1)} %get-tuple-element.42), channel_id=1, source_target_pairs={{0,12},{1,13},{2,14},{3,15},{4,0},{5,1},{6,2},{7,3},{8,4},{9,5},{1... | collective-permute-start | bytes 1966088 | tf_op jit(solution)/shard_map/ppermute | solution.py:67
  65.1 5.0 %collective-permute-done.18.refs_3_.refs_5_ = bf16[4,64,1280]{2,1,0:T(8,128)(2,1)} collective-permute-done((bf16[4,64,1280]{2,1,0:T(8,128)(2,1)}, bf16[4,64,1280]{2,1,0:T(8,128)(2,1)}, u32[]{:S(2)}, u32[]{:S(2)}) %collective-permute-start.18) | collective-permute-done | bytes 655392 | tf_op jit(solution)/shard_map/ppermute | solution.py:67
  70.1 3.7 %collective-permute-start.19 = (bf16[4,64,1280]{2,1,0:T(8,128)(2,1)}, bf16[4,64,1280]{2,1,0:T(8,128)(2,1)}, u32[]{:S(2)}, u32[]{:S(2)}) collective-permute-start(bf16[4,64,1280]{2,1,0:T(8,128)(2,1)} %collective-permute-done.18.refs_3_.refs_5_), channel_id=1, source_target_pairs={{0,12},{1,13},{2,14},{3,15},{4,0},{5,1},{6,2},{7,3},{8,4},{9,5},{1... | collective-permute-start | bytes 1966088 | tf_op jit(solution)/shard_map/ppermute | solution.py:67
  76.5 1.0 select_reduce_fusion
  77.4 5.7 %collective-permute-done.15.refs_8_.refs_4_ = bf16[4,64,256]{2,1,0:T(8,128)(2,1)S(1)} collective-permute-done((bf16[4,64,256]{2,1,0:T(8,128)(2,1)S(1)}, bf16[4,64,256]{2,1,0:T(8,128)(2,1)S(1)}, u32[]{:S(2)}, u32[]{:S(2)}) %collective-permute-start.15) | collective-permute-done | bytes 131104 | tf_op jit(solution)/shard_map/ppermute | solution.py:67
  83.2 1.1 copy-done.8
  84.3 2.8 %context_out.1.refs_1_ = bf16[256,512]{1,0:T(8,128)(2,1)} custom-call(s32[38]{0:T(128)S(1)} %copy-done.25, bf16[8,256,64]{2,1,0:T(8,128)(2,1)S(1)} %span_attention.1.refs_7_.refs_1_, bf16[8,256,64]{2,1,0:T(8,128)(2,1)} %collective-permute-done.7.refs_2_, bf16[16,256,64]{2,1,0:T(8,128)(2,1)S(1)} %both_rows.1.refs_1_.refs_7_.refs_3_, ...), custom_call_target="tpu_custom_call" | custom-call | flops 268435456 | bytes 4194304 | tf_op jit(solution)/shard_map/context_out/pallas_call | solution.py:101
  87.6 1.3 iota_add_fusion
  89.8 1.5 join_proj.1.refs_7_.refs_4_
  91.3 1.1 copy-done.6
  92.4 1.1 copy-done.9
  93.5 3.1 %norm_up.1 = (bf16[256,1024]{1,0:T(8,128)(2,1)S(1)}, bf16[16,256,64]{2,1,0:T(8,128)(2,1)S(1)}) custom-call(s32[38]{0:T(128)S(1)} %copy-done.25, bf16[256,512]{1,0:T(8,128)(2,1)} %context_out.1.refs_1_, bf16[256,512]{1,0:T(8,128)(2,1)} %collective-permute-done.16.refs_2_, bf16[4,64,1536]{2,1,0:T(8,128)(2,1)S(1)} %copy-done.9, ...), custom_call_target="tpu_custom_call" | custom-call | flops 536870912 | bytes 3670016 | tf_op jit(solution)/shard_map/norm_up/pallas_call | solution.py:101
  96.6 1.1 copy-done.15
  97.7 2.3 %down.1 = (f32[128,1024]{1,0:T(8,128)S(1)}, bf16[128,1024]{1,0:T(8,128)(2,1)S(1)}) custom-call(s32[38]{0:T(128)S(1)} %copy-done.25, bf16[16,256,64]{2,1,0:T(8,128)(2,1)S(1)} %get-tuple-element.39.refs_1_, bf16[256,1024]{1,0:T(8,128)(2,1)S(1)} %get-tuple-element.40.refs_2_, bf16[4,64,1280]{2,1,0:T(8,128)(2,1)S(1)} %copy-done.15, ...), custom_call_target="tpu_custom_call" | custom-call | flops 536870912 | bytes 3670016 | tf_op jit(solution)/shard_map/down/pallas_call | solution.py:101
  101.8 1.7 norm_pool.1
  103.5 8.9 %all-to-all-start = ((bf16[128,8,128]{2,1,0:T(8,128)(2,1)}), bf16[128,8,128]{2,1,0:T(8,128)(2,1)S(1)}, u32[]{:S(2)}, u32[]{:S(2)}) async-start(bf16[128,8,128]{2,1,0:T(8,128)(2,1)} %bitcast.8), calls=%async_computation | async-start | bytes 524288 | tf_op jit(solution)/shard_map/all_to_all | solution.py:692
  112.4 10.8 %all-to-all-done.refs_1_ = bf16[128,8,128]{2,1,0:T(8,128)(2,1)S(1)} async-done(((bf16[128,8,128]{2,1,0:T(8,128)(2,1)}), bf16[128,8,128]{2,1,0:T(8,128)(2,1)S(1)}, u32[]{:S(2)}, u32[]{:S(2)}) %all-to-all-start) | async-done | bytes 262176 | tf_op jit(solution)/shard_map/all_to_all | solution.py:692
  123.2 1.6 copy-done.10
  124.8 2.6 %embed.1.refs_1_ = bf16[128,512]{1,0:T(8,128)(2,1)S(1)} custom-call(s32[38]{0:T(128)S(1)} %copy-done.25, bf16[128,8,128]{2,1,0:T(8,128)(2,1)S(1)} %all-to-all-done.refs_1_, bf16[128,128]{1,0:T(8,128)(2,1)S(1)} %fusion.refs_2_, bf16[1024,1024]{1,0:T(8,128)(2,1)S(1)} %copy-done.10, bf16[4,4,64,256]{3,2,1,0:T(8,128)(2,1)S(1)} %join_proj.1.refs_7_.refs_4_, ...), custom_call_target="tpu_custom_call" | custom-call | flops 402653184 | bytes 3440640 | tf_op jit(solution)/shard_map/embed/pallas_call | solution.py:101
  128.1 2.6 %collective-permute-start.23 = (bf16[128,512]{1,0:T(8,128)(2,1)S(1)}, bf16[128,512]{1,0:T(8,128)(2,1)S(1)}, u32[]{:S(2)}, u32[]{:S(2)}) collective-permute-start(bf16[128,512]{1,0:T(8,128)(2,1)S(1)} %embed.1.refs_1_), channel_id=1, source_target_pairs={{0,3},{1,0},{2,1},{3,2},{4,7},{5,4},{6,5},{7,6},{8,11},{9,8},{10,9... | collective-permute-start | bytes 393224 | tf_op jit(solution)/shard_map/ppermute | solution.py:67
  130.7 1.9 select_reduce_fusion.3
  132.6 1.0 collective-permute-done.22.refs_2_
  133.7 1.0 collective-permute-done.23.refs_3_
  134.6 2.5 %collective-permute-done.24.refs_4_ = bf16[128,512]{1,0:T(8,128)(2,1)S(1)} collective-permute-done((bf16[128,512]{1,0:T(8,128)(2,1)S(1)}, bf16[128,512]{1,0:T(8,128)(2,1)S(1)}, u32[]{:S(2)}, u32[]{:S(2)}) %collective-permute-start.24) | collective-permute-done | bytes 131104 | tf_op jit(solution)/shard_map/ppermute | solution.py:67
  139.4 2.7 %collective-permute-start.27 = (bf16[4,128,512]{2,1,0:T(8,128)(2,1)S(1)}, bf16[4,128,512]{2,1,0:T(8,128)(2,1)}, u32[]{:S(2)}, u32[]{:S(2)}) collective-permute-start(bf16[4,128,512]{2,1,0:T(8,128)(2,1)S(1)} %join_columns.1.refs_1_), channel_id=1, source_target_pairs={{0,12},{1,13},{2,14},{3,15},{4,0},{5,1},{6,2},{7,3},{8,4},{9,5},{1... | collective-permute-start | bytes 1572872 | tf_op jit(solution)/shard_map/ppermute | solution.py:67
  142.1 3.4 %copy-done = bf16[8192,512]{1,0:T(8,128)(2,1)S(1)} copy-done((bf16[8192,512]{1,0:T(8,128)(2,1)S(1)}, bf16[8192,512]{1,0:T(8,128)(2,1)}, u32[]{:S(2)}) %copy-start) | copy-done | bytes 8388632
  145.5 1.1 project_own.1
  147.4 1.0 collective-permute-done.25.refs_1_
  151.5 1.3 broadcast_in_dim.111
  152.8 1.4 copy.22
  156.0 3.4 %copy-done.1 = bf16[8192,512]{1,0:T(8,128)(2,1)S(1)} copy-done((bf16[8192,512]{1,0:T(8,128)(2,1)S(1)}, bf16[8192,512]{1,0:T(8,128)(2,1)}, u32[]{:S(2)}) %copy-start.1) | copy-done | bytes 8388632
  161.1 2.3 %project_near.1 = (f32[128,512]{1,0:T(8,128)S(1)}, f32[128,128]{1,0:T(8,128)S(1)}, f32[128,1]{1,0:T(8,128)S(1)}) custom-call(s32[38]{0:T(128)S(1)} %copy-done.25, bf16[4,128,512]{2,1,0:T(8,128)(2,1)} %collective-permute-done.25.refs_1_, bf16[4,128,512]{2,1,0:T(8,128)(2,1)} %collective-permute-done.27.refs_2_, f32[16,1,512]{2,1,0:T(1,128)S(1)} %bitcast.21, ...), custom_call_target="tpu_custom_call" | custom-call | flops 671088640 | bytes 11895296 | tf_op jit(solution)/shard_map/project_near/pallas_call | solution.py:101
  163.4 1.2 last_keys.1
  165.0 3.4 %copy-done.2 = bf16[8192,512]{1,0:T(8,128)(2,1)S(1)} copy-done((bf16[8192,512]{1,0:T(8,128)(2,1)S(1)}, bf16[8192,512]{1,0:T(8,128)(2,1)}, u32[]{:S(2)}) %copy-start.2) | copy-done | bytes 8388632
  168.3 1.3 last_queries.1.refs_1_
  169.7 3.4 %copy-done.4 = bf16[512,8192]{1,0:T(8,128)(2,1)S(1)} copy-done((bf16[512,8192]{1,0:T(8,128)(2,1)S(1)}, bf16[512,8192]{1,0:T(8,128)(2,1)}, u32[]{:S(2)}) %copy-start.4) | copy-done | bytes 8388632
  173.1 3.6 %attend_out.1 = (bf16[32,8192]{1,0:T(8,128)(2,1)S(1)}, bf16[32,8192]{1,0:T(8,128)(2,1)}, bf16[32,8192]{1,0:T(8,128)(2,1)}, bf16[32,8192]{1,0:T(8,128)(2,1)}) custom-call(s32[38]{0:T(128)S(1)} %copy-done.25, bf16[128,512]{1,0:T(8,128)(2,1)S(1)} %last_queries.1.refs_1_, bf16[2,128,64]{2,1,0:T(8,128)(2,1)S(1)} %get-tuple-element.54.refs_2_, ...), custom_call_target="tpu_custom_call" | custom-call | flops 1073741824 | bytes 8683520 | tf_op jit(solution)/shard_map/attend_out/pallas_call | solution.py:101
  176.7 3.2 %collective-permute-start.30 = (bf16[32,8192]{1,0:T(8,128)(2,1)}, bf16[32,8192]{1,0:T(8,128)(2,1)S(1)}, u32[]{:S(2)}, u32[]{:S(2)}) collective-permute-start(bf16[32,8192]{1,0:T(8,128)(2,1)} %get-tuple-element.57), channel_id=1, source_target_pairs={{0,12},{1,13},{2,14},{3,15},{4,0},{5,1},{6,2},{7,3},{8,4},{9,5},{1... | collective-permute-start | bytes 1572872 | tf_op jit(solution)/shard_map/ppermute | solution.py:67
  179.9 1.5 collective-permute-start.31
  182.2 5.1 %collective-permute-done.29.refs_2_ = bf16[32,8192]{1,0:T(8,128)(2,1)S(1)} collective-permute-done((bf16[32,8192]{1,0:T(8,128)(2,1)}, bf16[32,8192]{1,0:T(8,128)(2,1)S(1)}, u32[]{:S(2)}, u32[]{:S(2)}) %collective-permute-start.29) | collective-permute-done | bytes 524320 | tf_op jit(solution)/shard_map/ppermute | solution.py:67
  187.3 5.3 %collective-permute-done.30.refs_3_ = bf16[32,8192]{1,0:T(8,128)(2,1)S(1)} collective-permute-done((bf16[32,8192]{1,0:T(8,128)(2,1)}, bf16[32,8192]{1,0:T(8,128)(2,1)S(1)}, u32[]{:S(2)}, u32[]{:S(2)}) %collective-permute-start.30) | collective-permute-done | bytes 524320 | tf_op jit(solution)/shard_map/ppermute | solution.py:67
  192.6 1.8 collective-permute-done.31.refs_4_
  195.2 2.1 %collective-permute-start.32 = (bf16[8,8192]{1,0:T(8,128)(2,1)S(1)}, bf16[8,8192]{1,0:T(8,128)(2,1)S(1)}, u32[]{:S(2)}, u32[]{:S(2)}) collective-permute-start(bf16[8,8192]{1,0:T(8,128)(2,1)S(1)} %get-tuple-element.60), channel_id=1, source_target_pairs={{0,1},{1,2},{2,3},{3,0},{4,5},{5,6},{6,7},{7,4},{8,9},{9,10},{10,1... | collective-permute-start | bytes 393224 | tf_op jit(solution)/shard_map/ppermute | solution.py:67
  197.3 1.2 collective-permute-start.33
  198.5 1.5 collective-permute-start.34
  202.2 2.7 %collective-permute-done.34.refs_4_ = bf16[8,8192]{1,0:T(8,128)(2,1)S(1)} collective-permute-done((bf16[8,8192]{1,0:T(8,128)(2,1)S(1)}, bf16[8,8192]{1,0:T(8,128)(2,1)S(1)}, u32[]{:S(2)}, u32[]{:S(2)}) %collective-permute-start.34) | collective-permute-done | bytes 131104 | tf_op jit(solution)/shard_map/ppermute | solution.py:67
  204.9 1.3 finish.1
  (155 shorter events, 34.9 us)
Async XLA Ops:
  0.0 46.0 %copy-start.32 = (s32[8]{0:T(128)S(1)}, s32[8]{0:T(128)}, u32[]{:S(2)}) copy-start(s32[8]{0:T(128)} %param.20) | copy-start | bytes 100
  1.3 1.0 copy-start.17
  2.3 6.0 %copy-start.21 = (s32[38]{0:T(128)}, s32[38]{0:T(128)S(1)}, u32[]{:S(2)}) copy-start(s32[38]{0:T(128)S(1)} %concatenate.9.refs_0_) | copy-start | bytes 460
  2.9 5.4 %copy-start.12 = (bf16[64,1536]{1,0:T(8,128)(2,1)}, bf16[64,1536]{1,0:T(8,128)(2,1)S(1)}, u32[]{:S(2)}) copy-start(bf16[64,1536]{1,0:T(8,128)(2,1)S(1)} %take_qkv.1.refs_1_.refs_5_) | copy-start | bytes 589828
  2.9 8.8 %collective-permute-start.1 = (bf16[64,1536]{1,0:T(8,128)(2,1)S(1)}, bf16[64,1536]{1,0:T(8,128)(2,1)S(1)}, u32[]{:S(2)}, u32[]{:S(2)}) collective-permute-start(bf16[64,1536]{1,0:T(8,128)(2,1)S(1)} %take_qkv.1.refs_1_.refs_5_), channel_id=1, source_target_pairs={{0,1},{1,2},{2,3},{3,0},{4,5},{5,6},{6,7},{7,4},{8,9},{9,10},{10,1... | collective-permute-start | bytes 589832 | tf_op jit(solution)/shard_map/ppermute | solution.py:67
  4.6 7.1 %collective-permute-start.2 = (bf16[64,1536]{1,0:T(8,128)(2,1)S(1)}, bf16[64,1536]{1,0:T(8,128)(2,1)S(1)}, u32[]{:S(2)}, u32[]{:S(2)}) collective-permute-start(bf16[64,1536]{1,0:T(8,128)(2,1)S(1)} %take_qkv.1.refs_1_.refs_5_), channel_id=1, source_target_pairs={{0,3},{1,0},{2,1},{3,2},{4,7},{5,4},{6,5},{7,6},{8,11},{9,8},{10,9... | collective-permute-start | bytes 589832 | tf_op jit(solution)/shard_map/ppermute | solution.py:67
  6.2 7.2 %collective-permute-start.3 = (bf16[64,1536]{1,0:T(8,128)(2,1)S(1)}, bf16[64,1536]{1,0:T(8,128)(2,1)S(1)}, u32[]{:S(2)}, u32[]{:S(2)}) collective-permute-start(bf16[64,1536]{1,0:T(8,128)(2,1)S(1)} %take_qkv.1.refs_1_.refs_5_), channel_id=1, source_target_pairs={{0,2},{1,3},{2,0},{3,1},{4,6},{5,7},{6,4},{7,5},{8,10},{9,11},{10,... | collective-permute-start | bytes 589832 | tf_op jit(solution)/shard_map/ppermute | solution.py:67
  11.1 36.1 %copy-start.25 = (s32[38]{0:T(128)S(1)}, s32[38]{0:T(128)}, u32[]{:S(2)}) copy-start(s32[38]{0:T(128)} %copy-done.21) | copy-start | bytes 460
  11.1 10.1 %collective-permute-start.8 = (bf16[64,3584]{1,0:T(8,128)(2,1)}, bf16[64,3584]{1,0:T(8,128)(2,1)S(1)}, u32[]{:S(2)}, u32[]{:S(2)}) collective-permute-start(bf16[64,3584]{1,0:T(8,128)(2,1)} %get-tuple-element.34.refs_1_), channel_id=1, source_target_pairs={{0,1},{1,2},{2,3},{3,0},{4,5},{5,6},{6,7},{7,4},{8,9},{9,10},{10,1... | collective-permute-start | bytes 1376264 | tf_op jit(solution)/shard_map/ppermute | solution.py:67
  13.4 0.9 copy-start.13
  14.9 29.4 %copy-start.33 = (bf16[64,1024]{1,0:T(8,128)(2,1)S(1)}, bf16[64,1024]{1,0:T(8,128)(2,1)}, u32[]{:S(2)}) copy-start(bf16[64,1024]{1,0:T(8,128)(2,1)} %get-tuple-element.37) | copy-start | bytes 393220
  14.9 40.7 %copy-start.28 = (bf16[64,1024]{1,0:T(8,128)(2,1)S(1)}, bf16[64,1024]{1,0:T(8,128)(2,1)}, u32[]{:S(2)}) copy-start(bf16[64,1024]{1,0:T(8,128)(2,1)} %get-tuple-element.36.refs_5_) | copy-start | bytes 393220
  15.5 17.1 %collective-permute-start.5 = (bf16[4,64,1536]{2,1,0:T(8,128)(2,1)S(1)}, bf16[4,64,1536]{2,1,0:T(8,128)(2,1)S(1)}, u32[]{:S(2)}, u32[]{:S(2)}) collective-permute-start(bf16[4,64,1536]{2,1,0:T(8,128)(2,1)S(1)} %join_qkv.1.refs_2_), channel_id=1, source_target_pairs={{0,12},{1,13},{2,14},{3,15},{4,0},{5,1},{6,2},{7,3},{8,4},{9,5},{1... | collective-permute-start | bytes 2359304 | tf_op jit(solution)/shard_map/ppermute | solution.py:67
  18.4 20.3 %collective-permute-start.4 = (bf16[4,64,1536]{2,1,0:T(8,128)(2,1)S(1)}, bf16[4,64,1536]{2,1,0:T(8,128)(2,1)S(1)}, u32[]{:S(2)}, u32[]{:S(2)}) collective-permute-start(bf16[4,64,1536]{2,1,0:T(8,128)(2,1)S(1)} %join_qkv.1.refs_2_), channel_id=1, source_target_pairs={{0,4},{1,5},{2,6},{3,7},{4,8},{5,9},{6,10},{7,11},{8,12},{9,13},{1... | collective-permute-start | bytes 2359304 | tf_op jit(solution)/shard_map/ppermute | solution.py:67
  18.4 20.3 %collective-permute-start.9 = (bf16[64,3584]{1,0:T(8,128)(2,1)}, bf16[64,3584]{1,0:T(8,128)(2,1)S(1)}, u32[]{:S(2)}, u32[]{:S(2)}) collective-permute-start(bf16[64,3584]{1,0:T(8,128)(2,1)} %get-tuple-element.35), channel_id=1, source_target_pairs={{0,3},{1,0},{2,1},{3,2},{4,7},{5,4},{6,5},{7,6},{8,11},{9,8},{10,9... | collective-permute-start | bytes 1376264 | tf_op jit(solution)/shard_map/ppermute | solution.py:67
  21.1 17.6 %collective-permute-start.10 = (bf16[64,3584]{1,0:T(8,128)(2,1)S(1)}, bf16[64,3584]{1,0:T(8,128)(2,1)S(1)}, u32[]{:S(2)}, u32[]{:S(2)}) collective-permute-start(bf16[64,3584]{1,0:T(8,128)(2,1)S(1)} %collective-permute-done.8.refs_2_), channel_id=1, source_target_pairs={{0,1},{1,2},{2,3},{3,0},{4,5},{5,6},{6,7},{7,4},{8,9},{9,10},{10,1... | collective-permute-start | bytes 1376264 | tf_op jit(solution)/shard_map/ppermute | solution.py:67
  21.1 15.2 %collective-permute-start = (bf16[128,1024]{1,0:T(8,128)(2,1)}, bf16[128,1024]{1,0:T(8,128)(2,1)S(1)}, u32[]{:S(2)}, u32[]{:S(2)}) collective-permute-start(bf16[128,1024]{1,0:T(8,128)(2,1)} %bitcast.24), channel_id=1, source_target_pairs={{0,16},{16,0},{32,48},{48,32},{64,80},{80,64},{96,112},{112,96},{1... | collective-permute-start | bytes 786440 | tf_op jit(solution)/shard_map/ppermute | solution.py:71
  32.6 14.6 %collective-permute-start.6 = (bf16[4,64,1536]{2,1,0:T(8,128)(2,1)S(1)}, bf16[4,64,1536]{2,1,0:T(8,128)(2,1)S(1)}, u32[]{:S(2)}, u32[]{:S(2)}) collective-permute-start(bf16[4,64,1536]{2,1,0:T(8,128)(2,1)S(1)} %collective-permute-done.5.refs_4_.refs_6_), channel_id=1, source_target_pairs={{0,12},{1,13},{2,14},{3,15},{4,0},{5,1},{6,2},{7,3},{8,4},{9,5},{1... | collective-permute-start | bytes 2359304 | tf_op jit(solution)/shard_map/ppermute | solution.py:67
  36.3 1.0 copy-start.20
  38.7 1.0 copy-start.11
  40.9 14.7 %copy-start.7 = (bf16[4,64,1536]{2,1,0:T(8,128)(2,1)}, bf16[4,64,1536]{2,1,0:T(8,128)(2,1)S(1)}, u32[]{:S(2)}) copy-start(bf16[4,64,1536]{2,1,0:T(8,128)(2,1)S(1)} %join_middle.1.refs_4_.refs_3_) | copy-start | bytes 2359300
  40.9 14.3 %collective-permute-start.11 = (bf16[4,64,1536]{2,1,0:T(8,128)(2,1)S(1)}, bf16[4,64,1536]{2,1,0:T(8,128)(2,1)S(1)}, u32[]{:S(2)}, u32[]{:S(2)}) collective-permute-start(bf16[4,64,1536]{2,1,0:T(8,128)(2,1)S(1)} %join_middle.1.refs_4_.refs_3_), channel_id=1, source_target_pairs={{0,4},{1,5},{2,6},{3,7},{4,8},{5,9},{6,10},{7,11},{8,12},{9,13},{1... | collective-permute-start | bytes 2359304 | tf_op jit(solution)/shard_map/ppermute | solution.py:67
  41.0 14.6 %collective-permute-start.12 = (bf16[4,64,1536]{2,1,0:T(8,128)(2,1)S(1)}, bf16[4,64,1536]{2,1,0:T(8,128)(2,1)S(1)}, u32[]{:S(2)}, u32[]{:S(2)}) collective-permute-start(bf16[4,64,1536]{2,1,0:T(8,128)(2,1)S(1)} %join_middle.1.refs_4_.refs_3_), channel_id=1, source_target_pairs={{0,12},{1,13},{2,14},{3,15},{4,0},{5,1},{6,2},{7,3},{8,4},{9,5},{1... | collective-permute-start | bytes 2359304 | tf_op jit(solution)/shard_map/ppermute | solution.py:67
  44.3 6.6 %collective-permute-start.14 = (bf16[64,1024]{1,0:T(8,128)(2,1)S(1)}, bf16[64,1024]{1,0:T(8,128)(2,1)S(1)}, u32[]{:S(2)}, u32[]{:S(2)}) collective-permute-start(bf16[64,1024]{1,0:T(8,128)(2,1)S(1)} %copy-done.33), channel_id=1, source_target_pairs={{0,2},{1,3},{2,0},{3,1},{4,6},{5,7},{6,4},{7,5},{8,10},{9,11},{10,... | collective-permute-start | bytes 393224 | tf_op jit(solution)/shard_map/ppermute | solution.py:67
  55.6 33.2 %copy-start.5 = (bf16[4,64,1536]{2,1,0:T(8,128)(2,1)}, bf16[4,64,1536]{2,1,0:T(8,128)(2,1)S(1)}, u32[]{:S(2)}) copy-start(bf16[4,64,1536]{2,1,0:T(8,128)(2,1)S(1)} %collective-permute-done.12.refs_9_.refs_6_.refs_5_) | copy-start | bytes 2359300
  58.0 25.2 %copy-start.26 = (bf16[4,64,256]{2,1,0:T(8,128)(2,1)}, bf16[4,64,256]{2,1,0:T(8,128)(2,1)S(1)}, u32[]{:S(2)}) copy-start(bf16[4,64,256]{2,1,0:T(8,128)(2,1)S(1)} %get-tuple-element.43.refs_1_) | copy-start | bytes 393220
  58.0 12.1 %collective-permute-start.18 = (bf16[4,64,1280]{2,1,0:T(8,128)(2,1)}, bf16[4,64,1280]{2,1,0:T(8,128)(2,1)}, u32[]{:S(2)}, u32[]{:S(2)}) collective-permute-start(bf16[4,64,1280]{2,1,0:T(8,128)(2,1)} %get-tuple-element.42), channel_id=1, source_target_pairs={{0,12},{1,13},{2,14},{3,15},{4,0},{5,1},{6,2},{7,3},{8,4},{9,5},{1... | collective-permute-start | bytes 1966088 | tf_op jit(solution)/shard_map/ppermute | solution.py:67
  63.1 20.0 %collective-permute-start.13 = (bf16[4,64,1536]{2,1,0:T(8,128)(2,1)S(1)}, bf16[4,64,1536]{2,1,0:T(8,128)(2,1)}, u32[]{:S(2)}, u32[]{:S(2)}) collective-permute-start(bf16[4,64,1536]{2,1,0:T(8,128)(2,1)S(1)} %collective-permute-done.11.refs_8_.refs_5_.refs_4_), channel_id=1, source_target_pairs={{0,4},{1,5},{2,6},{3,7},{4,8},{5,9},{6,10},{7,11},{8,12},{9,13},{1... | collective-permute-start | bytes 2359304 | tf_op jit(solution)/shard_map/ppermute | solution.py:67
  65.0 18.2 %collective-permute-start.7 = (bf16[8,256,64]{2,1,0:T(8,128)(2,1)S(1)}, bf16[8,256,64]{2,1,0:T(8,128)(2,1)}, u32[]{:S(2)}, u32[]{:S(2)}) collective-permute-start(bf16[8,256,64]{2,1,0:T(8,128)(2,1)S(1)} %span_attention.1.refs_7_.refs_1_), channel_id=1, source_target_pairs={{0,16},{16,0},{32,48},{48,32},{64,80},{80,64},{96,112},{112,96},{1... | collective-permute-start | bytes 786440 | tf_op jit(solution)/shard_map/ppermute | solution.py:71
  65.0 23.9 %collective-permute-start.17 = (bf16[4,64,1280]{2,1,0:T(8,128)(2,1)}, bf16[4,64,1280]{2,1,0:T(8,128)(2,1)}, u32[]{:S(2)}, u32[]{:S(2)}) collective-permute-start(bf16[4,64,1280]{2,1,0:T(8,128)(2,1)} %copy-done.14), channel_id=1, source_target_pairs={{0,4},{1,5},{2,6},{3,7},{4,8},{5,9},{6,10},{7,11},{8,12},{9,13},{1... | collective-permute-start | bytes 1966088 | tf_op jit(solution)/shard_map/ppermute | solution.py:67
  70.1 26.5 %collective-permute-start.19 = (bf16[4,64,1280]{2,1,0:T(8,128)(2,1)}, bf16[4,64,1280]{2,1,0:T(8,128)(2,1)}, u32[]{:S(2)}, u32[]{:S(2)}) collective-permute-start(bf16[4,64,1280]{2,1,0:T(8,128)(2,1)} %collective-permute-done.18.refs_3_.refs_5_), channel_id=1, source_target_pairs={{0,12},{1,13},{2,14},{3,15},{4,0},{5,1},{6,2},{7,3},{8,4},{9,5},{1... | collective-permute-start | bytes 1966088 | tf_op jit(solution)/shard_map/ppermute | solution.py:67
  74.3 8.9 %collective-permute-start.15 = (bf16[4,64,256]{2,1,0:T(8,128)(2,1)S(1)}, bf16[4,64,256]{2,1,0:T(8,128)(2,1)S(1)}, u32[]{:S(2)}, u32[]{:S(2)}) collective-permute-start(bf16[4,64,256]{2,1,0:T(8,128)(2,1)S(1)} %get-tuple-element.38), channel_id=1, source_target_pairs={{0,8},{1,9},{2,10},{3,11},{4,12},{5,13},{6,14},{7,15},{8,0},{9,1},... | collective-permute-start | bytes 393224 | tf_op jit(solution)/shard_map/ppermute | solution.py:67
  83.2 1.1 copy-start.8
  87.1 4.2 %collective-permute-start.16 = (bf16[256,512]{1,0:T(8,128)(2,1)}, bf16[256,512]{1,0:T(8,128)(2,1)}, u32[]{:S(2)}, u32[]{:S(2)}) collective-permute-start(bf16[256,512]{1,0:T(8,128)(2,1)} %context_out.1.refs_1_), channel_id=1, source_target_pairs={{0,16},{16,0},{32,48},{48,32},{64,80},{80,64},{96,112},{112,96},{1... | collective-permute-start | bytes 786440 | tf_op jit(solution)/shard_map/ppermute | solution.py:71
  88.9 0.9 copy-start.27
  89.8 52.4 %copy-start.3 = (bf16[2,8192,64]{1,2,0:T(8,128)(2,1)S(1)}, bf16[2,8192,64]{1,2,0:T(8,128)(2,1)}, u32[]{:S(2)}) copy-start(bf16[2,8192,64]{1,2,0:T(8,128)(2,1)} %param.30) | copy-start | bytes 6291460
  91.3 1.1 copy-start.6
  92.4 1.1 copy-start.9
  93.5 48.6 %copy-start.16 = (f32[8192]{0:T(1024)S(1)}, f32[8192]{0:T(1024)}, u32[]{:S(2)}) copy-start(f32[8192]{0:T(1024)} %param.28) | copy-start | bytes 98308
  96.6 1.1 copy-start.15
  100.0 1.7 collective-permute-start.20
  101.3 11.1 %collective-permute-start.21 = (bf16[4,4,64,256]{3,2,1,0:T(8,128)(2,1)S(1)}, bf16[4,4,64,256]{3,2,1,0:T(8,128)(2,1)}, u32[]{:S(2)}, u32[]{:S(2)}) collective-permute-start(bf16[4,4,64,256]{3,2,1,0:T(8,128)(2,1)S(1)} %join_proj.1.refs_7_.refs_4_), channel_id=1, source_target_pairs={{0,16},{16,0},{32,48},{48,32},{64,80},{80,64},{96,112},{112,96},{1... | collective-permute-start | bytes 1572872 | tf_op jit(solution)/shard_map/ppermute | solution.py:71
  103.4 46.0 %copy-start.31 = (pred[8,8]{1,0:T(8,128)(4,1)S(1)}, pred[8,8]{1,0:T(8,128)(4,1)}, u32[]{:S(2)}) copy-start(pred[8,8]{1,0:T(8,128)(4,1)} %broadcast_compare_fusion) | copy-start | bytes 196
  103.5 19.8 %all-to-all-start = ((bf16[128,8,128]{2,1,0:T(8,128)(2,1)}), bf16[128,8,128]{2,1,0:T(8,128)(2,1)S(1)}, u32[]{:S(2)}, u32[]{:S(2)}) async-start(bf16[128,8,128]{2,1,0:T(8,128)(2,1)} %bitcast.8), calls=%async_computation | async-start | bytes 524288 | tf_op jit(solution)/shard_map/all_to_all | solution.py:692
  123.2 1.6 copy-start.10
  127.4 6.2 %collective-permute-start.22 = (bf16[128,512]{1,0:T(8,128)(2,1)S(1)}, bf16[128,512]{1,0:T(8,128)(2,1)S(1)}, u32[]{:S(2)}, u32[]{:S(2)}) collective-permute-start(bf16[128,512]{1,0:T(8,128)(2,1)S(1)} %embed.1.refs_1_), channel_id=1, source_target_pairs={{0,1},{1,2},{2,3},{3,0},{4,5},{5,6},{6,7},{7,4},{8,9},{9,10},{10,1... | collective-permute-start | bytes 393224 | tf_op jit(solution)/shard_map/ppermute | solution.py:67
  128.1 6.5 %collective-permute-start.23 = (bf16[128,512]{1,0:T(8,128)(2,1)S(1)}, bf16[128,512]{1,0:T(8,128)(2,1)S(1)}, u32[]{:S(2)}, u32[]{:S(2)}) collective-permute-start(bf16[128,512]{1,0:T(8,128)(2,1)S(1)} %embed.1.refs_1_), channel_id=1, source_target_pairs={{0,3},{1,0},{2,1},{3,2},{4,7},{5,4},{6,5},{7,6},{8,11},{9,8},{10,9... | collective-permute-start | bytes 393224 | tf_op jit(solution)/shard_map/ppermute | solution.py:67
  130.7 6.5 %collective-permute-start.24 = (bf16[128,512]{1,0:T(8,128)(2,1)S(1)}, bf16[128,512]{1,0:T(8,128)(2,1)S(1)}, u32[]{:S(2)}, u32[]{:S(2)}) collective-permute-start(bf16[128,512]{1,0:T(8,128)(2,1)S(1)} %embed.1.refs_1_), channel_id=1, source_target_pairs={{0,2},{1,3},{2,0},{3,1},{4,6},{5,7},{6,4},{7,5},{8,10},{9,11},{10,... | collective-permute-start | bytes 393224 | tf_op jit(solution)/shard_map/ppermute | solution.py:67
  137.8 10.6 %collective-permute-start.25 = (bf16[4,128,512]{2,1,0:T(8,128)(2,1)S(1)}, bf16[4,128,512]{2,1,0:T(8,128)(2,1)}, u32[]{:S(2)}, u32[]{:S(2)}) collective-permute-start(bf16[4,128,512]{2,1,0:T(8,128)(2,1)S(1)} %join_columns.1.refs_1_), channel_id=1, source_target_pairs={{0,4},{1,5},{2,6},{3,7},{4,8},{5,9},{6,10},{7,11},{8,12},{9,13},{1... | collective-permute-start | bytes 1572872 | tf_op jit(solution)/shard_map/ppermute | solution.py:67
  139.4 16.5 %collective-permute-start.27 = (bf16[4,128,512]{2,1,0:T(8,128)(2,1)S(1)}, bf16[4,128,512]{2,1,0:T(8,128)(2,1)}, u32[]{:S(2)}, u32[]{:S(2)}) collective-permute-start(bf16[4,128,512]{2,1,0:T(8,128)(2,1)S(1)} %join_columns.1.refs_1_), channel_id=1, source_target_pairs={{0,12},{1,13},{2,14},{3,15},{4,0},{5,1},{6,2},{7,3},{8,4},{9,5},{1... | collective-permute-start | bytes 1572872 | tf_op jit(solution)/shard_map/ppermute | solution.py:67
  142.1 3.4 %copy-start = (bf16[8192,512]{1,0:T(8,128)(2,1)S(1)}, bf16[8192,512]{1,0:T(8,128)(2,1)}, u32[]{:S(2)}) copy-start(bf16[8192,512]{1,0:T(8,128)(2,1)} %refs_3_.7) | copy-start | bytes 25165828
  147.4 7.6 %copy-start.29 = (f32[128,1]{1,0:T(8,128)}, f32[128,1]{1,0:T(8,128)S(1)}, u32[]{:S(2)}) copy-start(f32[128,1]{1,0:T(8,128)S(1)} %get-tuple-element.46.refs_8_) | copy-start | bytes 1540
  148.3 15.0 %collective-permute-start.26 = (bf16[4,128,512]{2,1,0:T(8,128)(2,1)}, bf16[4,128,512]{2,1,0:T(8,128)(2,1)S(1)}, u32[]{:S(2)}, u32[]{:S(2)}) collective-permute-start(bf16[4,128,512]{2,1,0:T(8,128)(2,1)} %collective-permute-done.25.refs_1_), channel_id=1, source_target_pairs={{0,4},{1,5},{2,6},{3,7},{4,8},{5,9},{6,10},{7,11},{8,12},{9,13},{1... | collective-permute-start | bytes 1572872 | tf_op jit(solution)/shard_map/ppermute | solution.py:67
  155.9 3.4 %copy-start.1 = (bf16[8192,512]{1,0:T(8,128)(2,1)S(1)}, bf16[8192,512]{1,0:T(8,128)(2,1)}, u32[]{:S(2)}) copy-start(bf16[8192,512]{1,0:T(8,128)(2,1)} %refs_3_.7) | copy-start | bytes 25165828
  159.3 0.9 copy-start.19
  164.6 5.1 %collective-permute-start.28 = (bf16[2,128,64]{2,1,0:T(8,128)(2,1)S(1)}, bf16[2,128,64]{2,1,0:T(8,128)(2,1)S(1)}, u32[]{:S(2)}, u32[]{:S(2)}) collective-permute-start(bf16[2,128,64]{2,1,0:T(8,128)(2,1)S(1)} %get-tuple-element.54.refs_2_), channel_id=1, source_target_pairs={{0,1},{1,0},{2,3},{3,2},{4,5},{5,4},{6,7},{7,6},{8,9},{9,8},{10,11... | collective-permute-start | bytes 98312 | tf_op jit(solution)/shard_map/ppermute | solution.py:762
  165.0 3.4 %copy-start.2 = (bf16[8192,512]{1,0:T(8,128)(2,1)S(1)}, bf16[8192,512]{1,0:T(8,128)(2,1)}, u32[]{:S(2)}) copy-start(bf16[8192,512]{1,0:T(8,128)(2,1)} %refs_3_.7) | copy-start | bytes 25165828
  169.7 3.4 %copy-start.4 = (bf16[512,8192]{1,0:T(8,128)(2,1)S(1)}, bf16[512,8192]{1,0:T(8,128)(2,1)}, u32[]{:S(2)}) copy-start(bf16[512,8192]{1,0:T(8,128)(2,1)} %refs_6_.1) | copy-start | bytes 25165828
  176.7 10.6 %collective-permute-start.29 = (bf16[32,8192]{1,0:T(8,128)(2,1)}, bf16[32,8192]{1,0:T(8,128)(2,1)S(1)}, u32[]{:S(2)}, u32[]{:S(2)}) collective-permute-start(bf16[32,8192]{1,0:T(8,128)(2,1)} %get-tuple-element.56), channel_id=1, source_target_pairs={{0,4},{1,5},{2,6},{3,7},{4,8},{5,9},{6,10},{7,11},{8,12},{9,13},{1... | collective-permute-start | bytes 1572872 | tf_op jit(solution)/shard_map/ppermute | solution.py:67
  176.7 15.9 %collective-permute-start.30 = (bf16[32,8192]{1,0:T(8,128)(2,1)}, bf16[32,8192]{1,0:T(8,128)(2,1)S(1)}, u32[]{:S(2)}, u32[]{:S(2)}) collective-permute-start(bf16[32,8192]{1,0:T(8,128)(2,1)} %get-tuple-element.57), channel_id=1, source_target_pairs={{0,12},{1,13},{2,14},{3,15},{4,0},{5,1},{6,2},{7,3},{8,4},{9,5},{1... | collective-permute-start | bytes 1572872 | tf_op jit(solution)/shard_map/ppermute | solution.py:67
  179.9 14.4 %collective-permute-start.31 = (bf16[32,8192]{1,0:T(8,128)(2,1)}, bf16[32,8192]{1,0:T(8,128)(2,1)S(1)}, u32[]{:S(2)}, u32[]{:S(2)}) collective-permute-start(bf16[32,8192]{1,0:T(8,128)(2,1)} %get-tuple-element.58), channel_id=1, source_target_pairs={{0,8},{1,9},{2,10},{3,11},{4,12},{5,13},{6,14},{7,15},{8,0},{9,1},... | collective-permute-start | bytes 1572872 | tf_op jit(solution)/shard_map/ppermute | solution.py:67
  195.2 6.2 %collective-permute-start.32 = (bf16[8,8192]{1,0:T(8,128)(2,1)S(1)}, bf16[8,8192]{1,0:T(8,128)(2,1)S(1)}, u32[]{:S(2)}, u32[]{:S(2)}) collective-permute-start(bf16[8,8192]{1,0:T(8,128)(2,1)S(1)} %get-tuple-element.60), channel_id=1, source_target_pairs={{0,1},{1,2},{2,3},{3,0},{4,5},{5,6},{6,7},{7,4},{8,9},{9,10},{10,1... | collective-permute-start | bytes 393224 | tf_op jit(solution)/shard_map/ppermute | solution.py:67
  197.3 5.0 %collective-permute-start.33 = (bf16[8,8192]{1,0:T(8,128)(2,1)S(1)}, bf16[8,8192]{1,0:T(8,128)(2,1)S(1)}, u32[]{:S(2)}, u32[]{:S(2)}) collective-permute-start(bf16[8,8192]{1,0:T(8,128)(2,1)S(1)} %get-tuple-element.61), channel_id=1, source_target_pairs={{0,3},{1,0},{2,1},{3,2},{4,7},{5,4},{6,5},{7,6},{8,11},{9,8},{10,9... | collective-permute-start | bytes 393224 | tf_op jit(solution)/shard_map/ppermute | solution.py:67
  198.5 6.5 %collective-permute-start.34 = (bf16[8,8192]{1,0:T(8,128)(2,1)S(1)}, bf16[8,8192]{1,0:T(8,128)(2,1)S(1)}, u32[]{:S(2)}, u32[]{:S(2)}) collective-permute-start(bf16[8,8192]{1,0:T(8,128)(2,1)S(1)} %get-tuple-element.62), channel_id=1, source_target_pairs={{0,2},{1,3},{2,0},{3,1},{4,6},{5,7},{6,4},{7,5},{8,10},{9,11},{10,... | collective-permute-start | bytes 393224 | tf_op jit(solution)/shard_map/ppermute | solution.py:67
  (6 other events, 4.2 us)

commit v9 on v6

--- a/solution.py
+++ b/solution.py
@@ -557,6 +557,12 @@
         (lane[:, None] ^ 1) == lane[None, :], jnp.where(lane[None, :] % 2 == 0, -1.0, 1.0), 0.0
     ).astype(jnp.float32)
 
+    kv_cols = key_value_weight.shape[2]
+    key_start = tensor_index * kv_cols % HEAD_WIDTH
+    key_cosine = lax.dynamic_slice_in_dim(cosine, key_start, kv_cols, 1)
+    key_sine = lax.dynamic_slice_in_dim(sine, key_start, kv_cols, 1)
+    early = [pick, order, deal, allowed, cosine, sine, key_cosine, key_sine, swap]
+
     own_tokens = span_tokens.reshape(spans * span_size, width)
     other_tokens = to_core(own_tokens)
     token_pieces = whole_call(
@@ -651,6 +657,7 @@
         (shape_of((all_rows, width)), shape_of((tensor_count, all_rows, units))),
         [pltpu.VMEM((tensor_count, all_rows, share), jnp.bfloat16)],
         flops=2 * all_rows * width * width,
+        after=[*early],
     )
     kept, sent = whole_call(
         down,
@@ -710,9 +717,6 @@
     near_right = to_ring(first_block, 2, -1)
     query_cols = q_weight.shape[1]
     kv_cols = key_value_weight.shape[2]
-    key_start = tensor_index * kv_cols % HEAD_WIDTH
-    key_cosine = lax.dynamic_slice_in_dim(cosine, key_start, kv_cols, 1)
-    key_sine = lax.dynamic_slice_in_dim(sine, key_start, kv_cols, 1)
     gain = norm_gain.reshape(tensor_count, 1, share_cols)
     kv_pair = key_value_weight.transpose(0, 2, 1).reshape(2 * kv_cols, model_width)
     sums = (
@@ -729,7 +733,8 @@
         sums,
         flops=block_flops,
     )
-    embedded = [first_block, near_left, near_right, to_ring(near_left, 2, 1)]
+    relayed, _ = lax.optimization_barrier((near_left, totals[2]))
+    embedded = [first_block, relayed, near_right, to_ring(relayed, 2, 1)]
     totals = whole_call(
         functools.partial(project, starts=(1, 2), count=2),
         "project_near",

time: 193 us -> 199 us (1.031)
  blocking collectives: 0 us -> 19.4 us
  waiting for transfers between devices: 77.4 us -> 67.3 us
  starting transfers between devices: 43.5 us -> 38.3 us
    all_to_all x0 -> x1, blocking collectives: none -> 19.4 us  [local(): lax.all_to_all(outgoing.reshape(device_count, width // 128, 128), AXES, 0...]
    all_to_all x1 -> x0, waiting for transfers between devices: 10.2 us -> none  [local(): lax.all_to_all(outgoing.reshape(device_count, width // 128, 128), AXES, 0...]
    all_to_all x1 -> x0, starting transfers between devices: 7.86 us -> none  [local(): lax.all_to_all(outgoing.reshape(device_count, width // 128, 128), AXES, 0...]
    unnamed x60 -> x84, local copies, waits for them, and re-layouts: 16.2 us -> 19.5 us
    ppermute x29, starting transfers between devices: 34.7 us -> 37.3 us  [to_ring(): return lax.ppermute(value, AXES, ring_pairs(phase, distance))]
  transfers between devices with their start and end apart: 36 -> 35, of which waited for: 24 -> 19; matrix products, arithmetic and copies ran while one was open for 8% -> 7% of each run, Pallas kernels for 11% -> 11%
where the time goes in v9:
time: 199 us; the launch traced here: 197 us
  waiting for transfers between devices  67.3 us (34%)
  starting transfers between devices  38.3 us (19%)
  Pallas kernels  36.2 us (18%)
  local copies, waits for them, and re-layouts  22.7 us (11%)
  blocking collectives  19.4 us (10%)
  other arithmetic  12 us (6%)
    ppermute x29, waiting for transfers between devices, to_ring(): return lax.ppermute(value, AXES, ring_pairs(phase, distance))  63.9 us
    ppermute x29, starting transfers between devices, to_ring(): return lax.ppermute(value, AXES, ring_pairs(phase, distance))  37.3 us
    pallas_call x21, Pallas kernels, whole_call(): pl.pallas_call(run, name=name, out_shape=outs, in_specs=[SMEM] + [VMEM] *...  36.2 us
    unnamed x84, local copies, waits for them, and re-layouts  19.5 us
    all_to_all x1, blocking collectives, local(): lax.all_to_all(outgoing.reshape(device_count, width // 128, 128), AXES, 0...  19.4 us
  transfers between devices with their start and end apart: 35, of which 19 were waited for; matrix products, arithmetic and copies ran while one was open for 7% of the time, Pallas kernels for 11%

profile of v9, /device:TPU:0, one launch (start us, length us, event | category | flops | bytes accessed | tf_op | source)
XLA Modules:
  0.0 197.2 jit_solution(2475921418061706085)
XLA Ops:
  1.3 1.0 copy-done.20
  2.9 1.7 collective-permute-start.1
  4.6 1.6 collective-permute-start.2
  6.2 2.1 %collective-permute-start.3 = (bf16[64,1536]{1,0:T(8,128)(2,1)S(1)}, bf16[64,1536]{1,0:T(8,128)(2,1)S(1)}, u32[]{:S(2)}, u32[]{:S(2)}) collective-permute-start(bf16[64,1536]{1,0:T(8,128)(2,1)S(1)} %take_qkv.1.refs_1_.refs_5_), channel_id=1, source_target_pairs={{0,2},{1,3},{2,0},{3,1},{4,6},{5,7},{6,4},{7,5},{8,10},{9,11},{10,... | collective-permute-start | bytes 589832 | tf_op jit(solution)/shard_map/ppermute | solution.py:67
  8.3 2.8 %take_rest.1 = (bf16[64,3584]{1,0:T(8,128)(2,1)}, bf16[64,3584]{1,0:T(8,128)(2,1)}, bf16[64,1024]{1,0:T(8,128)(2,1)}, bf16[64,1024]{1,0:T(8,128)(2,1)}) custom-call(s32[38]{0:T(128)} %copy-done.26, bf16[64,1024]{1,0:T(8,128)(2,1)} %refs_1_.3, bf16[64,2048]{1,0:T(8,128)(2,1)} %refs_2_.1, bf16[128,1024]{1,0:T(8,128)(2,1)} %refs_3_.4, ...), custom_call_target="tpu_custom_call" | custom-call | bytes 1703936 | tf_op jit(solution)/shard_map/take_rest/pallas_call | solution.py:101
  11.7 1.3 fusion.22
  13.7 1.3 select_reduce_fusion.2
  15.7 1.4 select_reduce_fusion.1
  17.6 2.6 %collective-permute-start.9 = (bf16[64,3584]{1,0:T(8,128)(2,1)}, bf16[64,3584]{1,0:T(8,128)(2,1)}, u32[]{:S(2)}, u32[]{:S(2)}) collective-permute-start(bf16[64,3584]{1,0:T(8,128)(2,1)} %get-tuple-element.35), channel_id=1, source_target_pairs={{0,3},{1,0},{2,1},{3,2},{4,7},{5,4},{6,5},{7,6},{8,11},{9,8},{10,9... | collective-permute-start | bytes 1376264 | tf_op jit(solution)/shard_map/ppermute | solution.py:67
  20.2 0.9 copy-done.10
  22.4 2.8 %collective-permute-start.5 = (bf16[4,64,1536]{2,1,0:T(8,128)(2,1)S(1)}, bf16[4,64,1536]{2,1,0:T(8,128)(2,1)}, u32[]{:S(2)}, u32[]{:S(2)}) collective-permute-start(bf16[4,64,1536]{2,1,0:T(8,128)(2,1)S(1)} %join_qkv.1.refs_2_), channel_id=1, source_target_pairs={{0,12},{1,13},{2,14},{3,15},{4,0},{5,1},{6,2},{7,3},{8,4},{9,5},{1... | collective-permute-start | bytes 2359304 | tf_op jit(solution)/shard_map/ppermute | solution.py:67
  25.8 2.0 %select_reduce_fusion.3 = s32[]{:T(128)} fusion(s32[8]{0:T(128)} %param.19, s32[]{:T(128)} %fusion.22), kind=kLoop, calls=%fused_computation.100 | loop fusion | flops 23 | bytes 40 | tf_op jit(solution)/shard_map/reduce_sum | solution.py:542
  29.0 5.9 %collective-permute-done.5.refs_4_.refs_6_ = bf16[4,64,1536]{2,1,0:T(8,128)(2,1)} collective-permute-done((bf16[4,64,1536]{2,1,0:T(8,128)(2,1)S(1)}, bf16[4,64,1536]{2,1,0:T(8,128)(2,1)}, u32[]{:S(2)}, u32[]{:S(2)}) %collective-permute-start.5) | collective-permute-done | bytes 786464 | tf_op jit(solution)/shard_map/ppermute | solution.py:67
  34.9 3.6 %collective-permute-start.6 = (bf16[4,64,1536]{2,1,0:T(8,128)(2,1)}, bf16[4,64,1536]{2,1,0:T(8,128)(2,1)}, u32[]{:S(2)}, u32[]{:S(2)}) collective-permute-start(bf16[4,64,1536]{2,1,0:T(8,128)(2,1)} %collective-permute-done.5.refs_4_.refs_6_), channel_id=1, source_target_pairs={{0,12},{1,13},{2,14},{3,15},{4,0},{5,1},{6,2},{7,3},{8,4},{9,5},{1... | collective-permute-start | bytes 2359304 | tf_op jit(solution)/shard_map/ppermute | solution.py:67
  38.6 0.9 collective-permute-start.15
  39.5 0.9 copy-done.25
  41.1 0.9 both_rows.1.refs_1_.refs_7_.refs_3_
  42.0 0.9 copy-done.1
  42.9 1.1 copy-done.2
  44.0 1.0 copy-done.5
  45.7 1.3 join_middle.1.refs_4_.refs_3_
  48.8 1.0 collective-permute-done.6.refs_5_
  49.8 1.1 copy-done.3
  50.9 3.5 %span_attention.1.refs_1_.refs_7_ = bf16[8,256,64]{2,1,0:T(8,128)(2,1)S(1)} custom-call(s32[38]{0:T(128)S(1)} %copy-done.30, bf16[16,256,64]{2,1,0:T(8,128)(2,1)S(1)} %both_rows.1.refs_1_.refs_7_.refs_3_, bf16[4,64,1536]{2,1,0:T(8,128)(2,1)S(1)} %join_qkv.1.refs_2_, bf16[4,64,1536]{2,1,0:T(8,128)(2,1)S(1)} %copy-done.3, ...), custom_call_target="tpu_custom_call" | custom-call | flops 805306368 | bytes 3670016 | tf_op jit(solution)/shard_map/span_attention/pallas_call | solution.py:101
  54.4 1.0 copy-done.6
  55.4 1.0 copy-done.8
  56.4 2.1 %join_lower.1 = (bf16[4,64,1280]{2,1,0:T(8,128)(2,1)S(1)}, bf16[4,64,1280]{2,1,0:T(8,128)(2,1)}, bf16[4,64,256]{2,1,0:T(8,128)(2,1)S(1)}, bf16[4,64,256]{2,1,0:T(8,128)(2,1)S(1)}) custom-call(s32[38]{0:T(128)S(1)} %copy-done.30, bf16[64,3584]{1,0:T(8,128)(2,1)S(1)} %copy-done.6, bf16[64,3584]{1,0:T(8,128)(2,1)S(1)} %copy-done.8, ...), custom_call_target="tpu_custom_call" | custom-call | bytes 2097152 | tf_op jit(solution)/shard_map/join_lower/pallas_call | solution.py:101
  60.4 3.4 %collective-permute-start.12 = (bf16[4,64,1536]{2,1,0:T(8,128)(2,1)S(1)}, bf16[4,64,1536]{2,1,0:T(8,128)(2,1)S(1)}, u32[]{:S(2)}, u32[]{:S(2)}) collective-permute-start(bf16[4,64,1536]{2,1,0:T(8,128)(2,1)S(1)} %join_middle.1.refs_4_.refs_3_), channel_id=1, source_target_pairs={{0,12},{1,13},{2,14},{3,15},{4,0},{5,1},{6,2},{7,3},{8,4},{9,5},{1... | collective-permute-start | bytes 2359304 | tf_op jit(solution)/shard_map/ppermute | solution.py:67
  64.5 3.2 %collective-permute-start.17 = (bf16[4,64,1280]{2,1,0:T(8,128)(2,1)}, bf16[4,64,1280]{2,1,0:T(8,128)(2,1)}, u32[]{:S(2)}, u32[]{:S(2)}) collective-permute-start(bf16[4,64,1280]{2,1,0:T(8,128)(2,1)} %get-tuple-element.41), channel_id=1, source_target_pairs={{0,12},{1,13},{2,14},{3,15},{4,0},{5,1},{6,2},{7,3},{8,4},{9,5},{1... | collective-permute-start | bytes 1966088 | tf_op jit(solution)/shard_map/ppermute | solution.py:67
  67.8 3.8 %collective-permute-done.16.refs_4_.refs_2_ = bf16[4,64,1280]{2,1,0:T(8,128)(2,1)} collective-permute-done((bf16[4,64,1280]{2,1,0:T(8,128)(2,1)S(1)}, bf16[4,64,1280]{2,1,0:T(8,128)(2,1)}, u32[]{:S(2)}, u32[]{:S(2)}) %collective-permute-start.16) | collective-permute-done | bytes 655392 | tf_op jit(solution)/shard_map/ppermute | solution.py:67
  73.3 6.7 %collective-permute-done.13.refs_7_.refs_6_ = bf16[4,64,1536]{2,1,0:T(8,128)(2,1)} collective-permute-done((bf16[4,64,1536]{2,1,0:T(8,128)(2,1)}, bf16[4,64,1536]{2,1,0:T(8,128)(2,1)}, u32[]{:S(2)}, u32[]{:S(2)}) %collective-permute-start.13) | collective-permute-done | bytes 786464 | tf_op jit(solution)/shard_map/ppermute | solution.py:67
  80.0 2.3 %context_out.1.refs_1_ = bf16[256,512]{1,0:T(8,128)(2,1)S(1)} custom-call(s32[38]{0:T(128)S(1)} %copy-done.30, bf16[8,256,64]{2,1,0:T(8,128)(2,1)S(1)} %span_attention.1.refs_1_.refs_7_, bf16[8,256,64]{2,1,0:T(8,128)(2,1)} %collective-permute-done.7.refs_2_, bf16[16,256,64]{2,1,0:T(8,128)(2,1)S(1)} %both_rows.1.refs_1_.refs_7_.refs_3_, ...), custom_call_target="tpu_custom_call" | custom-call | flops 268435456 | bytes 4194304 | tf_op jit(solution)/shard_map/context_out/pallas_call | solution.py:101
  88.1 3.3 %norm_up.1 = (bf16[256,1024]{1,0:T(8,128)(2,1)S(1)}, bf16[16,256,64]{2,1,0:T(8,128)(2,1)S(1)}) custom-call(s32[38]{0:T(128)S(1)} %copy-done.30, bf16[256,512]{1,0:T(8,128)(2,1)S(1)} %context_out.1.refs_1_, bf16[256,512]{1,0:T(8,128)(2,1)S(1)} %collective-permute-done.14.refs_2_, bf16[4,64,1536]{2,1,0:T(8,128)(2,1)S(1)} %join_middle.1.refs_4_.refs_3_, ...), custom_call_target="tpu_custom_call" | custom-call | flops 536870912 | bytes 3670016 | tf_op jit(solution)/shard_map/norm_up/pallas_call | solution.py:101
  91.4 1.1 copy-done.14
  92.5 2.3 %down.1 = (f32[128,1024]{1,0:T(8,128)S(1)}, bf16[128,1024]{1,0:T(8,128)(2,1)S(1)}) custom-call(s32[38]{0:T(128)S(1)} %copy-done.30, bf16[16,256,64]{2,1,0:T(8,128)(2,1)S(1)} %get-tuple-element.36.refs_1_, bf16[256,1024]{1,0:T(8,128)(2,1)S(1)} %get-tuple-element.37.refs_2_, bf16[4,64,1280]{2,1,0:T(8,128)(2,1)S(1)} %copy-done.14, ...), custom_call_target="tpu_custom_call" | custom-call | flops 536870912 | bytes 3670016 | tf_op jit(solution)/shard_map/down/pallas_call | solution.py:101
  95.2 1.0 collective-permute-start.20
  96.5 1.0 norm_pool.1.refs_5_
  97.5 4.4 %collective-permute-done.20.refs_4_ = bf16[4,64,256]{2,1,0:T(8,128)(2,1)S(1)} collective-permute-done((bf16[4,64,256]{2,1,0:T(8,128)(2,1)}, bf16[4,64,256]{2,1,0:T(8,128)(2,1)S(1)}, u32[]{:S(2)}, u32[]{:S(2)}) %collective-permute-start.20) | collective-permute-done | bytes 131104 | tf_op jit(solution)/shard_map/ppermute | solution.py:67
  101.8 0.9 copy-done.33
  102.8 1.3 join_proj.1.refs_4_
  104.2 19.4 %all_to_all.5.refs_1_ = bf16[128,8,128]{2,1,0:T(8,128)(2,1)S(1)} all-to-all(bf16[128,8,128]{2,1,0:T(8,128)(2,1)S(1)} %bitcast.24), channel_id=1, replica_groups=mesh['seq'=8,'tensor'=16] {'seq','tensor'}, dimensions={0} | all-to-all | bytes 524288 | tf_op jit(solution)/shard_map/all_to_all | solution.py:682
  124.3 2.1 %embed.1.refs_1_ = bf16[128,512]{1,0:T(8,128)(2,1)S(1)} custom-call(s32[38]{0:T(128)S(1)} %copy-done.30, bf16[128,8,128]{2,1,0:T(8,128)(2,1)S(1)} %all_to_all.5.refs_1_, bf16[128,128]{1,0:T(8,128)(2,1)S(1)} %copy-done.24, bf16[1024,1024]{1,0:T(8,128)(2,1)S(1)} %copy-done.4, bf16[4,4,64,256]{3,2,1,0:T(8,128)(2,1)S(1)} %join_proj.1.refs_4_, ...), custom_call_target="tpu_custom_call" | custom-call | flops 402653184 | bytes 3440640 | tf_op jit(solution)/shard_map/embed/pallas_call | solution.py:101
  127.1 2.6 %collective-permute-start.23 = (bf16[128,512]{1,0:T(8,128)(2,1)S(1)}, bf16[128,512]{1,0:T(8,128)(2,1)S(1)}, u32[]{:S(2)}, u32[]{:S(2)}) collective-permute-start(bf16[128,512]{1,0:T(8,128)(2,1)S(1)} %embed.1.refs_1_), channel_id=1, source_target_pairs={{0,3},{1,0},{2,1},{3,2},{4,7},{5,4},{6,5},{7,6},{8,11},{9,8},{10,9... | collective-permute-start | bytes 393224 | tf_op jit(solution)/shard_map/ppermute | solution.py:67
  129.7 2.9 %collective-permute-done.22.refs_2_ = bf16[128,512]{1,0:T(8,128)(2,1)S(1)} collective-permute-done((bf16[128,512]{1,0:T(8,128)(2,1)S(1)}, bf16[128,512]{1,0:T(8,128)(2,1)S(1)}, u32[]{:S(2)}, u32[]{:S(2)}) %collective-permute-start.22) | collective-permute-done | bytes 131104 | tf_op jit(solution)/shard_map/ppermute | solution.py:67
  132.6 1.0 collective-permute-done.23.refs_3_
  133.6 2.5 %collective-permute-done.24.refs_4_ = bf16[128,512]{1,0:T(8,128)(2,1)S(1)} collective-permute-done((bf16[128,512]{1,0:T(8,128)(2,1)S(1)}, bf16[128,512]{1,0:T(8,128)(2,1)S(1)}, u32[]{:S(2)}, u32[]{:S(2)}) %collective-permute-start.24) | collective-permute-done | bytes 131104 | tf_op jit(solution)/shard_map/ppermute | solution.py:67
  137.4 2.7 %collective-permute-start.27 = (bf16[4,128,512]{2,1,0:T(8,128)(2,1)S(1)}, bf16[4,128,512]{2,1,0:T(8,128)(2,1)S(1)}, u32[]{:S(2)}, u32[]{:S(2)}) collective-permute-start(bf16[4,128,512]{2,1,0:T(8,128)(2,1)S(1)} %join_columns.1.refs_1_), channel_id=1, source_target_pairs={{0,12},{1,13},{2,14},{3,15},{4,0},{5,1},{6,2},{7,3},{8,4},{9,5},{1... | collective-permute-start | bytes 1572872 | tf_op jit(solution)/shard_map/ppermute | solution.py:67
  140.1 1.2 project_own.1
  141.3 5.9 %collective-permute-done.25.refs_1_ = bf16[4,128,512]{2,1,0:T(8,128)(2,1)S(1)} collective-permute-done((bf16[4,128,512]{2,1,0:T(8,128)(2,1)S(1)}, bf16[4,128,512]{2,1,0:T(8,128)(2,1)S(1)}, u32[]{:S(2)}, u32[]{:S(2)}) %collective-permute-start.25) | collective-permute-done | bytes 524320 | tf_op jit(solution)/shard_map/ppermute | solution.py:67
  147.2 1.7 project_near.1
  148.9 8.7 %collective-permute-done.26.refs_1_ = bf16[4,128,512]{2,1,0:T(8,128)(2,1)S(1)} collective-permute-done((bf16[4,128,512]{2,1,0:T(8,128)(2,1)S(1)}, bf16[4,128,512]{2,1,0:T(8,128)(2,1)S(1)}, u32[]{:S(2)}, u32[]{:S(2)}) %collective-permute-start.26) | collective-permute-done | bytes 524320 | tf_op jit(solution)/shard_map/ppermute | solution.py:67
  157.6 1.2 last_keys.1
  159.1 1.3 last_queries.1.refs_1_
  160.5 2.9 %collective-permute-done.28.refs_3_ = bf16[2,128,64]{2,1,0:T(8,128)(2,1)S(1)} collective-permute-done((bf16[2,128,64]{2,1,0:T(8,128)(2,1)S(1)}, bf16[2,128,64]{2,1,0:T(8,128)(2,1)S(1)}, u32[]{:S(2)}, u32[]{:S(2)}) %collective-permute-start.28) | collective-permute-done | bytes 32800 | tf_op jit(solution)/shard_map/ppermute | solution.py:762
  163.4 3.6 %attend_out.1 = (bf16[32,8192]{1,0:T(8,128)(2,1)S(1)}, bf16[32,8192]{1,0:T(8,128)(2,1)}, bf16[32,8192]{1,0:T(8,128)(2,1)}, bf16[32,8192]{1,0:T(8,128)(2,1)}) custom-call(s32[38]{0:T(128)S(1)} %copy-done.30, bf16[128,512]{1,0:T(8,128)(2,1)S(1)} %last_queries.1.refs_1_, bf16[2,128,64]{2,1,0:T(8,128)(2,1)S(1)} %get-tuple-element.54.refs_2_, ...), custom_call_target="tpu_custom_call" | custom-call | flops 1073741824 | bytes 8683520 | tf_op jit(solution)/shard_map/attend_out/pallas_call | solution.py:101
  167.0 3.2 %collective-permute-start.30 = (bf16[32,8192]{1,0:T(8,128)(2,1)}, bf16[32,8192]{1,0:T(8,128)(2,1)}, u32[]{:S(2)}, u32[]{:S(2)}) collective-permute-start(bf16[32,8192]{1,0:T(8,128)(2,1)} %get-tuple-element.57), channel_id=1, source_target_pairs={{0,12},{1,13},{2,14},{3,15},{4,0},{5,1},{6,2},{7,3},{8,4},{9,5},{1... | collective-permute-start | bytes 1572872 | tf_op jit(solution)/shard_map/ppermute | solution.py:67
  170.4 13.1 %collective-permute-done.29.refs_2_ = bf16[32,8192]{1,0:T(8,128)(2,1)S(1)} collective-permute-done((bf16[32,8192]{1,0:T(8,128)(2,1)}, bf16[32,8192]{1,0:T(8,128)(2,1)S(1)}, u32[]{:S(2)}, u32[]{:S(2)}) %collective-permute-start.29) | collective-permute-done | bytes 524320 | tf_op jit(solution)/shard_map/ppermute | solution.py:67
  183.4 1.2 collective-permute-done.30.refs_3_
  184.6 1.5 add_ring.1
  186.2 3.2 %collective-permute-start.33 = (bf16[8,8192]{1,0:T(8,128)(2,1)S(1)}, bf16[8,8192]{1,0:T(8,128)(2,1)S(1)}, u32[]{:S(2)}, u32[]{:S(2)}) collective-permute-start(bf16[8,8192]{1,0:T(8,128)(2,1)S(1)} %get-tuple-element.61), channel_id=1, source_target_pairs={{0,3},{1,0},{2,1},{3,2},{4,7},{5,4},{6,5},{7,6},{8,11},{9,8},{10,9... | collective-permute-start | bytes 393224 | tf_op jit(solution)/shard_map/ppermute | solution.py:67
  189.4 2.9 %collective-permute-done.32.refs_2_ = bf16[8,8192]{1,0:T(8,128)(2,1)S(1)} collective-permute-done((bf16[8,8192]{1,0:T(8,128)(2,1)S(1)}, bf16[8,8192]{1,0:T(8,128)(2,1)S(1)}, u32[]{:S(2)}, u32[]{:S(2)}) %collective-permute-start.32) | collective-permute-done | bytes 131104 | tf_op jit(solution)/shard_map/ppermute | solution.py:67
  192.3 1.0 collective-permute-done.33.refs_3_
  193.3 2.5 %collective-permute-done.34.refs_4_ = bf16[8,8192]{1,0:T(8,128)(2,1)S(1)} collective-permute-done((bf16[8,8192]{1,0:T(8,128)(2,1)S(1)}, bf16[8,8192]{1,0:T(8,128)(2,1)S(1)}, u32[]{:S(2)}, u32[]{:S(2)}) %collective-permute-start.34) | collective-permute-done | bytes 131104 | tf_op jit(solution)/shard_map/ppermute | solution.py:67
  195.9 1.3 finish.1
  (172 shorter events, 23.9 us)
Async XLA Ops:
  1.2 10.5 %copy-start.36 = (s32[16]{0:T(128)}, s32[16]{0:T(128)S(1)}, u32[]{:S(2)}) copy-start(s32[16]{0:T(128)S(1)} %broadcast_select_fusion.2) | copy-start | bytes 196
  1.3 1.0 copy-start.20
  2.3 6.0 %copy-start.26 = (s32[38]{0:T(128)}, s32[38]{0:T(128)S(1)}, u32[]{:S(2)}) copy-start(s32[38]{0:T(128)S(1)} %concatenate.9.refs_0_) | copy-start | bytes 460
  2.9 5.4 %copy-start.9 = (bf16[64,1536]{1,0:T(8,128)(2,1)}, bf16[64,1536]{1,0:T(8,128)(2,1)S(1)}, u32[]{:S(2)}) copy-start(bf16[64,1536]{1,0:T(8,128)(2,1)S(1)} %take_qkv.1.refs_1_.refs_5_) | copy-start | bytes 589828
  2.9 14.7 %collective-permute-start.1 = (bf16[64,1536]{1,0:T(8,128)(2,1)S(1)}, bf16[64,1536]{1,0:T(8,128)(2,1)S(1)}, u32[]{:S(2)}, u32[]{:S(2)}) collective-permute-start(bf16[64,1536]{1,0:T(8,128)(2,1)S(1)} %take_qkv.1.refs_1_.refs_5_), channel_id=1, source_target_pairs={{0,1},{1,2},{2,3},{3,0},{4,5},{5,6},{6,7},{7,4},{8,9},{9,10},{10,1... | collective-permute-start | bytes 589832 | tf_op jit(solution)/shard_map/ppermute | solution.py:67
  4.6 15.6 %collective-permute-start.2 = (bf16[64,1536]{1,0:T(8,128)(2,1)S(1)}, bf16[64,1536]{1,0:T(8,128)(2,1)S(1)}, u32[]{:S(2)}, u32[]{:S(2)}) collective-permute-start(bf16[64,1536]{1,0:T(8,128)(2,1)S(1)} %take_qkv.1.refs_1_.refs_5_), channel_id=1, source_target_pairs={{0,3},{1,0},{2,1},{3,2},{4,7},{5,4},{6,5},{7,6},{8,11},{9,8},{10,9... | collective-permute-start | bytes 589832 | tf_op jit(solution)/shard_map/ppermute | solution.py:67
  6.2 14.0 %collective-permute-start.3 = (bf16[64,1536]{1,0:T(8,128)(2,1)S(1)}, bf16[64,1536]{1,0:T(8,128)(2,1)S(1)}, u32[]{:S(2)}, u32[]{:S(2)}) collective-permute-start(bf16[64,1536]{1,0:T(8,128)(2,1)S(1)} %take_qkv.1.refs_1_.refs_5_), channel_id=1, source_target_pairs={{0,2},{1,3},{2,0},{3,1},{4,6},{5,7},{6,4},{7,5},{8,10},{9,11},{10,... | collective-permute-start | bytes 589832 | tf_op jit(solution)/shard_map/ppermute | solution.py:67
  8.3 30.4 %collective-permute-start = (bf16[128,1024]{1,0:T(8,128)(2,1)}, bf16[128,1024]{1,0:T(8,128)(2,1)S(1)}, u32[]{:S(2)}, u32[]{:S(2)}) collective-permute-start(bf16[128,1024]{1,0:T(8,128)(2,1)} %bitcast.29), channel_id=1, source_target_pairs={{0,16},{16,0},{32,48},{48,32},{64,80},{80,64},{96,112},{112,96},{1... | collective-permute-start | bytes 786440 | tf_op jit(solution)/shard_map/ppermute | solution.py:71
  11.0 38.7 %copy-start.30 = (s32[38]{0:T(128)S(1)}, s32[38]{0:T(128)}, u32[]{:S(2)}) copy-start(s32[38]{0:T(128)} %copy-done.26) | copy-start | bytes 460
  11.0 14.6 %collective-permute-start.8 = (bf16[64,3584]{1,0:T(8,128)(2,1)}, bf16[64,3584]{1,0:T(8,128)(2,1)S(1)}, u32[]{:S(2)}, u32[]{:S(2)}) collective-permute-start(bf16[64,3584]{1,0:T(8,128)(2,1)} %get-tuple-element.34.refs_1_), channel_id=1, source_target_pairs={{0,1},{1,2},{2,3},{3,0},{4,5},{5,6},{6,7},{7,4},{8,9},{9,10},{10,1... | collective-permute-start | bytes 1376264 | tf_op jit(solution)/shard_map/ppermute | solution.py:67
  17.6 24.4 %collective-permute-start.9 = (bf16[64,3584]{1,0:T(8,128)(2,1)}, bf16[64,3584]{1,0:T(8,128)(2,1)}, u32[]{:S(2)}, u32[]{:S(2)}) collective-permute-start(bf16[64,3584]{1,0:T(8,128)(2,1)} %get-tuple-element.35), channel_id=1, source_target_pairs={{0,3},{1,0},{2,1},{3,2},{4,7},{5,4},{6,5},{7,6},{8,11},{9,8},{10,9... | collective-permute-start | bytes 1376264 | tf_op jit(solution)/shard_map/ppermute | solution.py:67
  20.2 0.9 copy-start.10
  22.4 12.5 %collective-permute-start.5 = (bf16[4,64,1536]{2,1,0:T(8,128)(2,1)S(1)}, bf16[4,64,1536]{2,1,0:T(8,128)(2,1)}, u32[]{:S(2)}, u32[]{:S(2)}) collective-permute-start(bf16[4,64,1536]{2,1,0:T(8,128)(2,1)S(1)} %join_qkv.1.refs_2_), channel_id=1, source_target_pairs={{0,12},{1,13},{2,14},{3,15},{4,0},{5,1},{6,2},{7,3},{8,4},{9,5},{1... | collective-permute-start | bytes 2359304 | tf_op jit(solution)/shard_map/ppermute | solution.py:67
  25.5 16.5 %collective-permute-start.4 = (bf16[4,64,1536]{2,1,0:T(8,128)(2,1)S(1)}, bf16[4,64,1536]{2,1,0:T(8,128)(2,1)S(1)}, u32[]{:S(2)}, u32[]{:S(2)}) collective-permute-start(bf16[4,64,1536]{2,1,0:T(8,128)(2,1)S(1)} %join_qkv.1.refs_2_), channel_id=1, source_target_pairs={{0,4},{1,5},{2,6},{3,7},{4,8},{5,9},{6,10},{7,11},{8,12},{9,13},{1... | collective-permute-start | bytes 2359304 | tf_op jit(solution)/shard_map/ppermute | solution.py:67
  25.7 23.1 %copy-start.7 = (bf16[64,3584]{1,0:T(8,128)(2,1)}, bf16[64,3584]{1,0:T(8,128)(2,1)S(1)}, u32[]{:S(2)}) copy-start(bf16[64,3584]{1,0:T(8,128)(2,1)S(1)} %collective-permute-done.8.refs_2_) | copy-start | bytes 1376260
  25.7 16.3 %collective-permute-start.10 = (bf16[64,3584]{1,0:T(8,128)(2,1)S(1)}, bf16[64,3584]{1,0:T(8,128)(2,1)}, u32[]{:S(2)}, u32[]{:S(2)}) collective-permute-start(bf16[64,3584]{1,0:T(8,128)(2,1)S(1)} %collective-permute-done.8.refs_2_), channel_id=1, source_target_pairs={{0,1},{1,2},{2,3},{3,0},{4,5},{5,6},{6,7},{7,4},{8,9},{9,10},{10,1... | collective-permute-start | bytes 1376264 | tf_op jit(solution)/shard_map/ppermute | solution.py:67
  34.9 14.9 %collective-permute-start.6 = (bf16[4,64,1536]{2,1,0:T(8,128)(2,1)}, bf16[4,64,1536]{2,1,0:T(8,128)(2,1)}, u32[]{:S(2)}, u32[]{:S(2)}) collective-permute-start(bf16[4,64,1536]{2,1,0:T(8,128)(2,1)} %collective-permute-done.5.refs_4_.refs_6_), channel_id=1, source_target_pairs={{0,12},{1,13},{2,14},{3,15},{4,0},{5,1},{6,2},{7,3},{8,4},{9,5},{1... | collective-permute-start | bytes 2359304 | tf_op jit(solution)/shard_map/ppermute | solution.py:67
  38.6 15.8 %collective-permute-start.15 = (bf16[64,1024]{1,0:T(8,128)(2,1)}, bf16[64,1024]{1,0:T(8,128)(2,1)}, u32[]{:S(2)}, u32[]{:S(2)}) collective-permute-start(bf16[64,1024]{1,0:T(8,128)(2,1)} %get-tuple-element.39), channel_id=1, source_target_pairs={{0,2},{1,3},{2,0},{3,1},{4,6},{5,7},{6,4},{7,5},{8,10},{9,11},{10,... | collective-permute-start | bytes 393224 | tf_op jit(solution)/shard_map/ppermute | solution.py:67
  39.5 0.9 copy-start.25
  42.9 1.1 copy-start.2
  44.0 1.0 copy-start.5
  45.7 8.6 %copy-start.31 = (bf16[64,1024]{1,0:T(8,128)(2,1)S(1)}, bf16[64,1024]{1,0:T(8,128)(2,1)}, u32[]{:S(2)}) copy-start(bf16[64,1024]{1,0:T(8,128)(2,1)} %get-tuple-element.38.refs_5_) | copy-start | bytes 393220
  45.7 14.7 %copy-start.35 = (s32[8,8]{1,0:T(8,128)S(1)}, s32[8,8]{1,0:T(8,128)}, u32[]{:S(2)}) copy-start(s32[8,8]{1,0:T(8,128)} %select_reduce_fusion.1) | copy-start | bytes 772
  47.0 16.8 %collective-permute-start.11 = (bf16[4,64,1536]{2,1,0:T(8,128)(2,1)S(1)}, bf16[4,64,1536]{2,1,0:T(8,128)(2,1)}, u32[]{:S(2)}, u32[]{:S(2)}) collective-permute-start(bf16[4,64,1536]{2,1,0:T(8,128)(2,1)S(1)} %join_middle.1.refs_4_.refs_3_), channel_id=1, source_target_pairs={{0,4},{1,5},{2,6},{3,7},{4,8},{5,9},{6,10},{7,11},{8,12},{9,13},{1... | collective-permute-start | bytes 2359304 | tf_op jit(solution)/shard_map/ppermute | solution.py:67
  49.8 1.1 copy-start.3
  54.4 1.0 copy-start.6
  55.4 1.0 copy-start.8
  59.2 12.4 %copy-start.34 = (bf16[4,64,256]{2,1,0:T(8,128)(2,1)}, bf16[4,64,256]{2,1,0:T(8,128)(2,1)S(1)}, u32[]{:S(2)}) copy-start(bf16[4,64,256]{2,1,0:T(8,128)(2,1)S(1)} %get-tuple-element.45) | copy-start | bytes 393220
  59.2 12.4 %collective-permute-start.16 = (bf16[4,64,1280]{2,1,0:T(8,128)(2,1)S(1)}, bf16[4,64,1280]{2,1,0:T(8,128)(2,1)}, u32[]{:S(2)}, u32[]{:S(2)}) collective-permute-start(bf16[4,64,1280]{2,1,0:T(8,128)(2,1)S(1)} %get-tuple-element.40.refs_3_), channel_id=1, source_target_pairs={{0,4},{1,5},{2,6},{3,7},{4,8},{5,9},{6,10},{7,11},{8,12},{9,13},{1... | collective-permute-start | bytes 1966088 | tf_op jit(solution)/shard_map/ppermute | solution.py:67
  60.4 12.9 %collective-permute-start.12 = (bf16[4,64,1536]{2,1,0:T(8,128)(2,1)S(1)}, bf16[4,64,1536]{2,1,0:T(8,128)(2,1)S(1)}, u32[]{:S(2)}, u32[]{:S(2)}) collective-permute-start(bf16[4,64,1536]{2,1,0:T(8,128)(2,1)S(1)} %join_middle.1.refs_4_.refs_3_), channel_id=1, source_target_pairs={{0,12},{1,13},{2,14},{3,15},{4,0},{5,1},{6,2},{7,3},{8,4},{9,5},{1... | collective-permute-start | bytes 2359304 | tf_op jit(solution)/shard_map/ppermute | solution.py:67
  63.8 16.2 %collective-permute-start.13 = (bf16[4,64,1536]{2,1,0:T(8,128)(2,1)}, bf16[4,64,1536]{2,1,0:T(8,128)(2,1)}, u32[]{:S(2)}, u32[]{:S(2)}) collective-permute-start(bf16[4,64,1536]{2,1,0:T(8,128)(2,1)} %collective-permute-done.11.refs_5_.refs_4_), channel_id=1, source_target_pairs={{0,4},{1,5},{2,6},{3,7},{4,8},{5,9},{6,10},{7,11},{8,12},{9,13},{1... | collective-permute-start | bytes 2359304 | tf_op jit(solution)/shard_map/ppermute | solution.py:67
  64.5 8.8 %collective-permute-start.7 = (bf16[8,256,64]{2,1,0:T(8,128)(2,1)S(1)}, bf16[8,256,64]{2,1,0:T(8,128)(2,1)}, u32[]{:S(2)}, u32[]{:S(2)}) collective-permute-start(bf16[8,256,64]{2,1,0:T(8,128)(2,1)S(1)} %span_attention.1.refs_1_.refs_7_), channel_id=1, source_target_pairs={{0,16},{16,0},{32,48},{48,32},{64,80},{80,64},{96,112},{112,96},{1... | collective-permute-start | bytes 786440 | tf_op jit(solution)/shard_map/ppermute | solution.py:71
  64.5 26.9 %collective-permute-start.17 = (bf16[4,64,1280]{2,1,0:T(8,128)(2,1)}, bf16[4,64,1280]{2,1,0:T(8,128)(2,1)}, u32[]{:S(2)}, u32[]{:S(2)}) collective-permute-start(bf16[4,64,1280]{2,1,0:T(8,128)(2,1)} %get-tuple-element.41), channel_id=1, source_target_pairs={{0,12},{1,13},{2,14},{3,15},{4,0},{5,1},{6,2},{7,3},{8,4},{9,5},{1... | collective-permute-start | bytes 1966088 | tf_op jit(solution)/shard_map/ppermute | solution.py:67
  71.6 19.8 %collective-permute-start.18 = (bf16[4,64,1280]{2,1,0:T(8,128)(2,1)}, bf16[4,64,1280]{2,1,0:T(8,128)(2,1)}, u32[]{:S(2)}, u32[]{:S(2)}) collective-permute-start(bf16[4,64,1280]{2,1,0:T(8,128)(2,1)} %collective-permute-done.16.refs_4_.refs_2_), channel_id=1, source_target_pairs={{0,4},{1,5},{2,6},{3,7},{4,8},{5,9},{6,10},{7,11},{8,12},{9,13},{1... | collective-permute-start | bytes 1966088 | tf_op jit(solution)/shard_map/ppermute | solution.py:67
  82.3 1.8 collective-permute-start.14
  83.0 40.6 %copy-start.4 = (bf16[1024,1024]{1,0:T(8,128)(2,1)S(1)}, bf16[1024,1024]{1,0:T(8,128)(2,1)}, u32[]{:S(2)}) copy-start(bf16[1024,1024]{1,0:T(8,128)(2,1)} %refs_3_.5) | copy-start | bytes 6291460
  88.1 51.9 %slice-start = ((s8[8388608]{0:T(1024)(128)(4,1)}), s8[4194304]{0:T(1024)(128)(4,1)S(1)}, s32[]{:S(2)}) async-start(s8[8388608]{0:T(1024)(128)(4,1)} %bitcast.17), calls=%async_computation.1 | async-start | bytes 8388608
  88.1 51.9 %copy-start = (bf16[2,8192,64]{1,2,0:T(8,128)(2,1)S(1)}, bf16[2,8192,64]{1,2,0:T(8,128)(2,1)}, u32[]{:S(2)}) copy-start(bf16[2,8192,64]{1,2,0:T(8,128)(2,1)} %param.30) | copy-start | bytes 6291460
  91.4 1.1 copy-start.14
  92.5 47.5 %copy-start.19 = (f32[8192]{0:T(1024)S(1)}, f32[8192]{0:T(1024)}, u32[]{:S(2)}) copy-start(f32[8192]{0:T(1024)} %param.28) | copy-start | bytes 98308
  94.9 1.6 collective-permute-start.19
  95.2 6.7 %collective-permute-start.20 = (bf16[4,64,256]{2,1,0:T(8,128)(2,1)}, bf16[4,64,256]{2,1,0:T(8,128)(2,1)S(1)}, u32[]{:S(2)}, u32[]{:S(2)}) collective-permute-start(bf16[4,64,256]{2,1,0:T(8,128)(2,1)} %copy-done.34), channel_id=1, source_target_pairs={{0,8},{1,9},{2,10},{3,11},{4,12},{5,13},{6,14},{7,15},{8,0},{9,1},... | collective-permute-start | bytes 393224 | tf_op jit(solution)/shard_map/ppermute | solution.py:67
  96.5 43.6 %slice-start.1 = ((s8[8388608]{0:T(1024)(128)(4,1)}), s8[4194304]{0:T(1024)(128)(4,1)S(1)}, s32[]{:S(2)}) async-start(s8[8388608]{0:T(1024)(128)(4,1)} %bitcast.17), calls=%async_computation.2 | async-start | bytes 8388608
  104.1 43.1 %copy-start.12 = (f32[128,128]{1,0:T(8,128)S(1)}, f32[128,128]{1,0:T(8,128)}, u32[]{:S(2)}) copy-start(f32[128,128]{1,0:T(8,128)} %fusion.6.refs_15_.refs_8_) | copy-start | bytes 196612
  104.1 19.4 %collective-permute-start.21 = (bf16[4,4,64,256]{3,2,1,0:T(8,128)(2,1)S(1)}, bf16[4,4,64,256]{3,2,1,0:T(8,128)(2,1)S(1)}, u32[]{:S(2)}, u32[]{:S(2)}) collective-permute-start(bf16[4,4,64,256]{3,2,1,0:T(8,128)(2,1)S(1)} %join_proj.1.refs_4_), channel_id=1, source_target_pairs={{0,16},{16,0},{32,48},{48,32},{64,80},{80,64},{96,112},{112,96},{1... | collective-permute-start | bytes 1572872 | tf_op jit(solution)/shard_map/ppermute | solution.py:71
  126.4 6.2 %collective-permute-start.22 = (bf16[128,512]{1,0:T(8,128)(2,1)S(1)}, bf16[128,512]{1,0:T(8,128)(2,1)S(1)}, u32[]{:S(2)}, u32[]{:S(2)}) collective-permute-start(bf16[128,512]{1,0:T(8,128)(2,1)S(1)} %embed.1.refs_1_), channel_id=1, source_target_pairs={{0,1},{1,2},{2,3},{3,0},{4,5},{5,6},{6,7},{7,4},{8,9},{9,10},{10,1... | collective-permute-start | bytes 393224 | tf_op jit(solution)/shard_map/ppermute | solution.py:67
  127.1 6.5 %collective-permute-start.23 = (bf16[128,512]{1,0:T(8,128)(2,1)S(1)}, bf16[128,512]{1,0:T(8,128)(2,1)S(1)}, u32[]{:S(2)}, u32[]{:S(2)}) collective-permute-start(bf16[128,512]{1,0:T(8,128)(2,1)S(1)} %embed.1.refs_1_), channel_id=1, source_target_pairs={{0,3},{1,0},{2,1},{3,2},{4,7},{5,4},{6,5},{7,6},{8,11},{9,8},{10,9... | collective-permute-start | bytes 393224 | tf_op jit(solution)/shard_map/ppermute | solution.py:67
  129.7 6.5 %collective-permute-start.24 = (bf16[128,512]{1,0:T(8,128)(2,1)S(1)}, bf16[128,512]{1,0:T(8,128)(2,1)S(1)}, u32[]{:S(2)}, u32[]{:S(2)}) collective-permute-start(bf16[128,512]{1,0:T(8,128)(2,1)S(1)} %embed.1.refs_1_), channel_id=1, source_target_pairs={{0,2},{1,3},{2,0},{3,1},{4,6},{5,7},{6,4},{7,5},{8,10},{9,11},{10,... | collective-permute-start | bytes 393224 | tf_op jit(solution)/shard_map/ppermute | solution.py:67
  136.8 10.5 %collective-permute-start.25 = (bf16[4,128,512]{2,1,0:T(8,128)(2,1)S(1)}, bf16[4,128,512]{2,1,0:T(8,128)(2,1)S(1)}, u32[]{:S(2)}, u32[]{:S(2)}) collective-permute-start(bf16[4,128,512]{2,1,0:T(8,128)(2,1)S(1)} %join_columns.1.refs_1_), channel_id=1, source_target_pairs={{0,4},{1,5},{2,6},{3,7},{4,8},{5,9},{6,10},{7,11},{8,12},{9,13},{1... | collective-permute-start | bytes 1572872 | tf_op jit(solution)/shard_map/ppermute | solution.py:67
  137.4 9.8 %collective-permute-start.27 = (bf16[4,128,512]{2,1,0:T(8,128)(2,1)S(1)}, bf16[4,128,512]{2,1,0:T(8,128)(2,1)S(1)}, u32[]{:S(2)}, u32[]{:S(2)}) collective-permute-start(bf16[4,128,512]{2,1,0:T(8,128)(2,1)S(1)} %join_columns.1.refs_1_), channel_id=1, source_target_pairs={{0,12},{1,13},{2,14},{3,15},{4,0},{5,1},{6,2},{7,3},{8,4},{9,5},{1... | collective-permute-start | bytes 1572872 | tf_op jit(solution)/shard_map/ppermute | solution.py:67
  141.3 16.3 %copy-start.16 = (f32[128,64]{1,0:T(8,128)S(1)}, f32[128,64]{1,0:T(8,128)}, u32[]{:S(2)}) copy-start(f32[128,64]{1,0:T(8,128)} %get-tuple-element.76.refs_14_.refs_7_) | copy-start | bytes 98308
  141.3 16.3 %copy-start.18 = (f32[128,64]{1,0:T(8,128)S(1)}, f32[128,64]{1,0:T(8,128)}, u32[]{:S(2)}) copy-start(f32[128,64]{1,0:T(8,128)} %get-tuple-element.77.refs_13_.refs_6_) | copy-start | bytes 98308
  147.2 10.4 %collective-permute-start.26 = (bf16[4,128,512]{2,1,0:T(8,128)(2,1)S(1)}, bf16[4,128,512]{2,1,0:T(8,128)(2,1)S(1)}, u32[]{:S(2)}, u32[]{:S(2)}) collective-permute-start(bf16[4,128,512]{2,1,0:T(8,128)(2,1)S(1)} %collective-permute-done.25.refs_1_), channel_id=1, source_target_pairs={{0,4},{1,5},{2,6},{3,7},{4,8},{5,9},{6,10},{7,11},{8,12},{9,13},{1... | collective-permute-start | bytes 1572872 | tf_op jit(solution)/shard_map/ppermute | solution.py:67
  147.2 16.1 %slice-start.2 = ((s8[8388608]{0:T(1024)(128)(4,1)}), s8[4194304]{0:T(1024)(128)(4,1)S(1)}, s32[]{:S(2)}) async-start(s8[8388608]{0:T(1024)(128)(4,1)} %bitcast.22), calls=%async_computation.3 | async-start | bytes 8388608
  148.9 14.4 %copy-start.22 = (bf16[128,128]{1,0:T(8,128)(2,1)S(1)}, bf16[128,128]{1,0:T(8,128)(2,1)}, u32[]{:S(2)}) copy-start(bf16[128,128]{1,0:T(8,128)(2,1)} %fusion.1.refs_9_.refs_5_) | copy-start | bytes 98308
  157.6 5.8 %slice-start.3 = ((s8[8388608]{0:T(1024)(128)(4,1)}), s8[4194304]{0:T(1024)(128)(4,1)S(1)}, s32[]{:S(2)}) async-start(s8[8388608]{0:T(1024)(128)(4,1)} %bitcast.22), calls=%async_computation.4 | async-start | bytes 8388608
  158.8 4.6 %collective-permute-start.28 = (bf16[2,128,64]{2,1,0:T(8,128)(2,1)S(1)}, bf16[2,128,64]{2,1,0:T(8,128)(2,1)S(1)}, u32[]{:S(2)}, u32[]{:S(2)}) collective-permute-start(bf16[2,128,64]{2,1,0:T(8,128)(2,1)S(1)} %get-tuple-element.54.refs_2_), channel_id=1, source_target_pairs={{0,1},{1,0},{2,3},{3,2},{4,5},{5,4},{6,7},{7,6},{8,9},{9,8},{10,11... | collective-permute-start | bytes 98312 | tf_op jit(solution)/shard_map/ppermute | solution.py:762
  159.1 11.2 %copy-start.37 = (s32[16]{0:T(128)S(1)}, s32[16]{0:T(128)}, u32[]{:S(2)}) copy-start(s32[16]{0:T(128)} %copy-done.36) | copy-start | bytes 196
  167.0 16.4 %collective-permute-start.29 = (bf16[32,8192]{1,0:T(8,128)(2,1)}, bf16[32,8192]{1,0:T(8,128)(2,1)S(1)}, u32[]{:S(2)}, u32[]{:S(2)}) collective-permute-start(bf16[32,8192]{1,0:T(8,128)(2,1)} %get-tuple-element.56), channel_id=1, source_target_pairs={{0,4},{1,5},{2,6},{3,7},{4,8},{5,9},{6,10},{7,11},{8,12},{9,13},{1... | collective-permute-start | bytes 1572872 | tf_op jit(solution)/shard_map/ppermute | solution.py:67
  167.0 17.6 %collective-permute-start.30 = (bf16[32,8192]{1,0:T(8,128)(2,1)}, bf16[32,8192]{1,0:T(8,128)(2,1)}, u32[]{:S(2)}, u32[]{:S(2)}) collective-permute-start(bf16[32,8192]{1,0:T(8,128)(2,1)} %get-tuple-element.57), channel_id=1, source_target_pairs={{0,12},{1,13},{2,14},{3,15},{4,0},{5,1},{6,2},{7,3},{8,4},{9,5},{1... | collective-permute-start | bytes 1572872 | tf_op jit(solution)/shard_map/ppermute | solution.py:67
  170.3 14.4 %collective-permute-start.31 = (bf16[32,8192]{1,0:T(8,128)(2,1)}, bf16[32,8192]{1,0:T(8,128)(2,1)}, u32[]{:S(2)}, u32[]{:S(2)}) collective-permute-start(bf16[32,8192]{1,0:T(8,128)(2,1)} %get-tuple-element.58), channel_id=1, source_target_pairs={{0,8},{1,9},{2,10},{3,11},{4,12},{5,13},{6,14},{7,15},{8,0},{9,1},... | collective-permute-start | bytes 1572872 | tf_op jit(solution)/shard_map/ppermute | solution.py:67
  186.1 6.2 %collective-permute-start.32 = (bf16[8,8192]{1,0:T(8,128)(2,1)S(1)}, bf16[8,8192]{1,0:T(8,128)(2,1)S(1)}, u32[]{:S(2)}, u32[]{:S(2)}) collective-permute-start(bf16[8,8192]{1,0:T(8,128)(2,1)S(1)} %get-tuple-element.60), channel_id=1, source_target_pairs={{0,1},{1,2},{2,3},{3,0},{4,5},{5,6},{6,7},{7,4},{8,9},{9,10},{10,1... | collective-permute-start | bytes 393224 | tf_op jit(solution)/shard_map/ppermute | solution.py:67
  186.2 7.1 %collective-permute-start.33 = (bf16[8,8192]{1,0:T(8,128)(2,1)S(1)}, bf16[8,8192]{1,0:T(8,128)(2,1)S(1)}, u32[]{:S(2)}, u32[]{:S(2)}) collective-permute-start(bf16[8,8192]{1,0:T(8,128)(2,1)S(1)} %get-tuple-element.61), channel_id=1, source_target_pairs={{0,3},{1,0},{2,1},{3,2},{4,7},{5,4},{6,5},{7,6},{8,11},{9,8},{10,9... | collective-permute-start | bytes 393224 | tf_op jit(solution)/shard_map/ppermute | solution.py:67
  189.4 6.5 %collective-permute-start.34 = (bf16[8,8192]{1,0:T(8,128)(2,1)S(1)}, bf16[8,8192]{1,0:T(8,128)(2,1)S(1)}, u32[]{:S(2)}, u32[]{:S(2)}) collective-permute-start(bf16[8,8192]{1,0:T(8,128)(2,1)S(1)} %get-tuple-element.62), channel_id=1, source_target_pairs={{0,2},{1,3},{2,0},{3,1},{4,6},{5,7},{6,4},{7,5},{8,10},{9,11},{10,... | collective-permute-start | bytes 393224 | tf_op jit(solution)/shard_map/ppermute | solution.py:67
  (13 other events, 10.1 us)

commit v10 on v6

--- a/solution.py
+++ b/solution.py
@@ -663,6 +663,7 @@
         ),
         [pltpu.VMEM((all_rows, width), jnp.float32)],
         flops=2 * all_rows * width * width,
+        after=[far_beyond],
     )
     outgoing = whole_call(
         norm_pool,

time: 193 us -> 194 us (level)
  waiting for transfers between devices: 77.4 us -> 72.6 us
  starting transfers between devices: 43.5 us -> 46.1 us
  local copies, waits for them, and re-layouts: 22.6 us -> 24.8 us
    ppermute x29, waiting for transfers between devices: 62.4 us -> 57.5 us  [to_ring(): return lax.ppermute(value, AXES, ring_pairs(phase, distance))]
    unnamed x60 -> x58, local copies, waits for them, and re-layouts: 16.2 us -> 15.3 us
  transfers between devices with their start and end apart: 36 -> 36, of which waited for: 24 -> 23; matrix products, arithmetic and copies ran while one was open for 8% -> 10% of each run, Pallas kernels for 11% -> 11%
where the time goes in v10:
time: 194 us; the launch traced here: 192 us
  waiting for transfers between devices  72.6 us (37%)
  starting transfers between devices  46.1 us (24%)
  Pallas kernels  36.4 us (19%)
  local copies, waits for them, and re-layouts  24.8 us (13%)
  other arithmetic  11.2 us (6%)
    ppermute x29, waiting for transfers between devices, to_ring(): return lax.ppermute(value, AXES, ring_pairs(phase, distance))  57.5 us
    ppermute x29, starting transfers between devices, to_ring(): return lax.ppermute(value, AXES, ring_pairs(phase, distance))  36.6 us
    pallas_call x21, Pallas kernels, whole_call(): pl.pallas_call(run, name=name, out_shape=outs, in_specs=[SMEM] + [VMEM] *...  36.4 us
    unnamed x58, local copies, waits for them, and re-layouts  15.3 us
    all_to_all x1, waiting for transfers between devices, local(): lax.all_to_all(outgoing.reshape(device_count, width // 128, 128), AXES, 0...  10.2 us
    all_to_all x1, starting transfers between devices, local(): lax.all_to_all(outgoing.reshape(device_count, width // 128, 128), AXES, 0...  8.97 us
  transfers between devices with their start and end apart: 36, of which 23 were waited for; matrix products, arithmetic and copies ran while one was open for 10% of the time, Pallas kernels for 11%

profile of v10, /device:TPU:0, one launch (start us, length us, event | category | flops | bytes accessed | tf_op | source)
XLA Modules:
  0.0 192.3 jit_solution(480212018978171073)
XLA Ops:
  0.0 1.3 broadcast_add_fusion.2
  1.9 1.0 copy-done.10
  3.5 1.7 collective-permute-start.1
  5.2 1.6 collective-permute-start.2
  6.8 2.1 %collective-permute-start.3 = (bf16[64,1536]{1,0:T(8,128)(2,1)S(1)}, bf16[64,1536]{1,0:T(8,128)(2,1)S(1)}, u32[]{:S(2)}, u32[]{:S(2)}) collective-permute-start(bf16[64,1536]{1,0:T(8,128)(2,1)S(1)} %take_qkv.1.refs_1_.refs_5_), channel_id=1, source_target_pairs={{0,2},{1,3},{2,0},{3,1},{4,6},{5,7},{6,4},{7,5},{8,10},{9,11},{10,... | collective-permute-start | bytes 589832 | tf_op jit(solution)/shard_map/ppermute | solution.py:67
  8.9 1.6 collective-permute-done.1.refs_2_
  10.9 3.1 %collective-permute-done.3.refs_4_ = bf16[64,1536]{1,0:T(8,128)(2,1)S(1)} collective-permute-done((bf16[64,1536]{1,0:T(8,128)(2,1)S(1)}, bf16[64,1536]{1,0:T(8,128)(2,1)S(1)}, u32[]{:S(2)}, u32[]{:S(2)}) %collective-permute-start.3) | collective-permute-done | bytes 196640 | tf_op jit(solution)/shard_map/ppermute | solution.py:67
  14.6 2.9 %collective-permute-start.5 = (bf16[4,64,1536]{2,1,0:T(8,128)(2,1)S(1)}, bf16[4,64,1536]{2,1,0:T(8,128)(2,1)}, u32[]{:S(2)}, u32[]{:S(2)}) collective-permute-start(bf16[4,64,1536]{2,1,0:T(8,128)(2,1)S(1)} %join_qkv.1.refs_2_), channel_id=1, source_target_pairs={{0,12},{1,13},{2,14},{3,15},{4,0},{5,1},{6,2},{7,3},{8,4},{9,5},{1... | collective-permute-start | bytes 2359304 | tf_op jit(solution)/shard_map/ppermute | solution.py:67
  17.5 2.7 %take_rest.1 = (bf16[64,3584]{1,0:T(8,128)(2,1)}, bf16[64,3584]{1,0:T(8,128)(2,1)}, bf16[64,1024]{1,0:T(8,128)(2,1)}, bf16[64,1024]{1,0:T(8,128)(2,1)}) custom-call(s32[38]{0:T(128)} %copy-done.12, bf16[64,1024]{1,0:T(8,128)(2,1)} %refs_1_.3, bf16[64,2048]{1,0:T(8,128)(2,1)} %refs_2_.1, bf16[128,1024]{1,0:T(8,128)(2,1)} %refs_3_.4, ...), custom_call_target="tpu_custom_call" | custom-call | bytes 1703936 | tf_op jit(solution)/shard_map/take_rest/pallas_call | solution.py:101
  20.2 1.2 collective-permute-start.8
  21.5 2.0 %collective-permute-start.9 = (bf16[64,3584]{1,0:T(8,128)(2,1)}, bf16[64,3584]{1,0:T(8,128)(2,1)S(1)}, u32[]{:S(2)}, u32[]{:S(2)}) collective-permute-start(bf16[64,3584]{1,0:T(8,128)(2,1)} %get-tuple-element.34), channel_id=1, source_target_pairs={{0,3},{1,0},{2,1},{3,2},{4,7},{5,4},{6,5},{7,6},{8,11},{9,8},{10,9... | collective-permute-start | bytes 1376264 | tf_op jit(solution)/shard_map/ppermute | solution.py:67
  23.5 11.6 %collective-permute-done.8.refs_2_ = bf16[64,3584]{1,0:T(8,128)(2,1)S(1)} collective-permute-done((bf16[64,3584]{1,0:T(8,128)(2,1)}, bf16[64,3584]{1,0:T(8,128)(2,1)S(1)}, u32[]{:S(2)}, u32[]{:S(2)}) %collective-permute-start.8) | collective-permute-done | bytes 458784 | tf_op jit(solution)/shard_map/ppermute | solution.py:67
  35.1 0.8 collective-permute-start.6
  36.0 1.7 collective-permute-done.refs_2_
  37.7 0.9 copy-done.11
  39.3 0.9 both_rows.1.refs_1_.refs_7_.refs_3_
  40.1 4.7 %collective-permute-done.10.refs_4_ = bf16[64,3584]{1,0:T(8,128)(2,1)S(1)} collective-permute-done((bf16[64,3584]{1,0:T(8,128)(2,1)S(1)}, bf16[64,3584]{1,0:T(8,128)(2,1)S(1)}, u32[]{:S(2)}, u32[]{:S(2)}) %collective-permute-start.10) | collective-permute-done | bytes 458784 | tf_op jit(solution)/shard_map/ppermute | solution.py:67
  44.8 1.0 copy-done.6
  46.6 2.1 %collective-permute-done.6.refs_5_ = bf16[4,64,1536]{2,1,0:T(8,128)(2,1)S(1)} collective-permute-done((bf16[4,64,1536]{2,1,0:T(8,128)(2,1)}, bf16[4,64,1536]{2,1,0:T(8,128)(2,1)S(1)}, u32[]{:S(2)}, u32[]{:S(2)}) %collective-permute-start.6) | collective-permute-done | bytes 786464 | tf_op jit(solution)/shard_map/ppermute | solution.py:67
  48.7 1.1 copy-done.4
  49.9 3.2 %span_attention.1.refs_1_.refs_7_ = bf16[8,256,64]{2,1,0:T(8,128)(2,1)S(1)} custom-call(s32[38]{0:T(128)S(1)} %copy-done.13, bf16[16,256,64]{2,1,0:T(8,128)(2,1)S(1)} %both_rows.1.refs_1_.refs_7_.refs_3_, bf16[4,64,1536]{2,1,0:T(8,128)(2,1)S(1)} %copy-done.4, bf16[4,64,1536]{2,1,0:T(8,128)(2,1)S(1)} %collective-permute-done.4.refs_3_.refs_5_, ...), custom_call_target="tpu_custom_call" | custom-call | flops 805306368 | bytes 3670016 | tf_op jit(solution)/shard_map/span_attention/pallas_call | solution.py:101
  53.1 1.6 collective-permute-done.15.refs_6_
  54.7 1.5 join_lower.1
  57.5 2.7 %collective-permute-start.12 = (bf16[4,64,1536]{2,1,0:T(8,128)(2,1)S(1)}, bf16[4,64,1536]{2,1,0:T(8,128)(2,1)}, u32[]{:S(2)}, u32[]{:S(2)}) collective-permute-start(bf16[4,64,1536]{2,1,0:T(8,128)(2,1)S(1)} %join_middle.1.refs_4_.refs_3_), channel_id=1, source_target_pairs={{0,12},{1,13},{2,14},{3,15},{4,0},{5,1},{6,2},{7,3},{8,4},{9,5},{1... | collective-permute-start | bytes 2359304 | tf_op jit(solution)/shard_map/ppermute | solution.py:67
  62.4 3.3 %collective-permute-start.17 = (bf16[4,64,1280]{2,1,0:T(8,128)(2,1)}, bf16[4,64,1280]{2,1,0:T(8,128)(2,1)}, u32[]{:S(2)}, u32[]{:S(2)}) collective-permute-start(bf16[4,64,1280]{2,1,0:T(8,128)(2,1)} %copy-done.19), channel_id=1, source_target_pairs={{0,12},{1,13},{2,14},{3,15},{4,0},{5,1},{6,2},{7,3},{8,4},{9,5},{1... | collective-permute-start | bytes 1966088 | tf_op jit(solution)/shard_map/ppermute | solution.py:67
  65.7 3.2 %collective-permute-done.16.refs_4_.refs_2_ = bf16[4,64,1280]{2,1,0:T(8,128)(2,1)S(1)} collective-permute-done((bf16[4,64,1280]{2,1,0:T(8,128)(2,1)}, bf16[4,64,1280]{2,1,0:T(8,128)(2,1)S(1)}, u32[]{:S(2)}, u32[]{:S(2)}) %collective-permute-start.16) | collective-permute-done | bytes 655392 | tf_op jit(solution)/shard_map/ppermute | solution.py:67
  68.9 1.9 select_reduce_fusion.3
  77.4 3.0 %context_out.1.refs_1_ = bf16[256,512]{1,0:T(8,128)(2,1)} custom-call(s32[38]{0:T(128)S(1)} %copy-done.14, bf16[8,256,64]{2,1,0:T(8,128)(2,1)S(1)} %span_attention.1.refs_1_.refs_7_, bf16[8,256,64]{2,1,0:T(8,128)(2,1)S(1)} %collective-permute-done.7.refs_2_, bf16[16,256,64]{2,1,0:T(8,128)(2,1)S(1)} %both_rows.1.refs_1_.refs_7_.refs_3_, ...), custom_call_target="tpu_custom_call" | custom-call | flops 268435456 | bytes 4194304 | tf_op jit(solution)/shard_map/context_out/pallas_call | solution.py:101
  81.1 1.0 select_reduce_fusion
  82.1 2.7 %collective-permute-start.19 = (bf16[4,64,256]{2,1,0:T(8,128)(2,1)}, bf16[4,64,256]{2,1,0:T(8,128)(2,1)S(1)}, u32[]{:S(2)}, u32[]{:S(2)}) collective-permute-start(bf16[4,64,256]{2,1,0:T(8,128)(2,1)} %copy-done.20), channel_id=1, source_target_pairs={{0,8},{1,9},{2,10},{3,11},{4,12},{5,13},{6,14},{7,15},{8,0},{9,1},... | collective-permute-start | bytes 393224 | tf_op jit(solution)/shard_map/ppermute | solution.py:67
  85.4 3.7 %norm_up.1 = (bf16[256,1024]{1,0:T(8,128)(2,1)S(1)}, bf16[16,256,64]{2,1,0:T(8,128)(2,1)S(1)}) custom-call(s32[38]{0:T(128)S(1)} %copy-done.14, bf16[256,512]{1,0:T(8,128)(2,1)} %context_out.1.refs_1_, bf16[256,512]{1,0:T(8,128)(2,1)} %collective-permute-done.14.refs_2_, bf16[4,64,1536]{2,1,0:T(8,128)(2,1)S(1)} %join_middle.1.refs_4_.refs_3_, ...), custom_call_target="tpu_custom_call" | custom-call | flops 536870912 | bytes 3670016 | tf_op jit(solution)/shard_map/norm_up/pallas_call | solution.py:101
  89.1 2.3 %down.1 = (f32[128,1024]{1,0:T(8,128)S(1)}, bf16[128,1024]{1,0:T(8,128)(2,1)S(1)}) custom-call(s32[38]{0:T(128)S(1)} %copy-done.14, bf16[16,256,64]{2,1,0:T(8,128)(2,1)S(1)} %get-tuple-element.35.refs_1_, bf16[256,1024]{1,0:T(8,128)(2,1)S(1)} %get-tuple-element.36.refs_2_, bf16[4,64,1280]{2,1,0:T(8,128)(2,1)} %get-tuple-element.39.refs_3_, ...), custom_call_target="tpu_custom_call" | custom-call | flops 536870912 | bytes 3670016 | tf_op jit(solution)/shard_map/down/pallas_call | solution.py:101
  93.0 1.7 norm_pool.1.refs_5_
  94.7 1.1 join_proj.1.refs_4_
  96.2 9.0 %all-to-all-start = ((bf16[128,8,128]{2,1,0:T(8,128)(2,1)}), bf16[128,8,128]{2,1,0:T(8,128)(2,1)S(1)}, u32[]{:S(2)}, u32[]{:S(2)}) async-start(bf16[128,8,128]{2,1,0:T(8,128)(2,1)} %bitcast.8), calls=%async_computation | async-start | bytes 524288 | tf_op jit(solution)/shard_map/all_to_all | solution.py:676
  105.8 10.2 %all-to-all-done.refs_1_ = bf16[128,8,128]{2,1,0:T(8,128)(2,1)S(1)} async-done(((bf16[128,8,128]{2,1,0:T(8,128)(2,1)}), bf16[128,8,128]{2,1,0:T(8,128)(2,1)S(1)}, u32[]{:S(2)}, u32[]{:S(2)}) %all-to-all-start) | async-done | bytes 262176 | tf_op jit(solution)/shard_map/all_to_all | solution.py:676
  116.0 1.6 copy-done.5
  118.4 2.1 %embed.1.refs_1_ = bf16[128,512]{1,0:T(8,128)(2,1)S(1)} custom-call(s32[38]{0:T(128)S(1)} %copy-done.14, bf16[128,8,128]{2,1,0:T(8,128)(2,1)S(1)} %all-to-all-done.refs_1_, bf16[128,128]{1,0:T(8,128)(2,1)S(1)} %copy-done.15, bf16[1024,1024]{1,0:T(8,128)(2,1)S(1)} %copy-done.5, bf16[4,4,64,256]{3,2,1,0:T(8,128)(2,1)S(1)} %join_proj.1.refs_4_, ...), custom_call_target="tpu_custom_call" | custom-call | flops 402653184 | bytes 3440640 | tf_op jit(solution)/shard_map/embed/pallas_call | solution.py:101
  121.2 2.6 %collective-permute-start.23 = (bf16[128,512]{1,0:T(8,128)(2,1)S(1)}, bf16[128,512]{1,0:T(8,128)(2,1)S(1)}, u32[]{:S(2)}, u32[]{:S(2)}) collective-permute-start(bf16[128,512]{1,0:T(8,128)(2,1)S(1)} %embed.1.refs_1_), channel_id=1, source_target_pairs={{0,3},{1,0},{2,1},{3,2},{4,7},{5,4},{6,5},{7,6},{8,11},{9,8},{10,9... | collective-permute-start | bytes 393224 | tf_op jit(solution)/shard_map/ppermute | solution.py:67
  124.4 0.8 select_reduce_fusion.1
  125.2 1.5 collective-permute-done.22.refs_2_
  126.7 1.0 collective-permute-done.23.refs_3_
  127.7 2.5 %collective-permute-done.24.refs_4_ = bf16[128,512]{1,0:T(8,128)(2,1)S(1)} collective-permute-done((bf16[128,512]{1,0:T(8,128)(2,1)S(1)}, bf16[128,512]{1,0:T(8,128)(2,1)S(1)}, u32[]{:S(2)}, u32[]{:S(2)}) %collective-permute-start.24) | collective-permute-done | bytes 131104 | tf_op jit(solution)/shard_map/ppermute | solution.py:67
  131.5 0.9 multiply_sine_fusion
  132.4 2.7 %collective-permute-start.27 = (bf16[4,128,512]{2,1,0:T(8,128)(2,1)S(1)}, bf16[4,128,512]{2,1,0:T(8,128)(2,1)}, u32[]{:S(2)}, u32[]{:S(2)}) collective-permute-start(bf16[4,128,512]{2,1,0:T(8,128)(2,1)S(1)} %join_columns.1.refs_1_), channel_id=1, source_target_pairs={{0,12},{1,13},{2,14},{3,15},{4,0},{5,1},{6,2},{7,3},{8,4},{9,5},{1... | collective-permute-start | bytes 1572872 | tf_op jit(solution)/shard_map/ppermute | solution.py:67
  136.3 5.1 %collective-permute-done.25.refs_1_ = bf16[4,128,512]{2,1,0:T(8,128)(2,1)} collective-permute-done((bf16[4,128,512]{2,1,0:T(8,128)(2,1)S(1)}, bf16[4,128,512]{2,1,0:T(8,128)(2,1)}, u32[]{:S(2)}, u32[]{:S(2)}) %collective-permute-start.25) | collective-permute-done | bytes 524320 | tf_op jit(solution)/shard_map/ppermute | solution.py:67
  141.6 3.4 %copy-done = bf16[8192,512]{1,0:T(8,128)(2,1)S(1)} copy-done((bf16[8192,512]{1,0:T(8,128)(2,1)S(1)}, bf16[8192,512]{1,0:T(8,128)(2,1)}, u32[]{:S(2)}) %copy-start) | copy-done | bytes 8388632
  145.7 1.2 project_own.1
  146.9 3.4 %copy-done.1 = bf16[8192,512]{1,0:T(8,128)(2,1)S(1)} copy-done((bf16[8192,512]{1,0:T(8,128)(2,1)S(1)}, bf16[8192,512]{1,0:T(8,128)(2,1)}, u32[]{:S(2)}) %copy-start.1) | copy-done | bytes 8388632
  150.4 2.5 %project_near.1 = (f32[128,512]{1,0:T(8,128)S(1)}, f32[128,128]{1,0:T(8,128)S(1)}, f32[128,1]{1,0:T(8,128)S(1)}) custom-call(s32[38]{0:T(128)S(1)} %copy-done.14, bf16[4,128,512]{2,1,0:T(8,128)(2,1)} %collective-permute-done.25.refs_1_, bf16[4,128,512]{2,1,0:T(8,128)(2,1)} %collective-permute-done.27.refs_2_, f32[16,1,512]{2,1,0:T(1,128)S(1)} %bitcast.25, ...), custom_call_target="tpu_custom_call" | custom-call | flops 671088640 | bytes 11895296 | tf_op jit(solution)/shard_map/project_near/pallas_call | solution.py:101
  152.9 1.2 last_keys.1
  154.5 1.3 last_queries.1.refs_1_
  155.8 2.8 %collective-permute-done.28.refs_3_ = bf16[2,128,64]{2,1,0:T(8,128)(2,1)S(1)} collective-permute-done((bf16[2,128,64]{2,1,0:T(8,128)(2,1)S(1)}, bf16[2,128,64]{2,1,0:T(8,128)(2,1)S(1)}, u32[]{:S(2)}, u32[]{:S(2)}) %collective-permute-start.28) | collective-permute-done | bytes 32800 | tf_op jit(solution)/shard_map/ppermute | solution.py:758
  158.6 3.6 %attend_out.1 = (bf16[32,8192]{1,0:T(8,128)(2,1)S(1)}, bf16[32,8192]{1,0:T(8,128)(2,1)}, bf16[32,8192]{1,0:T(8,128)(2,1)}, bf16[32,8192]{1,0:T(8,128)(2,1)}) custom-call(s32[38]{0:T(128)S(1)} %copy-done.14, bf16[128,512]{1,0:T(8,128)(2,1)S(1)} %last_queries.1.refs_1_, bf16[2,128,64]{2,1,0:T(8,128)(2,1)S(1)} %get-tuple-element.52.refs_2_, ...), custom_call_target="tpu_custom_call" | custom-call | flops 1073741824 | bytes 8683520 | tf_op jit(solution)/shard_map/attend_out/pallas_call | solution.py:101
  162.3 3.2 %collective-permute-start.30 = (bf16[32,8192]{1,0:T(8,128)(2,1)}, bf16[32,8192]{1,0:T(8,128)(2,1)S(1)}, u32[]{:S(2)}, u32[]{:S(2)}) collective-permute-start(bf16[32,8192]{1,0:T(8,128)(2,1)} %get-tuple-element.55), channel_id=1, source_target_pairs={{0,12},{1,13},{2,14},{3,15},{4,0},{5,1},{6,2},{7,3},{8,4},{9,5},{1... | collective-permute-start | bytes 1572872 | tf_op jit(solution)/shard_map/ppermute | solution.py:67
  165.5 1.5 collective-permute-start.31
  167.8 5.0 %collective-permute-done.29.refs_2_ = bf16[32,8192]{1,0:T(8,128)(2,1)S(1)} collective-permute-done((bf16[32,8192]{1,0:T(8,128)(2,1)}, bf16[32,8192]{1,0:T(8,128)(2,1)S(1)}, u32[]{:S(2)}, u32[]{:S(2)}) %collective-permute-start.29) | collective-permute-done | bytes 524320 | tf_op jit(solution)/shard_map/ppermute | solution.py:67
  172.9 5.3 %collective-permute-done.30.refs_3_ = bf16[32,8192]{1,0:T(8,128)(2,1)S(1)} collective-permute-done((bf16[32,8192]{1,0:T(8,128)(2,1)}, bf16[32,8192]{1,0:T(8,128)(2,1)S(1)}, u32[]{:S(2)}, u32[]{:S(2)}) %collective-permute-start.30) | collective-permute-done | bytes 524320 | tf_op jit(solution)/shard_map/ppermute | solution.py:67
  178.1 2.3 %collective-permute-done.31.refs_4_ = bf16[32,8192]{1,0:T(8,128)(2,1)S(1)} collective-permute-done((bf16[32,8192]{1,0:T(8,128)(2,1)}, bf16[32,8192]{1,0:T(8,128)(2,1)S(1)}, u32[]{:S(2)}, u32[]{:S(2)}) %collective-permute-start.31) | collective-permute-done | bytes 524320 | tf_op jit(solution)/shard_map/ppermute | solution.py:67
  181.3 3.2 %collective-permute-start.33 = (bf16[8,8192]{1,0:T(8,128)(2,1)S(1)}, bf16[8,8192]{1,0:T(8,128)(2,1)S(1)}, u32[]{:S(2)}, u32[]{:S(2)}) collective-permute-start(bf16[8,8192]{1,0:T(8,128)(2,1)S(1)} %get-tuple-element.59), channel_id=1, source_target_pairs={{0,3},{1,0},{2,1},{3,2},{4,7},{5,4},{6,5},{7,6},{8,11},{9,8},{10,9... | collective-permute-start | bytes 393224 | tf_op jit(solution)/shard_map/ppermute | solution.py:67
  185.3 2.2 %collective-permute-done.32.refs_2_ = bf16[8,8192]{1,0:T(8,128)(2,1)S(1)} collective-permute-done((bf16[8,8192]{1,0:T(8,128)(2,1)S(1)}, bf16[8,8192]{1,0:T(8,128)(2,1)S(1)}, u32[]{:S(2)}, u32[]{:S(2)}) %collective-permute-start.32) | collective-permute-done | bytes 131104 | tf_op jit(solution)/shard_map/ppermute | solution.py:67
  187.5 1.0 collective-permute-done.33.refs_3_
  188.5 2.5 %collective-permute-done.34.refs_4_ = bf16[8,8192]{1,0:T(8,128)(2,1)S(1)} collective-permute-done((bf16[8,8192]{1,0:T(8,128)(2,1)S(1)}, bf16[8,8192]{1,0:T(8,128)(2,1)S(1)}, u32[]{:S(2)}, u32[]{:S(2)}) %collective-permute-start.34) | collective-permute-done | bytes 131104 | tf_op jit(solution)/shard_map/ppermute | solution.py:67
  191.0 1.3 finish.1
  (147 shorter events, 25.1 us)
Async XLA Ops:
  1.8 34.2 %copy-start.21 = (s32[16]{0:T(128)}, s32[16]{0:T(128)S(1)}, u32[]{:S(2)}) copy-start(s32[16]{0:T(128)S(1)} %broadcast_select_fusion.2) | copy-start | bytes 196
  1.9 1.0 copy-start.10
  2.9 14.6 %copy-start.12 = (s32[38]{0:T(128)}, s32[38]{0:T(128)S(1)}, u32[]{:S(2)}) copy-start(s32[38]{0:T(128)S(1)} %concatenate.9.refs_0_) | copy-start | bytes 460
  3.5 14.0 %copy-start.8 = (bf16[64,1536]{1,0:T(8,128)(2,1)}, bf16[64,1536]{1,0:T(8,128)(2,1)S(1)}, u32[]{:S(2)}) copy-start(bf16[64,1536]{1,0:T(8,128)(2,1)S(1)} %take_qkv.1.refs_1_.refs_5_) | copy-start | bytes 589828
  3.5 6.9 %collective-permute-start.1 = (bf16[64,1536]{1,0:T(8,128)(2,1)S(1)}, bf16[64,1536]{1,0:T(8,128)(2,1)S(1)}, u32[]{:S(2)}, u32[]{:S(2)}) collective-permute-start(bf16[64,1536]{1,0:T(8,128)(2,1)S(1)} %take_qkv.1.refs_1_.refs_5_), channel_id=1, source_target_pairs={{0,1},{1,2},{2,3},{3,0},{4,5},{5,6},{6,7},{7,4},{8,9},{9,10},{10,1... | collective-permute-start | bytes 589832 | tf_op jit(solution)/shard_map/ppermute | solution.py:67
  5.2 5.7 %collective-permute-start.2 = (bf16[64,1536]{1,0:T(8,128)(2,1)S(1)}, bf16[64,1536]{1,0:T(8,128)(2,1)S(1)}, u32[]{:S(2)}, u32[]{:S(2)}) collective-permute-start(bf16[64,1536]{1,0:T(8,128)(2,1)S(1)} %take_qkv.1.refs_1_.refs_5_), channel_id=1, source_target_pairs={{0,3},{1,0},{2,1},{3,2},{4,7},{5,4},{6,5},{7,6},{8,11},{9,8},{10,9... | collective-permute-start | bytes 589832 | tf_op jit(solution)/shard_map/ppermute | solution.py:67
  6.8 7.2 %collective-permute-start.3 = (bf16[64,1536]{1,0:T(8,128)(2,1)S(1)}, bf16[64,1536]{1,0:T(8,128)(2,1)S(1)}, u32[]{:S(2)}, u32[]{:S(2)}) collective-permute-start(bf16[64,1536]{1,0:T(8,128)(2,1)S(1)} %take_qkv.1.refs_1_.refs_5_), channel_id=1, source_target_pairs={{0,2},{1,3},{2,0},{3,1},{4,6},{5,7},{6,4},{7,5},{8,10},{9,11},{10,... | collective-permute-start | bytes 589832 | tf_op jit(solution)/shard_map/ppermute | solution.py:67
  14.6 32.0 %copy-start.3 = (bf16[4,64,1536]{2,1,0:T(8,128)(2,1)}, bf16[4,64,1536]{2,1,0:T(8,128)(2,1)S(1)}, u32[]{:S(2)}) copy-start(bf16[4,64,1536]{2,1,0:T(8,128)(2,1)S(1)} %join_qkv.1.refs_2_) | copy-start | bytes 2359300
  14.6 42.9 %copy-start.23 = (s32[1024]{0:T(1024)S(1)}, s32[1024]{0:T(1024)}, u32[]{:S(2)}) copy-start(s32[1024]{0:T(1024)} %param.18) | copy-start | bytes 12292
  14.6 45.6 %copy-start.24 = (s32[8]{0:T(128)S(1)}, s32[8]{0:T(128)}, u32[]{:S(2)}) copy-start(s32[8]{0:T(128)} %param.20) | copy-start | bytes 100
  14.6 20.5 %collective-permute-start.5 = (bf16[4,64,1536]{2,1,0:T(8,128)(2,1)S(1)}, bf16[4,64,1536]{2,1,0:T(8,128)(2,1)}, u32[]{:S(2)}, u32[]{:S(2)}) collective-permute-start(bf16[4,64,1536]{2,1,0:T(8,128)(2,1)S(1)} %join_qkv.1.refs_2_), channel_id=1, source_target_pairs={{0,12},{1,13},{2,14},{3,15},{4,0},{5,1},{6,2},{7,3},{8,4},{9,5},{1... | collective-permute-start | bytes 2359304 | tf_op jit(solution)/shard_map/ppermute | solution.py:67
  20.2 34.5 %copy-start.7 = (bf16[64,3584]{1,0:T(8,128)(2,1)S(1)}, bf16[64,3584]{1,0:T(8,128)(2,1)}, u32[]{:S(2)}) copy-start(bf16[64,3584]{1,0:T(8,128)(2,1)} %get-tuple-element.33.refs_1_) | copy-start | bytes 1376260
  20.2 14.9 %collective-permute-start.8 = (bf16[64,3584]{1,0:T(8,128)(2,1)}, bf16[64,3584]{1,0:T(8,128)(2,1)S(1)}, u32[]{:S(2)}, u32[]{:S(2)}) collective-permute-start(bf16[64,3584]{1,0:T(8,128)(2,1)} %get-tuple-element.33.refs_1_), channel_id=1, source_target_pairs={{0,1},{1,2},{2,3},{3,0},{4,5},{5,6},{6,7},{7,4},{8,9},{9,10},{10,1... | collective-permute-start | bytes 1376264 | tf_op jit(solution)/shard_map/ppermute | solution.py:67
  21.5 23.3 %collective-permute-start.4 = (bf16[4,64,1536]{2,1,0:T(8,128)(2,1)S(1)}, bf16[4,64,1536]{2,1,0:T(8,128)(2,1)S(1)}, u32[]{:S(2)}, u32[]{:S(2)}) collective-permute-start(bf16[4,64,1536]{2,1,0:T(8,128)(2,1)S(1)} %join_qkv.1.refs_2_), channel_id=1, source_target_pairs={{0,4},{1,5},{2,6},{3,7},{4,8},{5,9},{6,10},{7,11},{8,12},{9,13},{1... | collective-permute-start | bytes 2359304 | tf_op jit(solution)/shard_map/ppermute | solution.py:67
  21.5 18.7 %collective-permute-start.9 = (bf16[64,3584]{1,0:T(8,128)(2,1)}, bf16[64,3584]{1,0:T(8,128)(2,1)S(1)}, u32[]{:S(2)}, u32[]{:S(2)}) collective-permute-start(bf16[64,3584]{1,0:T(8,128)(2,1)} %get-tuple-element.34), channel_id=1, source_target_pairs={{0,3},{1,0},{2,1},{3,2},{4,7},{5,4},{6,5},{7,6},{8,11},{9,8},{10,9... | collective-permute-start | bytes 1376264 | tf_op jit(solution)/shard_map/ppermute | solution.py:67
  35.1 9.7 %collective-permute-start.10 = (bf16[64,3584]{1,0:T(8,128)(2,1)S(1)}, bf16[64,3584]{1,0:T(8,128)(2,1)S(1)}, u32[]{:S(2)}, u32[]{:S(2)}) collective-permute-start(bf16[64,3584]{1,0:T(8,128)(2,1)S(1)} %collective-permute-done.8.refs_2_), channel_id=1, source_target_pairs={{0,1},{1,2},{2,3},{3,0},{4,5},{5,6},{6,7},{7,4},{8,9},{9,10},{10,1... | collective-permute-start | bytes 1376264 | tf_op jit(solution)/shard_map/ppermute | solution.py:67
  35.1 13.6 %collective-permute-start.6 = (bf16[4,64,1536]{2,1,0:T(8,128)(2,1)}, bf16[4,64,1536]{2,1,0:T(8,128)(2,1)S(1)}, u32[]{:S(2)}, u32[]{:S(2)}) collective-permute-start(bf16[4,64,1536]{2,1,0:T(8,128)(2,1)} %collective-permute-done.5.refs_4_.refs_6_), channel_id=1, source_target_pairs={{0,12},{1,13},{2,14},{3,15},{4,0},{5,1},{6,2},{7,3},{8,4},{9,5},{1... | collective-permute-start | bytes 2359304 | tf_op jit(solution)/shard_map/ppermute | solution.py:67
  36.0 1.7 collective-permute-start
  37.7 1.0 copy-start.11
  39.3 15.5 %copy-start.14 = (s32[38]{0:T(128)S(1)}, s32[38]{0:T(128)}, u32[]{:S(2)}) copy-start(s32[38]{0:T(128)} %copy-done.12) | copy-start | bytes 460
  39.3 15.5 %copy-start.18 = (bf16[64,1024]{1,0:T(8,128)(2,1)S(1)}, bf16[64,1024]{1,0:T(8,128)(2,1)}, u32[]{:S(2)}) copy-start(bf16[64,1024]{1,0:T(8,128)(2,1)} %get-tuple-element.37.refs_5_) | copy-start | bytes 393220
  44.8 1.0 copy-start.6
  46.4 13.8 %collective-permute-start.11 = (bf16[4,64,1536]{2,1,0:T(8,128)(2,1)S(1)}, bf16[4,64,1536]{2,1,0:T(8,128)(2,1)}, u32[]{:S(2)}, u32[]{:S(2)}) collective-permute-start(bf16[4,64,1536]{2,1,0:T(8,128)(2,1)S(1)} %join_middle.1.refs_4_.refs_3_), channel_id=1, source_target_pairs={{0,4},{1,5},{2,6},{3,7},{4,8},{5,9},{6,10},{7,11},{8,12},{9,13},{1... | collective-permute-start | bytes 2359304 | tf_op jit(solution)/shard_map/ppermute | solution.py:67
  46.5 8.2 %collective-permute-start.15 = (bf16[64,1024]{1,0:T(8,128)(2,1)}, bf16[64,1024]{1,0:T(8,128)(2,1)S(1)}, u32[]{:S(2)}, u32[]{:S(2)}) collective-permute-start(bf16[64,1024]{1,0:T(8,128)(2,1)} %get-tuple-element.38), channel_id=1, source_target_pairs={{0,2},{1,3},{2,0},{3,1},{4,6},{5,7},{6,4},{7,5},{8,10},{9,11},{10,... | collective-permute-start | bytes 393224 | tf_op jit(solution)/shard_map/ppermute | solution.py:67
  48.7 1.1 copy-start.4
  56.2 0.6 copy-start.16
  56.9 3.3 %copy-start.19 = (bf16[4,64,1280]{2,1,0:T(8,128)(2,1)}, bf16[4,64,1280]{2,1,0:T(8,128)(2,1)S(1)}, u32[]{:S(2)}) copy-start(bf16[4,64,1280]{2,1,0:T(8,128)(2,1)S(1)} %get-tuple-element.40) | copy-start | bytes 1966084
  56.9 5.5 %copy-start.20 = (bf16[4,64,256]{2,1,0:T(8,128)(2,1)}, bf16[4,64,256]{2,1,0:T(8,128)(2,1)S(1)}, u32[]{:S(2)}) copy-start(bf16[4,64,256]{2,1,0:T(8,128)(2,1)S(1)} %get-tuple-element.41) | copy-start | bytes 393220
  56.9 12.0 %collective-permute-start.16 = (bf16[4,64,1280]{2,1,0:T(8,128)(2,1)}, bf16[4,64,1280]{2,1,0:T(8,128)(2,1)S(1)}, u32[]{:S(2)}, u32[]{:S(2)}) collective-permute-start(bf16[4,64,1280]{2,1,0:T(8,128)(2,1)} %get-tuple-element.39.refs_3_), channel_id=1, source_target_pairs={{0,4},{1,5},{2,6},{3,7},{4,8},{5,9},{6,10},{7,11},{8,12},{9,13},{1... | collective-permute-start | bytes 1966088 | tf_op jit(solution)/shard_map/ppermute | solution.py:67
  57.5 19.2 %collective-permute-start.12 = (bf16[4,64,1536]{2,1,0:T(8,128)(2,1)S(1)}, bf16[4,64,1536]{2,1,0:T(8,128)(2,1)}, u32[]{:S(2)}, u32[]{:S(2)}) collective-permute-start(bf16[4,64,1536]{2,1,0:T(8,128)(2,1)S(1)} %join_middle.1.refs_4_.refs_3_), channel_id=1, source_target_pairs={{0,12},{1,13},{2,14},{3,15},{4,0},{5,1},{6,2},{7,3},{8,4},{9,5},{1... | collective-permute-start | bytes 2359304 | tf_op jit(solution)/shard_map/ppermute | solution.py:67
  60.2 17.2 %collective-permute-start.13 = (bf16[4,64,1536]{2,1,0:T(8,128)(2,1)}, bf16[4,64,1536]{2,1,0:T(8,128)(2,1)}, u32[]{:S(2)}, u32[]{:S(2)}) collective-permute-start(bf16[4,64,1536]{2,1,0:T(8,128)(2,1)} %collective-permute-done.11.refs_5_.refs_4_), channel_id=1, source_target_pairs={{0,4},{1,5},{2,6},{3,7},{4,8},{5,9},{6,10},{7,11},{8,12},{9,13},{1... | collective-permute-start | bytes 2359304 | tf_op jit(solution)/shard_map/ppermute | solution.py:67
  62.4 14.3 %collective-permute-start.7 = (bf16[8,256,64]{2,1,0:T(8,128)(2,1)S(1)}, bf16[8,256,64]{2,1,0:T(8,128)(2,1)S(1)}, u32[]{:S(2)}, u32[]{:S(2)}) collective-permute-start(bf16[8,256,64]{2,1,0:T(8,128)(2,1)S(1)} %span_attention.1.refs_1_.refs_7_), channel_id=1, source_target_pairs={{0,16},{16,0},{32,48},{48,32},{64,80},{80,64},{96,112},{112,96},{1... | collective-permute-start | bytes 786440 | tf_op jit(solution)/shard_map/ppermute | solution.py:71
  62.4 26.7 %collective-permute-start.17 = (bf16[4,64,1280]{2,1,0:T(8,128)(2,1)}, bf16[4,64,1280]{2,1,0:T(8,128)(2,1)}, u32[]{:S(2)}, u32[]{:S(2)}) collective-permute-start(bf16[4,64,1280]{2,1,0:T(8,128)(2,1)} %copy-done.19), channel_id=1, source_target_pairs={{0,12},{1,13},{2,14},{3,15},{4,0},{5,1},{6,2},{7,3},{8,4},{9,5},{1... | collective-permute-start | bytes 1966088 | tf_op jit(solution)/shard_map/ppermute | solution.py:67
  68.9 20.2 %collective-permute-start.18 = (bf16[4,64,1280]{2,1,0:T(8,128)(2,1)S(1)}, bf16[4,64,1280]{2,1,0:T(8,128)(2,1)}, u32[]{:S(2)}, u32[]{:S(2)}) collective-permute-start(bf16[4,64,1280]{2,1,0:T(8,128)(2,1)S(1)} %collective-permute-done.16.refs_4_.refs_2_), channel_id=1, source_target_pairs={{0,4},{1,5},{2,6},{3,7},{4,8},{5,9},{6,10},{7,11},{8,12},{9,13},{1... | collective-permute-start | bytes 1966088 | tf_op jit(solution)/shard_map/ppermute | solution.py:67
  80.5 4.9 %collective-permute-start.14 = (bf16[256,512]{1,0:T(8,128)(2,1)}, bf16[256,512]{1,0:T(8,128)(2,1)}, u32[]{:S(2)}, u32[]{:S(2)}) collective-permute-start(bf16[256,512]{1,0:T(8,128)(2,1)} %context_out.1.refs_1_), channel_id=1, source_target_pairs={{0,16},{16,0},{32,48},{48,32},{64,80},{80,64},{96,112},{112,96},{1... | collective-permute-start | bytes 786440 | tf_op jit(solution)/shard_map/ppermute | solution.py:71
  81.1 13.6 %copy-start.17 = (bf16[4,64,256]{2,1,0:T(8,128)(2,1)S(1)}, bf16[4,64,256]{2,1,0:T(8,128)(2,1)}, u32[]{:S(2)}) copy-start(bf16[4,64,256]{2,1,0:T(8,128)(2,1)} %copy-done.16) | copy-start | bytes 393220
  82.1 7.0 %collective-permute-start.19 = (bf16[4,64,256]{2,1,0:T(8,128)(2,1)}, bf16[4,64,256]{2,1,0:T(8,128)(2,1)S(1)}, u32[]{:S(2)}, u32[]{:S(2)}) collective-permute-start(bf16[4,64,256]{2,1,0:T(8,128)(2,1)} %copy-done.20), channel_id=1, source_target_pairs={{0,8},{1,9},{2,10},{3,11},{4,12},{5,13},{6,14},{7,15},{8,0},{9,1},... | collective-permute-start | bytes 393224 | tf_op jit(solution)/shard_map/ppermute | solution.py:67
  85.4 56.2 %copy-start.2 = (bf16[2,8192,64]{1,2,0:T(8,128)(2,1)S(1)}, bf16[2,8192,64]{1,2,0:T(8,128)(2,1)}, u32[]{:S(2)}) copy-start(bf16[2,8192,64]{1,2,0:T(8,128)(2,1)} %param.30) | copy-start | bytes 6291460
  91.4 1.6 collective-permute-start.20
  95.9 20.2 %collective-permute-start.21 = (bf16[4,4,64,256]{3,2,1,0:T(8,128)(2,1)S(1)}, bf16[4,4,64,256]{3,2,1,0:T(8,128)(2,1)S(1)}, u32[]{:S(2)}, u32[]{:S(2)}) collective-permute-start(bf16[4,4,64,256]{3,2,1,0:T(8,128)(2,1)S(1)} %join_proj.1.refs_4_), channel_id=1, source_target_pairs={{0,16},{16,0},{32,48},{48,32},{64,80},{80,64},{96,112},{112,96},{1... | collective-permute-start | bytes 1572872 | tf_op jit(solution)/shard_map/ppermute | solution.py:71
  96.2 19.9 %all-to-all-start = ((bf16[128,8,128]{2,1,0:T(8,128)(2,1)}), bf16[128,8,128]{2,1,0:T(8,128)(2,1)S(1)}, u32[]{:S(2)}, u32[]{:S(2)}) async-start(bf16[128,8,128]{2,1,0:T(8,128)(2,1)} %bitcast.8), calls=%async_computation | async-start | bytes 524288 | tf_op jit(solution)/shard_map/all_to_all | solution.py:676
  116.0 1.6 copy-start.5
  117.6 0.8 copy-start.15
  120.4 6.2 %collective-permute-start.22 = (bf16[128,512]{1,0:T(8,128)(2,1)S(1)}, bf16[128,512]{1,0:T(8,128)(2,1)S(1)}, u32[]{:S(2)}, u32[]{:S(2)}) collective-permute-start(bf16[128,512]{1,0:T(8,128)(2,1)S(1)} %embed.1.refs_1_), channel_id=1, source_target_pairs={{0,1},{1,2},{2,3},{3,0},{4,5},{5,6},{6,7},{7,4},{8,9},{9,10},{10,1... | collective-permute-start | bytes 393224 | tf_op jit(solution)/shard_map/ppermute | solution.py:67
  121.2 6.5 %collective-permute-start.23 = (bf16[128,512]{1,0:T(8,128)(2,1)S(1)}, bf16[128,512]{1,0:T(8,128)(2,1)S(1)}, u32[]{:S(2)}, u32[]{:S(2)}) collective-permute-start(bf16[128,512]{1,0:T(8,128)(2,1)S(1)} %embed.1.refs_1_), channel_id=1, source_target_pairs={{0,3},{1,0},{2,1},{3,2},{4,7},{5,4},{6,5},{7,6},{8,11},{9,8},{10,9... | collective-permute-start | bytes 393224 | tf_op jit(solution)/shard_map/ppermute | solution.py:67
  123.7 6.5 %collective-permute-start.24 = (bf16[128,512]{1,0:T(8,128)(2,1)S(1)}, bf16[128,512]{1,0:T(8,128)(2,1)S(1)}, u32[]{:S(2)}, u32[]{:S(2)}) collective-permute-start(bf16[128,512]{1,0:T(8,128)(2,1)S(1)} %embed.1.refs_1_), channel_id=1, source_target_pairs={{0,2},{1,3},{2,0},{3,1},{4,6},{5,7},{6,4},{7,5},{8,10},{9,11},{10,... | collective-permute-start | bytes 393224 | tf_op jit(solution)/shard_map/ppermute | solution.py:67
  130.8 10.6 %collective-permute-start.25 = (bf16[4,128,512]{2,1,0:T(8,128)(2,1)S(1)}, bf16[4,128,512]{2,1,0:T(8,128)(2,1)}, u32[]{:S(2)}, u32[]{:S(2)}) collective-permute-start(bf16[4,128,512]{2,1,0:T(8,128)(2,1)S(1)} %join_columns.1.refs_1_), channel_id=1, source_target_pairs={{0,4},{1,5},{2,6},{3,7},{4,8},{5,9},{6,10},{7,11},{8,12},{9,13},{1... | collective-permute-start | bytes 1572872 | tf_op jit(solution)/shard_map/ppermute | solution.py:67
  132.4 14.5 %collective-permute-start.27 = (bf16[4,128,512]{2,1,0:T(8,128)(2,1)S(1)}, bf16[4,128,512]{2,1,0:T(8,128)(2,1)}, u32[]{:S(2)}, u32[]{:S(2)}) collective-permute-start(bf16[4,128,512]{2,1,0:T(8,128)(2,1)S(1)} %join_columns.1.refs_1_), channel_id=1, source_target_pairs={{0,12},{1,13},{2,14},{3,15},{4,0},{5,1},{6,2},{7,3},{8,4},{9,5},{1... | collective-permute-start | bytes 1572872 | tf_op jit(solution)/shard_map/ppermute | solution.py:67
  141.4 11.5 %collective-permute-start.26 = (bf16[4,128,512]{2,1,0:T(8,128)(2,1)}, bf16[4,128,512]{2,1,0:T(8,128)(2,1)S(1)}, u32[]{:S(2)}, u32[]{:S(2)}) collective-permute-start(bf16[4,128,512]{2,1,0:T(8,128)(2,1)} %collective-permute-done.25.refs_1_), channel_id=1, source_target_pairs={{0,4},{1,5},{2,6},{3,7},{4,8},{5,9},{6,10},{7,11},{8,12},{9,13},{1... | collective-permute-start | bytes 1572872 | tf_op jit(solution)/shard_map/ppermute | solution.py:67
  141.6 3.4 %copy-start = (bf16[8192,512]{1,0:T(8,128)(2,1)S(1)}, bf16[8192,512]{1,0:T(8,128)(2,1)}, u32[]{:S(2)}) copy-start(bf16[8192,512]{1,0:T(8,128)(2,1)} %refs_3_.7) | copy-start | bytes 25165828
  145.0 0.8 copy-start.9
  145.7 8.7 %slice-start = ((s8[8388608]{0:T(1024)(128)(4,1)}), s8[4194304]{0:T(1024)(128)(4,1)S(1)}, s32[]{:S(2)}) async-start(s8[8388608]{0:T(1024)(128)(4,1)} %bitcast.17), calls=%async_computation.1 | async-start | bytes 8388608
  146.9 3.4 %copy-start.1 = (bf16[8192,512]{1,0:T(8,128)(2,1)S(1)}, bf16[8192,512]{1,0:T(8,128)(2,1)}, u32[]{:S(2)}) copy-start(bf16[8192,512]{1,0:T(8,128)(2,1)} %refs_3_.7) | copy-start | bytes 25165828
  150.4 4.1 %slice-start.1 = ((s8[8388608]{0:T(1024)(128)(4,1)}), s8[4194304]{0:T(1024)(128)(4,1)S(1)}, s32[]{:S(2)}) async-start(s8[8388608]{0:T(1024)(128)(4,1)} %bitcast.17), calls=%async_computation.2 | async-start | bytes 8388608
  150.4 8.3 %slice-start.2 = ((s8[8388608]{0:T(1024)(128)(4,1)}), s8[4194304]{0:T(1024)(128)(4,1)S(1)}, s32[]{:S(2)}) async-start(s8[8388608]{0:T(1024)(128)(4,1)} %bitcast.22), calls=%async_computation.3 | async-start | bytes 8388608
  152.9 5.8 %slice-start.3 = ((s8[8388608]{0:T(1024)(128)(4,1)}), s8[4194304]{0:T(1024)(128)(4,1)S(1)}, s32[]{:S(2)}) async-start(s8[8388608]{0:T(1024)(128)(4,1)} %bitcast.22), calls=%async_computation.4 | async-start | bytes 8388608
  154.1 4.6 %collective-permute-start.28 = (bf16[2,128,64]{2,1,0:T(8,128)(2,1)S(1)}, bf16[2,128,64]{2,1,0:T(8,128)(2,1)S(1)}, u32[]{:S(2)}, u32[]{:S(2)}) collective-permute-start(bf16[2,128,64]{2,1,0:T(8,128)(2,1)S(1)} %get-tuple-element.52.refs_2_), channel_id=1, source_target_pairs={{0,1},{1,0},{2,3},{3,2},{4,5},{5,4},{6,7},{7,6},{8,9},{9,8},{10,11... | collective-permute-start | bytes 98312 | tf_op jit(solution)/shard_map/ppermute | solution.py:758
  154.5 12.5 %copy-start.22 = (s32[16]{0:T(128)S(1)}, s32[16]{0:T(128)}, u32[]{:S(2)}) copy-start(s32[16]{0:T(128)} %copy-done.21) | copy-start | bytes 196
  162.3 10.6 %collective-permute-start.29 = (bf16[32,8192]{1,0:T(8,128)(2,1)}, bf16[32,8192]{1,0:T(8,128)(2,1)S(1)}, u32[]{:S(2)}, u32[]{:S(2)}) collective-permute-start(bf16[32,8192]{1,0:T(8,128)(2,1)} %get-tuple-element.54), channel_id=1, source_target_pairs={{0,4},{1,5},{2,6},{3,7},{4,8},{5,9},{6,10},{7,11},{8,12},{9,13},{1... | collective-permute-start | bytes 1572872 | tf_op jit(solution)/shard_map/ppermute | solution.py:67
  162.3 15.9 %collective-permute-start.30 = (bf16[32,8192]{1,0:T(8,128)(2,1)}, bf16[32,8192]{1,0:T(8,128)(2,1)S(1)}, u32[]{:S(2)}, u32[]{:S(2)}) collective-permute-start(bf16[32,8192]{1,0:T(8,128)(2,1)} %get-tuple-element.55), channel_id=1, source_target_pairs={{0,12},{1,13},{2,14},{3,15},{4,0},{5,1},{6,2},{7,3},{8,4},{9,5},{1... | collective-permute-start | bytes 1572872 | tf_op jit(solution)/shard_map/ppermute | solution.py:67
  165.5 14.9 %collective-permute-start.31 = (bf16[32,8192]{1,0:T(8,128)(2,1)}, bf16[32,8192]{1,0:T(8,128)(2,1)S(1)}, u32[]{:S(2)}, u32[]{:S(2)}) collective-permute-start(bf16[32,8192]{1,0:T(8,128)(2,1)} %get-tuple-element.56), channel_id=1, source_target_pairs={{0,8},{1,9},{2,10},{3,11},{4,12},{5,13},{6,14},{7,15},{8,0},{9,1},... | collective-permute-start | bytes 1572872 | tf_op jit(solution)/shard_map/ppermute | solution.py:67
  181.3 6.2 %collective-permute-start.32 = (bf16[8,8192]{1,0:T(8,128)(2,1)S(1)}, bf16[8,8192]{1,0:T(8,128)(2,1)S(1)}, u32[]{:S(2)}, u32[]{:S(2)}) collective-permute-start(bf16[8,8192]{1,0:T(8,128)(2,1)S(1)} %get-tuple-element.58), channel_id=1, source_target_pairs={{0,1},{1,2},{2,3},{3,0},{4,5},{5,6},{6,7},{7,4},{8,9},{9,10},{10,1... | collective-permute-start | bytes 393224 | tf_op jit(solution)/shard_map/ppermute | solution.py:67
  181.3 7.1 %collective-permute-start.33 = (bf16[8,8192]{1,0:T(8,128)(2,1)S(1)}, bf16[8,8192]{1,0:T(8,128)(2,1)S(1)}, u32[]{:S(2)}, u32[]{:S(2)}) collective-permute-start(bf16[8,8192]{1,0:T(8,128)(2,1)S(1)} %get-tuple-element.59), channel_id=1, source_target_pairs={{0,3},{1,0},{2,1},{3,2},{4,7},{5,4},{6,5},{7,6},{8,11},{9,8},{10,9... | collective-permute-start | bytes 393224 | tf_op jit(solution)/shard_map/ppermute | solution.py:67
  184.6 6.5 %collective-permute-start.34 = (bf16[8,8192]{1,0:T(8,128)(2,1)S(1)}, bf16[8,8192]{1,0:T(8,128)(2,1)S(1)}, u32[]{:S(2)}, u32[]{:S(2)}) collective-permute-start(bf16[8,8192]{1,0:T(8,128)(2,1)S(1)} %get-tuple-element.60), channel_id=1, source_target_pairs={{0,2},{1,3},{2,0},{3,1},{4,6},{5,7},{6,4},{7,5},{8,10},{9,11},{10,... | collective-permute-start | bytes 393224 | tf_op jit(solution)/shard_map/ppermute | solution.py:67
  (1 other events, 0.6 us)

commit v11 on v6

--- a/solution.py
+++ b/solution.py
@@ -410,7 +410,7 @@
 
 
 def attend_out(info, query, mine, partner, allowed, deal, weight, *refs):
-    outs, context = refs[:4], refs[4]
+    outs, context = refs[:5], refs[5]
     odd = info[17] == 1
     own = mine[...].astype(jnp.float32)
     far = partner[...].astype(jnp.float32)
@@ -435,19 +435,26 @@
     step = weight.shape[1] // 8
     for start in range(0, weight.shape[1], step):
         result = dot32(dealt, weight[:, start : start + step])
-        for index, out in enumerate(outs):
-            piece = result[index * rows : (index + 1) * rows]
-            out[:, start : start + step] = piece.astype(jnp.bfloat16)
-
-
-def add_ring(info, own, left, right, opposite, kept, *sent):
+        for index in range(SIDE):
+            piece = result[index * rows : (index + 1) * rows].astype(jnp.bfloat16)
+            out, at = outs[index], start
+            if index == 3 and start >= out.shape[1]:
+                out, at = outs[4], start - out.shape[1]
+            out[:, at : at + step] = piece
+
+
+def add_ring(info, own, left, right, far_low, far_high, kept, *sent):
     rows = kept.shape[0]
     step = 1024
     for start in range(0, own.shape[1], step):
         lanes = slice(start, start + step)
         total = own[:, lanes].astype(jnp.float32)
-        for block in (left, right, opposite):
+        for block in (left, right):
             total = total + block[:, lanes].astype(jnp.float32)
+        far, at = (far_low, start)
+        if start >= far_low.shape[1]:
+            far, at = far_high, start - far_low.shape[1]
+        total = total + far[:, at : at + step].astype(jnp.float32)
         kept[:, lanes] = total[:rows]
         for index, out in enumerate(sent):
             piece = total[(index + 1) * rows : (index + 2) * rows]
@@ -770,13 +777,15 @@
         "attend_out",
         info,
         [query, own_kv, partner_kv, allowed, deal, out_weight],
-        (shape_of((rows // SIDE, model_width)),) * 4,
+        (shape_of((rows // SIDE, model_width)),) * 3
+        + (shape_of((rows // SIDE, model_width // 2)),) * 2,
         [pltpu.VMEM((rows, query_cols), jnp.bfloat16)],
         flops=2 * rows * model_width * query_cols,
     )
+    passing = to_ring(partial[4], 2, -1)
     arrived_sums = [
-        to_ring(part, 2, distance) for part, distance in zip(partial[1:], (1, -1, 2))
-    ]
+        to_ring(part, 2, distance) for part, distance in zip(partial[1:4], (1, -1, 2))
+    ] + [to_ring(passing, 2, -1)]
     kept_sum, *sent_sums = whole_call(
         add_ring,
         "add_ring",

time: 193 us -> 197 us (1.021)
  starting transfers between devices: 43.5 us -> 47.9 us
    ppermute x29 -> x31, starting transfers between devices: 34.7 us -> 39 us  [to_ring(): return lax.ppermute(value, AXES, ring_pairs(phase, distance))]
    ppermute x29 -> x31, waiting for transfers between devices: 62.4 us -> 60.5 us  [to_ring(): return lax.ppermute(value, AXES, ring_pairs(phase, distance))]
  transfers between devices with their start and end apart: 36 -> 38, of which waited for: 24 -> 25; matrix products, arithmetic and copies ran while one was open for 8% -> 8% of each run, Pallas kernels for 11% -> 11%
where the time goes in v11:
time: 197 us; the launch traced here: 194 us
  waiting for transfers between devices  75.5 us (38%)
  starting transfers between devices  47.9 us (24%)
  Pallas kernels  35.5 us (18%)
  local copies, waits for them, and re-layouts  22.6 us (11%)
  other arithmetic  11.7 us (6%)
    ppermute x31, waiting for transfers between devices, to_ring(): return lax.ppermute(value, AXES, ring_pairs(phase, distance))  60.5 us
    ppermute x31, starting transfers between devices, to_ring(): return lax.ppermute(value, AXES, ring_pairs(phase, distance))  39 us
    pallas_call x21, Pallas kernels, whole_call(): pl.pallas_call(run, name=name, out_shape=outs, in_specs=[SMEM] + [VMEM] *...  35.5 us
    unnamed x60, local copies, waits for them, and re-layouts  16.3 us
    all_to_all x1, waiting for transfers between devices, local(): lax.all_to_all(outgoing.reshape(device_count, width // 128, 128), AXES, 0...  10.2 us
    all_to_all x1, starting transfers between devices, local(): lax.all_to_all(outgoing.reshape(device_count, width // 128, 128), AXES, 0...  7.84 us
  transfers between devices with their start and end apart: 38, of which 25 were waited for; matrix products, arithmetic and copies ran while one was open for 8% of the time, Pallas kernels for 11%

profile of v11, /device:TPU:0, one launch (start us, length us, event | category | flops | bytes accessed | tf_op | source)
XLA Modules:
  0.0 194.4 jit_solution(6171288561788594620)
XLA Ops:
  0.0 1.2 broadcast_add_fusion.2
  1.8 1.0 copy-done.10
  3.4 1.7 collective-permute-start.1
  5.1 1.6 collective-permute-start.2
  6.7 2.1 %collective-permute-start.3 = (bf16[64,1536]{1,0:T(8,128)(2,1)S(1)}, bf16[64,1536]{1,0:T(8,128)(2,1)S(1)}, u32[]{:S(2)}, u32[]{:S(2)}) collective-permute-start(bf16[64,1536]{1,0:T(8,128)(2,1)S(1)} %take_qkv.1.refs_1_.refs_5_), channel_id=1, source_target_pairs={{0,2},{1,3},{2,0},{3,1},{4,6},{5,7},{6,4},{7,5},{8,10},{9,11},{10,... | collective-permute-start | bytes 589832 | tf_op jit(solution)/shard_map/ppermute | solution.py:67
  8.8 1.6 collective-permute-done.1.refs_2_
  10.8 3.1 %collective-permute-done.3.refs_4_ = bf16[64,1536]{1,0:T(8,128)(2,1)S(1)} collective-permute-done((bf16[64,1536]{1,0:T(8,128)(2,1)S(1)}, bf16[64,1536]{1,0:T(8,128)(2,1)S(1)}, u32[]{:S(2)}, u32[]{:S(2)}) %collective-permute-start.3) | collective-permute-done | bytes 196640 | tf_op jit(solution)/shard_map/ppermute | solution.py:67
  14.5 2.9 %collective-permute-start.5 = (bf16[4,64,1536]{2,1,0:T(8,128)(2,1)S(1)}, bf16[4,64,1536]{2,1,0:T(8,128)(2,1)}, u32[]{:S(2)}, u32[]{:S(2)}) collective-permute-start(bf16[4,64,1536]{2,1,0:T(8,128)(2,1)S(1)} %join_qkv.1.refs_2_), channel_id=1, source_target_pairs={{0,12},{1,13},{2,14},{3,15},{4,0},{5,1},{6,2},{7,3},{8,4},{9,5},{1... | collective-permute-start | bytes 2359304 | tf_op jit(solution)/shard_map/ppermute | solution.py:67
  17.5 2.7 %take_rest.1 = (bf16[64,3584]{1,0:T(8,128)(2,1)}, bf16[64,3584]{1,0:T(8,128)(2,1)}, bf16[64,1024]{1,0:T(8,128)(2,1)}, bf16[64,1024]{1,0:T(8,128)(2,1)}) custom-call(s32[38]{0:T(128)} %copy-done.12, bf16[64,1024]{1,0:T(8,128)(2,1)} %refs_1_.3, bf16[64,2048]{1,0:T(8,128)(2,1)} %refs_2_.1, bf16[128,1024]{1,0:T(8,128)(2,1)} %refs_3_.4, ...), custom_call_target="tpu_custom_call" | custom-call | bytes 1703936 | tf_op jit(solution)/shard_map/take_rest/pallas_call | solution.py:101
  20.2 1.2 collective-permute-start.8
  21.4 2.0 %collective-permute-start.9 = (bf16[64,3584]{1,0:T(8,128)(2,1)}, bf16[64,3584]{1,0:T(8,128)(2,1)S(1)}, u32[]{:S(2)}, u32[]{:S(2)}) collective-permute-start(bf16[64,3584]{1,0:T(8,128)(2,1)} %get-tuple-element.35), channel_id=1, source_target_pairs={{0,3},{1,0},{2,1},{3,2},{4,7},{5,4},{6,5},{7,6},{8,11},{9,8},{10,9... | collective-permute-start | bytes 1376264 | tf_op jit(solution)/shard_map/ppermute | solution.py:67
  23.4 11.6 %collective-permute-done.8.refs_2_ = bf16[64,3584]{1,0:T(8,128)(2,1)S(1)} collective-permute-done((bf16[64,3584]{1,0:T(8,128)(2,1)}, bf16[64,3584]{1,0:T(8,128)(2,1)S(1)}, u32[]{:S(2)}, u32[]{:S(2)}) %collective-permute-start.8) | collective-permute-done | bytes 458784 | tf_op jit(solution)/shard_map/ppermute | solution.py:67
  35.9 1.7 collective-permute-done.refs_2_
  37.6 0.9 copy-done.11
  40.2 4.6 %collective-permute-done.10.refs_4_ = bf16[64,3584]{1,0:T(8,128)(2,1)S(1)} collective-permute-done((bf16[64,3584]{1,0:T(8,128)(2,1)S(1)}, bf16[64,3584]{1,0:T(8,128)(2,1)S(1)}, u32[]{:S(2)}, u32[]{:S(2)}) %collective-permute-start.10) | collective-permute-done | bytes 458784 | tf_op jit(solution)/shard_map/ppermute | solution.py:67
  44.7 1.0 copy-done.6
  46.5 2.1 %collective-permute-done.6.refs_5_ = bf16[4,64,1536]{2,1,0:T(8,128)(2,1)S(1)} collective-permute-done((bf16[4,64,1536]{2,1,0:T(8,128)(2,1)}, bf16[4,64,1536]{2,1,0:T(8,128)(2,1)S(1)}, u32[]{:S(2)}, u32[]{:S(2)}) %collective-permute-start.6) | collective-permute-done | bytes 786464 | tf_op jit(solution)/shard_map/ppermute | solution.py:67
  48.7 1.1 copy-done.4
  49.8 3.2 %span_attention.1.refs_1_.refs_7_ = bf16[8,256,64]{2,1,0:T(8,128)(2,1)S(1)} custom-call(s32[38]{0:T(128)S(1)} %copy-done.13, bf16[16,256,64]{2,1,0:T(8,128)(2,1)S(1)} %both_rows.1.refs_1_.refs_7_.refs_3_, bf16[4,64,1536]{2,1,0:T(8,128)(2,1)S(1)} %copy-done.4, bf16[4,64,1536]{2,1,0:T(8,128)(2,1)S(1)} %collective-permute-done.4.refs_3_.refs_5_, ...), custom_call_target="tpu_custom_call" | custom-call | flops 805306368 | bytes 3670016 | tf_op jit(solution)/shard_map/span_attention/pallas_call | solution.py:101
  53.0 1.6 collective-permute-done.15.refs_6_
  54.7 1.5 join_lower.1
  58.6 2.7 %collective-permute-start.12 = (bf16[4,64,1536]{2,1,0:T(8,128)(2,1)S(1)}, bf16[4,64,1536]{2,1,0:T(8,128)(2,1)}, u32[]{:S(2)}, u32[]{:S(2)}) collective-permute-start(bf16[4,64,1536]{2,1,0:T(8,128)(2,1)S(1)} %join_middle.1.refs_4_.refs_3_), channel_id=1, source_target_pairs={{0,12},{1,13},{2,14},{3,15},{4,0},{5,1},{6,2},{7,3},{8,4},{9,5},{1... | collective-permute-start | bytes 2359304 | tf_op jit(solution)/shard_map/ppermute | solution.py:67
  62.0 3.3 %collective-permute-start.17 = (bf16[4,64,1280]{2,1,0:T(8,128)(2,1)}, bf16[4,64,1280]{2,1,0:T(8,128)(2,1)}, u32[]{:S(2)}, u32[]{:S(2)}) collective-permute-start(bf16[4,64,1280]{2,1,0:T(8,128)(2,1)} %copy-done.19), channel_id=1, source_target_pairs={{0,12},{1,13},{2,14},{3,15},{4,0},{5,1},{6,2},{7,3},{8,4},{9,5},{1... | collective-permute-start | bytes 1966088 | tf_op jit(solution)/shard_map/ppermute | solution.py:67
  65.3 4.4 %collective-permute-done.16.refs_4_.refs_2_ = bf16[4,64,1280]{2,1,0:T(8,128)(2,1)S(1)} collective-permute-done((bf16[4,64,1280]{2,1,0:T(8,128)(2,1)}, bf16[4,64,1280]{2,1,0:T(8,128)(2,1)S(1)}, u32[]{:S(2)}, u32[]{:S(2)}) %collective-permute-start.16) | collective-permute-done | bytes 655392 | tf_op jit(solution)/shard_map/ppermute | solution.py:67
  69.7 1.3 fusion.22
  75.1 3.1 %collective-permute-done.13.refs_7_.refs_6_ = bf16[4,64,1536]{2,1,0:T(8,128)(2,1)} collective-permute-done((bf16[4,64,1536]{2,1,0:T(8,128)(2,1)}, bf16[4,64,1536]{2,1,0:T(8,128)(2,1)}, u32[]{:S(2)}, u32[]{:S(2)}) %collective-permute-start.13) | collective-permute-done | bytes 786464 | tf_op jit(solution)/shard_map/ppermute | solution.py:67
  78.2 2.4 %context_out.1.refs_1_ = bf16[256,512]{1,0:T(8,128)(2,1)S(1)} custom-call(s32[38]{0:T(128)S(1)} %copy-done.14, bf16[8,256,64]{2,1,0:T(8,128)(2,1)S(1)} %span_attention.1.refs_1_.refs_7_, bf16[8,256,64]{2,1,0:T(8,128)(2,1)S(1)} %collective-permute-done.7.refs_2_, bf16[16,256,64]{2,1,0:T(8,128)(2,1)S(1)} %both_rows.1.refs_1_.refs_7_.refs_3_, ...), custom_call_target="tpu_custom_call" | custom-call | flops 268435456 | bytes 4194304 | tf_op jit(solution)/shard_map/context_out/pallas_call | solution.py:101
  80.9 1.2 fusion.refs_2_
  82.4 3.5 %norm_up.1 = (bf16[256,1024]{1,0:T(8,128)(2,1)S(1)}, bf16[16,256,64]{2,1,0:T(8,128)(2,1)S(1)}) custom-call(s32[38]{0:T(128)S(1)} %copy-done.14, bf16[256,512]{1,0:T(8,128)(2,1)S(1)} %context_out.1.refs_1_, bf16[256,512]{1,0:T(8,128)(2,1)S(1)} %collective-permute-done.14.refs_2_, bf16[4,64,1536]{2,1,0:T(8,128)(2,1)S(1)} %join_middle.1.refs_4_.refs_3_, ...), custom_call_target="tpu_custom_call" | custom-call | flops 536870912 | bytes 3670016 | tf_op jit(solution)/shard_map/norm_up/pallas_call | solution.py:101
  85.9 2.3 %down.1 = (f32[128,1024]{1,0:T(8,128)S(1)}, bf16[128,1024]{1,0:T(8,128)(2,1)S(1)}) custom-call(s32[38]{0:T(128)S(1)} %copy-done.14, bf16[16,256,64]{2,1,0:T(8,128)(2,1)S(1)} %get-tuple-element.36.refs_1_, bf16[256,1024]{1,0:T(8,128)(2,1)S(1)} %get-tuple-element.37.refs_2_, bf16[4,64,1280]{2,1,0:T(8,128)(2,1)} %get-tuple-element.40.refs_3_, ...), custom_call_target="tpu_custom_call" | custom-call | flops 536870912 | bytes 3670016 | tf_op jit(solution)/shard_map/down/pallas_call | solution.py:101
  90.5 2.0 %select_reduce_fusion.3 = s32[]{:T(128)} fusion(s32[8]{0:T(128)} %param.19, s32[]{:T(128)} %fusion.22), kind=kLoop, calls=%fused_computation.100 | loop fusion | flops 23 | bytes 40 | tf_op jit(solution)/shard_map/reduce_sum | solution.py:549
  92.5 1.7 norm_pool.1.refs_5_
  94.2 1.4 collective-permute-done.20.refs_4_
  95.6 1.1 join_proj.1.refs_4_
  96.9 7.8 %all-to-all-start = ((bf16[128,8,128]{2,1,0:T(8,128)(2,1)}), bf16[128,8,128]{2,1,0:T(8,128)(2,1)S(1)}, u32[]{:S(2)}, u32[]{:S(2)}) async-start(bf16[128,8,128]{2,1,0:T(8,128)(2,1)} %bitcast.8), calls=%async_computation | async-start | bytes 524288 | tf_op jit(solution)/shard_map/all_to_all | solution.py:682
  105.5 10.2 %all-to-all-done.refs_1_ = bf16[128,8,128]{2,1,0:T(8,128)(2,1)S(1)} async-done(((bf16[128,8,128]{2,1,0:T(8,128)(2,1)}), bf16[128,8,128]{2,1,0:T(8,128)(2,1)S(1)}, u32[]{:S(2)}, u32[]{:S(2)}) %all-to-all-start) | async-done | bytes 262176 | tf_op jit(solution)/shard_map/all_to_all | solution.py:682
  115.7 1.6 copy-done.5
  118.0 2.1 %embed.1.refs_1_ = bf16[128,512]{1,0:T(8,128)(2,1)S(1)} custom-call(s32[38]{0:T(128)S(1)} %copy-done.14, bf16[128,8,128]{2,1,0:T(8,128)(2,1)S(1)} %all-to-all-done.refs_1_, bf16[128,128]{1,0:T(8,128)(2,1)S(1)} %copy-done.15, bf16[1024,1024]{1,0:T(8,128)(2,1)S(1)} %copy-done.5, bf16[4,4,64,256]{3,2,1,0:T(8,128)(2,1)S(1)} %join_proj.1.refs_4_, ...), custom_call_target="tpu_custom_call" | custom-call | flops 402653184 | bytes 3440640 | tf_op jit(solution)/shard_map/embed/pallas_call | solution.py:101
  120.8 2.6 %collective-permute-start.23 = (bf16[128,512]{1,0:T(8,128)(2,1)S(1)}, bf16[128,512]{1,0:T(8,128)(2,1)S(1)}, u32[]{:S(2)}, u32[]{:S(2)}) collective-permute-start(bf16[128,512]{1,0:T(8,128)(2,1)S(1)} %embed.1.refs_1_), channel_id=1, source_target_pairs={{0,3},{1,0},{2,1},{3,2},{4,7},{5,4},{6,5},{7,6},{8,11},{9,8},{10,9... | collective-permute-start | bytes 393224 | tf_op jit(solution)/shard_map/ppermute | solution.py:67
  124.9 1.5 collective-permute-done.22.refs_2_
  126.3 1.0 collective-permute-done.23.refs_3_
  127.3 2.5 %collective-permute-done.24.refs_4_ = bf16[128,512]{1,0:T(8,128)(2,1)S(1)} collective-permute-done((bf16[128,512]{1,0:T(8,128)(2,1)S(1)}, bf16[128,512]{1,0:T(8,128)(2,1)S(1)}, u32[]{:S(2)}, u32[]{:S(2)}) %collective-permute-start.24) | collective-permute-done | bytes 131104 | tf_op jit(solution)/shard_map/ppermute | solution.py:67
  131.1 1.0 multiply_sine_fusion
  132.1 2.7 %collective-permute-start.27 = (bf16[4,128,512]{2,1,0:T(8,128)(2,1)S(1)}, bf16[4,128,512]{2,1,0:T(8,128)(2,1)}, u32[]{:S(2)}, u32[]{:S(2)}) collective-permute-start(bf16[4,128,512]{2,1,0:T(8,128)(2,1)S(1)} %join_columns.1.refs_1_), channel_id=1, source_target_pairs={{0,12},{1,13},{2,14},{3,15},{4,0},{5,1},{6,2},{7,3},{8,4},{9,5},{1... | collective-permute-start | bytes 1572872 | tf_op jit(solution)/shard_map/ppermute | solution.py:67
  136.0 5.1 %collective-permute-done.25.refs_1_ = bf16[4,128,512]{2,1,0:T(8,128)(2,1)} collective-permute-done((bf16[4,128,512]{2,1,0:T(8,128)(2,1)S(1)}, bf16[4,128,512]{2,1,0:T(8,128)(2,1)}, u32[]{:S(2)}, u32[]{:S(2)}) %collective-permute-start.25) | collective-permute-done | bytes 524320 | tf_op jit(solution)/shard_map/ppermute | solution.py:67
  141.2 3.4 %copy-done = bf16[8192,512]{1,0:T(8,128)(2,1)S(1)} copy-done((bf16[8192,512]{1,0:T(8,128)(2,1)S(1)}, bf16[8192,512]{1,0:T(8,128)(2,1)}, u32[]{:S(2)}) %copy-start) | copy-done | bytes 8388632
  145.4 1.2 project_own.1
  146.6 3.4 %copy-done.1 = bf16[8192,512]{1,0:T(8,128)(2,1)S(1)} copy-done((bf16[8192,512]{1,0:T(8,128)(2,1)S(1)}, bf16[8192,512]{1,0:T(8,128)(2,1)}, u32[]{:S(2)}) %copy-start.1) | copy-done | bytes 8388632
  150.0 2.5 %project_near.1 = (f32[128,512]{1,0:T(8,128)S(1)}, f32[128,128]{1,0:T(8,128)S(1)}, f32[128,1]{1,0:T(8,128)S(1)}) custom-call(s32[38]{0:T(128)S(1)} %copy-done.14, bf16[4,128,512]{2,1,0:T(8,128)(2,1)} %collective-permute-done.25.refs_1_, bf16[4,128,512]{2,1,0:T(8,128)(2,1)} %collective-permute-done.27.refs_2_, f32[16,1,512]{2,1,0:T(1,128)S(1)} %bitcast.25, ...), custom_call_target="tpu_custom_call" | custom-call | flops 671088640 | bytes 11895296 | tf_op jit(solution)/shard_map/project_near/pallas_call | solution.py:101
  152.5 1.2 last_keys.1
  154.2 1.3 last_queries.1.refs_1_
  155.5 2.8 %collective-permute-done.28.refs_3_ = bf16[2,128,64]{2,1,0:T(8,128)(2,1)S(1)} collective-permute-done((bf16[2,128,64]{2,1,0:T(8,128)(2,1)S(1)}, bf16[2,128,64]{2,1,0:T(8,128)(2,1)S(1)}, u32[]{:S(2)}, u32[]{:S(2)}) %collective-permute-start.28) | collective-permute-done | bytes 32800 | tf_op jit(solution)/shard_map/ppermute | solution.py:764
  158.3 3.5 %attend_out.1 = (bf16[32,8192]{1,0:T(8,128)(2,1)S(1)}, bf16[32,8192]{1,0:T(8,128)(2,1)}, bf16[32,8192]{1,0:T(8,128)(2,1)}, bf16[32,4096]{1,0:T(8,128)(2,1)}, bf16[32,4096]{1,0:T(8,128)(2,1)S(1)}) custom-call(s32[38]{0:T(128)S(1)} %copy-done.14, bf16[128,512]{1,0:T(8,128)(2,1)S(1)} %last_queries.1.refs_1_, bf16[2,128,64]{2,1,0:T(8,128)(2,1)S(1)} %get-tuple-element.53.refs_2_, ...), custom_call_target="tpu_custom_call" | custom-call | flops 1073741824 | bytes 8683520 | tf_op jit(solution)/shard_map/attend_out/pallas_call | solution.py:101
  161.8 3.2 %collective-permute-start.32 = (bf16[32,4096]{1,0:T(8,128)(2,1)S(1)}, bf16[32,4096]{1,0:T(8,128)(2,1)}, u32[]{:S(2)}, u32[]{:S(2)}) collective-permute-start(bf16[32,4096]{1,0:T(8,128)(2,1)S(1)} %get-tuple-element.58), channel_id=1, source_target_pairs={{0,12},{1,13},{2,14},{3,15},{4,0},{5,1},{6,2},{7,3},{8,4},{9,5},{1... | collective-permute-start | bytes 786440 | tf_op jit(solution)/shard_map/ppermute | solution.py:67
  165.1 2.0 %collective-permute-start.30 = (bf16[32,8192]{1,0:T(8,128)(2,1)}, bf16[32,8192]{1,0:T(8,128)(2,1)S(1)}, u32[]{:S(2)}, u32[]{:S(2)}) collective-permute-start(bf16[32,8192]{1,0:T(8,128)(2,1)} %get-tuple-element.56), channel_id=1, source_target_pairs={{0,12},{1,13},{2,14},{3,15},{4,0},{5,1},{6,2},{7,3},{8,4},{9,5},{1... | collective-permute-start | bytes 1572872 | tf_op jit(solution)/shard_map/ppermute | solution.py:67
  167.1 1.9 collective-permute-done.32
  168.9 3.8 %collective-permute-start.33 = (bf16[32,4096]{1,0:T(8,128)(2,1)}, bf16[32,4096]{1,0:T(8,128)(2,1)S(1)}, u32[]{:S(2)}, u32[]{:S(2)}) collective-permute-start(bf16[32,4096]{1,0:T(8,128)(2,1)} %collective-permute-done.32), channel_id=1, source_target_pairs={{0,12},{1,13},{2,14},{3,15},{4,0},{5,1},{6,2},{7,3},{8,4},{9,5},{1... | collective-permute-start | bytes 786440 | tf_op jit(solution)/shard_map/ppermute | solution.py:67
  173.6 3.1 %collective-permute-done.31.refs_4_ = bf16[32,4096]{1,0:T(8,128)(2,1)S(1)} collective-permute-done((bf16[32,4096]{1,0:T(8,128)(2,1)}, bf16[32,4096]{1,0:T(8,128)(2,1)S(1)}, u32[]{:S(2)}, u32[]{:S(2)}) %collective-permute-start.31) | collective-permute-done | bytes 262176 | tf_op jit(solution)/shard_map/ppermute | solution.py:67
  177.5 5.0 %collective-permute-done.33.refs_5_ = bf16[32,4096]{1,0:T(8,128)(2,1)S(1)} collective-permute-done((bf16[32,4096]{1,0:T(8,128)(2,1)}, bf16[32,4096]{1,0:T(8,128)(2,1)S(1)}, u32[]{:S(2)}, u32[]{:S(2)}) %collective-permute-start.33) | collective-permute-done | bytes 262176 | tf_op jit(solution)/shard_map/ppermute | solution.py:67
  183.4 3.2 %collective-permute-start.35 = (bf16[8,8192]{1,0:T(8,128)(2,1)S(1)}, bf16[8,8192]{1,0:T(8,128)(2,1)S(1)}, u32[]{:S(2)}, u32[]{:S(2)}) collective-permute-start(bf16[8,8192]{1,0:T(8,128)(2,1)S(1)} %get-tuple-element.61), channel_id=1, source_target_pairs={{0,3},{1,0},{2,1},{3,2},{4,7},{5,4},{6,5},{7,6},{8,11},{9,8},{10,9... | collective-permute-start | bytes 393224 | tf_op jit(solution)/shard_map/ppermute | solution.py:67
  187.4 2.2 %collective-permute-done.34.refs_2_ = bf16[8,8192]{1,0:T(8,128)(2,1)S(1)} collective-permute-done((bf16[8,8192]{1,0:T(8,128)(2,1)S(1)}, bf16[8,8192]{1,0:T(8,128)(2,1)S(1)}, u32[]{:S(2)}, u32[]{:S(2)}) %collective-permute-start.34) | collective-permute-done | bytes 131104 | tf_op jit(solution)/shard_map/ppermute | solution.py:67
  189.5 1.0 collective-permute-done.35.refs_3_
  190.5 2.5 %collective-permute-done.36.refs_4_ = bf16[8,8192]{1,0:T(8,128)(2,1)S(1)} collective-permute-done((bf16[8,8192]{1,0:T(8,128)(2,1)S(1)}, bf16[8,8192]{1,0:T(8,128)(2,1)S(1)}, u32[]{:S(2)}, u32[]{:S(2)}) %collective-permute-start.36) | collective-permute-done | bytes 131104 | tf_op jit(solution)/shard_map/ppermute | solution.py:67
  193.1 1.3 finish.1
  (153 shorter events, 25.6 us)
Async XLA Ops:
  1.7 54.4 %copy-start.22 = (s32[16]{0:T(128)}, s32[16]{0:T(128)S(1)}, u32[]{:S(2)}) copy-start(s32[16]{0:T(128)S(1)} %broadcast_select_fusion.2) | copy-start | bytes 196
  1.8 1.0 copy-start.10
  2.8 14.6 %copy-start.12 = (s32[38]{0:T(128)}, s32[38]{0:T(128)S(1)}, u32[]{:S(2)}) copy-start(s32[38]{0:T(128)S(1)} %concatenate.9.refs_0_) | copy-start | bytes 460
  3.4 14.0 %copy-start.8 = (bf16[64,1536]{1,0:T(8,128)(2,1)}, bf16[64,1536]{1,0:T(8,128)(2,1)S(1)}, u32[]{:S(2)}) copy-start(bf16[64,1536]{1,0:T(8,128)(2,1)S(1)} %take_qkv.1.refs_1_.refs_5_) | copy-start | bytes 589828
  3.4 6.9 %collective-permute-start.1 = (bf16[64,1536]{1,0:T(8,128)(2,1)S(1)}, bf16[64,1536]{1,0:T(8,128)(2,1)S(1)}, u32[]{:S(2)}, u32[]{:S(2)}) collective-permute-start(bf16[64,1536]{1,0:T(8,128)(2,1)S(1)} %take_qkv.1.refs_1_.refs_5_), channel_id=1, source_target_pairs={{0,1},{1,2},{2,3},{3,0},{4,5},{5,6},{6,7},{7,4},{8,9},{9,10},{10,1... | collective-permute-start | bytes 589832 | tf_op jit(solution)/shard_map/ppermute | solution.py:67
  5.1 5.7 %collective-permute-start.2 = (bf16[64,1536]{1,0:T(8,128)(2,1)S(1)}, bf16[64,1536]{1,0:T(8,128)(2,1)S(1)}, u32[]{:S(2)}, u32[]{:S(2)}) collective-permute-start(bf16[64,1536]{1,0:T(8,128)(2,1)S(1)} %take_qkv.1.refs_1_.refs_5_), channel_id=1, source_target_pairs={{0,3},{1,0},{2,1},{3,2},{4,7},{5,4},{6,5},{7,6},{8,11},{9,8},{10,9... | collective-permute-start | bytes 589832 | tf_op jit(solution)/shard_map/ppermute | solution.py:67
  6.7 7.2 %collective-permute-start.3 = (bf16[64,1536]{1,0:T(8,128)(2,1)S(1)}, bf16[64,1536]{1,0:T(8,128)(2,1)S(1)}, u32[]{:S(2)}, u32[]{:S(2)}) collective-permute-start(bf16[64,1536]{1,0:T(8,128)(2,1)S(1)} %take_qkv.1.refs_1_.refs_5_), channel_id=1, source_target_pairs={{0,2},{1,3},{2,0},{3,1},{4,6},{5,7},{6,4},{7,5},{8,10},{9,11},{10,... | collective-permute-start | bytes 589832 | tf_op jit(solution)/shard_map/ppermute | solution.py:67
  14.5 32.0 %copy-start.3 = (bf16[4,64,1536]{2,1,0:T(8,128)(2,1)}, bf16[4,64,1536]{2,1,0:T(8,128)(2,1)S(1)}, u32[]{:S(2)}) copy-start(bf16[4,64,1536]{2,1,0:T(8,128)(2,1)S(1)} %join_qkv.1.refs_2_) | copy-start | bytes 2359300
  14.5 43.8 %copy-start.24 = (s32[1024]{0:T(1024)S(1)}, s32[1024]{0:T(1024)}, u32[]{:S(2)}) copy-start(s32[1024]{0:T(1024)} %param.18) | copy-start | bytes 12292
  14.5 43.8 %copy-start.25 = (s32[8]{0:T(128)S(1)}, s32[8]{0:T(128)}, u32[]{:S(2)}) copy-start(s32[8]{0:T(128)} %param.20) | copy-start | bytes 100
  14.5 20.5 %collective-permute-start.5 = (bf16[4,64,1536]{2,1,0:T(8,128)(2,1)S(1)}, bf16[4,64,1536]{2,1,0:T(8,128)(2,1)}, u32[]{:S(2)}, u32[]{:S(2)}) collective-permute-start(bf16[4,64,1536]{2,1,0:T(8,128)(2,1)S(1)} %join_qkv.1.refs_2_), channel_id=1, source_target_pairs={{0,12},{1,13},{2,14},{3,15},{4,0},{5,1},{6,2},{7,3},{8,4},{9,5},{1... | collective-permute-start | bytes 2359304 | tf_op jit(solution)/shard_map/ppermute | solution.py:67
  20.2 34.5 %copy-start.7 = (bf16[64,3584]{1,0:T(8,128)(2,1)S(1)}, bf16[64,3584]{1,0:T(8,128)(2,1)}, u32[]{:S(2)}) copy-start(bf16[64,3584]{1,0:T(8,128)(2,1)} %get-tuple-element.34.refs_1_) | copy-start | bytes 1376260
  20.2 14.9 %collective-permute-start.8 = (bf16[64,3584]{1,0:T(8,128)(2,1)}, bf16[64,3584]{1,0:T(8,128)(2,1)S(1)}, u32[]{:S(2)}, u32[]{:S(2)}) collective-permute-start(bf16[64,3584]{1,0:T(8,128)(2,1)} %get-tuple-element.34.refs_1_), channel_id=1, source_target_pairs={{0,1},{1,2},{2,3},{3,0},{4,5},{5,6},{6,7},{7,4},{8,9},{9,10},{10,1... | collective-permute-start | bytes 1376264 | tf_op jit(solution)/shard_map/ppermute | solution.py:67
  21.4 23.3 %collective-permute-start.4 = (bf16[4,64,1536]{2,1,0:T(8,128)(2,1)S(1)}, bf16[4,64,1536]{2,1,0:T(8,128)(2,1)S(1)}, u32[]{:S(2)}, u32[]{:S(2)}) collective-permute-start(bf16[4,64,1536]{2,1,0:T(8,128)(2,1)S(1)} %join_qkv.1.refs_2_), channel_id=1, source_target_pairs={{0,4},{1,5},{2,6},{3,7},{4,8},{5,9},{6,10},{7,11},{8,12},{9,13},{1... | collective-permute-start | bytes 2359304 | tf_op jit(solution)/shard_map/ppermute | solution.py:67
  21.4 18.7 %collective-permute-start.9 = (bf16[64,3584]{1,0:T(8,128)(2,1)}, bf16[64,3584]{1,0:T(8,128)(2,1)S(1)}, u32[]{:S(2)}, u32[]{:S(2)}) collective-permute-start(bf16[64,3584]{1,0:T(8,128)(2,1)} %get-tuple-element.35), channel_id=1, source_target_pairs={{0,3},{1,0},{2,1},{3,2},{4,7},{5,4},{6,5},{7,6},{8,11},{9,8},{10,9... | collective-permute-start | bytes 1376264 | tf_op jit(solution)/shard_map/ppermute | solution.py:67
  35.0 9.7 %collective-permute-start.10 = (bf16[64,3584]{1,0:T(8,128)(2,1)S(1)}, bf16[64,3584]{1,0:T(8,128)(2,1)S(1)}, u32[]{:S(2)}, u32[]{:S(2)}) collective-permute-start(bf16[64,3584]{1,0:T(8,128)(2,1)S(1)} %collective-permute-done.8.refs_2_), channel_id=1, source_target_pairs={{0,1},{1,2},{2,3},{3,0},{4,5},{5,6},{6,7},{7,4},{8,9},{9,10},{10,1... | collective-permute-start | bytes 1376264 | tf_op jit(solution)/shard_map/ppermute | solution.py:67
  35.1 13.6 %collective-permute-start.6 = (bf16[4,64,1536]{2,1,0:T(8,128)(2,1)}, bf16[4,64,1536]{2,1,0:T(8,128)(2,1)S(1)}, u32[]{:S(2)}, u32[]{:S(2)}) collective-permute-start(bf16[4,64,1536]{2,1,0:T(8,128)(2,1)} %collective-permute-done.5.refs_4_.refs_6_), channel_id=1, source_target_pairs={{0,12},{1,13},{2,14},{3,15},{4,0},{5,1},{6,2},{7,3},{8,4},{9,5},{1... | collective-permute-start | bytes 2359304 | tf_op jit(solution)/shard_map/ppermute | solution.py:67
  35.9 1.7 collective-permute-start
  37.6 1.0 copy-start.11
  39.3 15.4 %copy-start.14 = (s32[38]{0:T(128)S(1)}, s32[38]{0:T(128)}, u32[]{:S(2)}) copy-start(s32[38]{0:T(128)} %copy-done.12) | copy-start | bytes 460
  39.3 15.4 %copy-start.18 = (bf16[64,1024]{1,0:T(8,128)(2,1)S(1)}, bf16[64,1024]{1,0:T(8,128)(2,1)}, u32[]{:S(2)}) copy-start(bf16[64,1024]{1,0:T(8,128)(2,1)} %get-tuple-element.38.refs_5_) | copy-start | bytes 393220
  44.7 1.0 copy-start.6
  46.4 14.9 %collective-permute-start.11 = (bf16[4,64,1536]{2,1,0:T(8,128)(2,1)S(1)}, bf16[4,64,1536]{2,1,0:T(8,128)(2,1)}, u32[]{:S(2)}, u32[]{:S(2)}) collective-permute-start(bf16[4,64,1536]{2,1,0:T(8,128)(2,1)S(1)} %join_middle.1.refs_4_.refs_3_), channel_id=1, source_target_pairs={{0,4},{1,5},{2,6},{3,7},{4,8},{5,9},{6,10},{7,11},{8,12},{9,13},{1... | collective-permute-start | bytes 2359304 | tf_op jit(solution)/shard_map/ppermute | solution.py:67
  46.4 8.2 %collective-permute-start.15 = (bf16[64,1024]{1,0:T(8,128)(2,1)}, bf16[64,1024]{1,0:T(8,128)(2,1)S(1)}, u32[]{:S(2)}, u32[]{:S(2)}) collective-permute-start(bf16[64,1024]{1,0:T(8,128)(2,1)} %get-tuple-element.39), channel_id=1, source_target_pairs={{0,2},{1,3},{2,0},{3,1},{4,6},{5,7},{6,4},{7,5},{8,10},{9,11},{10,... | collective-permute-start | bytes 393224 | tf_op jit(solution)/shard_map/ppermute | solution.py:67
  48.7 1.1 copy-start.4
  56.8 0.8 copy-start.19
  57.7 4.3 %copy-start.20 = (bf16[4,64,256]{2,1,0:T(8,128)(2,1)}, bf16[4,64,256]{2,1,0:T(8,128)(2,1)S(1)}, u32[]{:S(2)}) copy-start(bf16[4,64,256]{2,1,0:T(8,128)(2,1)S(1)} %get-tuple-element.45) | copy-start | bytes 393220
  57.7 12.0 %collective-permute-start.16 = (bf16[4,64,1280]{2,1,0:T(8,128)(2,1)}, bf16[4,64,1280]{2,1,0:T(8,128)(2,1)S(1)}, u32[]{:S(2)}, u32[]{:S(2)}) collective-permute-start(bf16[4,64,1280]{2,1,0:T(8,128)(2,1)} %get-tuple-element.40.refs_3_), channel_id=1, source_target_pairs={{0,4},{1,5},{2,6},{3,7},{4,8},{5,9},{6,10},{7,11},{8,12},{9,13},{1... | collective-permute-start | bytes 1966088 | tf_op jit(solution)/shard_map/ppermute | solution.py:67
  58.6 16.5 %collective-permute-start.12 = (bf16[4,64,1536]{2,1,0:T(8,128)(2,1)S(1)}, bf16[4,64,1536]{2,1,0:T(8,128)(2,1)}, u32[]{:S(2)}, u32[]{:S(2)}) collective-permute-start(bf16[4,64,1536]{2,1,0:T(8,128)(2,1)S(1)} %join_middle.1.refs_4_.refs_3_), channel_id=1, source_target_pairs={{0,12},{1,13},{2,14},{3,15},{4,0},{5,1},{6,2},{7,3},{8,4},{9,5},{1... | collective-permute-start | bytes 2359304 | tf_op jit(solution)/shard_map/ppermute | solution.py:67
  61.3 16.9 %collective-permute-start.13 = (bf16[4,64,1536]{2,1,0:T(8,128)(2,1)}, bf16[4,64,1536]{2,1,0:T(8,128)(2,1)}, u32[]{:S(2)}, u32[]{:S(2)}) collective-permute-start(bf16[4,64,1536]{2,1,0:T(8,128)(2,1)} %collective-permute-done.11.refs_5_.refs_4_), channel_id=1, source_target_pairs={{0,4},{1,5},{2,6},{3,7},{4,8},{5,9},{6,10},{7,11},{8,12},{9,13},{1... | collective-permute-start | bytes 2359304 | tf_op jit(solution)/shard_map/ppermute | solution.py:67
  62.0 13.2 %collective-permute-start.7 = (bf16[8,256,64]{2,1,0:T(8,128)(2,1)S(1)}, bf16[8,256,64]{2,1,0:T(8,128)(2,1)S(1)}, u32[]{:S(2)}, u32[]{:S(2)}) collective-permute-start(bf16[8,256,64]{2,1,0:T(8,128)(2,1)S(1)} %span_attention.1.refs_1_.refs_7_), channel_id=1, source_target_pairs={{0,16},{16,0},{32,48},{48,32},{64,80},{80,64},{96,112},{112,96},{1... | collective-permute-start | bytes 786440 | tf_op jit(solution)/shard_map/ppermute | solution.py:71
  62.0 23.9 %collective-permute-start.17 = (bf16[4,64,1280]{2,1,0:T(8,128)(2,1)}, bf16[4,64,1280]{2,1,0:T(8,128)(2,1)}, u32[]{:S(2)}, u32[]{:S(2)}) collective-permute-start(bf16[4,64,1280]{2,1,0:T(8,128)(2,1)} %copy-done.19), channel_id=1, source_target_pairs={{0,12},{1,13},{2,14},{3,15},{4,0},{5,1},{6,2},{7,3},{8,4},{9,5},{1... | collective-permute-start | bytes 1966088 | tf_op jit(solution)/shard_map/ppermute | solution.py:67
  69.7 16.2 %collective-permute-start.18 = (bf16[4,64,1280]{2,1,0:T(8,128)(2,1)S(1)}, bf16[4,64,1280]{2,1,0:T(8,128)(2,1)}, u32[]{:S(2)}, u32[]{:S(2)}) collective-permute-start(bf16[4,64,1280]{2,1,0:T(8,128)(2,1)S(1)} %collective-permute-done.16.refs_4_.refs_2_), channel_id=1, source_target_pairs={{0,4},{1,5},{2,6},{3,7},{4,8},{5,9},{6,10},{7,11},{8,12},{9,13},{1... | collective-permute-start | bytes 1966088 | tf_op jit(solution)/shard_map/ppermute | solution.py:67
  74.4 14.8 %copy-start.21 = (bf16[4,64,256]{2,1,0:T(8,128)(2,1)S(1)}, bf16[4,64,256]{2,1,0:T(8,128)(2,1)}, u32[]{:S(2)}) copy-start(bf16[4,64,256]{2,1,0:T(8,128)(2,1)} %copy-done.20) | copy-start | bytes 393220
  74.4 21.3 %copy-start.17 = (bf16[4,64,256]{2,1,0:T(8,128)(2,1)S(1)}, bf16[4,64,256]{2,1,0:T(8,128)(2,1)}, u32[]{:S(2)}) copy-start(bf16[4,64,256]{2,1,0:T(8,128)(2,1)} %copy-done.16) | copy-start | bytes 393220
  80.6 1.8 collective-permute-start.14
  82.1 59.1 %copy-start.2 = (bf16[2,8192,64]{1,2,0:T(8,128)(2,1)S(1)}, bf16[2,8192,64]{1,2,0:T(8,128)(2,1)}, u32[]{:S(2)}) copy-start(bf16[2,8192,64]{1,2,0:T(8,128)(2,1)} %param.30) | copy-start | bytes 6291460
  88.2 4.3 %collective-permute-start.19 = (bf16[128,1024]{1,0:T(8,128)(2,1)S(1)}, bf16[128,1024]{1,0:T(8,128)(2,1)S(1)}, u32[]{:S(2)}, u32[]{:S(2)}) collective-permute-start(bf16[128,1024]{1,0:T(8,128)(2,1)S(1)} %get-tuple-element.43), channel_id=1, source_target_pairs={{0,16},{16,0},{32,48},{48,32},{64,80},{80,64},{96,112},{112,96},{1... | collective-permute-start | bytes 786440 | tf_op jit(solution)/shard_map/ppermute | solution.py:71
  89.2 6.5 %collective-permute-start.20 = (bf16[4,64,256]{2,1,0:T(8,128)(2,1)S(1)}, bf16[4,64,256]{2,1,0:T(8,128)(2,1)S(1)}, u32[]{:S(2)}, u32[]{:S(2)}) collective-permute-start(bf16[4,64,256]{2,1,0:T(8,128)(2,1)S(1)} %copy-done.21), channel_id=1, source_target_pairs={{0,8},{1,9},{2,10},{3,11},{4,12},{5,13},{6,14},{7,15},{8,0},{9,1},... | collective-permute-start | bytes 393224 | tf_op jit(solution)/shard_map/ppermute | solution.py:67
  96.8 18.9 %collective-permute-start.21 = (bf16[4,4,64,256]{3,2,1,0:T(8,128)(2,1)S(1)}, bf16[4,4,64,256]{3,2,1,0:T(8,128)(2,1)S(1)}, u32[]{:S(2)}, u32[]{:S(2)}) collective-permute-start(bf16[4,4,64,256]{3,2,1,0:T(8,128)(2,1)S(1)} %join_proj.1.refs_4_), channel_id=1, source_target_pairs={{0,16},{16,0},{32,48},{48,32},{64,80},{80,64},{96,112},{112,96},{1... | collective-permute-start | bytes 1572872 | tf_op jit(solution)/shard_map/ppermute | solution.py:71
  96.9 18.7 %all-to-all-start = ((bf16[128,8,128]{2,1,0:T(8,128)(2,1)}), bf16[128,8,128]{2,1,0:T(8,128)(2,1)S(1)}, u32[]{:S(2)}, u32[]{:S(2)}) async-start(bf16[128,8,128]{2,1,0:T(8,128)(2,1)} %bitcast.8), calls=%async_computation | async-start | bytes 524288 | tf_op jit(solution)/shard_map/all_to_all | solution.py:682
  115.7 1.6 copy-start.5
  120.1 6.2 %collective-permute-start.22 = (bf16[128,512]{1,0:T(8,128)(2,1)S(1)}, bf16[128,512]{1,0:T(8,128)(2,1)S(1)}, u32[]{:S(2)}, u32[]{:S(2)}) collective-permute-start(bf16[128,512]{1,0:T(8,128)(2,1)S(1)} %embed.1.refs_1_), channel_id=1, source_target_pairs={{0,1},{1,2},{2,3},{3,0},{4,5},{5,6},{6,7},{7,4},{8,9},{9,10},{10,1... | collective-permute-start | bytes 393224 | tf_op jit(solution)/shard_map/ppermute | solution.py:67
  120.8 6.5 %collective-permute-start.23 = (bf16[128,512]{1,0:T(8,128)(2,1)S(1)}, bf16[128,512]{1,0:T(8,128)(2,1)S(1)}, u32[]{:S(2)}, u32[]{:S(2)}) collective-permute-start(bf16[128,512]{1,0:T(8,128)(2,1)S(1)} %embed.1.refs_1_), channel_id=1, source_target_pairs={{0,3},{1,0},{2,1},{3,2},{4,7},{5,4},{6,5},{7,6},{8,11},{9,8},{10,9... | collective-permute-start | bytes 393224 | tf_op jit(solution)/shard_map/ppermute | solution.py:67
  123.4 6.5 %collective-permute-start.24 = (bf16[128,512]{1,0:T(8,128)(2,1)S(1)}, bf16[128,512]{1,0:T(8,128)(2,1)S(1)}, u32[]{:S(2)}, u32[]{:S(2)}) collective-permute-start(bf16[128,512]{1,0:T(8,128)(2,1)S(1)} %embed.1.refs_1_), channel_id=1, source_target_pairs={{0,2},{1,3},{2,0},{3,1},{4,6},{5,7},{6,4},{7,5},{8,10},{9,11},{10,... | collective-permute-start | bytes 393224 | tf_op jit(solution)/shard_map/ppermute | solution.py:67
  130.4 10.6 %collective-permute-start.25 = (bf16[4,128,512]{2,1,0:T(8,128)(2,1)S(1)}, bf16[4,128,512]{2,1,0:T(8,128)(2,1)}, u32[]{:S(2)}, u32[]{:S(2)}) collective-permute-start(bf16[4,128,512]{2,1,0:T(8,128)(2,1)S(1)} %join_columns.1.refs_1_), channel_id=1, source_target_pairs={{0,4},{1,5},{2,6},{3,7},{4,8},{5,9},{6,10},{7,11},{8,12},{9,13},{1... | collective-permute-start | bytes 1572872 | tf_op jit(solution)/shard_map/ppermute | solution.py:67
  132.1 14.5 %collective-permute-start.27 = (bf16[4,128,512]{2,1,0:T(8,128)(2,1)S(1)}, bf16[4,128,512]{2,1,0:T(8,128)(2,1)}, u32[]{:S(2)}, u32[]{:S(2)}) collective-permute-start(bf16[4,128,512]{2,1,0:T(8,128)(2,1)S(1)} %join_columns.1.refs_1_), channel_id=1, source_target_pairs={{0,12},{1,13},{2,14},{3,15},{4,0},{5,1},{6,2},{7,3},{8,4},{9,5},{1... | collective-permute-start | bytes 1572872 | tf_op jit(solution)/shard_map/ppermute | solution.py:67
  141.0 11.5 %collective-permute-start.26 = (bf16[4,128,512]{2,1,0:T(8,128)(2,1)}, bf16[4,128,512]{2,1,0:T(8,128)(2,1)S(1)}, u32[]{:S(2)}, u32[]{:S(2)}) collective-permute-start(bf16[4,128,512]{2,1,0:T(8,128)(2,1)} %collective-permute-done.25.refs_1_), channel_id=1, source_target_pairs={{0,4},{1,5},{2,6},{3,7},{4,8},{5,9},{6,10},{7,11},{8,12},{9,13},{1... | collective-permute-start | bytes 1572872 | tf_op jit(solution)/shard_map/ppermute | solution.py:67
  141.2 3.4 %copy-start = (bf16[8192,512]{1,0:T(8,128)(2,1)S(1)}, bf16[8192,512]{1,0:T(8,128)(2,1)}, u32[]{:S(2)}) copy-start(bf16[8192,512]{1,0:T(8,128)(2,1)} %refs_3_.7) | copy-start | bytes 25165828
  145.4 8.7 %slice-start = ((s8[8388608]{0:T(1024)(128)(4,1)}), s8[4194304]{0:T(1024)(128)(4,1)S(1)}, s32[]{:S(2)}) async-start(s8[8388608]{0:T(1024)(128)(4,1)} %bitcast.17), calls=%async_computation.1 | async-start | bytes 8388608
  146.6 3.4 %copy-start.1 = (bf16[8192,512]{1,0:T(8,128)(2,1)S(1)}, bf16[8192,512]{1,0:T(8,128)(2,1)}, u32[]{:S(2)}) copy-start(bf16[8192,512]{1,0:T(8,128)(2,1)} %refs_3_.7) | copy-start | bytes 25165828
  150.0 4.1 %slice-start.1 = ((s8[8388608]{0:T(1024)(128)(4,1)}), s8[4194304]{0:T(1024)(128)(4,1)S(1)}, s32[]{:S(2)}) async-start(s8[8388608]{0:T(1024)(128)(4,1)} %bitcast.17), calls=%async_computation.2 | async-start | bytes 8388608
  150.0 8.3 %slice-start.2 = ((s8[8388608]{0:T(1024)(128)(4,1)}), s8[4194304]{0:T(1024)(128)(4,1)S(1)}, s32[]{:S(2)}) async-start(s8[8388608]{0:T(1024)(128)(4,1)} %bitcast.22), calls=%async_computation.3 | async-start | bytes 8388608
  152.5 5.8 %slice-start.3 = ((s8[8388608]{0:T(1024)(128)(4,1)}), s8[4194304]{0:T(1024)(128)(4,1)S(1)}, s32[]{:S(2)}) async-start(s8[8388608]{0:T(1024)(128)(4,1)} %bitcast.22), calls=%async_computation.4 | async-start | bytes 8388608
  153.7 4.6 %collective-permute-start.28 = (bf16[2,128,64]{2,1,0:T(8,128)(2,1)S(1)}, bf16[2,128,64]{2,1,0:T(8,128)(2,1)S(1)}, u32[]{:S(2)}, u32[]{:S(2)}) collective-permute-start(bf16[2,128,64]{2,1,0:T(8,128)(2,1)S(1)} %get-tuple-element.53.refs_2_), channel_id=1, source_target_pairs={{0,1},{1,0},{2,3},{3,2},{4,5},{5,4},{6,7},{7,6},{8,9},{9,8},{10,11... | collective-permute-start | bytes 98312 | tf_op jit(solution)/shard_map/ppermute | solution.py:764
  154.1 18.6 %copy-start.23 = (s32[16]{0:T(128)S(1)}, s32[16]{0:T(128)}, u32[]{:S(2)}) copy-start(s32[16]{0:T(128)} %copy-done.22) | copy-start | bytes 196
  161.8 14.9 %collective-permute-start.29 = (bf16[32,8192]{1,0:T(8,128)(2,1)}, bf16[32,8192]{1,0:T(8,128)(2,1)S(1)}, u32[]{:S(2)}, u32[]{:S(2)}) collective-permute-start(bf16[32,8192]{1,0:T(8,128)(2,1)} %get-tuple-element.55), channel_id=1, source_target_pairs={{0,4},{1,5},{2,6},{3,7},{4,8},{5,9},{6,10},{7,11},{8,12},{9,13},{1... | collective-permute-start | bytes 1572872 | tf_op jit(solution)/shard_map/ppermute | solution.py:67
  161.8 7.1 %collective-permute-start.32 = (bf16[32,4096]{1,0:T(8,128)(2,1)S(1)}, bf16[32,4096]{1,0:T(8,128)(2,1)}, u32[]{:S(2)}, u32[]{:S(2)}) collective-permute-start(bf16[32,4096]{1,0:T(8,128)(2,1)S(1)} %get-tuple-element.58), channel_id=1, source_target_pairs={{0,12},{1,13},{2,14},{3,15},{4,0},{5,1},{6,2},{7,3},{8,4},{9,5},{1... | collective-permute-start | bytes 786440 | tf_op jit(solution)/shard_map/ppermute | solution.py:67
  165.1 12.5 %collective-permute-start.30 = (bf16[32,8192]{1,0:T(8,128)(2,1)}, bf16[32,8192]{1,0:T(8,128)(2,1)S(1)}, u32[]{:S(2)}, u32[]{:S(2)}) collective-permute-start(bf16[32,8192]{1,0:T(8,128)(2,1)} %get-tuple-element.56), channel_id=1, source_target_pairs={{0,12},{1,13},{2,14},{3,15},{4,0},{5,1},{6,2},{7,3},{8,4},{9,5},{1... | collective-permute-start | bytes 1572872 | tf_op jit(solution)/shard_map/ppermute | solution.py:67
  167.1 9.6 %collective-permute-start.31 = (bf16[32,4096]{1,0:T(8,128)(2,1)}, bf16[32,4096]{1,0:T(8,128)(2,1)S(1)}, u32[]{:S(2)}, u32[]{:S(2)}) collective-permute-start(bf16[32,4096]{1,0:T(8,128)(2,1)} %get-tuple-element.57), channel_id=1, source_target_pairs={{0,8},{1,9},{2,10},{3,11},{4,12},{5,13},{6,14},{7,15},{8,0},{9,1},... | collective-permute-start | bytes 786440 | tf_op jit(solution)/shard_map/ppermute | solution.py:67
  168.9 13.5 %collective-permute-start.33 = (bf16[32,4096]{1,0:T(8,128)(2,1)}, bf16[32,4096]{1,0:T(8,128)(2,1)S(1)}, u32[]{:S(2)}, u32[]{:S(2)}) collective-permute-start(bf16[32,4096]{1,0:T(8,128)(2,1)} %collective-permute-done.32), channel_id=1, source_target_pairs={{0,12},{1,13},{2,14},{3,15},{4,0},{5,1},{6,2},{7,3},{8,4},{9,5},{1... | collective-permute-start | bytes 786440 | tf_op jit(solution)/shard_map/ppermute | solution.py:67
  183.3 6.2 %collective-permute-start.34 = (bf16[8,8192]{1,0:T(8,128)(2,1)S(1)}, bf16[8,8192]{1,0:T(8,128)(2,1)S(1)}, u32[]{:S(2)}, u32[]{:S(2)}) collective-permute-start(bf16[8,8192]{1,0:T(8,128)(2,1)S(1)} %get-tuple-element.60), channel_id=1, source_target_pairs={{0,1},{1,2},{2,3},{3,0},{4,5},{5,6},{6,7},{7,4},{8,9},{9,10},{10,1... | collective-permute-start | bytes 393224 | tf_op jit(solution)/shard_map/ppermute | solution.py:67
  183.4 7.1 %collective-permute-start.35 = (bf16[8,8192]{1,0:T(8,128)(2,1)S(1)}, bf16[8,8192]{1,0:T(8,128)(2,1)S(1)}, u32[]{:S(2)}, u32[]{:S(2)}) collective-permute-start(bf16[8,8192]{1,0:T(8,128)(2,1)S(1)} %get-tuple-element.61), channel_id=1, source_target_pairs={{0,3},{1,0},{2,1},{3,2},{4,7},{5,4},{6,5},{7,6},{8,11},{9,8},{10,9... | collective-permute-start | bytes 393224 | tf_op jit(solution)/shard_map/ppermute | solution.py:67
  186.6 6.5 %collective-permute-start.36 = (bf16[8,8192]{1,0:T(8,128)(2,1)S(1)}, bf16[8,8192]{1,0:T(8,128)(2,1)S(1)}, u32[]{:S(2)}, u32[]{:S(2)}) collective-permute-start(bf16[8,8192]{1,0:T(8,128)(2,1)S(1)} %get-tuple-element.62), channel_id=1, source_target_pairs={{0,2},{1,3},{2,0},{3,1},{4,6},{5,7},{6,4},{7,5},{8,10},{9,11},{10,... | collective-permute-start | bytes 393224 | tf_op jit(solution)/shard_map/ppermute | solution.py:67
  (4 other events, 2.8 us)
